TPU v7x, 32 devices: a whole 2x2x4 slice. The times are simulated.
32 devices in a mesh: omega: 4 (over x, core), row: 4 (over z), col: 2 (over y).
Axes of the slice: x: 2, y: 2, z: 4, core: 2. Of those that a mesh axis runs over, the one named last changes fastest.
Arguments:
- frames: bfloat16 [2, 64, 512, 2048], P(None, 'omega', 'row', 'col'), may hold values from -6 to 6
- omega_taps: float32 [15], replicated, may hold values from 0.1 to 1
- smooth_kernel: float32 [5, 5], replicated, may hold values from 0.05 to 0.15
- spots: int32 [2, 3, 4096], P(None, None, ('omega', 'row', 'col')), may hold values from 0 to 2032, as said below
- counts: int32 [2, 32], P(None, ('omega', 'row', 'col')), may hold values from 1 to 128, as said below
Outputs:
- smoothed: bfloat16 [2, 64, 512, 2048], P(None, 'omega', 'row', 'col')
- scores: float32 [4096, 128], P(('omega', 'row', 'col'))
Inputs may be any that keep to these rules, and one draw needn't show every extreme that they name: `spots`: slot i belongs to block i div 128; its spot's frame lies in that block's frames and its whole 16 x 16 patch lies in that block's rows and columns. `counts`: some block of each slab has all 128 slots live.
All inputs are finite; a program needn't handle non-finite values.
Results may differ from a plain program's by a relative error of at most 0.0022.
Values may be sent and summed in bfloat16 or wider, within the bound.
No kernel may reach another device: no remote copies, remote signals or barrier semaphores. Data moves between devices by JAX's collectives and lax.ppermute only.
A program may use at most 192 MiB of HBM per device.

v0:
```python
import jax
import jax.numpy as jnp
from jax import lax
from jax.sharding import PartitionSpec as P

TAPS = 15
PATCH = 16


def extended_2(block, sides, width):
    for axis, dim in sides:
        count = lax.axis_size(axis)
        forward = [(i, i + 1) for i in range(count - 1)]
        backward = [(target, source) for source, target in forward]
        low = lax.ppermute(
            lax.slice_in_dim(block, block.shape[dim] - width, None, axis=dim), axis, forward
        )
        high = lax.ppermute(lax.slice_in_dim(block, 0, width, axis=dim), axis, backward)
        block = jnp.concatenate([low, block, high], axis=dim)
    return block


def partner(block, axis, apart):
    count = lax.axis_size(axis)
    route = []
    for low in range(count):
        high = low | 1 << apart
        if high != low and high < count:
            route += [(low, high), (high, low)]
    return lax.ppermute(block, axis, route)


def normalize(values, live):
    mean_value = jnp.mean(values, axis=1, keepdims=True)
    centered = values - mean_value
    spread = jnp.mean(centered * centered, axis=1, keepdims=True)
    normed = centered / jnp.sqrt(spread + 1e-05)
    return jnp.where(live[:, None], normed, 0.0).astype(jnp.bfloat16)


def shards(frames, omega_taps, smooth_kernel, spots, counts):
    frame_count = frames.shape[1]
    row_count = frames.shape[2]
    col_count = frames.shape[3]
    first_frame = lax.axis_index("omega") * frame_count
    first_row = lax.axis_index("row") * row_count
    first_col = lax.axis_index("col") * col_count
    frame_total = frame_count * lax.axis_size("omega")
    frame_ids = first_frame + jnp.arange(frame_count, dtype=jnp.int32)
    weights = []
    norm = jnp.zeros((frame_count,), jnp.float32)
    for offset in range(TAPS):
        source = frame_ids + offset - 7
        valid = ((source >= 0) & (source < frame_total)).astype(jnp.float32)
        weights.append(omega_taps[offset] * valid)
        norm = norm + omega_taps[offset] * valid
    extended = extended_2(frames, (("omega", 1),), 7)
    background = jnp.zeros((2, frame_count) + extended.shape[2:], jnp.float32)
    for offset in range(TAPS):
        background = background + weights[offset][None, :, None, None] * extended[
            :, offset : offset + frame_count
        ].astype(jnp.float32)
    center = extended[:, 7 : 7 + frame_count].astype(jnp.float32)
    corrected = center - background / norm[None, :, None, None]
    padded = extended_2(corrected, (("row", 2), ("col", 3)), 2)
    total = jnp.zeros((2, frame_count, row_count, col_count), jnp.float32)
    for row_shift in range(5):
        for col_shift in range(5):
            total = (
                total
                + smooth_kernel[row_shift, col_shift]
                * padded[:, :, row_shift : row_shift + row_count, col_shift : col_shift + col_count]
            )
    smoothed = total.astype(jnp.bfloat16)
    slot_count = spots.shape[2]
    slot_ids = jnp.arange(slot_count, dtype=jnp.int32)
    patch_steps = jnp.arange(PATCH, dtype=jnp.int32)
    col_ids = jnp.arange(col_count, dtype=jnp.int32)

    def patches_of(slab):
        plane_rows = smoothed[slab].reshape(frame_count * row_count, col_count)
        local_frame = spots[slab, 0] - first_frame
        local_row = spots[slab, 1] - first_row
        local_col = spots[slab, 2] - first_col
        row_index = (local_frame * row_count + local_row)[:, None] + patch_steps[None, :]
        picked = jnp.take(plane_rows, row_index.reshape(-1), axis=0).reshape(
            slot_count, PATCH, col_count
        )
        target = local_col[:, None] + patch_steps[None, :]
        selector = (col_ids[None, :, None] == target[:, None, :]).astype(jnp.bfloat16)
        values = jnp.einsum("kuc,kcv->kuv", picked, selector, preferred_element_type=jnp.float32)
        live = slot_ids < counts[slab, 0]
        return normalize(values.reshape(slot_count, PATCH * PATCH), live)

    first = patches_of(0)
    second = patches_of(1)
    for bit_number in range(lax.axis_size(("row", "col")).bit_length() - 1):
        second = partner(second, ("row", "col"), bit_number)
    scores = (
        lax.dot_general(first, second, (((1,), (1,)), ((), ())), preferred_element_type=jnp.float32)
        / 256.0
    )
    return (smoothed, scores)


def solution(mesh):
    return jax.shard_map(
        shards,
        mesh=mesh,
        in_specs=(
            P(None, "omega", "row", "col"),
            P(),
            P(),
            P(None, None, ("omega", "row", "col")),
            P(None, ("omega", "row", "col")),
        ),
        out_specs=(P(None, "omega", "row", "col"), P(("omega", "row", "col"), None)),
        check_vma=False,
    )
```

profile of v0, /device:TPU:2, one launch (start us, length us, event | category | flops | bytes accessed | tf_op | source)
XLA Modules:
  0.0 484.5 jit_solution(1726010764307590298)
XLA Ops:
  0.6 7.5 %fusion.60 = (bf16[2,7,128,1024]{3,2,1,0:T(8,128)(2,1)}, bf16[2,7,128,1024]{3,2,1,0:T(8,128)(2,1)}) fusion(bf16[2,16,128,1024]{3,2,1,0:T(8,128)(2,1)} %param.7), kind=kLoop, calls=%fused_computation.154 | loop fusion | bytes 14680064 | tf_op jit(solution)/shard_map/slice | solution.py:18
  8.1 1.9 collective-permute-start
  10.0 3.6 collective-permute-start.1
  13.7 0.8 subtract_bitcast_fusion
  14.4 0.7 iota_add_fusion
  15.2 0.7 iota_add_fusion.2
  16.0 1.3 fusion.63
  17.4 1.9 fusion.64
  19.3 9.6 %add_add_fusion = (f32[16]{0:T(128)S(1)}, f32[16]{0:T(128)S(1)}, f32[16]{0:T(128)S(1)}, f32[16]{0:T(128)S(1)}, f32[16]{0:T(128)S(1)}, /*index=5*/f32[16]{0:T(128...) fusion(f32[]{:T(128)} %bitcast.2, s32[]{:T(128)S(6)} %mul.424, ...), kind=kLoop, calls=%fused_computation.148 | loop fusion | flops 1424 | bytes 1088 | tf_op jit(solution)/shard_map/add | solution.py:56
  28.9 1.6 fusion.62
  30.4 2.1 fusion.61
  34.3 12.1 %constant_dynamic-update-slice_fusion = (bf16[2,23,128,1024]{3,1,2,0:T(8,128)(2,1)}, bf16[2,16,128,1024]{3,1,2,0:T(8,128)(2,1)}) fusion(bf16[2,16,128,1024]{3,2,1,0:T(8,128)(2,1)} %param.7), kind=kLoop, calls=%fused_computation.124 | loop fusion | bytes 25165824
  46.5 6.2 %collective-permute-done = bf16[2,7,128,1024]{3,2,1,0:T(8,128)(2,1)} collective-permute-done((bf16[2,7,128,1024]{3,2,1,0:T(8,128)(2,1)}, bf16[2,7,128,1024]{3,2,1,0:T(8,128)(2,1)}, u32[]{:S(2)}, u32[]{:S(2)}) %collective-permute-start) | collective-permute-done | bytes 3670048 | tf_op jit(solution)/shard_map/ppermute | solution.py:15
  52.6 6.0 %copy.24 = bf16[2,7,128,1024]{3,1,2,0:T(8,128)(2,1)} copy(bf16[2,7,128,1024]{3,2,1,0:T(8,128)(2,1)} %collective-permute-done) | data formatting | bytes 7340032 | tf_op jit(solution)/shard_map/ppermute | solution.py:15
  58.6 6.2 %copy_dynamic-update-slice_fusion = bf16[2,23,128,1024]{3,1,2,0:T(8,128)(2,1)} fusion(bf16[2,23,128,1024]{3,1,2,0:T(8,128)(2,1)} %get-tuple-element.33, bf16[2,7,128,1024]{3,2,1,0:T(8,128)(2,1)} %collective-permute-done.1), kind=kLoop, calls=%fused_computation.95 | loop fusion | bytes 7864320 | tf_op jit(solution)/shard_map/concatenate | solution.py:19
  64.8 106.8 %convert_subtract_fusion = f32[2,16,128,1024]{3,1,2,0:T(8,128)} fusion(bf16[2,16,128,1024]{3,1,2,0:T(8,128)(2,1)} %get-tuple-element.34, bf16[2,7,128,1024]{3,1,2,0:T(8,128)(2,1)} %copy.24, bf16[2,23,128,1024]{3,1,2,0:T(8,128)(2,1)} %copy_dynamic-update-slice_fusion, f32[16]{0:T(128)S(1)} %get-tuple-element.7, f32[16]{0:T(128)S(1)} %get-tuple-element.22, ...), kind=kLoop, calls=%fused_computation.8 | loop fusion | flops 281018368 | bytes 87557120 | tf_op jit(solution)/shard_map/sub | solution.py:64
  171.6 1.1 fusion.58
  172.7 3.5 collective-permute-start.2
  176.2 1.3 collective-permute-start.3
  178.7 1.4 collective-permute-done.2
  180.0 4.4 collective-permute-done.3
  184.4 4.3 pad_maximum_fusion.6
  188.7 2.8 copy.28
  191.6 3.4 collective-permute-start.4
  195.0 1.3 copy.30
  196.3 1.3 collective-permute-start.5
  197.6 1.1 iota_compare_fusion.5
  198.7 1.5 copy.29
  200.2 2.2 collective-permute-done.5
  202.5 2.6 copy.31
  205.1 30.2 %maximum_maximum_fusion = (f32[2,16,132,1026]{3,1,2,0:T(8,128)}, f32[2,16,132,1026]{3,1,2,0:T(8,128)}) fusion(f32[2,16,2,1024]{3,1,2,0:T(8,128)S(1)} %collective-permute-done.3, f32[2,16,128,1024]{3,1,2,0:T(8,128)} %convert_subtract_fusion, f32[2,16,2,1024]{3,1,2,0:T(8,128)S(1)} %collective-permute-done.2, f32[2,16,132,2]{3,1,2,0:T(8,128)S(1)} %copy.29, ...), kind=kLoop, calls=%fused_computation.10 | loop fusion | flops 26002944 | bytes 52039680 | tf_op jit(solution)/shard_map/concatenate | solution.py:19
  235.3 170.8 %fusion.10 = bf16[2,16,128,1024]{3,1,2,0:T(8,128)(2,1)} fusion(f32[2,16,128,1024]{3,1,2,0:T(8,128)} %convert_subtract_fusion, f32[2,16,2,1024]{3,1,2,0:T(8,128)S(1)} %collective-permute-done.3, f32[2,16,2,1024]{3,1,2,0:T(8,128)S(1)} %collective-permute-done.2, f32[2,16,132,1026]{3,1,2,0:T(8,128)} %get-tuple-element.24, ...), kind=kLoop, calls=%fused_computation.26 | loop fusion | flops 226492416 | bytes 361234528 | tf_op jit(solution)/shard_map/convert_element_type | solution.py:74
  406.1 5.4 %fusion.59 = (bf16[1,16,128,1024]{3,1,2,0:T(8,128)(2,1)S(1)}, bf16[1,16,128,1024]{3,1,2,0:T(8,128)(2,1)}) fusion(bf16[2,16,128,1024]{3,1,2,0:T(8,128)(2,1)} %fusion.10), kind=kLoop, calls=%fused_computation.153 | loop fusion | bytes 16777216 | tf_op jit(solution)/shard_map/slice | solution.py:81
  411.6 4.3 copy.34
  415.8 13.8 %gather_fusion.1 = bf16[2048,1024]{1,0:T(8,128)(2,1)} fusion(bf16[2048,1024]{1,0:T(8,128)(2,1)} %bitcast.74, s32[2048]{0:T(1024)S(1)} %copy-done.2), kind=kCustom, calls=%fused_computation.1.clone | custom fusion | bytes 8396800 | tf_op jit(solution)/shard_map/jit(_take)/gather | solution.py:86
  429.7 2.9 broadcast_select_fusion
  432.6 2.4 fusion.66
  435.5 1.9 multiply_reduce_fusion
  437.9 6.5 %copy.32 = bf16[1,16,128,1024]{3,2,1,0:T(8,128)(2,1)} copy(bf16[1,16,128,1024]{3,1,2,0:T(8,128)(2,1)} %get-tuple-element.30) | data formatting | bytes 8388608 | tf_op jit(solution)/shard_map/slice | solution.py:81
  444.3 13.7 %gather_fusion = bf16[2048,1024]{1,0:T(8,128)(2,1)} fusion(bf16[2048,1024]{1,0:T(8,128)(2,1)} %bitcast.75, s32[2048]{0:T(1024)S(1)} %copy-done.3), kind=kCustom, calls=%fused_computation.clone | custom fusion | bytes 8396800 | tf_op jit(solution)/shard_map/jit(_take)/gather | solution.py:86
  458.0 2.5 broadcast_select_fusion.1
  460.6 2.6 fusion.65
  463.2 1.9 multiply_reduce_fusion.1
  465.1 1.6 collective-permute-start.7
  467.1 2.3 collective-permute-done.7
  469.4 2.6 collective-permute-start.8
  472.0 11.5 %copy.36 = bf16[2,16,128,1024]{3,2,1,0:T(8,128)(2,1)} copy(bf16[2,16,128,1024]{3,1,2,0:T(8,128)(2,1)} %fusion.10) | data formatting | bytes 16777216
  483.5 0.8 convolution_multiply_fusion
  (34 shorter events, 4.6 us)
Async XLA Ops:
  8.1 44.5 %collective-permute-start = (bf16[2,7,128,1024]{3,2,1,0:T(8,128)(2,1)}, bf16[2,7,128,1024]{3,2,1,0:T(8,128)(2,1)}, u32[]{:S(2)}, u32[]{:S(2)}) collective-permute-start(bf16[2,7,128,1024]{3,2,1,0:T(8,128)(2,1)} %get-tuple-element.32), channel_id=1, source_target_pairs={{0,8},{8,16},{16,24},{1,9},{9,17},{17,25},{2,10},{10,18},{18,26},{... | collective-permute-start | bytes 11010056 | tf_op jit(solution)/shard_map/ppermute | solution.py:15
  10.0 48.6 %collective-permute-start.1 = (bf16[2,7,128,1024]{3,2,1,0:T(8,128)(2,1)}, bf16[2,7,128,1024]{3,2,1,0:T(8,128)(2,1)}, u32[]{:S(2)}, u32[]{:S(2)}) collective-permute-start(bf16[2,7,128,1024]{3,2,1,0:T(8,128)(2,1)} %get-tuple-element.31), channel_id=1, source_target_pairs={{8,0},{16,8},{24,16},{9,1},{17,9},{25,17},{10,2},{18,10},{26,18},{... | collective-permute-start | bytes 11010056 | tf_op jit(solution)/shard_map/ppermute | solution.py:18
  172.7 7.4 %collective-permute-start.2 = (f32[2,16,2,1024]{3,1,2,0:T(8,128)S(1)}, f32[2,16,2,1024]{3,1,2,0:T(8,128)S(1)}, u32[]{:S(2)}, u32[]{:S(2)}) collective-permute-start(f32[2,16,2,1024]{3,1,2,0:T(8,128)S(1)} %get-tuple-element.27), channel_id=1, source_target_pairs={{0,2},{2,4},{4,6},{1,3},{3,5},{5,7},{8,10},{10,12},{12,14},{9,11},... | collective-permute-start | bytes 786440 | tf_op jit(solution)/shard_map/ppermute | solution.py:15
  176.2 8.3 %collective-permute-start.3 = (f32[2,16,2,1024]{3,1,2,0:T(8,128)S(1)}, f32[2,16,2,1024]{3,1,2,0:T(8,128)S(1)}, u32[]{:S(2)}, u32[]{:S(2)}) collective-permute-start(f32[2,16,2,1024]{3,1,2,0:T(8,128)S(1)} %get-tuple-element.28), channel_id=1, source_target_pairs={{2,0},{4,2},{6,4},{3,1},{5,3},{7,5},{10,8},{12,10},{14,12},{11,9},... | collective-permute-start | bytes 786440 | tf_op jit(solution)/shard_map/ppermute | solution.py:18
  191.6 7.1 %collective-permute-start.4 = (f32[2,16,132,2]{2,1,3,0:T(8,128)S(1)}, f32[2,16,132,2]{2,1,3,0:T(8,128)S(1)}, u32[]{:S(2)}, u32[]{:S(2)}) collective-permute-start(f32[2,16,132,2]{2,1,3,0:T(8,128)S(1)} %copy.28), channel_id=1, source_target_pairs={{0,1},{2,3},{4,5},{6,7},{8,9},{10,11},{12,13},{14,15},{16,17},{18,... | collective-permute-start | bytes 101384 | tf_op jit(solution)/shard_map/ppermute | solution.py:15
  196.3 6.2 %collective-permute-start.5 = (f32[2,16,132,2]{2,1,3,0:T(8,128)S(1)}, f32[2,16,132,2]{2,1,3,0:T(8,128)S(1)}, u32[]{:S(2)}, u32[]{:S(2)}) collective-permute-start(f32[2,16,132,2]{2,1,3,0:T(8,128)S(1)} %copy.30), channel_id=1, source_target_pairs={{1,0},{3,2},{5,4},{7,6},{9,8},{11,10},{13,12},{15,14},{17,16},{19,... | collective-permute-start | bytes 101384 | tf_op jit(solution)/shard_map/ppermute | solution.py:18
  406.1 9.7 %copy-start.2 = (s32[2048]{0:T(1024)S(1)}, s32[2048]{0:T(1024)}, u32[]{:S(2)}) copy-start(s32[2048]{0:T(1024)} %fusion.57) | copy-start | bytes 24580
  415.8 13.8 %copy-start.5 = (pred[2048]{0:T(1024)(128)(4,1)S(1)}, pred[2048]{0:T(1024)(128)(4,1)}, u32[]{:S(2)}) copy-start(pred[2048]{0:T(1024)(128)(4,1)} %compare_and_fusion) | copy-start | bytes 6148
  415.8 16.7 %copy-start.1 = (s32[128,16]{1,0:T(8,128)S(1)}, s32[128,16]{1,0:T(8,128)}, u32[]{:S(2)}) copy-start(s32[128,16]{1,0:T(8,128)} %get-tuple-element.85) | copy-start | bytes 24580
  429.7 14.7 %copy-start.3 = (s32[2048]{0:T(1024)S(1)}, s32[2048]{0:T(1024)}, u32[]{:S(2)}) copy-start(s32[2048]{0:T(1024)} %fusion.56) | copy-start | bytes 24580
  437.4 27.7 %collective-permute-start.6 = (bf16[128,256]{0,1:T(8,128)(2,1)S(1)}, bf16[128,256]{0,1:T(8,128)(2,1)S(1)}, u32[]{:S(2)}, u32[]{:S(2)}) collective-permute-start(bf16[128,256]{0,1:T(8,128)(2,1)S(1)} %fusion.52), channel_id=1, source_target_pairs={{0,1},{1,0},{2,3},{3,2},{4,5},{5,4},{6,7},{7,6},{8,9},{9,8},{10,11... | collective-permute-start | bytes 196616 | tf_op jit(solution)/shard_map/ppermute | solution.py:30
  444.3 13.7 %copy-start.4 = (pred[2048]{0:T(1024)(128)(4,1)S(1)}, pred[2048]{0:T(1024)(128)(4,1)}, u32[]{:S(2)}) copy-start(pred[2048]{0:T(1024)(128)(4,1)} %compare_and_fusion.1) | copy-start | bytes 6148
  444.3 16.2 %copy-start = (s32[128,16]{1,0:T(8,128)S(1)}, s32[128,16]{1,0:T(8,128)}, u32[]{:S(2)}) copy-start(s32[128,16]{1,0:T(8,128)} %get-tuple-element.87) | copy-start | bytes 24580
  458.0 13.9 %copy-start.6 = (pred[128]{0:T(512)(128)(4,1)S(1)}, pred[128]{0:T(512)(128)(4,1)}, u32[]{:S(2)}) copy-start(pred[128]{0:T(512)(128)(4,1)} %iota_compare_fusion.5) | copy-start | bytes 388
  465.1 4.3 collective-permute-start.7
  469.4 14.1 %collective-permute-start.8 = (bf16[128,256]{0,1:T(8,128)(2,1)S(1)}, bf16[128,256]{0,1:T(8,128)(2,1)S(1)}, u32[]{:S(2)}, u32[]{:S(2)}) collective-permute-start(bf16[128,256]{0,1:T(8,128)(2,1)S(1)} %collective-permute-done.7), channel_id=1, source_target_pairs={{0,4},{4,0},{1,5},{5,1},{2,6},{6,2},{3,7},{7,3},{8,12},{12,8},{9,1... | collective-permute-start | bytes 196616 | tf_op jit(solution)/shard_map/ppermute | solution.py:30
where the time goes:
time: 492 us; the launch traced here: 485 us
  other arithmetic  337 us (68%)
  local copies, waits for them, and re-layouts  104 us (21%)
  starting transfers between devices  19.8 us (4%)
  waiting for transfers between devices  16.4 us (3%)
  matrix products  5.89 us (1%)
    convert_element_type x1, other arithmetic, shards(): smoothed = total.astype(jnp.bfloat16)  171 us
    sub x1, other arithmetic, shards(): corrected = center - background / norm[None, :, None, None]  107 us
    concatenate x1, other arithmetic, extended_2(): block = jnp.concatenate([low, block, high], axis=dim)  30.2 us
    gather x2, local copies, waits for them, and re-layouts, patches_of(): jnp.take(plane_rows, row_index.reshape(-1), axis=0)  27.5 us
    unnamed x16, local copies, waits for them, and re-layouts  23.7 us
    slice x3, local copies, waits for them, and re-layouts, patches_of(): plane_rows = smoothed[slab].reshape(frame_count * row_count, col_count)  16.2 us
  transfers between devices with their start and end apart: 9, of which 5 were waited for; matrix products, arithmetic and copies ran while one was open for 17% of the time, Pallas kernels for 0%

commit v1 on v0

v1 whole, which is shorter than its diff:
```python
import functools
import jax
import jax.numpy as jnp
from jax import lax
from jax.experimental import pallas as pl
from jax.experimental.pallas import tpu as pltpu
from jax.sharding import PartitionSpec as P

TAPS = 15
HALF = TAPS // 2
PATCH = 16
SIDE = 5
REACH = SIDE // 2
TILE = 128
WIN = 48
PAD = 16
bf16 = jnp.bfloat16
f32 = jnp.float32


def shifted(block, axis, step):
    count = lax.axis_size(axis)
    route = [(i, i + step) for i in range(count) if 0 <= i + step < count]
    return lax.ppermute(block, axis, route)


def split(values):
    high = lax.reduce_precision(values, 8, 7)
    return high.astype(bf16), (values - high).astype(bf16)


def omega_matrix(omega_taps, first_frame, frame_count, frame_total):
    out_ids = jnp.arange(frame_count, dtype=jnp.int32)[:, None]
    in_ids = jnp.arange(frame_count + 2 * HALF, dtype=jnp.int32)[None, :]
    source = first_frame + in_ids - HALF
    valid = (source >= 0) & (source < frame_total)
    tap = jnp.where(valid, in_ids - out_ids, -1)
    hit = tap[:, :, None] == jnp.arange(TAPS, dtype=jnp.int32)
    weights = jnp.sum(jnp.where(hit, omega_taps, 0.0), axis=2)
    norm = jnp.sum(weights, axis=1, keepdims=True)
    center = (in_ids - out_ids == HALF).astype(f32)
    matrix = center - weights / norm
    same = jnp.eye(8, dtype=bf16)
    parts = jnp.stack(split(matrix))
    wide = parts[:, :, None, :, None] * same[None, None, :, None, :]
    return wide.reshape(2 * frame_count * 8, (frame_count + 2 * HALF) * 8)


def smooth_matrix(smooth_kernel, rows):
    depth = rows + 2 * PAD
    out_ids = jnp.arange(rows, dtype=jnp.int32)[:, None]
    in_ids = jnp.arange(depth, dtype=jnp.int32)[None, :]
    step = in_ids - out_ids - (PAD - REACH)
    hit = step[None, :, :, None] == jnp.arange(SIDE, dtype=jnp.int32)
    table = jnp.sum(jnp.where(hit, smooth_kernel.T[:, None, None, :], 0.0), axis=3)
    high, low = split(table)
    return jnp.concatenate([high, high, low], axis=2).reshape(SIDE * rows, 3 * depth)


def windows_of(row_count):
    return [(at, min(WIN, row_count - at)) for at in range(0, row_count, WIN)]


def slab_kernel(
    slab, row_step, frame_step, with_scores,
    spots_ref, w1_ref, w2_refs, low_ref, own_ref, high_ref, edge_ref, halo_ref, other_ref,
    out_ref, last_ref, chi, clo, kept, window, flat,
):
    frame_count, row_count, col_count = kept.shape
    half_rows = frame_count * 8
    steps_1 = row_count // row_step
    steps_2 = frame_count // frame_step
    at = pl.program_id(0)

    def filtered(block):
        wide = block.astype(f32)
        outs = []
        for q in range(block.shape[1] // 8):
            part = wide[:, 8 * q : 8 * q + 8, :]
            part = part.reshape(part.shape[0] * 8, part.shape[2]).astype(bf16)
            both = jnp.dot(w1_ref[...], part, preferred_element_type=f32)
            outs.append((both[:half_rows] + both[half_rows:]).reshape(frame_count, 8, -1))
        return outs

    def keep(outs, place, cols):
        value = jnp.concatenate(outs, axis=1)
        high = value.astype(bf16)
        chi[:, place, cols] = high
        clo[:, place, cols] = (value - high.astype(f32)).astype(bf16)

    col_cuts = [(c, min(256, col_count - c)) for c in range(0, col_count, 256)]

    @pl.when(at == 0)
    def _():
        for c, n in col_cuts + [(col_count, TILE)]:
            one = filtered(halo_ref[0, :, :, c : c + n])[0]
            keep([one, one], slice(0, PAD), slice(c, c + n))
            keep([one, one], slice(PAD + row_count, 2 * PAD + row_count), slice(c, c + n))

    @pl.when(at < steps_1)
    def _():
        for h in range(row_step // 16):
            rows = slice(16 * h, 16 * h + 16)
            place = pl.ds(pl.multiple_of(PAD + at * row_step + 16 * h, 16), 16)
            for c, n in col_cuts:
                cols = slice(c, c + n)
                block = jnp.concatenate(
                    [low_ref[:, rows, cols], own_ref[0, :, rows, cols], high_ref[:, rows, cols]],
                    axis=0,
                )
                keep(filtered(block), place, cols)
            keep(filtered(edge_ref[0, :, rows, :]), place, slice(col_count, col_count + TILE))

    @pl.when((at >= steps_1) & (at < steps_1 + steps_2))
    def _():
        def one_frame(k, carry):
            frame = (at - steps_1) * frame_step + k
            for (row, n), w2_ref in zip(windows_of(row_count), w2_refs):
                depth = n + 2 * PAD
                high = chi[frame, row : row + depth, :]
                low = clo[frame, row : row + depth, :]
                stacked = jnp.concatenate([high, low, high], axis=0)
                cols = jnp.dot(w2_ref[...], stacked, preferred_element_type=f32)
                total = cols[REACH * n : (REACH + 1) * n]
                for b in range(SIDE):
                    if b != REACH:
                        turn = (REACH - b) % cols.shape[1]
                        total = total + pltpu.roll(cols[b * n : (b + 1) * n], turn, 1)
                value = total[:, :col_count].astype(bf16)
                out_ref[0, k, row : row + n, :] = value
                kept[frame, row : row + n, :] = value
            return carry

        lax.fori_loop(0, frame_step, one_frame, 0)

    @pl.when(at == steps_1 + steps_2)
    def _():
        slot_count = flat.shape[0] // PATCH
        def some(i8, carry):
            for j in range(8):
                i = i8 * 8 + j
                frame, row, col = spots_ref[0, i], spots_ref[1, i], spots_ref[2, i]
                row_at = pl.multiple_of(jnp.minimum(row // 16 * 16, row_count - 32), 16)
                col_at = pl.multiple_of(jnp.minimum(col // TILE * TILE, col_count - 256), TILE)
                found = kept[frame, pl.ds(row_at, 32), pl.ds(col_at, 256)].astype(f32)
                window[j, :32] = found[:, :TILE]
                window[j, 32:] = found[:, TILE:]
                part = jnp.concatenate(
                    [window[j, pl.ds(row - row_at + k, PATCH), :] for k in (0, 32)], axis=1
                )
                part = pltpu.roll(part, 256 - (col - col_at), 1)[:, :TILE]
                flat[pl.ds(pl.multiple_of(i * PATCH, PATCH), PATCH), :] = part.astype(bf16)
            return carry

        lax.fori_loop(0, slot_count // 8, some, 0)
        lane = lax.broadcasted_iota(jnp.int32, (TILE, PATCH * PATCH), 1)
        sub = lax.broadcasted_iota(jnp.int32, (TILE, PATCH * PATCH), 0)
        spread_out = (lane % PATCH == sub).astype(bf16)
        rows = jnp.dot(flat[...], spread_out, preferred_element_type=f32)
        lane = lax.broadcasted_iota(jnp.int32, rows.shape, 1)
        sub = lax.broadcasted_iota(jnp.int32, rows.shape, 0)
        rows = jnp.where(lane // PATCH == sub % PATCH, rows, 0.0).astype(bf16)
        lane = lax.broadcasted_iota(jnp.int32, (slot_count, rows.shape[0]), 1)
        sub = lax.broadcasted_iota(jnp.int32, (slot_count, rows.shape[0]), 0)
        values = jnp.dot(
            (lane // PATCH == sub).astype(bf16), rows, preferred_element_type=f32
        )
        mean = jnp.sum(values, axis=1, keepdims=True) / (PATCH * PATCH)
        centered = values - mean
        spread = jnp.sum(centered * centered, axis=1, keepdims=True) / (PATCH * PATCH)
        normed = centered / jnp.sqrt(spread + 1e-05)
        slot = lax.broadcasted_iota(jnp.int32, (slot_count, 1), 0)
        normed = jnp.where(slot < spots_ref[3, 0], normed, 0.0).astype(bf16)
        if with_scores:
            last_ref[...] = lax.dot_general(
                normed, other_ref[...], (((1,), (1,)), ((), ())), preferred_element_type=f32
            ) / (PATCH * PATCH)
        else:
            last_ref[...] = normed


def run_slab(slab, smoothed, other, spots, w1, w2s, low, frames, high, edge, halo):
    _, frame_count, row_count, col_count = frames.shape
    slot_count = spots.shape[1]
    row_step, frame_step = 32, 4
    steps_1 = row_count // row_step
    steps_2 = frame_count // frame_step
    wide = col_count + TILE
    near = frame_count + 2 * HALF

    def row_block(at):
        return jnp.minimum(at, steps_1 - 1)

    def whole(array):
        return pl.BlockSpec(array.shape, lambda at: (0,) * array.ndim)

    def body(*refs):
        refs = list(refs)
        spots_ref, w1_ref = refs[:2]
        w2_refs = refs[2 : 2 + len(w2s)]
        refs = refs[2 + len(w2s) :]
        low_ref, own_ref, high_ref, edge_ref, halo_ref = refs[:5]
        refs = refs[5:]
        other_ref = None
        if other is not None:
            other_ref = refs[0]
            refs = refs[2:]
        slab_kernel(
            slab, row_step, frame_step, other is not None,
            spots_ref, w1_ref, w2_refs, low_ref, own_ref, high_ref, edge_ref, halo_ref, other_ref,
            *refs,
        )

    operands = [spots, w1, *w2s, low, frames, high, edge, halo]
    in_specs = [
        pl.BlockSpec(memory_space=pltpu.SMEM),
        whole(w1),
        *[whole(w2) for w2 in w2s],
        pl.BlockSpec((HALF, row_step, col_count), lambda at: (0, row_block(at), 0)),
        pl.BlockSpec((1, frame_count, row_step, col_count), lambda at: (slab, 0, row_block(at), 0)),
        pl.BlockSpec((HALF, row_step, col_count), lambda at: (0, row_block(at), 0)),
        pl.BlockSpec((1, near, row_step, TILE), lambda at: (slab, 0, row_block(at), 0)),
        pl.BlockSpec((1, near, 8, wide), lambda at: (slab, 0, 0, 0)),
    ]
    aliases = {}
    last_shape = jax.ShapeDtypeStruct((slot_count, PATCH * PATCH), bf16)
    if other is not None:
        operands += [other, smoothed]
        in_specs += [whole(other), pl.BlockSpec(memory_space=pl.ANY)]
        aliases = {len(operands) - 1: 0}
        last_shape = jax.ShapeDtypeStruct((slot_count, other.shape[0]), f32)
    return pl.pallas_call(
        body,
        grid=(steps_1 + steps_2 + 1,),
        in_specs=in_specs,
        out_specs=[
            pl.BlockSpec(
                (1, frame_step, row_count, col_count),
                lambda at: (slab, jnp.clip(at - steps_1, 0, steps_2 - 1), 0, 0),
            ),
            pl.BlockSpec(last_shape.shape, lambda at: (0, 0)),
        ],
        out_shape=[jax.ShapeDtypeStruct(frames.shape, bf16), last_shape],
        scratch_shapes=[
            pltpu.VMEM((frame_count, row_count + 2 * PAD, wide), bf16),
            pltpu.VMEM((frame_count, row_count + 2 * PAD, wide), bf16),
            pltpu.VMEM((frame_count, row_count, col_count), bf16),
            pltpu.VMEM((8, 64, TILE), f32),
            pltpu.VMEM((slot_count * PATCH, TILE), bf16),
        ],
        input_output_aliases=aliases,
        compiler_params=pltpu.CompilerParams(vmem_limit_bytes=56 * 1024 * 1024),
        cost_estimate=pl.CostEstimate(
            flops=20_000_000_000, bytes_accessed=16_000_000, transcendentals=0
        ),
        name=f"slab_{slab}",
    )(*operands)


def shards(frames, omega_taps, smooth_kernel, spots, counts):
    _, frame_count, row_count, col_count = frames.shape
    first_frame = lax.axis_index("omega") * frame_count
    first_row = lax.axis_index("row") * row_count
    first_col = lax.axis_index("col") * col_count

    rows = jnp.concatenate([frames[:, :, :REACH], frames[:, :, -REACH:]], axis=2)
    cols = jnp.concatenate([frames[..., :REACH], frames[..., -REACH:]], axis=3)
    rim = jnp.concatenate([rows, jnp.swapaxes(cols, 2, 3)], axis=3)
    rim = jnp.concatenate(
        [shifted(rim[:, -HALF:], "omega", 1), rim, shifted(rim[:, :HALF], "omega", -1)], axis=1
    )
    low1 = shifted(frames[1, -HALF:], "omega", 1)
    high1 = shifted(frames[1, :HALF], "omega", -1)
    low0 = shifted(frames[0, -HALF:], "omega", 1)
    high0 = shifted(frames[0, :HALF], "omega", -1)
    left = shifted(rim[:, :, REACH:, col_count:], "col", 1)
    right = shifted(rim[:, :, :REACH, col_count:], "col", -1)
    place = jnp.arange(2 * REACH, dtype=jnp.int32)
    place = jnp.where(place < REACH, place, TILE - 2 * REACH + place)
    place = (place[:, None] == jnp.arange(TILE, dtype=jnp.int32)[None, :]).astype(bf16)
    edge = jnp.einsum(
        "sfkr,kc->sfrc", jnp.concatenate([right, left], axis=2), place, preferred_element_type=bf16
    )
    ends = jnp.concatenate([edge[:, :, :REACH], edge[:, :, -REACH:]], axis=2)
    line = jnp.concatenate([rim[..., :col_count], ends], axis=3)
    above = shifted(line[:, :, REACH:], "row", 1)
    below = shifted(line[:, :, :REACH], "row", -1)
    gap = jnp.zeros(above.shape[:2] + (8 - 2 * REACH, line.shape[3]), bf16)
    halo = jnp.concatenate([below, gap, above], axis=2)

    w1 = omega_matrix(omega_taps, first_frame, frame_count, frame_count * lax.axis_size("omega"))
    sizes = [n for _, n in windows_of(row_count)]
    w2 = {n: smooth_matrix(smooth_kernel, n) for n in set(sizes)}
    w2s = [w2[n] for n in sizes]
    base = jnp.stack([first_frame, first_row, first_col]).astype(jnp.int32)
    local = spots - base[None, :, None]
    live = jnp.broadcast_to(counts[:, :, None], (2, 1, spots.shape[2]))
    local = jnp.concatenate([local, live], axis=1)

    smoothed, second = run_slab(
        1, None, None, local[1], w1, w2s, low1, frames, high1, edge, halo
    )
    count = lax.axis_size("row") * lax.axis_size("col")
    second = lax.ppermute(second, ("row", "col"), [(i, count - 1 - i) for i in range(count)])
    smoothed, scores = run_slab(
        0, smoothed, second, local[0], w1, w2s, low0, frames, high0, edge, halo
    )
    return (smoothed, scores)


def solution(mesh):
    return jax.shard_map(
        shards,
        mesh=mesh,
        in_specs=(
            P(None, "omega", "row", "col"),
            P(),
            P(),
            P(None, None, ("omega", "row", "col")),
            P(None, ("omega", "row", "col")),
        ),
        out_specs=(P(None, "omega", "row", "col"), P(("omega", "row", "col"), None)),
        check_vma=False,
    )
```

time: 492 us -> 117 us (0.24); the launches traced: 485 us -> 115 us
  other arithmetic: 337 us -> 5.51 us
  local copies, waits for them, and re-layouts: 104 us -> 17.6 us
  Pallas kernels: 0 us -> 54.7 us
  waiting for transfers between devices: 16.4 us -> 4.5 us
  starting transfers between devices: 19.8 us -> 31.3 us
  matrix products: 5.89 us -> 0.88 us
    convert_element_type x3 -> x4, other arithmetic: 171 us -> 0.13 us  [the longest x3 0.12 us: split(): return (high.astype(bf16), (values - high).astype(bf16))]
    sub x2 -> x3, other arithmetic: 108 us -> 0.09 us  [the longest x1 0.07 us: shards(): local = spots - base[None, :, None]]
    pallas_call x0 -> x2, Pallas kernels: none -> 54.7 us  [run_slab(): pl.pallas_call(body, grid=(steps_1 + steps_2 + 1,), in_specs=in_specs, ou...]
    slice x11 -> x4, local copies, waits for them, and re-layouts: 35.7 us -> 3.88 us  [the longest x1 2.03 us: shards(): cols = jnp.concatenate([frames[..., :REACH], frames[..., -REACH:]], axis=3)]
    gather x2 -> x0, local copies, waits for them, and re-layouts: 27.5 us -> none  [patches_of(): jnp.take(plane_rows, row_index.reshape(-1), axis=0)]
    concatenate x1 -> x4, other arithmetic: 30.2 us -> 3.57 us  [the longest x1 1.64 us: shards(): halo = jnp.concatenate([below, gap, above], axis=2)]
    unnamed x16, local copies, waits for them, and re-layouts: 23.7 us -> 2.63 us
    ppermute x9 -> x11, waiting for transfers between devices: 16.4 us -> 4.5 us  [the longest x1 2.95 us: shards(): lax.ppermute(second, ('row', 'col'), [(i, count - 1 - i) for i in range(c...]
  transfers between devices with their start and end apart: 9 -> 11, of which waited for: 5 -> 2; matrix products, arithmetic and copies ran while one was open for 17% -> 15% of each run, Pallas kernels for 0% -> 24%
where the time goes in v1:
time: 117 us; the launch traced here: 115 us
  Pallas kernels  54.7 us (47%)
  starting transfers between devices  31.3 us (27%)
  local copies, waits for them, and re-layouts  17.6 us (15%)
  other arithmetic  5.51 us (5%)
  waiting for transfers between devices  4.5 us (4%)
    pallas_call x2, Pallas kernels, run_slab(): pl.pallas_call(body, grid=(steps_1 + steps_2 + 1,), in_specs=in_specs, ou...  54.7 us
    ppermute x10, starting transfers between devices, shifted(): return lax.ppermute(block, axis, route)  27 us
    squeeze x1, local copies, waits for them, and re-layouts, shards(): high1 = shifted(frames[1, :HALF], 'omega', -1)  6.74 us
    ppermute x1, starting transfers between devices, shards(): lax.ppermute(second, ('row', 'col'), [(i, count - 1 - i) for i in range(c...  4.31 us
    mul x2, local copies, waits for them, and re-layouts, omega_matrix(): wide = parts[:, :, None, :, None] * same[None, None, :, None, :]  4.02 us
    ppermute x1, waiting for transfers between devices, shards(): lax.ppermute(second, ('row', 'col'), [(i, count - 1 - i) for i in range(c...  2.95 us
    unnamed x16, local copies, waits for them, and re-layouts  2.63 us
  transfers between devices with their start and end apart: 11, of which 2 were waited for; matrix products, arithmetic and copies ran while one was open for 15% of the time, Pallas kernels for 24%

profile of v1, /device:TPU:2, one launch (start us, length us, event | category | flops | bytes accessed | tf_op | source)
XLA Modules:
  0.0 115.5 jit_solution(15072245657893989349)
XLA Ops:
  0.6 1.4 %fusion.23 = (bf16[2,16,2,1024]{3,2,1,0:T(2,128)(2,1)S(1)}, bf16[2,16,2,1024]{3,2,1,0:T(2,128)(2,1)S(1)}) fusion(bf16[2,16,128,1024]{3,2,1,0:T(8,128)(2,1)} %refs_6_.3), kind=kLoop, calls=%fused_computation.66 | loop fusion | bytes 524288 | tf_op jit(solution)/shard_map/slice | solution.py:266
  2.0 2.0 %fusion.24 = (bf16[2,16,128,2]{3,2,1,0:T(8,128)(2,1)S(1)}, bf16[2,16,128,2]{3,2,1,0:T(8,128)(2,1)S(1)}) fusion(bf16[2,16,128,1024]{3,2,1,0:T(8,128)(2,1)} %refs_6_.3), kind=kLoop, calls=%fused_computation.67 | loop fusion | bytes 65536 | tf_op jit(solution)/shard_map/slice | solution.py:267
  4.1 0.4 copy.37
  4.5 0.4 copy.38
  4.9 0.3 pad_maximum_fusion.4
  5.2 1.9 %collective-permute-start.2 = (bf16[2,7,4,1152]{3,2,1,0:T(4,128)(2,1)S(1)}, bf16[2,7,4,1152]{3,2,1,0:T(4,128)(2,1)S(1)}, u32[]{:S(2)}, u32[]{:S(2)}) collective-permute-start(bf16[2,7,4,1152]{3,2,1,0:T(4,128)(2,1)S(1)} %get-tuple-element.22), channel_id=1, source_target_pairs={{0,8},{8,16},{16,24},{1,9},{9,17},{17,25},{2,10},{10,18},{18,26},{... | collective-permute-start | bytes 387080 | tf_op jit(solution)/shard_map/ppermute | solution.py:24
  7.1 0.0 copy-start.1
  7.1 0.0 copy-start.3
  7.1 3.6 %collective-permute-start.3 = (bf16[2,7,4,1152]{3,2,1,0:T(4,128)(2,1)S(1)}, bf16[2,7,4,1152]{3,2,1,0:T(4,128)(2,1)S(1)}, u32[]{:S(2)}, u32[]{:S(2)}) collective-permute-start(bf16[2,7,4,1152]{3,2,1,0:T(4,128)(2,1)S(1)} %get-tuple-element.23), channel_id=1, source_target_pairs={{8,0},{16,8},{24,16},{9,1},{17,9},{25,17},{10,2},{18,10},{26,18},{... | collective-permute-start | bytes 387080 | tf_op jit(solution)/shard_map/ppermute | solution.py:24
  10.8 6.7 %slice_bitcast_fusion = (bf16[7,128,1024]{2,1,0:T(8,128)(2,1)}, bf16[7,128,1024]{2,1,0:T(8,128)(2,1)}, bf16[7,128,1024]{2,1,0:T(8,128)(2,1)}, bf16[7,128,1024]{2,1,0:T(8,128)(2,1)}) fusion(bf16[2,16,128,1024]{3,2,1,0:T(8,128)(2,1)} %refs_6_.3), kind=kLoop, calls=%fused_computation | loop fusion | bytes 14680064 | tf_op jit(solution)/shard_map/squeeze | solution.py:273
  17.5 2.0 %collective-permute-start.9 = (bf16[7,128,1024]{2,1,0:T(8,128)(2,1)}, bf16[7,128,1024]{2,1,0:T(8,128)(2,1)}, u32[]{:S(2)}, u32[]{:S(2)}) collective-permute-start(bf16[7,128,1024]{2,1,0:T(8,128)(2,1)} %get-tuple-element.8), channel_id=1, source_target_pairs={{8,0},{16,8},{24,16},{9,1},{17,9},{25,17},{10,2},{18,10},{26,18},{... | collective-permute-start | bytes 5505032 | tf_op jit(solution)/shard_map/ppermute | solution.py:24
  19.6 3.7 %collective-permute-start.8 = (bf16[7,128,1024]{2,1,0:T(8,128)(2,1)}, bf16[7,128,1024]{2,1,0:T(8,128)(2,1)}, u32[]{:S(2)}, u32[]{:S(2)}) collective-permute-start(bf16[7,128,1024]{2,1,0:T(8,128)(2,1)} %get-tuple-element.9), channel_id=1, source_target_pairs={{0,8},{8,16},{16,24},{1,9},{9,17},{17,25},{2,10},{10,18},{18,26},{... | collective-permute-start | bytes 5505032 | tf_op jit(solution)/shard_map/ppermute | solution.py:24
  23.3 1.9 %collective-permute-start.1 = (bf16[7,128,1024]{2,1,0:T(8,128)(2,1)}, bf16[7,128,1024]{2,1,0:T(8,128)(2,1)}, u32[]{:S(2)}, u32[]{:S(2)}) collective-permute-start(bf16[7,128,1024]{2,1,0:T(8,128)(2,1)} %get-tuple-element.10), channel_id=1, source_target_pairs={{8,0},{16,8},{24,16},{9,1},{17,9},{25,17},{10,2},{18,10},{26,18},{... | collective-permute-start | bytes 5505032 | tf_op jit(solution)/shard_map/ppermute | solution.py:24
  25.3 0.1 copy.30
  25.4 0.2 select_reduce_fusion.3
  25.5 0.1 reduce-precision_convert_fusion.2
  25.6 0.1 copy.29
  25.8 0.1 select_reduce_fusion.1
  25.9 0.1 select_reduce_fusion
  26.1 0.2 broadcast_multiply_fusion
  26.3 0.1 pad_add_fusion.1
  26.4 0.1 copy_subtract_fusion
  26.5 0.1 pad_maximum_fusion.8
  26.5 1.3 %collective-permute-start.4 = (bf16[2,30,2,128]{3,2,1,0:T(2,128)(2,1)S(1)}, bf16[2,30,2,128]{3,2,1,0:T(2,128)(2,1)S(1)}, u32[]{:S(2)}, u32[]{:S(2)}) collective-permute-start(bf16[2,30,2,128]{3,2,1,0:T(2,128)(2,1)S(1)} %get-tuple-element.20), channel_id=1, source_target_pairs={{1,0},{3,2},{5,4},{7,6},{9,8},{11,10},{13,12},{15,14},{17,16},{19,... | collective-permute-start | bytes 92168 | tf_op jit(solution)/shard_map/ppermute | solution.py:24
  27.8 4.5 %collective-permute-start.5 = (bf16[2,30,2,128]{3,2,1,0:T(2,128)(2,1)S(1)}, bf16[2,30,2,128]{3,2,1,0:T(2,128)(2,1)S(1)}, u32[]{:S(2)}, u32[]{:S(2)}) collective-permute-start(bf16[2,30,2,128]{3,2,1,0:T(2,128)(2,1)S(1)} %get-tuple-element.21), channel_id=1, source_target_pairs={{0,1},{2,3},{4,5},{6,7},{8,9},{10,11},{12,13},{14,15},{16,17},{18,... | collective-permute-start | bytes 92168 | tf_op jit(solution)/shard_map/ppermute | solution.py:24
  32.4 0.0 copy-start.6
  32.4 1.5 %collective-permute-done.5 = bf16[2,30,2,128]{3,2,1,0:T(2,128)(2,1)S(1)} collective-permute-done((bf16[2,30,2,128]{3,2,1,0:T(2,128)(2,1)S(1)}, bf16[2,30,2,128]{3,2,1,0:T(2,128)(2,1)S(1)}, u32[]{:S(2)}, u32[]{:S(2)}) %collective-permute-start.5) | collective-permute-done | bytes 30752 | tf_op jit(solution)/shard_map/ppermute | solution.py:24
  34.0 0.9 fusion.9.refs_8_
  34.9 0.1 fusion.25
  34.9 1.2 %copy-done = bf16[2,30,128,128]{3,2,1,0:T(8,128)(2,1)} copy-done((bf16[2,30,128,128]{3,2,1,0:T(8,128)(2,1)}, bf16[2,30,128,128]{3,2,1,0:T(8,128)(2,1)S(1)}, u32[]{:S(2)}) %copy-start) | copy-done | bytes 1966104
  36.1 0.5 fusion.5
  36.6 0.4 fusion.26
  37.0 1.3 %collective-permute-start.6 = (bf16[2,30,2,1152]{3,2,1,0:T(2,128)(2,1)S(1)}, bf16[2,30,2,1152]{3,2,1,0:T(2,128)(2,1)S(1)}, u32[]{:S(2)}, u32[]{:S(2)}) collective-permute-start(bf16[2,30,2,1152]{3,2,1,0:T(2,128)(2,1)S(1)} %get-tuple-element.18), channel_id=1, source_target_pairs={{2,0},{4,2},{6,4},{3,1},{5,3},{7,5},{10,8},{12,10},{14,12},{11,9},... | collective-permute-start | bytes 829448 | tf_op jit(solution)/shard_map/ppermute | solution.py:24
  38.3 4.6 %collective-permute-start.7 = (bf16[2,30,2,1152]{3,2,1,0:T(2,128)(2,1)S(1)}, bf16[2,30,2,1152]{3,2,1,0:T(2,128)(2,1)S(1)}, u32[]{:S(2)}, u32[]{:S(2)}) collective-permute-start(bf16[2,30,2,1152]{3,2,1,0:T(2,128)(2,1)S(1)} %get-tuple-element.19), channel_id=1, source_target_pairs={{0,2},{2,4},{4,6},{1,3},{3,5},{5,7},{8,10},{10,12},{12,14},{9,11},... | collective-permute-start | bytes 829448 | tf_op jit(solution)/shard_map/ppermute | solution.py:24
  42.9 0.1 broadcast_in_dim.92
  42.9 0.6 fusion.18
  43.5 3.3 %mul.32 = bf16[256,240]{0,1:T(8,128)(2,1)S(1)} reshape(bf16[2,16,8,30,8]{2,1,0,4,3:T(8,128)(2,1)S(1)} %broadcast_multiply_fusion) | data formatting | bytes 245760 | tf_op jit(solution)/shard_map/mul | solution.py:45
  46.8 0.8 copy.35.refs_1_
  47.6 0.1 pad.1.clone
  47.7 0.7 pad_maximum_fusion.6.refs_4_
  48.4 0.8 pad_maximum_fusion.5.refs_2_.refs_3_
  49.1 2.1 %collective-permute-start = (bf16[7,128,1024]{2,1,0:T(8,128)(2,1)}, bf16[7,128,1024]{2,1,0:T(8,128)(2,1)S(1)}, u32[]{:S(2)}, u32[]{:S(2)}) collective-permute-start(bf16[7,128,1024]{2,1,0:T(8,128)(2,1)} %get-tuple-element.11), channel_id=1, source_target_pairs={{0,8},{8,16},{16,24},{1,9},{9,17},{17,25},{2,10},{10,18},{18,26},{... | collective-permute-start | bytes 5505032 | tf_op jit(solution)/shard_map/ppermute | solution.py:24
  51.3 1.6 %pad_maximum_fusion.refs_9_ = bf16[2,30,8,1152]{3,2,1,0:T(8,128)(2,1)} fusion(bf16[2,30,2,1152]{3,2,1,0:T(2,128)(2,1)S(1)} %collective-permute-done.7, bf16[2,30,2,1152]{3,2,1,0:T(2,128)(2,1)S(1)} %collective-permute-done.6, bf16[8]{0:T(256)(128)(2,1)S(1)} %pad.1.clone), kind=kLoop, calls=%fused_computation.8 | loop fusion | flops 3317760 | bytes 1658896 | tf_op jit(solution)/shard_map/concatenate | solution.py:289
  52.9 27.2 %slab_1.1 = (bf16[2,16,128,1024]{3,2,1,0:T(8,128)(2,1)}, bf16[128,256]{1,0:T(8,128)(2,1)}) custom-call(s32[4,128]{1,0:T(4,128)} %get-tuple-element.30.refs_0_, bf16[256,240]{1,0:T(8,128)(2,1)} %copy.35.refs_1_, bf16[240,240]{1,0:T(8,128)(2,1)} %pad_maximum_fusion.5.refs_2_.refs_3_, bf16[240,240]{1,0:T(8,128)(2,1)} %pad_maximum_fusion.5.refs_2_.refs_3_, ...), custom_call_target="tpu_custom_call" | custom-call | flops 20000000000 | bytes 16000000 | tf_op jit(solution)/shard_map/slab_1/pallas_call | solution.py:232
  80.1 4.3 %collective-permute-start.10 = (bf16[128,256]{1,0:T(8,128)(2,1)}, bf16[128,256]{1,0:T(8,128)(2,1)S(1)}, u32[]{:S(2)}, u32[]{:S(2)}) collective-permute-start(bf16[128,256]{1,0:T(8,128)(2,1)} %get-tuple-element.4), channel_id=1, source_target_pairs={{0,7},{1,6},{2,5},{3,4},{4,3},{5,2},{6,1},{7,0},{8,15},{9,14},{10,... | collective-permute-start | bytes 196616 | tf_op jit(solution)/shard_map/ppermute | solution.py:304
  84.4 3.0 %collective-permute-done.10.refs_10_ = bf16[128,256]{1,0:T(8,128)(2,1)S(1)} collective-permute-done((bf16[128,256]{1,0:T(8,128)(2,1)}, bf16[128,256]{1,0:T(8,128)(2,1)S(1)}, u32[]{:S(2)}, u32[]{:S(2)}) %collective-permute-start.10) | collective-permute-done | bytes 65568 | tf_op jit(solution)/shard_map/ppermute | solution.py:304
  87.3 0.6 copy-done.5
  88.0 27.5 %slab_0.1 = (bf16[2,16,128,1024]{3,2,1,0:T(8,128)(2,1)}, f32[128,128]{1,0:T(8,128)}) custom-call(s32[4,128]{1,0:T(4,128)} %get-tuple-element.31.refs_0_, bf16[256,240]{1,0:T(8,128)(2,1)} %copy.35.refs_1_, bf16[240,240]{1,0:T(8,128)(2,1)} %pad_maximum_fusion.5.refs_2_.refs_3_, ...), custom_call_target="tpu_custom_call", output_to_operand_aliasing={{0}: (11, {})} | custom-call | flops 20000000000 | bytes 16000000 | tf_op jit(solution)/shard_map/slab_0/pallas_call | solution.py:232
  (31 shorter events, 0.2 us)
Async XLA Ops:
  5.2 21.3 %collective-permute-start.2 = (bf16[2,7,4,1152]{3,2,1,0:T(4,128)(2,1)S(1)}, bf16[2,7,4,1152]{3,2,1,0:T(4,128)(2,1)S(1)}, u32[]{:S(2)}, u32[]{:S(2)}) collective-permute-start(bf16[2,7,4,1152]{3,2,1,0:T(4,128)(2,1)S(1)} %get-tuple-element.22), channel_id=1, source_target_pairs={{0,8},{8,16},{16,24},{1,9},{9,17},{17,25},{2,10},{10,18},{18,26},{... | collective-permute-start | bytes 387080 | tf_op jit(solution)/shard_map/ppermute | solution.py:24
  7.1 18.2 %copy-start.1 = (f32[5,5]{1,0:T(8,128)S(1)}, f32[5,5]{1,0:T(8,128)}, u32[]{:S(2)}) copy-start(f32[5,5]{1,0:T(8,128)} %param.7) | copy-start | bytes 304
  7.1 18.3 %copy-start.3 = (f32[15]{0:T(128)S(1)}, f32[15]{0:T(128)}, u32[]{:S(2)}) copy-start(f32[15]{0:T(128)} %param.6) | copy-start | bytes 184
  7.1 19.4 %collective-permute-start.3 = (bf16[2,7,4,1152]{3,2,1,0:T(4,128)(2,1)S(1)}, bf16[2,7,4,1152]{3,2,1,0:T(4,128)(2,1)S(1)}, u32[]{:S(2)}, u32[]{:S(2)}) collective-permute-start(bf16[2,7,4,1152]{3,2,1,0:T(4,128)(2,1)S(1)} %get-tuple-element.23), channel_id=1, source_target_pairs={{8,0},{16,8},{24,16},{9,1},{17,9},{25,17},{10,2},{18,10},{26,18},{... | collective-permute-start | bytes 387080 | tf_op jit(solution)/shard_map/ppermute | solution.py:24
  17.5 8.9 %copy-start.2 = (s32[2,3,128]{2,0,1:T(2,128)S(1)}, s32[2,3,128]{2,0,1:T(2,128)}, u32[]{:S(2)}) copy-start(s32[2,3,128]{2,0,1:T(2,128)} %param.8) | copy-start | bytes 9220
  17.5 35.4 %collective-permute-start.9 = (bf16[7,128,1024]{2,1,0:T(8,128)(2,1)}, bf16[7,128,1024]{2,1,0:T(8,128)(2,1)}, u32[]{:S(2)}, u32[]{:S(2)}) collective-permute-start(bf16[7,128,1024]{2,1,0:T(8,128)(2,1)} %get-tuple-element.8), channel_id=1, source_target_pairs={{8,0},{16,8},{24,16},{9,1},{17,9},{25,17},{10,2},{18,10},{26,18},{... | collective-permute-start | bytes 5505032 | tf_op jit(solution)/shard_map/ppermute | solution.py:24
  19.6 33.3 %collective-permute-start.8 = (bf16[7,128,1024]{2,1,0:T(8,128)(2,1)}, bf16[7,128,1024]{2,1,0:T(8,128)(2,1)}, u32[]{:S(2)}, u32[]{:S(2)}) collective-permute-start(bf16[7,128,1024]{2,1,0:T(8,128)(2,1)} %get-tuple-element.9), channel_id=1, source_target_pairs={{0,8},{8,16},{16,24},{1,9},{9,17},{17,25},{2,10},{10,18},{18,26},{... | collective-permute-start | bytes 5505032 | tf_op jit(solution)/shard_map/ppermute | solution.py:24
  23.3 61.1 %collective-permute-start.1 = (bf16[7,128,1024]{2,1,0:T(8,128)(2,1)}, bf16[7,128,1024]{2,1,0:T(8,128)(2,1)}, u32[]{:S(2)}, u32[]{:S(2)}) collective-permute-start(bf16[7,128,1024]{2,1,0:T(8,128)(2,1)} %get-tuple-element.10), channel_id=1, source_target_pairs={{8,0},{16,8},{24,16},{9,1},{17,9},{25,17},{10,2},{18,10},{26,18},{... | collective-permute-start | bytes 5505032 | tf_op jit(solution)/shard_map/ppermute | solution.py:24
  26.5 5.9 %collective-permute-start.4 = (bf16[2,30,2,128]{3,2,1,0:T(2,128)(2,1)S(1)}, bf16[2,30,2,128]{3,2,1,0:T(2,128)(2,1)S(1)}, u32[]{:S(2)}, u32[]{:S(2)}) collective-permute-start(bf16[2,30,2,128]{3,2,1,0:T(2,128)(2,1)S(1)} %get-tuple-element.20), channel_id=1, source_target_pairs={{1,0},{3,2},{5,4},{7,6},{9,8},{11,10},{13,12},{15,14},{17,16},{19,... | collective-permute-start | bytes 92168 | tf_op jit(solution)/shard_map/ppermute | solution.py:24
  27.8 6.1 %collective-permute-start.5 = (bf16[2,30,2,128]{3,2,1,0:T(2,128)(2,1)S(1)}, bf16[2,30,2,128]{3,2,1,0:T(2,128)(2,1)S(1)}, u32[]{:S(2)}, u32[]{:S(2)}) collective-permute-start(bf16[2,30,2,128]{3,2,1,0:T(2,128)(2,1)S(1)} %get-tuple-element.21), channel_id=1, source_target_pairs={{0,1},{2,3},{4,5},{6,7},{8,9},{10,11},{12,13},{14,15},{16,17},{18,... | collective-permute-start | bytes 92168 | tf_op jit(solution)/shard_map/ppermute | solution.py:24
  32.4 10.5 %copy-start.6 = (s32[2,1]{0,1:T(1,128)S(1)}, s32[2,1]{0,1:T(1,128)}, u32[]{:S(2)}) copy-start(s32[2,1]{0,1:T(1,128)} %param.9) | copy-start | bytes 28
  34.8 1.3 %copy-start = (bf16[2,30,128,128]{3,2,1,0:T(8,128)(2,1)}, bf16[2,30,128,128]{3,2,1,0:T(8,128)(2,1)S(1)}, u32[]{:S(2)}) copy-start(bf16[2,30,128,128]{3,2,1,0:T(8,128)(2,1)S(1)} %fusion.9.refs_8_) | copy-start | bytes 5898244
  37.0 12.1 %collective-permute-start.6 = (bf16[2,30,2,1152]{3,2,1,0:T(2,128)(2,1)S(1)}, bf16[2,30,2,1152]{3,2,1,0:T(2,128)(2,1)S(1)}, u32[]{:S(2)}, u32[]{:S(2)}) collective-permute-start(bf16[2,30,2,1152]{3,2,1,0:T(2,128)(2,1)S(1)} %get-tuple-element.18), channel_id=1, source_target_pairs={{2,0},{4,2},{6,4},{3,1},{5,3},{7,5},{10,8},{12,10},{14,12},{11,9},... | collective-permute-start | bytes 829448 | tf_op jit(solution)/shard_map/ppermute | solution.py:24
  38.3 13.0 %collective-permute-start.7 = (bf16[2,30,2,1152]{3,2,1,0:T(2,128)(2,1)S(1)}, bf16[2,30,2,1152]{3,2,1,0:T(2,128)(2,1)S(1)}, u32[]{:S(2)}, u32[]{:S(2)}) collective-permute-start(bf16[2,30,2,1152]{3,2,1,0:T(2,128)(2,1)S(1)} %get-tuple-element.19), channel_id=1, source_target_pairs={{0,2},{2,4},{4,6},{1,3},{3,5},{5,7},{8,10},{10,12},{12,14},{9,11},... | collective-permute-start | bytes 829448 | tf_op jit(solution)/shard_map/ppermute | solution.py:24
  49.1 35.2 %collective-permute-start = (bf16[7,128,1024]{2,1,0:T(8,128)(2,1)}, bf16[7,128,1024]{2,1,0:T(8,128)(2,1)S(1)}, u32[]{:S(2)}, u32[]{:S(2)}) collective-permute-start(bf16[7,128,1024]{2,1,0:T(8,128)(2,1)} %get-tuple-element.11), channel_id=1, source_target_pairs={{0,8},{8,16},{16,24},{1,9},{9,17},{17,25},{2,10},{10,18},{18,26},{... | collective-permute-start | bytes 5505032 | tf_op jit(solution)/shard_map/ppermute | solution.py:24
  80.1 7.3 %collective-permute-start.10 = (bf16[128,256]{1,0:T(8,128)(2,1)}, bf16[128,256]{1,0:T(8,128)(2,1)S(1)}, u32[]{:S(2)}, u32[]{:S(2)}) collective-permute-start(bf16[128,256]{1,0:T(8,128)(2,1)} %get-tuple-element.4), channel_id=1, source_target_pairs={{0,7},{1,6},{2,5},{3,4},{4,3},{5,2},{6,1},{7,0},{8,15},{9,14},{10,... | collective-permute-start | bytes 196616 | tf_op jit(solution)/shard_map/ppermute | solution.py:304
  84.4 3.0 %copy-start.4 = (bf16[7,128,1024]{2,1,0:T(8,128)(2,1)}, bf16[7,128,1024]{2,1,0:T(8,128)(2,1)S(1)}, u32[]{:S(2)}) copy-start(bf16[7,128,1024]{2,1,0:T(8,128)(2,1)S(1)} %collective-permute-done.refs_5_) | copy-start | bytes 5505028
  87.3 0.6 copy-start.5

commit v2 on v1

v2 whole, which is shorter than its diff:
```python
import jax
import jax.numpy as jnp
from jax import lax
from jax.experimental import pallas as pl
from jax.experimental.pallas import tpu as pltpu
from jax.sharding import PartitionSpec as P

TAPS = 15
HALF = TAPS // 2
PATCH = 16
SIDE = 5
REACH = SIDE // 2
TILE = 128
BLOCK = 16
bf16 = jnp.bfloat16
f32 = jnp.float32


def shifted(block, axis, step):
    count = lax.axis_size(axis)
    route = [(i, i + step) for i in range(count) if 0 <= i + step < count]
    return lax.ppermute(block, axis, route)


def split(values):
    high = lax.reduce_precision(values, 8, 7)
    return high.astype(bf16), (values - high).astype(bf16)


def omega_matrix(omega_taps, first_frame, frame_count, frame_total):
    out_ids = jnp.arange(frame_count, dtype=jnp.int32)[:, None]
    in_ids = jnp.arange(frame_count + 2 * HALF, dtype=jnp.int32)[None, :]
    source = first_frame + in_ids - HALF
    valid = (source >= 0) & (source < frame_total)
    tap = jnp.where(valid, in_ids - out_ids, -1)
    hit = tap[:, :, None] == jnp.arange(TAPS, dtype=jnp.int32)
    weights = jnp.sum(jnp.where(hit, omega_taps, 0.0), axis=2)
    norm = jnp.sum(weights, axis=1, keepdims=True)
    center = (in_ids - out_ids == HALF).astype(f32)
    matrix = center - weights / norm
    return jnp.stack(split(matrix), axis=1).reshape(2 * frame_count, matrix.shape[1])


def smooth_matrix(smooth_kernel):
    depth = 3 * BLOCK
    out_ids = jnp.arange(BLOCK, dtype=jnp.int32)[:, None]
    in_ids = jnp.arange(depth, dtype=jnp.int32)[None, :]
    step = in_ids - out_ids - (BLOCK - REACH)
    hit = step[None, :, :, None] == jnp.arange(SIDE, dtype=jnp.int32)
    table = jnp.sum(jnp.where(hit, smooth_kernel.T[:, None, None, :], 0.0), axis=3)
    high, low = split(table)
    return jnp.concatenate([high, high, low], axis=2).reshape(SIDE * BLOCK, 3 * depth)


def iota(shape, dim):
    return lax.broadcasted_iota(jnp.int32, shape, dim)


def slab_kernel(
    row_step, frame_step,
    spots_ref, taps_ref, w2_ref, low_ref, own_ref, high_ref, edge_ref, halo_ref,
    out_ref, last_ref, w1, chi, clo, kept, window, flat,
):
    frame_count, row_count, col_count = kept.shape
    near = taps_ref.shape[1]
    tiles = col_count // TILE
    steps_1 = row_count // row_step
    steps_2 = frame_count // frame_step
    at = pl.program_id(0)

    def filtered(block):
        part = block.reshape(near * 8, block.shape[2]).astype(bf16)
        both = jnp.dot(w1[...], part, preferred_element_type=f32)
        both = both.reshape(frame_count, 2, 8, block.shape[2])
        return both[:, 0] + both[:, 1]

    def keep(value, tile, place):
        high = value.astype(bf16)
        chi[:, tile, place, :] = high
        clo[:, tile, place, :] = (value - high.astype(f32)).astype(bf16)

    @pl.when(at == 0)
    def _():
        count = 2 * frame_count
        tall = (iota((8 * count, count), 0) // 8 == iota((8 * count, count), 1)).astype(bf16)
        wide = (iota((near, 8 * near), 1) // 8 == iota((near, 8 * near), 0)).astype(bf16)
        full = jnp.dot(tall, taps_ref[...], preferred_element_type=f32).astype(bf16)
        full = jnp.dot(full, wide, preferred_element_type=f32)
        same = iota(full.shape, 0) % 8 == iota(full.shape, 1) % 8
        w1[...] = jnp.where(same, full, 0.0).astype(bf16)
        for tile in range(tiles + 1):
            cols = slice(tile * TILE, tile * TILE + TILE)
            one = filtered(halo_ref[0, :, :, cols].astype(f32))
            two = jnp.concatenate([one, one], axis=1)
            keep(two, tile, slice(0, BLOCK))
            keep(two, tile, slice(BLOCK + row_count, 2 * BLOCK + row_count))

    @pl.when(at < steps_1)
    def _():
        for h in range(row_step // BLOCK):
            rows = slice(BLOCK * h, BLOCK * h + BLOCK)
            place = pl.ds(pl.multiple_of(BLOCK + at * row_step + BLOCK * h, BLOCK), BLOCK)
            for tile in range(0, tiles, 2):
                cols = slice(tile * TILE, (tile + 2) * TILE)
                block = jnp.concatenate(
                    [low_ref[:, rows, cols], own_ref[0, :, rows, cols], high_ref[:, rows, cols]],
                    axis=0,
                ).astype(f32)
                value = jnp.concatenate([filtered(block[:, :8]), filtered(block[:, 8:])], axis=1)
                keep(value[..., :TILE], tile, place)
                keep(value[..., TILE:], tile + 1, place)
            block = edge_ref[0, :, rows, :].astype(f32)
            value = filtered(jnp.concatenate([block[:, :8], block[:, 8:]], axis=2))
            value = jnp.concatenate([value[..., :TILE], value[..., TILE:]], axis=1)
            keep(value, tiles, place)

    @pl.when((at >= steps_1) & (at < steps_1 + steps_2))
    def _():
        lane = iota((BLOCK, TILE), 1)
        edge_of = [lane < 2, lane < 1, None, lane >= TILE - 1, lane >= TILE - 2]

        def one_frame(k, carry):
            frame = (at - steps_1) * frame_step + k
            for row in range(0, row_count, BLOCK):
                turned = {}
                order = [tiles] + list(range(tiles))
                for p in range(0, len(order), 2):
                    pair = order[p : p + 2]
                    parts = []
                    for tile in pair:
                        high = chi[frame, tile, row : row + 3 * BLOCK, :]
                        low = clo[frame, tile, row : row + 3 * BLOCK, :]
                        parts.append(jnp.concatenate([high, low, high], axis=0))
                    both = jnp.dot(
                        w2_ref[...], jnp.concatenate(parts, axis=1), preferred_element_type=f32
                    )
                    for q, tile in enumerate(pair):
                        for b in range(SIDE):
                            part = both[b * BLOCK : (b + 1) * BLOCK, q * TILE : (q + 1) * TILE]
                            if b != REACH:
                                part = pltpu.roll(part, (REACH - b) % TILE, 1)
                            turned[b, tile] = part
                for tile in range(tiles):
                    total = turned[REACH, tile]
                    for b in range(SIDE):
                        if b != REACH:
                            beside = (tile + (1 if b > REACH else -1)) % (tiles + 1)
                            total = total + jnp.where(
                                edge_of[b], turned[b, beside], turned[b, tile]
                            )
                    value = total.astype(bf16)
                    out_ref[0, k, row : row + BLOCK, tile * TILE : (tile + 1) * TILE] = value
                    kept[frame, row : row + BLOCK, tile * TILE : (tile + 1) * TILE] = value
            return carry

        lax.fori_loop(0, frame_step, one_frame, 0)

    @pl.when(at == steps_1 + steps_2)
    def _():
        slot_count = flat.shape[0] // PATCH

        def some(i8, carry):
            for j in range(8):
                i = i8 * 8 + j
                frame, row, col = spots_ref[0, i], spots_ref[1, i], spots_ref[2, i]
                row_at = pl.multiple_of(jnp.minimum(row // 16 * 16, row_count - 32), 16)
                col_at = pl.multiple_of(jnp.minimum(col // TILE * TILE, col_count - 256), TILE)
                found = kept[frame, pl.ds(row_at, 32), pl.ds(col_at, 256)].astype(f32)
                window[j, :32] = found[:, :TILE]
                window[j, 32:] = found[:, TILE:]
                part = jnp.concatenate(
                    [window[j, pl.ds(row - row_at + k, PATCH), :] for k in (0, 32)], axis=1
                )
                part = pltpu.roll(part, 256 - (col - col_at), 1)[:, :TILE]
                flat[pl.ds(pl.multiple_of(i * PATCH, PATCH), PATCH), :] = part.astype(bf16)
            return carry

        lax.fori_loop(0, slot_count // 8, some, 0)
        shape = (TILE, PATCH * PATCH)
        repeat = (iota(shape, 1) % PATCH == iota(shape, 0)).astype(bf16)
        rows = jnp.dot(flat[...], repeat, preferred_element_type=f32)
        mine = iota(rows.shape, 1) // PATCH == iota(rows.shape, 0) % PATCH
        rows = jnp.where(mine, rows, 0.0).astype(bf16)
        shape = (slot_count, rows.shape[0])
        owner = (iota(shape, 1) // PATCH == iota(shape, 0)).astype(bf16)
        values = jnp.dot(owner, rows, preferred_element_type=f32)
        mean = jnp.sum(values, axis=1, keepdims=True) / (PATCH * PATCH)
        centered = values - mean
        spread = jnp.sum(centered * centered, axis=1, keepdims=True) / (PATCH * PATCH)
        normed = centered / jnp.sqrt(spread + 1e-05)
        live = iota((slot_count, 1), 0) < spots_ref[3, 0]
        last_ref[...] = jnp.where(live, normed, 0.0).astype(bf16)


def run_slab(slab, smoothed, spots, taps, w2, low, frames, high, edge, halo):
    _, frame_count, row_count, col_count = frames.shape
    slot_count = spots.shape[1]
    row_step, frame_step = 32, 4
    steps_1 = row_count // row_step
    steps_2 = frame_count // frame_step
    wide = col_count + TILE
    near = frame_count + 2 * HALF

    def row_block(at):
        return jnp.minimum(at, steps_1 - 1)

    def whole(array):
        return pl.BlockSpec(array.shape, lambda at: (0,) * array.ndim)

    operands = [spots, taps, w2, low, frames, high, edge, halo]
    in_specs = [
        pl.BlockSpec(memory_space=pltpu.SMEM),
        whole(taps),
        whole(w2),
        pl.BlockSpec((HALF, row_step, col_count), lambda at: (0, row_block(at), 0)),
        pl.BlockSpec((1, frame_count, row_step, col_count), lambda at: (slab, 0, row_block(at), 0)),
        pl.BlockSpec((HALF, row_step, col_count), lambda at: (0, row_block(at), 0)),
        pl.BlockSpec((1, near, row_step, TILE), lambda at: (slab, 0, row_block(at), 0)),
        pl.BlockSpec((1, near, 8, wide), lambda at: (slab, 0, 0, 0)),
    ]
    aliases = {}
    if smoothed is not None:
        operands.append(smoothed)
        in_specs.append(pl.BlockSpec(memory_space=pl.ANY))
        aliases = {len(operands) - 1: 0}
    count = len(operands)

    def body(*refs):
        slab_kernel(row_step, frame_step, *refs[:8], *refs[count:])

    tall = row_count + 2 * BLOCK
    return pl.pallas_call(
        body,
        grid=(steps_1 + steps_2 + 1,),
        in_specs=in_specs,
        out_specs=[
            pl.BlockSpec(
                (1, frame_step, row_count, col_count),
                lambda at: (slab, jnp.clip(at - steps_1, 0, steps_2 - 1), 0, 0),
            ),
            pl.BlockSpec((slot_count, PATCH * PATCH), lambda at: (0, 0)),
        ],
        out_shape=[
            jax.ShapeDtypeStruct(frames.shape, bf16),
            jax.ShapeDtypeStruct((slot_count, PATCH * PATCH), bf16),
        ],
        scratch_shapes=[
            pltpu.VMEM((16 * frame_count, 8 * near), bf16),
            pltpu.VMEM((frame_count, wide // TILE, tall, TILE), bf16),
            pltpu.VMEM((frame_count, wide // TILE, tall, TILE), bf16),
            pltpu.VMEM((frame_count, row_count, col_count), bf16),
            pltpu.VMEM((8, 64, TILE), f32),
            pltpu.VMEM((slot_count * PATCH, TILE), bf16),
        ],
        input_output_aliases=aliases,
        compiler_params=pltpu.CompilerParams(vmem_limit_bytes=56 * 1024 * 1024),
        cost_estimate=pl.CostEstimate(
            flops=20_000_000_000, bytes_accessed=16_000_000, transcendentals=0
        ),
        name=f"slab_{slab}",
    )(*operands)


def shards(frames, omega_taps, smooth_kernel, spots, counts):
    _, frame_count, row_count, col_count = frames.shape
    first_frame = lax.axis_index("omega") * frame_count
    first_row = lax.axis_index("row") * row_count
    first_col = lax.axis_index("col") * col_count

    rows = jnp.concatenate([frames[:, :, :REACH], frames[:, :, -REACH:]], axis=2)
    cols = jnp.concatenate([frames[..., :REACH], frames[..., -REACH:]], axis=3)
    rim = jnp.concatenate([rows, jnp.swapaxes(cols, 2, 3)], axis=3)
    send1 = (frames[1, -HALF:], frames[1, :HALF])
    later, send1, rim = lax.optimization_barrier((frames, send1, rim))
    rim = jnp.concatenate(
        [shifted(rim[:, -HALF:], "omega", 1), rim, shifted(rim[:, :HALF], "omega", -1)], axis=1
    )
    low1 = shifted(send1[0], "omega", 1)
    high1 = shifted(send1[1], "omega", -1)
    low0 = shifted(later[0, -HALF:], "omega", 1)
    high0 = shifted(later[0, :HALF], "omega", -1)
    lane = jnp.arange(TILE, dtype=jnp.int32)[None, :]
    step = jnp.arange(REACH, dtype=jnp.int32)[:, None]
    after = (lane == step).astype(bf16)
    before = (lane == TILE - REACH + step).astype(bf16)
    if lax.axis_size("col") == 2:
        first = lax.axis_index("col") == 0
        sides = jnp.where(first, rim[:, :, REACH:, col_count:], rim[:, :, :REACH, col_count:])
        sides = lax.ppermute(sides, "col", [(0, 1), (1, 0)])
        place = jnp.where(first, after, before)
    else:
        left = shifted(rim[:, :, REACH:, col_count:], "col", 1)
        right = shifted(rim[:, :, :REACH, col_count:], "col", -1)
        sides = jnp.concatenate([right, left], axis=2)
        place = jnp.concatenate([after, before], axis=0)
    edge = jnp.einsum("sfkr,kc->sfrc", sides, place, preferred_element_type=bf16)
    ends = jnp.concatenate([edge[:, :, :REACH], edge[:, :, -REACH:]], axis=2)
    line = jnp.concatenate([rim[..., :col_count], ends], axis=3)
    above = shifted(line[:, :, REACH:], "row", 1)
    below = shifted(line[:, :, :REACH], "row", -1)
    gap = jnp.zeros(above.shape[:2] + (8 - 2 * REACH, line.shape[3]), bf16)
    halo = jnp.concatenate([below, gap, above], axis=2)

    taps = omega_matrix(
        omega_taps, first_frame, frame_count, frame_count * lax.axis_size("omega")
    )
    w2 = smooth_matrix(smooth_kernel)
    base = jnp.stack([first_frame, first_row, first_col]).astype(jnp.int32)
    local = spots - base[None, :, None]
    live = jnp.broadcast_to(counts[:, :, None], (2, 1, spots.shape[2]))
    local = jnp.concatenate([local, live], axis=1)

    smoothed, second = run_slab(1, None, local[1], taps, w2, low1, frames, high1, edge, halo)
    count = lax.axis_size("row") * lax.axis_size("col")
    second = lax.ppermute(second, ("row", "col"), [(i, count - 1 - i) for i in range(count)])
    smoothed, first = run_slab(0, smoothed, local[0], taps, w2, low0, frames, high0, edge, halo)
    scores = (
        lax.dot_general(first, second, (((1,), (1,)), ((), ())), preferred_element_type=f32)
        / float(PATCH * PATCH)
    )
    return (smoothed, scores)


def solution(mesh):
    return jax.shard_map(
        shards,
        mesh=mesh,
        in_specs=(
            P(None, "omega", "row", "col"),
            P(),
            P(),
            P(None, None, ("omega", "row", "col")),
            P(None, ("omega", "row", "col")),
        ),
        out_specs=(P(None, "omega", "row", "col"), P(("omega", "row", "col"), None)),
        check_vma=False,
    )
```

time: 117 us -> 110 us (0.940)
  starting transfers between devices: 31.3 us -> 27.3 us
  matrix products: 0.88 us -> 2.52 us
  local copies, waits for them, and re-layouts: 17.6 us -> 16 us
  other arithmetic: 5.51 us -> 4.23 us
    ppermute x10 -> x8, starting transfers between devices: 27 us -> 21.2 us  [shifted(): return lax.ppermute(block, axis, route)]
    mul x2 -> x0, local copies, waits for them, and re-layouts: 4.02 us -> none  [omega_matrix(): wide = parts[:, :, None, :, None] * same[None, None, :, None, :]]
    ppermute x1, waiting for transfers between devices: 2.95 us -> 0.01 us  [shards(): lax.ppermute(second, ('row', 'col'), [(i, count - 1 - i) for i in range(c...]
    ppermute x0 -> x1, waiting for transfers between devices: none -> 2.17 us  [shards(): sides = lax.ppermute(sides, 'col', [(0, 1), (1, 0)])]
    squeeze x1 -> x2, local copies, waits for them, and re-layouts: 6.74 us -> 8.67 us  [the longest x1 4.34 us: shards(): send1 = (frames[1, -HALF:], frames[1, :HALF])]
    dot_general x1 -> x2, matrix products: 0.88 us -> 2.52 us  [the longest x1 1.64 us: shards(): lax.dot_general(first, second, (((1,), (1,)), ((), ())), preferred_elemen...]
    ppermute x0 -> x1, starting transfers between devices: none -> 1.6 us  [shards(): sides = lax.ppermute(sides, 'col', [(0, 1), (1, 0)])]
    unnamed x16 -> x20, local copies, waits for them, and re-layouts: 2.63 us -> 2.26 us
  transfers between devices with their start and end apart: 11 -> 10, of which waited for: 2 -> 2; matrix products, arithmetic and copies ran while one was open for 15% -> 10% of each run, Pallas kernels for 24% -> 49%
where the time goes in v2:
time: 110 us; the launch traced here: 109 us
  Pallas kernels  53.8 us (49%)
  starting transfers between devices  27.3 us (25%)
  local copies, waits for them, and re-layouts  16 us (15%)
  waiting for transfers between devices  4.24 us (4%)
  other arithmetic  4.23 us (4%)
  matrix products  2.52 us (2%)
    pallas_call x2, Pallas kernels, run_slab(): pl.pallas_call(body, grid=(steps_1 + steps_2 + 1,), in_specs=in_specs, ou...  53.8 us
    ppermute x8, starting transfers between devices, shifted(): return lax.ppermute(block, axis, route)  21.2 us
    ppermute x1, starting transfers between devices, shards(): lax.ppermute(second, ('row', 'col'), [(i, count - 1 - i) for i in range(c...  4.54 us
    squeeze x1, local copies, waits for them, and re-layouts, shards(): send1 = (frames[1, -HALF:], frames[1, :HALF])  4.34 us
    squeeze x1, local copies, waits for them, and re-layouts, shards(): high0 = shifted(later[0, :HALF], 'omega', -1)  4.32 us
    unnamed x20, local copies, waits for them, and re-layouts  2.26 us
  transfers between devices with their start and end apart: 10, of which 2 were waited for; matrix products, arithmetic and copies ran while one was open for 10% of the time, Pallas kernels for 49%

profile of v2, /device:TPU:2, one launch (start us, length us, event | category | flops | bytes accessed | tf_op | source)
XLA Modules:
  0.0 109.1 jit_solution(13616486984018144604)
XLA Ops:
  0.6 1.4 %fusion.10 = (bf16[2,16,2,1024]{3,2,1,0:T(2,128)(2,1)S(1)}, bf16[2,16,2,1024]{3,2,1,0:T(2,128)(2,1)S(1)}) fusion(bf16[2,16,128,1024]{3,2,1,0:T(8,128)(2,1)} %refs_4_.3), kind=kLoop, calls=%fused_computation.47 | loop fusion | bytes 524288 | tf_op jit(solution)/shard_map/slice | solution.py:270
  2.0 2.0 %fusion.11 = (bf16[2,16,128,2]{3,2,1,0:T(8,128)(2,1)S(1)}, bf16[2,16,128,2]{3,2,1,0:T(8,128)(2,1)S(1)}) fusion(bf16[2,16,128,1024]{3,2,1,0:T(8,128)(2,1)} %refs_4_.3), kind=kLoop, calls=%fused_computation.48 | loop fusion | bytes 65536 | tf_op jit(solution)/shard_map/slice | solution.py:271
  4.1 4.3 %slice_bitcast_fusion.2 = (bf16[7,128,1024]{2,1,0:T(8,128)(2,1)}, bf16[7,128,1024]{2,1,0:T(8,128)(2,1)}) fusion(bf16[2,16,128,1024]{3,2,1,0:T(8,128)(2,1)} %refs_4_.3), kind=kLoop, calls=%fused_computation.2 | loop fusion | bytes 7340032 | tf_op jit(solution)/shard_map/squeeze | solution.py:273
  8.4 0.4 copy.18
  8.8 0.4 copy.19
  9.2 0.3 pad_maximum_fusion.1
  9.5 0.1 fusion.14
  9.6 1.9 %collective-permute-start.3 = (bf16[2,7,4,1152]{3,2,1,0:T(4,128)(2,1)S(1)}, bf16[2,7,4,1152]{3,2,1,0:T(4,128)(2,1)S(1)}, u32[]{:S(2)}, u32[]{:S(2)}) collective-permute-start(bf16[2,7,4,1152]{3,2,1,0:T(4,128)(2,1)S(1)} %get-tuple-element.32), channel_id=1, source_target_pairs={{8,0},{16,8},{24,16},{9,1},{17,9},{25,17},{10,2},{18,10},{26,18},{... | collective-permute-start | bytes 387080 | tf_op jit(solution)/shard_map/ppermute | solution.py:22
  11.6 0.0 copy-start.3
  11.6 0.0 copy-start.5
  11.6 2.5 %collective-permute-start.2 = (bf16[2,7,4,1152]{3,2,1,0:T(4,128)(2,1)S(1)}, bf16[2,7,4,1152]{3,2,1,0:T(4,128)(2,1)S(1)}, u32[]{:S(2)}, u32[]{:S(2)}) collective-permute-start(bf16[2,7,4,1152]{3,2,1,0:T(4,128)(2,1)S(1)} %get-tuple-element.33), channel_id=1, source_target_pairs={{0,8},{8,16},{16,24},{1,9},{9,17},{17,25},{2,10},{10,18},{18,26},{... | collective-permute-start | bytes 387080 | tf_op jit(solution)/shard_map/ppermute | solution.py:22
  14.2 1.9 %collective-permute-start.7 = (bf16[7,128,1024]{2,1,0:T(8,128)(2,1)}, bf16[7,128,1024]{2,1,0:T(8,128)(2,1)}, u32[]{:S(2)}, u32[]{:S(2)}) collective-permute-start(bf16[7,128,1024]{2,1,0:T(8,128)(2,1)} %get-tuple-element.12), channel_id=1, source_target_pairs={{0,8},{8,16},{16,24},{1,9},{9,17},{17,25},{2,10},{10,18},{18,26},{... | collective-permute-start | bytes 5505032 | tf_op jit(solution)/shard_map/ppermute | solution.py:22
  16.1 3.6 %collective-permute-start.8 = (bf16[7,128,1024]{2,1,0:T(8,128)(2,1)S(1)}, bf16[7,128,1024]{2,1,0:T(8,128)(2,1)}, u32[]{:S(2)}, u32[]{:S(2)}) collective-permute-start(bf16[7,128,1024]{2,1,0:T(8,128)(2,1)S(1)} %copy-done.1), channel_id=1, source_target_pairs={{8,0},{16,8},{24,16},{9,1},{17,9},{25,17},{10,2},{18,10},{26,18},{... | collective-permute-start | bytes 5505032 | tf_op jit(solution)/shard_map/ppermute | solution.py:22
  19.8 4.3 %slice_bitcast_fusion = (bf16[7,128,1024]{2,1,0:T(8,128)(2,1)}, bf16[7,128,1024]{2,1,0:T(8,128)(2,1)}) fusion(bf16[2,16,128,1024]{3,2,1,0:T(8,128)(2,1)} %refs_4_.3), kind=kLoop, calls=%fused_computation | loop fusion | bytes 7340032 | tf_op jit(solution)/shard_map/squeeze | solution.py:281
  24.1 3.2 %collective-permute-start.1 = (bf16[7,128,1024]{2,1,0:T(8,128)(2,1)}, bf16[7,128,1024]{2,1,0:T(8,128)(2,1)}, u32[]{:S(2)}, u32[]{:S(2)}) collective-permute-start(bf16[7,128,1024]{2,1,0:T(8,128)(2,1)} %get-tuple-element.20), channel_id=1, source_target_pairs={{8,0},{16,8},{24,16},{9,1},{17,9},{25,17},{10,2},{18,10},{26,18},{... | collective-permute-start | bytes 5505032 | tf_op jit(solution)/shard_map/ppermute | solution.py:22
  27.3 0.1 copy.14
  27.5 0.1 select_reduce_fusion
  27.6 0.2 select_reduce_fusion.2
  27.8 0.1 reduce-precision_convert_fusion.1
  27.9 0.1 pad_add_fusion.1
  27.9 0.1 copy_subtract_fusion
  28.0 0.1 constant_dynamic-update-slice_fusion.2
  28.1 0.1 constant_dynamic-update-slice_fusion.1
  28.2 0.1 constant_dynamic-update-slice_fusion
  28.3 0.1 broadcast_select_fusion
  28.4 1.6 %collective-permute-start.4 = (bf16[2,30,2,128]{3,2,1,0:T(2,128)(2,1)S(1)}, bf16[2,30,2,128]{3,2,1,0:T(2,128)(2,1)S(1)}, u32[]{:S(2)}, u32[]{:S(2)}) collective-permute-start(bf16[2,30,2,128]{3,2,1,0:T(2,128)(2,1)S(1)} %broadcast_select_fusion), channel_id=1, source_target_pairs={{0,1},{1,0},{2,3},{3,2},{4,5},{5,4},{6,7},{7,6},{8,9},{9,8},{10,11... | collective-permute-start | bytes 92168 | tf_op jit(solution)/shard_map/ppermute | solution.py:289
  30.0 0.2 slice.80
  30.1 0.0 copy-start.2
  30.2 2.2 %collective-permute-done.4 = bf16[2,30,2,128]{3,2,1,0:T(2,128)(2,1)S(1)} collective-permute-done((bf16[2,30,2,128]{3,2,1,0:T(2,128)(2,1)S(1)}, bf16[2,30,2,128]{3,2,1,0:T(2,128)(2,1)S(1)}, u32[]{:S(2)}, u32[]{:S(2)}) %collective-permute-start.4) | collective-permute-done | bytes 30752 | tf_op jit(solution)/shard_map/ppermute | solution.py:289
  32.3 0.9 fusion.7.refs_6_
  33.2 0.1 fusion.12
  33.3 0.3 maximum_maximum_fusion
  33.6 0.4 fusion.13
  34.0 1.3 %collective-permute-start.5 = (bf16[2,30,2,1152]{3,2,1,0:T(2,128)(2,1)S(1)}, bf16[2,30,2,1152]{3,2,1,0:T(2,128)(2,1)S(1)}, u32[]{:S(2)}, u32[]{:S(2)}) collective-permute-start(bf16[2,30,2,1152]{3,2,1,0:T(2,128)(2,1)S(1)} %get-tuple-element.30), channel_id=1, source_target_pairs={{2,0},{4,2},{6,4},{3,1},{5,3},{7,5},{10,8},{12,10},{14,12},{11,9},... | collective-permute-start | bytes 829448 | tf_op jit(solution)/shard_map/ppermute | solution.py:22
  35.3 4.6 %collective-permute-start.6 = (bf16[2,30,2,1152]{3,2,1,0:T(2,128)(2,1)S(1)}, bf16[2,30,2,1152]{3,2,1,0:T(2,128)(2,1)S(1)}, u32[]{:S(2)}, u32[]{:S(2)}) collective-permute-start(bf16[2,30,2,1152]{3,2,1,0:T(2,128)(2,1)S(1)} %get-tuple-element.31), channel_id=1, source_target_pairs={{0,2},{2,4},{4,6},{1,3},{3,5},{5,7},{8,10},{10,12},{12,14},{9,11},... | collective-permute-start | bytes 829448 | tf_op jit(solution)/shard_map/ppermute | solution.py:22
  39.9 0.6 copy.13
  40.5 0.1 pad.1.clone
  40.6 0.1 broadcast_in_dim.65
  40.6 0.6 fusion.5
  41.3 0.7 pad_maximum_fusion.2.refs_2_
  42.0 2.1 %collective-permute-done.5 = bf16[2,30,2,1152]{3,2,1,0:T(2,128)(2,1)S(1)} collective-permute-done((bf16[2,30,2,1152]{3,2,1,0:T(2,128)(2,1)S(1)}, bf16[2,30,2,1152]{3,2,1,0:T(2,128)(2,1)S(1)}, u32[]{:S(2)}, u32[]{:S(2)}) %collective-permute-start.5) | collective-permute-done | bytes 276512 | tf_op jit(solution)/shard_map/ppermute | solution.py:22
  44.0 2.1 %collective-permute-start = (bf16[7,128,1024]{2,1,0:T(8,128)(2,1)S(1)}, bf16[7,128,1024]{2,1,0:T(8,128)(2,1)S(1)}, u32[]{:S(2)}, u32[]{:S(2)}) collective-permute-start(bf16[7,128,1024]{2,1,0:T(8,128)(2,1)S(1)} %copy-done.2), channel_id=1, source_target_pairs={{0,8},{8,16},{16,24},{1,9},{9,17},{17,25},{2,10},{10,18},{18,26},{... | collective-permute-start | bytes 5505032 | tf_op jit(solution)/shard_map/ppermute | solution.py:22
  46.1 1.6 %pad_maximum_fusion.refs_7_ = bf16[2,30,8,1152]{3,2,1,0:T(8,128)(2,1)} fusion(bf16[2,30,2,1152]{3,2,1,0:T(2,128)(2,1)S(1)} %collective-permute-done.6, bf16[2,30,2,1152]{3,2,1,0:T(2,128)(2,1)S(1)} %collective-permute-done.5, bf16[8]{0:T(256)(128)(2,1)S(1)} %pad.1.clone), kind=kLoop, calls=%fused_computation.5 | loop fusion | flops 3317760 | bytes 1658896 | tf_op jit(solution)/shard_map/concatenate | solution.py:302
  47.8 26.9 %slab_1.1 = (bf16[2,16,128,1024]{3,2,1,0:T(8,128)(2,1)}, bf16[128,256]{1,0:T(8,128)(2,1)}) custom-call(s32[4,128]{1,0:T(4,128)} %get-tuple-element.38.refs_0_, bf16[32,30]{1,0:T(8,128)(2,1)} %bitcast.39, bf16[80,144]{1,0:T(8,128)(2,1)} %pad_maximum_fusion.2.refs_2_, bf16[7,128,1024]{2,1,0:T(8,128)(2,1)} %collective-permute-done.7.refs_3_, ...), custom_call_target="tpu_custom_call" | custom-call | flops 20000000000 | bytes 16000000 | tf_op jit(solution)/shard_map/slab_1/pallas_call | solution.py:232
  74.7 4.5 %collective-permute-start.9 = (bf16[128,256]{1,0:T(8,128)(2,1)}, bf16[128,256]{1,0:T(8,128)(2,1)S(1)}, u32[]{:S(2)}, u32[]{:S(2)}) collective-permute-start(bf16[128,256]{1,0:T(8,128)(2,1)} %get-tuple-element.17), channel_id=1, source_target_pairs={{0,7},{1,6},{2,5},{3,4},{4,3},{5,2},{6,1},{7,0},{8,15},{9,14},{10,... | collective-permute-start | bytes 196616 | tf_op jit(solution)/shard_map/ppermute | solution.py:315
  79.3 1.3 %copy-done.6 = bf16[7,128,1024]{2,1,0:T(8,128)(2,1)} copy-done((bf16[7,128,1024]{2,1,0:T(8,128)(2,1)}, bf16[7,128,1024]{2,1,0:T(8,128)(2,1)S(1)}, u32[]{:S(2)}) %copy-start.6) | copy-done | bytes 1835032
  80.5 26.9 %slab_0.1 = (bf16[2,16,128,1024]{3,2,1,0:T(8,128)(2,1)}, bf16[128,256]{1,0:T(8,128)(2,1)}) custom-call(s32[4,128]{1,0:T(4,128)} %get-tuple-element.39.refs_0_, bf16[32,30]{1,0:T(8,128)(2,1)} %bitcast.40, bf16[80,144]{1,0:T(8,128)(2,1)} %pad_maximum_fusion.2.refs_2_, bf16[7,128,1024]{2,1,0:T(8,128)(2,1)} %copy-done.6, ...), custom_call_target="tpu_custom_call", output_to_operand_aliasing={{0}: (8, {})} | custom-call | flops 20000000000 | bytes 16000000 | tf_op jit(solution)/shard_map/slab_0/pallas_call | solution.py:232
  107.4 1.6 %convolution_multiply_fusion = f32[128,128]{1,0:T(8,128)} fusion(bf16[128,256]{1,0:T(8,128)(2,1)} %get-tuple-element.16, bf16[128,256]{1,0:T(8,128)(2,1)S(1)} %collective-permute-done.9), kind=kOutput, calls=%fused_computation.4 | convolution fusion | flops 8404992 | bytes 196608 | tf_op jit(solution)/shard_map/dot_general | solution.py:318
  (29 shorter events, 0.2 us)
Async XLA Ops:
  8.8 7.3 %copy-start.1 = (bf16[7,128,1024]{2,1,0:T(8,128)(2,1)S(1)}, bf16[7,128,1024]{2,1,0:T(8,128)(2,1)}, u32[]{:S(2)}) copy-start(bf16[7,128,1024]{2,1,0:T(8,128)(2,1)} %get-tuple-element.13) | copy-start | bytes 5505028
  9.6 18.6 %collective-permute-start.3 = (bf16[2,7,4,1152]{3,2,1,0:T(4,128)(2,1)S(1)}, bf16[2,7,4,1152]{3,2,1,0:T(4,128)(2,1)S(1)}, u32[]{:S(2)}, u32[]{:S(2)}) collective-permute-start(bf16[2,7,4,1152]{3,2,1,0:T(4,128)(2,1)S(1)} %get-tuple-element.32), channel_id=1, source_target_pairs={{8,0},{16,8},{24,16},{9,1},{17,9},{25,17},{10,2},{18,10},{26,18},{... | collective-permute-start | bytes 387080 | tf_op jit(solution)/shard_map/ppermute | solution.py:22
  11.6 15.8 %copy-start.3 = (f32[5,5]{1,0:T(8,128)S(1)}, f32[5,5]{1,0:T(8,128)}, u32[]{:S(2)}) copy-start(f32[5,5]{1,0:T(8,128)} %param.7) | copy-start | bytes 304
  11.6 16.0 %copy-start.5 = (f32[15]{0:T(128)S(1)}, f32[15]{0:T(128)}, u32[]{:S(2)}) copy-start(f32[15]{0:T(128)} %param.6) | copy-start | bytes 184
  11.6 16.3 %copy-start.4 = (s32[2,3,128]{2,0,1:T(2,128)S(1)}, s32[2,3,128]{2,0,1:T(2,128)}, u32[]{:S(2)}) copy-start(s32[2,3,128]{2,0,1:T(2,128)} %param.8) | copy-start | bytes 9220
  11.6 16.4 %collective-permute-start.2 = (bf16[2,7,4,1152]{3,2,1,0:T(4,128)(2,1)S(1)}, bf16[2,7,4,1152]{3,2,1,0:T(4,128)(2,1)S(1)}, u32[]{:S(2)}, u32[]{:S(2)}) collective-permute-start(bf16[2,7,4,1152]{3,2,1,0:T(4,128)(2,1)S(1)} %get-tuple-element.33), channel_id=1, source_target_pairs={{0,8},{8,16},{16,24},{1,9},{9,17},{17,25},{2,10},{10,18},{18,26},{... | collective-permute-start | bytes 387080 | tf_op jit(solution)/shard_map/ppermute | solution.py:22
  14.2 33.6 %collective-permute-start.7 = (bf16[7,128,1024]{2,1,0:T(8,128)(2,1)}, bf16[7,128,1024]{2,1,0:T(8,128)(2,1)}, u32[]{:S(2)}, u32[]{:S(2)}) collective-permute-start(bf16[7,128,1024]{2,1,0:T(8,128)(2,1)} %get-tuple-element.12), channel_id=1, source_target_pairs={{0,8},{8,16},{16,24},{1,9},{9,17},{17,25},{2,10},{10,18},{18,26},{... | collective-permute-start | bytes 5505032 | tf_op jit(solution)/shard_map/ppermute | solution.py:22
  16.1 31.7 %collective-permute-start.8 = (bf16[7,128,1024]{2,1,0:T(8,128)(2,1)S(1)}, bf16[7,128,1024]{2,1,0:T(8,128)(2,1)}, u32[]{:S(2)}, u32[]{:S(2)}) collective-permute-start(bf16[7,128,1024]{2,1,0:T(8,128)(2,1)S(1)} %copy-done.1), channel_id=1, source_target_pairs={{8,0},{16,8},{24,16},{9,1},{17,9},{25,17},{10,2},{18,10},{26,18},{... | collective-permute-start | bytes 5505032 | tf_op jit(solution)/shard_map/ppermute | solution.py:22
  24.1 55.2 %collective-permute-start.1 = (bf16[7,128,1024]{2,1,0:T(8,128)(2,1)}, bf16[7,128,1024]{2,1,0:T(8,128)(2,1)}, u32[]{:S(2)}, u32[]{:S(2)}) collective-permute-start(bf16[7,128,1024]{2,1,0:T(8,128)(2,1)} %get-tuple-element.20), channel_id=1, source_target_pairs={{8,0},{16,8},{24,16},{9,1},{17,9},{25,17},{10,2},{18,10},{26,18},{... | collective-permute-start | bytes 5505032 | tf_op jit(solution)/shard_map/ppermute | solution.py:22
  28.4 4.0 %collective-permute-start.4 = (bf16[2,30,2,128]{3,2,1,0:T(2,128)(2,1)S(1)}, bf16[2,30,2,128]{3,2,1,0:T(2,128)(2,1)S(1)}, u32[]{:S(2)}, u32[]{:S(2)}) collective-permute-start(bf16[2,30,2,128]{3,2,1,0:T(2,128)(2,1)S(1)} %broadcast_select_fusion), channel_id=1, source_target_pairs={{0,1},{1,0},{2,3},{3,2},{4,5},{5,4},{6,7},{7,6},{8,9},{9,8},{10,11... | collective-permute-start | bytes 92168 | tf_op jit(solution)/shard_map/ppermute | solution.py:289
  30.1 10.4 %copy-start.7 = (s32[2,1]{0,1:T(1,128)S(1)}, s32[2,1]{0,1:T(1,128)}, u32[]{:S(2)}) copy-start(s32[2,1]{0,1:T(1,128)} %param.9) | copy-start | bytes 28
  30.1 13.9 %copy-start.2 = (bf16[7,128,1024]{2,1,0:T(8,128)(2,1)S(1)}, bf16[7,128,1024]{2,1,0:T(8,128)(2,1)}, u32[]{:S(2)}) copy-start(bf16[7,128,1024]{2,1,0:T(8,128)(2,1)} %get-tuple-element.21) | copy-start | bytes 5505028
  33.2 14.6 %copy-start = (bf16[2,30,128,128]{3,2,1,0:T(8,128)(2,1)}, bf16[2,30,128,128]{3,2,1,0:T(8,128)(2,1)S(1)}, u32[]{:S(2)}) copy-start(bf16[2,30,128,128]{3,2,1,0:T(8,128)(2,1)S(1)} %fusion.7.refs_6_) | copy-start | bytes 5898244
  34.0 10.0 %collective-permute-start.5 = (bf16[2,30,2,1152]{3,2,1,0:T(2,128)(2,1)S(1)}, bf16[2,30,2,1152]{3,2,1,0:T(2,128)(2,1)S(1)}, u32[]{:S(2)}, u32[]{:S(2)}) collective-permute-start(bf16[2,30,2,1152]{3,2,1,0:T(2,128)(2,1)S(1)} %get-tuple-element.30), channel_id=1, source_target_pairs={{2,0},{4,2},{6,4},{3,1},{5,3},{7,5},{10,8},{12,10},{14,12},{11,9},... | collective-permute-start | bytes 829448 | tf_op jit(solution)/shard_map/ppermute | solution.py:22
  35.3 10.8 %collective-permute-start.6 = (bf16[2,30,2,1152]{3,2,1,0:T(2,128)(2,1)S(1)}, bf16[2,30,2,1152]{3,2,1,0:T(2,128)(2,1)S(1)}, u32[]{:S(2)}, u32[]{:S(2)}) collective-permute-start(bf16[2,30,2,1152]{3,2,1,0:T(2,128)(2,1)S(1)} %get-tuple-element.31), channel_id=1, source_target_pairs={{0,2},{2,4},{4,6},{1,3},{3,5},{5,7},{8,10},{10,12},{12,14},{9,11},... | collective-permute-start | bytes 829448 | tf_op jit(solution)/shard_map/ppermute | solution.py:22
  44.0 35.2 %collective-permute-start = (bf16[7,128,1024]{2,1,0:T(8,128)(2,1)S(1)}, bf16[7,128,1024]{2,1,0:T(8,128)(2,1)S(1)}, u32[]{:S(2)}, u32[]{:S(2)}) collective-permute-start(bf16[7,128,1024]{2,1,0:T(8,128)(2,1)S(1)} %copy-done.2), channel_id=1, source_target_pairs={{0,8},{8,16},{16,24},{1,9},{9,17},{17,25},{2,10},{10,18},{18,26},{... | collective-permute-start | bytes 5505032 | tf_op jit(solution)/shard_map/ppermute | solution.py:22
  74.7 32.7 %collective-permute-start.9 = (bf16[128,256]{1,0:T(8,128)(2,1)}, bf16[128,256]{1,0:T(8,128)(2,1)S(1)}, u32[]{:S(2)}, u32[]{:S(2)}) collective-permute-start(bf16[128,256]{1,0:T(8,128)(2,1)} %get-tuple-element.17), channel_id=1, source_target_pairs={{0,7},{1,6},{2,5},{3,4},{4,3},{5,2},{6,1},{7,0},{8,15},{9,14},{10,... | collective-permute-start | bytes 196616 | tf_op jit(solution)/shard_map/ppermute | solution.py:315
  79.3 1.3 %copy-start.6 = (bf16[7,128,1024]{2,1,0:T(8,128)(2,1)}, bf16[7,128,1024]{2,1,0:T(8,128)(2,1)S(1)}, u32[]{:S(2)}) copy-start(bf16[7,128,1024]{2,1,0:T(8,128)(2,1)S(1)} %collective-permute-done.refs_3_) | copy-start | bytes 5505028

commit v3 on v2

--- a/solution.py
+++ b/solution.py
@@ -58,12 +58,11 @@
 
 def slab_kernel(
     row_step, frame_step,
-    spots_ref, taps_ref, w2_ref, low_ref, own_ref, high_ref, edge_ref, halo_ref,
-    out_ref, last_ref, w1, chi, clo, kept, window, flat,
+    spots_ref, taps_ref, w2_ref, low_ref, own_ref, high_ref, edge_ref, below_ref, above_ref,
+    out_ref, last_ref, w1, chi, clo, kept, flat,
 ):
-    frame_count, row_count, col_count = kept.shape
+    frame_count, tiles, row_count, _ = kept.shape
     near = taps_ref.shape[1]
-    tiles = col_count // TILE
     steps_1 = row_count // row_step
     steps_2 = frame_count // frame_step
     at = pl.program_id(0)
@@ -90,7 +89,10 @@
         w1[...] = jnp.where(same, full, 0.0).astype(bf16)
         for tile in range(tiles + 1):
             cols = slice(tile * TILE, tile * TILE + TILE)
-            one = filtered(halo_ref[0, :, :, cols].astype(f32))
+            below = below_ref[0, :, :, cols].astype(f32)
+            above = above_ref[0, :, :, cols].astype(f32)
+            gap = jnp.zeros((near, 8 - 2 * REACH, TILE), f32)
+            one = filtered(jnp.concatenate([below, gap, above], axis=1))
             two = jnp.concatenate([one, one], axis=1)
             keep(two, tile, slice(0, BLOCK))
             keep(two, tile, slice(BLOCK + row_count, 2 * BLOCK + row_count))
@@ -150,7 +152,7 @@
                             )
                     value = total.astype(bf16)
                     out_ref[0, k, row : row + BLOCK, tile * TILE : (tile + 1) * TILE] = value
-                    kept[frame, row : row + BLOCK, tile * TILE : (tile + 1) * TILE] = value
+                    kept[frame, tile, row : row + BLOCK, :] = value.astype(f32)
             return carry
 
         lax.fori_loop(0, frame_step, one_frame, 0)
@@ -159,40 +161,110 @@
     def _():
         slot_count = flat.shape[0] // PATCH
 
+        lane = iota((PATCH, TILE), 1)
+
         def some(i8, carry):
             for j in range(8):
                 i = i8 * 8 + j
-                frame, row, col = spots_ref[0, i], spots_ref[1, i], spots_ref[2, i]
-                row_at = pl.multiple_of(jnp.minimum(row // 16 * 16, row_count - 32), 16)
-                col_at = pl.multiple_of(jnp.minimum(col // TILE * TILE, col_count - 256), TILE)
-                found = kept[frame, pl.ds(row_at, 32), pl.ds(col_at, 256)].astype(f32)
-                window[j, :32] = found[:, :TILE]
-                window[j, 32:] = found[:, TILE:]
-                part = jnp.concatenate(
-                    [window[j, pl.ds(row - row_at + k, PATCH), :] for k in (0, 32)], axis=1
-                )
-                part = pltpu.roll(part, 256 - (col - col_at), 1)[:, :TILE]
+                frame, row, tile = spots_ref[0, i], spots_ref[1, i], spots_ref[2, i]
+                beside, turn = spots_ref[3, i], spots_ref[4, i]
+                here = kept[frame, tile, pl.ds(row, PATCH), :]
+                there = kept[frame, beside, pl.ds(row, PATCH), :]
+                shift = turn & (TILE - 1)
+                here, there = pltpu.roll(here, shift, 1), pltpu.roll(there, shift, 1)
+                part = jnp.where(lane < turn, here, there)
                 flat[pl.ds(pl.multiple_of(i * PATCH, PATCH), PATCH), :] = part.astype(bf16)
             return carry
 
         lax.fori_loop(0, slot_count // 8, some, 0)
+        low_bits = PATCH - 1
+        bits = low_bits.bit_length()
         shape = (TILE, PATCH * PATCH)
-        repeat = (iota(shape, 1) % PATCH == iota(shape, 0)).astype(bf16)
+        repeat = (iota(shape, 1) & low_bits == iota(shape, 0)).astype(bf16)
         rows = jnp.dot(flat[...], repeat, preferred_element_type=f32)
-        mine = iota(rows.shape, 1) // PATCH == iota(rows.shape, 0) % PATCH
+        mine = iota(rows.shape, 1) >> bits == iota(rows.shape, 0) & low_bits
         rows = jnp.where(mine, rows, 0.0).astype(bf16)
         shape = (slot_count, rows.shape[0])
-        owner = (iota(shape, 1) // PATCH == iota(shape, 0)).astype(bf16)
+        owner = (iota(shape, 1) >> bits == iota(shape, 0)).astype(bf16)
         values = jnp.dot(owner, rows, preferred_element_type=f32)
         mean = jnp.sum(values, axis=1, keepdims=True) / (PATCH * PATCH)
         centered = values - mean
         spread = jnp.sum(centered * centered, axis=1, keepdims=True) / (PATCH * PATCH)
         normed = centered / jnp.sqrt(spread + 1e-05)
-        live = iota((slot_count, 1), 0) < spots_ref[3, 0]
+        live = iota((slot_count, 1), 0) < spots_ref[5, 0]
         last_ref[...] = jnp.where(live, normed, 0.0).astype(bf16)
 
 
-def run_slab(slab, smoothed, spots, taps, w2, low, frames, high, edge, halo):
+def cut_kernel(frames, rim, low1, high1, low0, high0, top, bottom, left, right, sems):
+    slabs, frame_count, row_count, col_count = frames.shape
+    narrow = row_count
+    reads = [
+        (frames.at[:, :, pl.ds(0, BLOCK), :], top),
+        (frames.at[:, :, pl.ds(row_count - BLOCK, BLOCK), :], bottom),
+        (frames.at[:, :, :, pl.ds(0, TILE)], left),
+        (frames.at[:, :, :, pl.ds(col_count - TILE, TILE)], right),
+    ]
+    writes = [
+        (frames.at[1, pl.ds(frame_count - HALF, HALF)], low1),
+        (frames.at[1, pl.ds(0, HALF)], high1),
+        (frames.at[0, pl.ds(frame_count - HALF, HALF)], low0),
+        (frames.at[0, pl.ds(0, HALF)], high0),
+    ]
+    copies = [
+        pltpu.make_async_copy(source, target, sems.at[i])
+        for i, (source, target) in enumerate(reads + writes)
+    ]
+    for copy in copies:
+        copy.start()
+    for copy in copies[:4]:
+        copy.wait()
+    for s in range(slabs):
+        rows = jnp.concatenate(
+            [
+                top[s, :, :8, :].astype(f32)[:, :REACH],
+                bottom[s, :, BLOCK - 8 :, :].astype(f32)[:, 8 - REACH :],
+            ],
+            axis=1,
+        )
+        rim[s, :, :, :col_count] = rows.astype(bf16)
+        line = iota((8, TILE), 0)
+        lane = iota((8, TILE), 1)
+        first = ((line == lane) & (line < REACH)).astype(bf16)
+        last = ((line + TILE - 2 * REACH == lane) & (line >= REACH)).astype(bf16)
+        over_lanes = (((1,), (1,)), ((), ()))
+        for f in range(frame_count):
+            cols = lax.dot_general(first, left[s, f], over_lanes, preferred_element_type=f32)
+            cols += lax.dot_general(last, right[s, f], over_lanes, preferred_element_type=f32)
+            rim[s, f, :, col_count : col_count + narrow] = cols[: 2 * REACH].astype(bf16)
+    for copy in copies[4:]:
+        copy.wait()
+
+
+def cut(frames):
+    slabs, frame_count, row_count, col_count = frames.shape
+    piece = jax.ShapeDtypeStruct((HALF, row_count, col_count), bf16)
+    anywhere = pl.BlockSpec(memory_space=pl.ANY)
+    return pl.pallas_call(
+        cut_kernel,
+        in_specs=[anywhere],
+        out_specs=[pl.BlockSpec(memory_space=pltpu.VMEM)] + [anywhere] * 4,
+        out_shape=[
+            jax.ShapeDtypeStruct((slabs, frame_count, 2 * REACH, col_count + row_count), bf16),
+            piece, piece, piece, piece,
+        ],
+        scratch_shapes=[
+            pltpu.VMEM((slabs, frame_count, BLOCK, col_count), bf16),
+            pltpu.VMEM((slabs, frame_count, BLOCK, col_count), bf16),
+            pltpu.VMEM((slabs, frame_count, row_count, TILE), bf16),
+            pltpu.VMEM((slabs, frame_count, row_count, TILE), bf16),
+            pltpu.SemaphoreType.DMA((8,)),
+        ],
+        compiler_params=pltpu.CompilerParams(vmem_limit_bytes=60 * 1024 * 1024),
+        name="cut",
+    )(frames)
+
+
+def run_slab(slab, smoothed, spots, taps, w2, low, frames, high, edge, below, above):
     _, frame_count, row_count, col_count = frames.shape
     slot_count = spots.shape[1]
     row_step, frame_step = 32, 4
@@ -207,7 +279,7 @@
     def whole(array):
         return pl.BlockSpec(array.shape, lambda at: (0,) * array.ndim)
 
-    operands = [spots, taps, w2, low, frames, high, edge, halo]
+    operands = [spots, taps, w2, low, frames, high, edge, below, above]
     in_specs = [
         pl.BlockSpec(memory_space=pltpu.SMEM),
         whole(taps),
@@ -216,7 +288,8 @@
         pl.BlockSpec((1, frame_count, row_step, col_count), lambda at: (slab, 0, row_block(at), 0)),
         pl.BlockSpec((HALF, row_step, col_count), lambda at: (0, row_block(at), 0)),
         pl.BlockSpec((1, near, row_step, TILE), lambda at: (slab, 0, row_block(at), 0)),
-        pl.BlockSpec((1, near, 8, wide), lambda at: (slab, 0, 0, 0)),
+        pl.BlockSpec((1, near, REACH, wide), lambda at: (slab, 0, 0, 0)),
+        pl.BlockSpec((1, near, REACH, wide), lambda at: (slab, 0, 0, 0)),
     ]
     aliases = {}
     if smoothed is not None:
@@ -226,7 +299,7 @@
     count = len(operands)
 
     def body(*refs):
-        slab_kernel(row_step, frame_step, *refs[:8], *refs[count:])
+        slab_kernel(row_step, frame_step, *refs[:9], *refs[count:])
 
     tall = row_count + 2 * BLOCK
     return pl.pallas_call(
@@ -248,12 +321,11 @@
             pltpu.VMEM((16 * frame_count, 8 * near), bf16),
             pltpu.VMEM((frame_count, wide // TILE, tall, TILE), bf16),
             pltpu.VMEM((frame_count, wide // TILE, tall, TILE), bf16),
-            pltpu.VMEM((frame_count, row_count, col_count), bf16),
-            pltpu.VMEM((8, 64, TILE), f32),
+            pltpu.VMEM((frame_count, col_count // TILE, row_count, TILE), f32),
             pltpu.VMEM((slot_count * PATCH, TILE), bf16),
         ],
         input_output_aliases=aliases,
-        compiler_params=pltpu.CompilerParams(vmem_limit_bytes=56 * 1024 * 1024),
+        compiler_params=pltpu.CompilerParams(vmem_limit_bytes=60 * 1024 * 1024),
         cost_estimate=pl.CostEstimate(
             flops=20_000_000_000, bytes_accessed=16_000_000, transcendentals=0
         ),
@@ -267,18 +339,14 @@
     first_row = lax.axis_index("row") * row_count
     first_col = lax.axis_index("col") * col_count
 
-    rows = jnp.concatenate([frames[:, :, :REACH], frames[:, :, -REACH:]], axis=2)
-    cols = jnp.concatenate([frames[..., :REACH], frames[..., -REACH:]], axis=3)
-    rim = jnp.concatenate([rows, jnp.swapaxes(cols, 2, 3)], axis=3)
-    send1 = (frames[1, -HALF:], frames[1, :HALF])
-    later, send1, rim = lax.optimization_barrier((frames, send1, rim))
+    rim, send_low1, send_high1, send_low0, send_high0 = cut(frames)
     rim = jnp.concatenate(
         [shifted(rim[:, -HALF:], "omega", 1), rim, shifted(rim[:, :HALF], "omega", -1)], axis=1
     )
-    low1 = shifted(send1[0], "omega", 1)
-    high1 = shifted(send1[1], "omega", -1)
-    low0 = shifted(later[0, -HALF:], "omega", 1)
-    high0 = shifted(later[0, :HALF], "omega", -1)
+    low1 = shifted(send_low1, "omega", 1)
+    high1 = shifted(send_high1, "omega", -1)
+    low0 = shifted(send_low0, "omega", 1)
+    high0 = shifted(send_high0, "omega", -1)
     lane = jnp.arange(TILE, dtype=jnp.int32)[None, :]
     step = jnp.arange(REACH, dtype=jnp.int32)[:, None]
     after = (lane == step).astype(bf16)
@@ -298,22 +366,21 @@
     line = jnp.concatenate([rim[..., :col_count], ends], axis=3)
     above = shifted(line[:, :, REACH:], "row", 1)
     below = shifted(line[:, :, :REACH], "row", -1)
-    gap = jnp.zeros(above.shape[:2] + (8 - 2 * REACH, line.shape[3]), bf16)
-    halo = jnp.concatenate([below, gap, above], axis=2)
 
     taps = omega_matrix(
         omega_taps, first_frame, frame_count, frame_count * lax.axis_size("omega")
     )
     w2 = smooth_matrix(smooth_kernel)
-    base = jnp.stack([first_frame, first_row, first_col]).astype(jnp.int32)
-    local = spots - base[None, :, None]
-    live = jnp.broadcast_to(counts[:, :, None], (2, 1, spots.shape[2]))
-    local = jnp.concatenate([local, live], axis=1)
-
-    smoothed, second = run_slab(1, None, local[1], taps, w2, low1, frames, high1, edge, halo)
+    frame, row, col = spots[:, 0] - first_frame, spots[:, 1] - first_row, spots[:, 2] - first_col
+    tile = col // TILE
+    beside = jnp.minimum(tile + 1, col_count // TILE - 1)
+    live = jnp.broadcast_to(counts, frame.shape)
+    local = jnp.stack([frame, row, tile, beside, TILE - col % TILE, live], axis=1)
+
+    smoothed, second = run_slab(1, None, local[1], taps, w2, low1, frames, high1, edge, below, above)
     count = lax.axis_size("row") * lax.axis_size("col")
     second = lax.ppermute(second, ("row", "col"), [(i, count - 1 - i) for i in range(count)])
-    smoothed, first = run_slab(0, smoothed, local[0], taps, w2, low0, frames, high0, edge, halo)
+    smoothed, first = run_slab(0, smoothed, local[0], taps, w2, low0, frames, high0, edge, below, above)
     scores = (
         lax.dot_general(first, second, (((1,), (1,)), ((), ())), preferred_element_type=f32)
         / float(PATCH * PATCH)

time: 110 us -> 333 us (3.03)
  Pallas kernels: 53.8 us -> 276 us
  waiting for transfers between devices: 4.24 us -> 21.8 us
  local copies, waits for them, and re-layouts: 16 us -> 4.31 us
    pallas_call x0 -> x1, Pallas kernels: none -> 224 us  [cut(): pl.pallas_call(cut_kernel, in_specs=[anywhere], out_specs=[pl.BlockSpec(m...]
    ppermute x8, waiting for transfers between devices: 2.07 us -> 19.6 us  [shifted(): return lax.ppermute(block, axis, route)]
    squeeze x2 -> x1, local copies, waits for them, and re-layouts: 8.67 us -> 0.62 us  [shards(): local[1]]
    slice x3 -> x1, local copies, waits for them, and re-layouts: 3.83 us -> 0.39 us  [shards(): above = shifted(line[:, :, REACH:], 'row', 1)]
  transfers between devices with their start and end apart: 10 -> 10, of which waited for: 2 -> 4; matrix products, arithmetic and copies ran while one was open for 10% -> 2% of each run, Pallas kernels for 49% -> 16%
where the time goes in v3:
time: 333 us
  Pallas kernels  276 us (83%)
  starting transfers between devices  25.7 us (8%)
  waiting for transfers between devices  21.8 us (7%)
  local copies, waits for them, and re-layouts  4.31 us (1%)
    pallas_call x1, Pallas kernels, cut(): pl.pallas_call(cut_kernel, in_specs=[anywhere], out_specs=[pl.BlockSpec(m...  224 us
    pallas_call x2, Pallas kernels, run_slab(): pl.pallas_call(body, grid=(steps_1 + steps_2 + 1,), in_specs=in_specs, ou...  51.6 us
    ppermute x8, waiting for transfers between devices, shifted(): return lax.ppermute(block, axis, route)  19.6 us
    ppermute x8, starting transfers between devices, shifted(): return lax.ppermute(block, axis, route)  19.6 us
  transfers between devices with their start and end apart: 10, of which 4 were waited for; matrix products, arithmetic and copies ran while one was open for 2% of the time, Pallas kernels for 16%

profile of v3, /device:TPU:2, one launch (start us, length us, event | category | flops | bytes accessed | tf_op | source)
XLA Modules:
  0.0 332.7 jit_solution(3499008029320549512)
XLA Ops:
  0.6 0.0 copy-start.1
  0.6 0.0 copy-start.2
  0.7 0.0 copy-start.3
  0.7 224.2 %cut.1 = (bf16[2,16,4,1152]{3,2,1,0:T(4,128)(2,1)}, bf16[7,128,1024]{2,1,0:T(8,128)(2,1)}, bf16[7,128,1024]{2,1,0:T(8,128)(2,1)}, bf16[7,128,1024]{2,1,0:T(8,128)(2,1)}, bf16[7,128,1024]{2,1,0:T(8,128)(2,1)}) custom-call(bf16[2,16,128,1024]{3,2,1,0:T(8,128)(2,1)} %refs_4_.3), custom_call_target="tpu_custom_call" | custom-call | tf_op jit(solution)/shard_map/cut/pallas_call | solution.py:247
  224.9 1.1 fusion.10
  226.0 1.9 collective-permute-start.3
  227.9 2.4 collective-permute-start.2
  230.3 1.9 collective-permute-start
  232.3 1.9 collective-permute-start.7
  234.2 3.6 %collective-permute-start.8 = (bf16[7,128,1024]{2,1,0:T(8,128)(2,1)}, bf16[7,128,1024]{2,1,0:T(8,128)(2,1)}, u32[]{:S(2)}, u32[]{:S(2)}) collective-permute-start(bf16[7,128,1024]{2,1,0:T(8,128)(2,1)} %get-tuple-element.15), channel_id=1, source_target_pairs={{8,0},{16,8},{24,16},{9,1},{17,9},{25,17},{10,2},{18,10},{26,18},{... | collective-permute-start | bytes 5505032 | tf_op jit(solution)/shard_map/ppermute | solution.py:22
  237.9 0.0 copy-done.1
  237.9 0.1 copy.25
  238.0 0.1 select_reduce_fusion
  238.1 0.0 copy-done.2
  238.2 0.0 copy-done.3
  238.2 0.2 select_reduce_fusion.2
  238.4 0.1 reduce-precision_convert_fusion.1
  238.5 0.7 pad_maximum_fusion.refs_2_
  239.2 0.0 collective-permute-done.2
  239.2 1.1 constant_dynamic-update-slice_fusion.1
  240.3 0.0 collective-permute-done.3
  240.3 0.1 constant_dynamic-update-slice_fusion
  240.4 0.1 broadcast_select_fusion
  240.5 1.6 collective-permute-start.4
  242.1 0.2 slice.59
  242.2 0.0 copy-start.5
  242.3 2.2 collective-permute-done.4
  244.4 0.9 fusion.5.refs_6_
  245.3 0.1 fusion.8
  245.4 0.3 maximum_maximum_fusion
  245.7 0.4 fusion.9
  246.1 3.5 %collective-permute-start.6 = (bf16[2,30,2,1152]{3,2,1,0:T(2,128)(2,1)S(1)}, bf16[2,30,2,1152]{3,2,1,0:T(2,128)(2,1)S(1)}, u32[]{:S(2)}, u32[]{:S(2)}) collective-permute-start(bf16[2,30,2,1152]{3,2,1,0:T(2,128)(2,1)S(1)} %get-tuple-element.28), channel_id=1, source_target_pairs={{0,2},{2,4},{4,6},{1,3},{3,5},{5,7},{8,10},{10,12},{12,14},{9,11},... | collective-permute-start | bytes 829448 | tf_op jit(solution)/shard_map/ppermute | solution.py:22
  249.6 1.3 collective-permute-start.5
  250.9 0.6 copy.24
  251.5 0.1 stack_broadcast_in_dim.2
  251.6 0.6 slice_bitcast_fusion
  252.2 2.6 collective-permute-done.6.refs_8_
  254.8 3.0 collective-permute-start.1
  257.8 1.2 collective-permute-done.5.refs_7_
  259.1 15.8 %collective-permute-done.7.refs_3_ = bf16[7,128,1024]{2,1,0:T(8,128)(2,1)} collective-permute-done((bf16[7,128,1024]{2,1,0:T(8,128)(2,1)}, bf16[7,128,1024]{2,1,0:T(8,128)(2,1)}, u32[]{:S(2)}, u32[]{:S(2)}) %collective-permute-start.7) | collective-permute-done | bytes 1835040 | tf_op jit(solution)/shard_map/ppermute | solution.py:22
  274.8 0.0 collective-permute-done.8.refs_5_
  274.9 25.8 %slab_1.1 = (bf16[2,16,128,1024]{3,2,1,0:T(8,128)(2,1)}, bf16[128,256]{1,0:T(8,128)(2,1)}) custom-call(s32[6,128]{1,0:T(8,128)} %get-tuple-element.36.refs_0_, bf16[32,30]{1,0:T(8,128)(2,1)} %bitcast.31, bf16[80,144]{1,0:T(8,128)(2,1)} %pad_maximum_fusion.refs_2_, bf16[7,128,1024]{2,1,0:T(8,128)(2,1)} %collective-permute-done.7.refs_3_, ...), custom_call_target="tpu_custom_call" | custom-call | flops 20000000000 | bytes 16000000 | tf_op jit(solution)/shard_map/slab_1/pallas_call | solution.py:305
  300.7 4.6 %collective-permute-start.9 = (bf16[128,256]{1,0:T(8,128)(2,1)}, bf16[128,256]{1,0:T(8,128)(2,1)S(1)}, u32[]{:S(2)}, u32[]{:S(2)}) collective-permute-start(bf16[128,256]{1,0:T(8,128)(2,1)} %get-tuple-element.19), channel_id=1, source_target_pairs={{0,7},{1,6},{2,5},{3,4},{4,3},{5,2},{6,1},{7,0},{8,15},{9,14},{10,... | collective-permute-start | bytes 196616 | tf_op jit(solution)/shard_map/ppermute | solution.py:382
  305.2 0.0 collective-permute-done.refs_3_
  305.2 0.0 collective-permute-done.1.refs_5_
  305.2 25.8 %slab_0.1 = (bf16[2,16,128,1024]{3,2,1,0:T(8,128)(2,1)}, bf16[128,256]{1,0:T(8,128)(2,1)}) custom-call(s32[6,128]{1,0:T(8,128)} %get-tuple-element.37.refs_0_, bf16[32,30]{1,0:T(8,128)(2,1)} %bitcast.32, bf16[80,144]{1,0:T(8,128)(2,1)} %pad_maximum_fusion.refs_2_, ...), custom_call_target="tpu_custom_call", output_to_operand_aliasing={{0}: (9, {})} | custom-call | flops 20000000000 | bytes 16000000 | tf_op jit(solution)/shard_map/slab_0/pallas_call | solution.py:305
  331.0 0.0 collective-permute-done.9
  331.0 1.6 convolution_multiply_fusion
  (17 shorter events, 0.2 us)
Async XLA Ops:
  0.6 237.2 %copy-start.1 = (f32[5,5]{1,0:T(8,128)S(1)}, f32[5,5]{1,0:T(8,128)}, u32[]{:S(2)}) copy-start(f32[5,5]{1,0:T(8,128)} %param.7) | copy-start | bytes 304
  0.6 237.5 %copy-start.2 = (s32[2,3,128]{2,0,1:T(2,128)S(1)}, s32[2,3,128]{2,0,1:T(2,128)}, u32[]{:S(2)}) copy-start(s32[2,3,128]{2,0,1:T(2,128)} %param.8) | copy-start | bytes 9220
  0.7 237.5 %copy-start.3 = (f32[15]{0:T(128)S(1)}, f32[15]{0:T(128)}, u32[]{:S(2)}) copy-start(f32[15]{0:T(128)} %param.6) | copy-start | bytes 184
  226.0 14.4 %collective-permute-start.3 = (bf16[2,7,4,1152]{3,2,1,0:T(4,128)(2,1)S(1)}, bf16[2,7,4,1152]{3,2,1,0:T(4,128)(2,1)S(1)}, u32[]{:S(2)}, u32[]{:S(2)}) collective-permute-start(bf16[2,7,4,1152]{3,2,1,0:T(4,128)(2,1)S(1)} %get-tuple-element.30), channel_id=1, source_target_pairs={{8,0},{16,8},{24,16},{9,1},{17,9},{25,17},{10,2},{18,10},{26,18},{... | collective-permute-start | bytes 387080 | tf_op jit(solution)/shard_map/ppermute | solution.py:22
  227.9 11.3 %collective-permute-start.2 = (bf16[2,7,4,1152]{3,2,1,0:T(4,128)(2,1)S(1)}, bf16[2,7,4,1152]{3,2,1,0:T(4,128)(2,1)S(1)}, u32[]{:S(2)}, u32[]{:S(2)}) collective-permute-start(bf16[2,7,4,1152]{3,2,1,0:T(4,128)(2,1)S(1)} %get-tuple-element.31), channel_id=1, source_target_pairs={{0,8},{8,16},{16,24},{1,9},{9,17},{17,25},{2,10},{10,18},{18,26},{... | collective-permute-start | bytes 387080 | tf_op jit(solution)/shard_map/ppermute | solution.py:22
  230.3 74.9 %collective-permute-start = (bf16[7,128,1024]{2,1,0:T(8,128)(2,1)}, bf16[7,128,1024]{2,1,0:T(8,128)(2,1)}, u32[]{:S(2)}, u32[]{:S(2)}) collective-permute-start(bf16[7,128,1024]{2,1,0:T(8,128)(2,1)} %get-tuple-element.11), channel_id=1, source_target_pairs={{0,8},{8,16},{16,24},{1,9},{9,17},{17,25},{2,10},{10,18},{18,26},{... | collective-permute-start | bytes 5505032 | tf_op jit(solution)/shard_map/ppermute | solution.py:22
  232.3 42.6 %collective-permute-start.7 = (bf16[7,128,1024]{2,1,0:T(8,128)(2,1)}, bf16[7,128,1024]{2,1,0:T(8,128)(2,1)}, u32[]{:S(2)}, u32[]{:S(2)}) collective-permute-start(bf16[7,128,1024]{2,1,0:T(8,128)(2,1)} %get-tuple-element.14), channel_id=1, source_target_pairs={{0,8},{8,16},{16,24},{1,9},{9,17},{17,25},{2,10},{10,18},{18,26},{... | collective-permute-start | bytes 5505032 | tf_op jit(solution)/shard_map/ppermute | solution.py:22
  234.2 40.7 %collective-permute-start.8 = (bf16[7,128,1024]{2,1,0:T(8,128)(2,1)}, bf16[7,128,1024]{2,1,0:T(8,128)(2,1)}, u32[]{:S(2)}, u32[]{:S(2)}) collective-permute-start(bf16[7,128,1024]{2,1,0:T(8,128)(2,1)} %get-tuple-element.15), channel_id=1, source_target_pairs={{8,0},{16,8},{24,16},{9,1},{17,9},{25,17},{10,2},{18,10},{26,18},{... | collective-permute-start | bytes 5505032 | tf_op jit(solution)/shard_map/ppermute | solution.py:22
  240.5 4.0 %collective-permute-start.4 = (bf16[2,30,2,128]{3,2,1,0:T(2,128)(2,1)S(1)}, bf16[2,30,2,128]{3,2,1,0:T(2,128)(2,1)S(1)}, u32[]{:S(2)}, u32[]{:S(2)}) collective-permute-start(bf16[2,30,2,128]{3,2,1,0:T(2,128)(2,1)S(1)} %broadcast_select_fusion), channel_id=1, source_target_pairs={{0,1},{1,0},{2,3},{3,2},{4,5},{5,4},{6,7},{7,6},{8,9},{9,8},{10,11... | collective-permute-start | bytes 92168 | tf_op jit(solution)/shard_map/ppermute | solution.py:357
  242.2 9.3 %copy-start.5 = (s32[2,1]{0,1:T(1,128)S(1)}, s32[2,1]{0,1:T(1,128)}, u32[]{:S(2)}) copy-start(s32[2,1]{0,1:T(1,128)} %param.9) | copy-start | bytes 28
  245.3 29.5 %copy-start = (bf16[2,30,128,128]{3,2,1,0:T(8,128)(2,1)}, bf16[2,30,128,128]{3,2,1,0:T(8,128)(2,1)S(1)}, u32[]{:S(2)}) copy-start(bf16[2,30,128,128]{3,2,1,0:T(8,128)(2,1)S(1)} %fusion.5.refs_6_) | copy-start | bytes 5898244
  246.1 8.7 %collective-permute-start.6 = (bf16[2,30,2,1152]{3,2,1,0:T(2,128)(2,1)S(1)}, bf16[2,30,2,1152]{3,2,1,0:T(2,128)(2,1)S(1)}, u32[]{:S(2)}, u32[]{:S(2)}) collective-permute-start(bf16[2,30,2,1152]{3,2,1,0:T(2,128)(2,1)S(1)} %get-tuple-element.28), channel_id=1, source_target_pairs={{0,2},{2,4},{4,6},{1,3},{3,5},{5,7},{8,10},{10,12},{12,14},{9,11},... | collective-permute-start | bytes 829448 | tf_op jit(solution)/shard_map/ppermute | solution.py:22
  249.6 9.4 %collective-permute-start.5 = (bf16[2,30,2,1152]{3,2,1,0:T(2,128)(2,1)S(1)}, bf16[2,30,2,1152]{3,2,1,0:T(2,128)(2,1)}, u32[]{:S(2)}, u32[]{:S(2)}) collective-permute-start(bf16[2,30,2,1152]{3,2,1,0:T(2,128)(2,1)S(1)} %get-tuple-element.29), channel_id=1, source_target_pairs={{2,0},{4,2},{6,4},{3,1},{5,3},{7,5},{10,8},{12,10},{14,12},{11,9},... | collective-permute-start | bytes 829448 | tf_op jit(solution)/shard_map/ppermute | solution.py:22
  254.8 20.0 %copy-start.4 = (bf16[2,30,2,1152]{3,2,1,0:T(2,128)(2,1)}, bf16[2,30,2,1152]{3,2,1,0:T(2,128)(2,1)S(1)}, u32[]{:S(2)}) copy-start(bf16[2,30,2,1152]{3,2,1,0:T(2,128)(2,1)S(1)} %collective-permute-done.6.refs_8_) | copy-start | bytes 829444
  254.8 50.4 %collective-permute-start.1 = (bf16[7,128,1024]{2,1,0:T(8,128)(2,1)}, bf16[7,128,1024]{2,1,0:T(8,128)(2,1)}, u32[]{:S(2)}, u32[]{:S(2)}) collective-permute-start(bf16[7,128,1024]{2,1,0:T(8,128)(2,1)} %get-tuple-element.12), channel_id=1, source_target_pairs={{8,0},{16,8},{24,16},{9,1},{17,9},{25,17},{10,2},{18,10},{26,18},{... | collective-permute-start | bytes 5505032 | tf_op jit(solution)/shard_map/ppermute | solution.py:22
  300.7 30.4 %collective-permute-start.9 = (bf16[128,256]{1,0:T(8,128)(2,1)}, bf16[128,256]{1,0:T(8,128)(2,1)S(1)}, u32[]{:S(2)}, u32[]{:S(2)}) collective-permute-start(bf16[128,256]{1,0:T(8,128)(2,1)} %get-tuple-element.19), channel_id=1, source_target_pairs={{0,7},{1,6},{2,5},{3,4},{4,3},{5,2},{6,1},{7,0},{8,15},{9,14},{10,... | collective-permute-start | bytes 196616 | tf_op jit(solution)/shard_map/ppermute | solution.py:382

commit v4 on v3

--- a/solution.py
+++ b/solution.py
@@ -12,6 +12,8 @@
 REACH = SIDE // 2
 TILE = 128
 BLOCK = 16
+WINDOW = 64
+EDGE = 8
 bf16 = jnp.bfloat16
 f32 = jnp.float32
 
@@ -42,14 +44,15 @@
 
 
 def smooth_matrix(smooth_kernel):
-    depth = 3 * BLOCK
-    out_ids = jnp.arange(BLOCK, dtype=jnp.int32)[:, None]
+    depth = WINDOW + 2 * EDGE
+    out_ids = jnp.arange(WINDOW, dtype=jnp.int32)[:, None]
     in_ids = jnp.arange(depth, dtype=jnp.int32)[None, :]
-    step = in_ids - out_ids - (BLOCK - REACH)
+    step = in_ids - out_ids - (EDGE - REACH)
     hit = step[None, :, :, None] == jnp.arange(SIDE, dtype=jnp.int32)
     table = jnp.sum(jnp.where(hit, smooth_kernel.T[:, None, None, :], 0.0), axis=3)
+    table = jnp.swapaxes(table.reshape(SIDE, WINDOW // BLOCK, BLOCK, depth), 0, 1)
     high, low = split(table)
-    return jnp.concatenate([high, high, low], axis=2).reshape(SIDE * BLOCK, 3 * depth)
+    return jnp.concatenate([high, high, low], axis=3).reshape(SIDE * WINDOW, 3 * depth)
 
 
 def iota(shape, dim):
@@ -59,7 +62,7 @@
 def slab_kernel(
     row_step, frame_step,
     spots_ref, taps_ref, w2_ref, low_ref, own_ref, high_ref, edge_ref, below_ref, above_ref,
-    out_ref, last_ref, w1, chi, clo, kept, flat,
+    out_ref, last_ref, w1, chi, clo, carry, outer, kept, flat,
 ):
     frame_count, tiles, row_count, _ = kept.shape
     near = taps_ref.shape[1]
@@ -73,7 +76,8 @@
         both = both.reshape(frame_count, 2, 8, block.shape[2])
         return both[:, 0] + both[:, 1]
 
-    def keep(value, tile, place):
+    def keep(above, below, tile, place):
+        value = jnp.concatenate([above, below], axis=1)
         high = value.astype(bf16)
         chi[:, tile, place, :] = high
         clo[:, tile, place, :] = (value - high.astype(f32)).astype(bf16)
@@ -93,67 +97,92 @@
             above = above_ref[0, :, :, cols].astype(f32)
             gap = jnp.zeros((near, 8 - 2 * REACH, TILE), f32)
             one = filtered(jnp.concatenate([below, gap, above], axis=1))
-            two = jnp.concatenate([one, one], axis=1)
-            keep(two, tile, slice(0, BLOCK))
-            keep(two, tile, slice(BLOCK + row_count, 2 * BLOCK + row_count))
+            carry[:, tile] = one
+            outer[:, tile] = one
 
     @pl.when(at < steps_1)
     def _():
-        for h in range(row_step // BLOCK):
-            rows = slice(BLOCK * h, BLOCK * h + BLOCK)
-            place = pl.ds(pl.multiple_of(BLOCK + at * row_step + BLOCK * h, BLOCK), BLOCK)
-            for tile in range(0, tiles, 2):
-                cols = slice(tile * TILE, (tile + 2) * TILE)
+        def keep_all(tile, parts):
+            parts = [carry[:, tile]] + parts
+            for q in range(0, len(parts) - 1, 2):
+                place = pl.ds(pl.multiple_of(at * row_step + EDGE * q, BLOCK), BLOCK)
+                keep(parts[q], parts[q + 1], tile, place)
+            carry[:, tile] = parts[-1]
+
+        for tile in range(0, tiles, 2):
+            cols = slice(tile * TILE, (tile + 2) * TILE)
+            parts = []
+            for h in range(0, row_step, BLOCK):
+                rows = slice(h, h + BLOCK)
                 block = jnp.concatenate(
                     [low_ref[:, rows, cols], own_ref[0, :, rows, cols], high_ref[:, rows, cols]],
                     axis=0,
                 ).astype(f32)
-                value = jnp.concatenate([filtered(block[:, :8]), filtered(block[:, 8:])], axis=1)
-                keep(value[..., :TILE], tile, place)
-                keep(value[..., TILE:], tile + 1, place)
-            block = edge_ref[0, :, rows, :].astype(f32)
-            value = filtered(jnp.concatenate([block[:, :8], block[:, 8:]], axis=2))
-            value = jnp.concatenate([value[..., :TILE], value[..., TILE:]], axis=1)
-            keep(value, tiles, place)
+                parts += [filtered(block[:, :EDGE]), filtered(block[:, EDGE:])]
+            keep_all(tile, [part[..., :TILE] for part in parts])
+            keep_all(tile + 1, [part[..., TILE:] for part in parts])
+        parts = []
+        for h in range(0, row_step, BLOCK):
+            block = edge_ref[0, :, h : h + BLOCK, :].astype(f32)
+            both = filtered(jnp.concatenate([block[:, :EDGE], block[:, EDGE:]], axis=2))
+            parts += [both[..., :TILE], both[..., TILE:]]
+        keep_all(tiles, parts)
+
+    @pl.when(at == steps_1 - 1)
+    def _():
+        for tile in range(tiles + 1):
+            keep(carry[:, tile], outer[:, tile], tile, slice(row_count, row_count + BLOCK))
 
     @pl.when((at >= steps_1) & (at < steps_1 + steps_2))
     def _():
         lane = iota((BLOCK, TILE), 1)
         edge_of = [lane < 2, lane < 1, None, lane >= TILE - 1, lane >= TILE - 2]
 
-        def one_frame(k, carry):
+        def one_frame(k, unused):
             frame = (at - steps_1) * frame_step + k
-            for row in range(0, row_count, BLOCK):
+            depth = WINDOW + 2 * EDGE
+            parts_of = range(WINDOW // BLOCK)
+            for row in range(0, row_count, WINDOW):
                 turned = {}
+
+                def finish(tile):
+                    for m in parts_of:
+                        total = turned[m, REACH, tile]
+                        for b in range(SIDE):
+                            if b != REACH:
+                                beside = (tile + (1 if b > REACH else -1)) % (tiles + 1)
+                                total = total + jnp.where(
+                                    edge_of[b], turned[m, b, beside], turned[m, b, tile]
+                                )
+                        value = total.astype(bf16)
+                        rows = slice(row + m * BLOCK, row + (m + 1) * BLOCK)
+                        out_ref[0, k, rows, tile * TILE : (tile + 1) * TILE] = value
+                        kept[frame, tile, rows, :] = value.astype(f32)
+
                 order = [tiles] + list(range(tiles))
+                done = 0
                 for p in range(0, len(order), 2):
                     pair = order[p : p + 2]
-                    parts = []
+                    stacks = []
                     for tile in pair:
-                        high = chi[frame, tile, row : row + 3 * BLOCK, :]
-                        low = clo[frame, tile, row : row + 3 * BLOCK, :]
-                        parts.append(jnp.concatenate([high, low, high], axis=0))
+                        high = chi[frame, tile, row : row + depth, :]
+                        low = clo[frame, tile, row : row + depth, :]
+                        stacks.append(jnp.concatenate([high, low, high], axis=0))
                     both = jnp.dot(
-                        w2_ref[...], jnp.concatenate(parts, axis=1), preferred_element_type=f32
+                        w2_ref[...], jnp.concatenate(stacks, axis=1), preferred_element_type=f32
                     )
                     for q, tile in enumerate(pair):
-                        for b in range(SIDE):
-                            part = both[b * BLOCK : (b + 1) * BLOCK, q * TILE : (q + 1) * TILE]
-                            if b != REACH:
-                                part = pltpu.roll(part, (REACH - b) % TILE, 1)
-                            turned[b, tile] = part
-                for tile in range(tiles):
-                    total = turned[REACH, tile]
-                    for b in range(SIDE):
-                        if b != REACH:
-                            beside = (tile + (1 if b > REACH else -1)) % (tiles + 1)
-                            total = total + jnp.where(
-                                edge_of[b], turned[b, beside], turned[b, tile]
-                            )
-                    value = total.astype(bf16)
-                    out_ref[0, k, row : row + BLOCK, tile * TILE : (tile + 1) * TILE] = value
-                    kept[frame, tile, row : row + BLOCK, :] = value.astype(f32)
-            return carry
+                        for m in parts_of:
+                            for b in range(SIDE):
+                                at_row = (m * SIDE + b) * BLOCK
+                                part = both[at_row : at_row + BLOCK, q * TILE : (q + 1) * TILE]
+                                if b != REACH:
+                                    part = pltpu.roll(part, (REACH - b) % TILE, 1)
+                                turned[m, b, tile] = part
+                    while done < pair[-1] or (done < tiles and pair[-1] == tiles - 1):
+                        finish(done)
+                        done += 1
+            return unused
 
         lax.fori_loop(0, frame_step, one_frame, 0)
 
@@ -163,7 +192,7 @@
 
         lane = iota((PATCH, TILE), 1)
 
-        def some(i8, carry):
+        def some(i8, unused):
             for j in range(8):
                 i = i8 * 8 + j
                 frame, row, tile = spots_ref[0, i], spots_ref[1, i], spots_ref[2, i]
@@ -174,7 +203,7 @@
                 here, there = pltpu.roll(here, shift, 1), pltpu.roll(there, shift, 1)
                 part = jnp.where(lane < turn, here, there)
                 flat[pl.ds(pl.multiple_of(i * PATCH, PATCH), PATCH), :] = part.astype(bf16)
-            return carry
+            return unused
 
         lax.fori_loop(0, slot_count // 8, some, 0)
         low_bits = PATCH - 1
@@ -195,7 +224,7 @@
         last_ref[...] = jnp.where(live, normed, 0.0).astype(bf16)
 
 
-def cut_kernel(frames, rim, low1, high1, low0, high0, top, bottom, left, right, sems):
+def cut_kernel(frames, rim, low1, high1, low0, high0, top, bottom, left, right, pieces, sems):
     slabs, frame_count, row_count, col_count = frames.shape
     narrow = row_count
     reads = [
@@ -204,17 +233,20 @@
         (frames.at[:, :, :, pl.ds(0, TILE)], left),
         (frames.at[:, :, :, pl.ds(col_count - TILE, TILE)], right),
     ]
+    fetches = [
+        (frames.at[1, pl.ds(frame_count - HALF, HALF)], pieces.at[0]),
+        (frames.at[1, pl.ds(0, HALF)], pieces.at[1]),
+        (frames.at[0, pl.ds(frame_count - HALF, HALF)], pieces.at[2]),
+        (frames.at[0, pl.ds(0, HALF)], pieces.at[3]),
+    ]
     writes = [
-        (frames.at[1, pl.ds(frame_count - HALF, HALF)], low1),
-        (frames.at[1, pl.ds(0, HALF)], high1),
-        (frames.at[0, pl.ds(frame_count - HALF, HALF)], low0),
-        (frames.at[0, pl.ds(0, HALF)], high0),
+        (pieces.at[i], target) for i, target in enumerate([low1, high1, low0, high0])
     ]
     copies = [
         pltpu.make_async_copy(source, target, sems.at[i])
-        for i, (source, target) in enumerate(reads + writes)
+        for i, (source, target) in enumerate(reads + fetches + writes)
     ]
-    for copy in copies:
+    for copy in copies[:8]:
         copy.start()
     for copy in copies[:4]:
         copy.wait()
@@ -236,7 +268,10 @@
             cols = lax.dot_general(first, left[s, f], over_lanes, preferred_element_type=f32)
             cols += lax.dot_general(last, right[s, f], over_lanes, preferred_element_type=f32)
             rim[s, f, :, col_count : col_count + narrow] = cols[: 2 * REACH].astype(bf16)
-    for copy in copies[4:]:
+    for fetch, write in zip(copies[4:8], copies[8:]):
+        fetch.wait()
+        write.start()
+    for copy in copies[8:]:
         copy.wait()
 
 
@@ -257,7 +292,8 @@
             pltpu.VMEM((slabs, frame_count, BLOCK, col_count), bf16),
             pltpu.VMEM((slabs, frame_count, row_count, TILE), bf16),
             pltpu.VMEM((slabs, frame_count, row_count, TILE), bf16),
-            pltpu.SemaphoreType.DMA((8,)),
+            pltpu.VMEM((4, HALF, row_count, col_count), bf16),
+            pltpu.SemaphoreType.DMA((12,)),
         ],
         compiler_params=pltpu.CompilerParams(vmem_limit_bytes=60 * 1024 * 1024),
         name="cut",
@@ -301,7 +337,7 @@
     def body(*refs):
         slab_kernel(row_step, frame_step, *refs[:9], *refs[count:])
 
-    tall = row_count + 2 * BLOCK
+    tall = row_count + 2 * EDGE
     return pl.pallas_call(
         body,
         grid=(steps_1 + steps_2 + 1,),
@@ -321,6 +357,8 @@
             pltpu.VMEM((16 * frame_count, 8 * near), bf16),
             pltpu.VMEM((frame_count, wide // TILE, tall, TILE), bf16),
             pltpu.VMEM((frame_count, wide // TILE, tall, TILE), bf16),
+            pltpu.VMEM((frame_count, wide // TILE, EDGE, TILE), f32),
+            pltpu.VMEM((frame_count, wide // TILE, EDGE, TILE), f32),
             pltpu.VMEM((frame_count, col_count // TILE, row_count, TILE), f32),
             pltpu.VMEM((slot_count * PATCH, TILE), bf16),
         ],
@@ -345,8 +383,6 @@
     )
     low1 = shifted(send_low1, "omega", 1)
     high1 = shifted(send_high1, "omega", -1)
-    low0 = shifted(send_low0, "omega", 1)
-    high0 = shifted(send_high0, "omega", -1)
     lane = jnp.arange(TILE, dtype=jnp.int32)[None, :]
     step = jnp.arange(REACH, dtype=jnp.int32)[:, None]
     after = (lane == step).astype(bf16)
@@ -361,6 +397,9 @@
         right = shifted(rim[:, :, :REACH, col_count:], "col", -1)
         sides = jnp.concatenate([right, left], axis=2)
         place = jnp.concatenate([after, before], axis=0)
+    send_low0, send_high0, sides = lax.optimization_barrier((send_low0, send_high0, sides))
+    low0 = shifted(send_low0, "omega", 1)
+    high0 = shifted(send_high0, "omega", -1)
     edge = jnp.einsum("sfkr,kc->sfrc", sides, place, preferred_element_type=bf16)
     ends = jnp.concatenate([edge[:, :, :REACH], edge[:, :, -REACH:]], axis=2)
     line = jnp.concatenate([rim[..., :col_count], ends], axis=3)

time: 333 us -> 101 us (0.30)
  the two profiles are of different devices: /device:TPU:2 before, /device:TPU:1 now
where the time goes in v4:
time: 101 us
  Pallas kernels  59.4 us (59%)
  starting transfers between devices  27.7 us (27%)
  waiting for transfers between devices  5.06 us (5%)
  local copies, waits for them, and re-layouts  4.08 us (4%)
  matrix products  2.52 us (2%)
  other arithmetic  1.06 us (1%)
    pallas_call x2, Pallas kernels, run_slab(): pl.pallas_call(body, grid=(steps_1 + steps_2 + 1,), in_specs=in_specs, ou...  51.9 us
    ppermute x8, starting transfers between devices, shifted(): return lax.ppermute(block, axis, route)  22.2 us
    pallas_call x1, Pallas kernels, cut(): pl.pallas_call(cut_kernel, in_specs=[anywhere], out_specs=[pl.BlockSpec(m...  7.52 us
    ppermute x1, starting transfers between devices, shards(): lax.ppermute(second, ('row', 'col'), [(i, count - 1 - i) for i in range(c...  4.25 us
    ppermute x8, waiting for transfers between devices, shifted(): return lax.ppermute(block, axis, route)  3.43 us
  transfers between devices with their start and end apart: 10, of which 3 were waited for; matrix products, arithmetic and copies ran while one was open for 5% of the time, Pallas kernels for 51%

profile of v4, /device:TPU:1, one launch (start us, length us, event | category | flops | bytes accessed | tf_op | source)
XLA Modules:
  0.0 100.9 jit_solution(2585132983197690459)
XLA Ops:
  0.6 0.0 copy-start.2
  0.6 0.0 copy-start.3
  0.7 0.0 copy-start.4
  0.7 7.5 %cut.1 = (bf16[2,16,4,1152]{3,2,1,0:T(4,128)(2,1)}, bf16[7,128,1024]{2,1,0:T(8,128)(2,1)}, bf16[7,128,1024]{2,1,0:T(8,128)(2,1)}, bf16[7,128,1024]{2,1,0:T(8,128)(2,1)}, bf16[7,128,1024]{2,1,0:T(8,128)(2,1)}) custom-call(bf16[2,16,128,1024]{3,2,1,0:T(8,128)(2,1)} %refs_4_.3), custom_call_target="tpu_custom_call" | custom-call | tf_op jit(solution)/shard_map/cut/pallas_call | solution.py:282
  8.2 1.1 %fusion.10 = (bf16[2,7,4,1152]{3,2,1,0:T(4,128)(2,1)S(1)}, bf16[2,7,4,1152]{3,2,1,0:T(4,128)(2,1)S(1)}) fusion(bf16[2,16,4,1152]{3,2,1,0:T(4,128)(2,1)} %get-tuple-element.16), kind=kLoop, calls=%fused_computation.45 | loop fusion | bytes 516096 | tf_op jit(solution)/shard_map/slice | solution.py:382
  9.3 2.0 %collective-permute-start.1 = (bf16[2,7,4,1152]{3,2,1,0:T(4,128)(2,1)S(1)}, bf16[2,7,4,1152]{3,2,1,0:T(4,128)(2,1)S(1)}, u32[]{:S(2)}, u32[]{:S(2)}) collective-permute-start(bf16[2,7,4,1152]{3,2,1,0:T(4,128)(2,1)S(1)} %get-tuple-element.36), channel_id=1, source_target_pairs={{8,0},{16,8},{24,16},{9,1},{17,9},{25,17},{10,2},{18,10},{26,18},{... | collective-permute-start | bytes 387080 | tf_op jit(solution)/shard_map/ppermute | solution.py:24
  11.3 4.5 %collective-permute-start = (bf16[2,7,4,1152]{3,2,1,0:T(4,128)(2,1)S(1)}, bf16[2,7,4,1152]{3,2,1,0:T(4,128)(2,1)S(1)}, u32[]{:S(2)}, u32[]{:S(2)}) collective-permute-start(bf16[2,7,4,1152]{3,2,1,0:T(4,128)(2,1)S(1)} %get-tuple-element.37), channel_id=1, source_target_pairs={{0,8},{8,16},{16,24},{1,9},{9,17},{17,25},{2,10},{10,18},{18,26},{... | collective-permute-start | bytes 387080 | tf_op jit(solution)/shard_map/ppermute | solution.py:24
  15.7 2.4 %collective-permute-start.7 = (bf16[7,128,1024]{2,1,0:T(8,128)(2,1)}, bf16[7,128,1024]{2,1,0:T(8,128)(2,1)}, u32[]{:S(2)}, u32[]{:S(2)}) collective-permute-start(bf16[7,128,1024]{2,1,0:T(8,128)(2,1)} %get-tuple-element.20), channel_id=1, source_target_pairs={{0,8},{8,16},{16,24},{1,9},{9,17},{17,25},{2,10},{10,18},{18,26},{... | collective-permute-start | bytes 5505032 | tf_op jit(solution)/shard_map/ppermute | solution.py:24
  18.2 3.2 %collective-permute-start.8 = (bf16[7,128,1024]{2,1,0:T(8,128)(2,1)}, bf16[7,128,1024]{2,1,0:T(8,128)(2,1)}, u32[]{:S(2)}, u32[]{:S(2)}) collective-permute-start(bf16[7,128,1024]{2,1,0:T(8,128)(2,1)} %get-tuple-element.21), channel_id=1, source_target_pairs={{8,0},{16,8},{24,16},{9,1},{17,9},{25,17},{10,2},{18,10},{26,18},{... | collective-permute-start | bytes 5505032 | tf_op jit(solution)/shard_map/ppermute | solution.py:24
  21.4 0.1 copy.33
  21.6 0.2 select_reduce_fusion
  21.8 0.0 copy-done.3
  21.8 0.2 select_reduce_fusion.2
  22.0 0.1 reduce-precision_convert_fusion.1
  22.1 0.1 pad_maximum_fusion
  22.3 0.0 collective-permute-done
  22.4 0.0 copy-done.1
  22.4 0.1 constant_dynamic-update-slice_fusion.1
  22.5 0.0 collective-permute-done.1
  22.5 0.1 constant_dynamic-update-slice_fusion
  22.6 0.1 broadcast_select_fusion
  22.6 1.3 %collective-permute-start.2 = (bf16[2,30,2,128]{3,2,1,0:T(2,128)(2,1)S(1)}, bf16[2,30,2,128]{3,2,1,0:T(2,128)(2,1)S(1)}, u32[]{:S(2)}, u32[]{:S(2)}) collective-permute-start(bf16[2,30,2,128]{3,2,1,0:T(2,128)(2,1)S(1)} %broadcast_select_fusion), channel_id=1, source_target_pairs={{0,1},{1,0},{2,3},{3,2},{4,5},{5,4},{6,7},{7,6},{8,9},{9,8},{10,11... | collective-permute-start | bytes 92168 | tf_op jit(solution)/shard_map/ppermute | solution.py:393
  24.0 0.2 slice.59
  24.1 1.6 %collective-permute-done.2 = bf16[2,30,2,128]{3,2,1,0:T(2,128)(2,1)S(1)} collective-permute-done((bf16[2,30,2,128]{3,2,1,0:T(2,128)(2,1)S(1)}, bf16[2,30,2,128]{3,2,1,0:T(2,128)(2,1)S(1)}, u32[]{:S(2)}, u32[]{:S(2)}) %collective-permute-start.2) | collective-permute-done | bytes 30752 | tf_op jit(solution)/shard_map/ppermute | solution.py:393
  25.8 0.9 fusion.5.refs_6_
  26.7 0.0 copy-start.7
  26.7 0.1 fusion.8
  26.7 0.3 maximum_maximum_fusion
  27.0 0.4 fusion.9
  27.4 3.2 %collective-permute-start.6 = (bf16[2,30,2,1152]{3,2,1,0:T(2,128)(2,1)S(1)}, bf16[2,30,2,1152]{3,2,1,0:T(2,128)(2,1)S(1)}, u32[]{:S(2)}, u32[]{:S(2)}) collective-permute-start(bf16[2,30,2,1152]{3,2,1,0:T(2,128)(2,1)S(1)} %get-tuple-element.34), channel_id=1, source_target_pairs={{0,2},{2,4},{4,6},{1,3},{3,5},{5,7},{8,10},{10,12},{12,14},{9,11},... | collective-permute-start | bytes 829448 | tf_op jit(solution)/shard_map/ppermute | solution.py:24
  30.7 1.3 %collective-permute-start.5 = (bf16[2,30,2,1152]{3,2,1,0:T(2,128)(2,1)S(1)}, bf16[2,30,2,1152]{3,2,1,0:T(2,128)(2,1)S(1)}, u32[]{:S(2)}, u32[]{:S(2)}) collective-permute-start(bf16[2,30,2,1152]{3,2,1,0:T(2,128)(2,1)S(1)} %get-tuple-element.35), channel_id=1, source_target_pairs={{2,0},{4,2},{6,4},{3,1},{5,3},{7,5},{10,8},{12,10},{14,12},{11,9},... | collective-permute-start | bytes 829448 | tf_op jit(solution)/shard_map/ppermute | solution.py:24
  32.0 0.6 copy.32
  32.6 0.7 copy.34
  33.3 0.1 stack_broadcast_in_dim.2
  33.4 0.6 slice_bitcast_fusion
  34.0 3.5 %collective-permute-start.3 = (bf16[7,128,1024]{2,1,0:T(8,128)(2,1)}, bf16[7,128,1024]{2,1,0:T(8,128)(2,1)}, u32[]{:S(2)}, u32[]{:S(2)}) collective-permute-start(bf16[7,128,1024]{2,1,0:T(8,128)(2,1)} %get-tuple-element.17), channel_id=1, source_target_pairs={{0,8},{8,16},{16,24},{1,9},{9,17},{17,25},{2,10},{10,18},{18,26},{... | collective-permute-start | bytes 5505032 | tf_op jit(solution)/shard_map/ppermute | solution.py:24
  37.4 0.0 collective-permute-done.6.refs_8_
  37.4 2.2 %collective-permute-start.4 = (bf16[7,128,1024]{2,1,0:T(8,128)(2,1)}, bf16[7,128,1024]{2,1,0:T(8,128)(2,1)}, u32[]{:S(2)}, u32[]{:S(2)}) collective-permute-start(bf16[7,128,1024]{2,1,0:T(8,128)(2,1)} %get-tuple-element.18), channel_id=1, source_target_pairs={{8,0},{16,8},{24,16},{9,1},{17,9},{25,17},{10,2},{18,10},{26,18},{... | collective-permute-start | bytes 5505032 | tf_op jit(solution)/shard_map/ppermute | solution.py:24
  39.6 0.4 collective-permute-done.5.refs_7_
  40.0 0.0 collective-permute-done.7.refs_3_
  40.0 3.0 %collective-permute-done.8.refs_5_ = bf16[7,128,1024]{2,1,0:T(8,128)(2,1)} collective-permute-done((bf16[7,128,1024]{2,1,0:T(8,128)(2,1)}, bf16[7,128,1024]{2,1,0:T(8,128)(2,1)}, u32[]{:S(2)}, u32[]{:S(2)}) %collective-permute-start.8) | collective-permute-done | bytes 1835040 | tf_op jit(solution)/shard_map/ppermute | solution.py:24
  43.0 26.0 %slab_1.1 = (bf16[2,16,128,1024]{3,2,1,0:T(8,128)(2,1)}, bf16[128,256]{1,0:T(8,128)(2,1)}) custom-call(s32[6,128]{1,0:T(8,128)} %get-tuple-element.42.refs_0_, bf16[32,30]{1,0:T(8,128)(2,1)} %bitcast.35, bf16[320,240]{1,0:T(8,128)(2,1)} %bitcast.31, bf16[7,128,1024]{2,1,0:T(8,128)(2,1)} %collective-permute-done.7.refs_3_, ...), custom_call_target="tpu_custom_call" | custom-call | flops 20000000000 | bytes 16000000 | tf_op jit(solution)/shard_map/slab_1/pallas_call | solution.py:341
  69.0 4.2 %collective-permute-start.9 = (bf16[128,256]{1,0:T(8,128)(2,1)}, bf16[128,256]{1,0:T(8,128)(2,1)S(1)}, u32[]{:S(2)}, u32[]{:S(2)}) collective-permute-start(bf16[128,256]{1,0:T(8,128)(2,1)} %get-tuple-element.25), channel_id=1, source_target_pairs={{0,7},{1,6},{2,5},{3,4},{4,3},{5,2},{6,1},{7,0},{8,15},{9,14},{10,... | collective-permute-start | bytes 196616 | tf_op jit(solution)/shard_map/ppermute | solution.py:421
  73.3 0.0 collective-permute-done.3.refs_3_
  73.3 0.0 collective-permute-done.4.refs_5_
  73.3 25.9 %slab_0.1 = (bf16[2,16,128,1024]{3,2,1,0:T(8,128)(2,1)}, bf16[128,256]{1,0:T(8,128)(2,1)}) custom-call(s32[6,128]{1,0:T(8,128)} %get-tuple-element.43.refs_0_, bf16[32,30]{1,0:T(8,128)(2,1)} %bitcast.36, bf16[320,240]{1,0:T(8,128)(2,1)} %bitcast.32, bf16[7,128,1024]{2,1,0:T(8,128)(2,1)} %collective-permute-done.3.refs_3_, ...), custom_call_target="tpu_custom_call", output_to_operand_aliasing={{0}: (9, {})} | custom-call | flops 20000000000 | bytes 16000000 | tf_op jit(solution)/shard_map/slab_0/pallas_call | solution.py:341
  99.2 0.0 collective-permute-done.9
  99.2 1.6 %convolution_multiply_fusion = f32[128,128]{1,0:T(8,128)} fusion(bf16[128,256]{1,0:T(8,128)(2,1)} %get-tuple-element.24, bf16[128,256]{1,0:T(8,128)(2,1)S(1)} %collective-permute-done.9), kind=kOutput, calls=%fused_computation | convolution fusion | flops 8404992 | bytes 196608 | tf_op jit(solution)/shard_map/dot_general | solution.py:424
  (22 shorter events, 0.2 us)
Async XLA Ops:
  0.6 20.8 %copy-start.2 = (f32[5,5]{1,0:T(8,128)S(1)}, f32[5,5]{1,0:T(8,128)}, u32[]{:S(2)}) copy-start(f32[5,5]{1,0:T(8,128)} %param.7) | copy-start | bytes 304
  0.6 21.1 %copy-start.3 = (s32[2,3,128]{2,0,1:T(2,128)S(1)}, s32[2,3,128]{2,0,1:T(2,128)}, u32[]{:S(2)}) copy-start(s32[2,3,128]{2,0,1:T(2,128)} %param.8) | copy-start | bytes 9220
  0.7 21.2 %copy-start.4 = (f32[15]{0:T(128)S(1)}, f32[15]{0:T(128)}, u32[]{:S(2)}) copy-start(f32[15]{0:T(128)} %param.6) | copy-start | bytes 184
  8.2 14.2 %copy-start.1 = (bf16[2,16,4,1152]{3,2,1,0:T(4,128)(2,1)S(1)}, bf16[2,16,4,1152]{3,2,1,0:T(4,128)(2,1)}, u32[]{:S(2)}) copy-start(bf16[2,16,4,1152]{3,2,1,0:T(4,128)(2,1)} %get-tuple-element.16) | copy-start | bytes 884740
  9.3 13.2 %collective-permute-start.1 = (bf16[2,7,4,1152]{3,2,1,0:T(4,128)(2,1)S(1)}, bf16[2,7,4,1152]{3,2,1,0:T(4,128)(2,1)S(1)}, u32[]{:S(2)}, u32[]{:S(2)}) collective-permute-start(bf16[2,7,4,1152]{3,2,1,0:T(4,128)(2,1)S(1)} %get-tuple-element.36), channel_id=1, source_target_pairs={{8,0},{16,8},{24,16},{9,1},{17,9},{25,17},{10,2},{18,10},{26,18},{... | collective-permute-start | bytes 387080 | tf_op jit(solution)/shard_map/ppermute | solution.py:24
  11.3 11.0 %collective-permute-start = (bf16[2,7,4,1152]{3,2,1,0:T(4,128)(2,1)S(1)}, bf16[2,7,4,1152]{3,2,1,0:T(4,128)(2,1)S(1)}, u32[]{:S(2)}, u32[]{:S(2)}) collective-permute-start(bf16[2,7,4,1152]{3,2,1,0:T(4,128)(2,1)S(1)} %get-tuple-element.37), channel_id=1, source_target_pairs={{0,8},{8,16},{16,24},{1,9},{9,17},{17,25},{2,10},{10,18},{18,26},{... | collective-permute-start | bytes 387080 | tf_op jit(solution)/shard_map/ppermute | solution.py:24
  15.7 24.3 %collective-permute-start.7 = (bf16[7,128,1024]{2,1,0:T(8,128)(2,1)}, bf16[7,128,1024]{2,1,0:T(8,128)(2,1)}, u32[]{:S(2)}, u32[]{:S(2)}) collective-permute-start(bf16[7,128,1024]{2,1,0:T(8,128)(2,1)} %get-tuple-element.20), channel_id=1, source_target_pairs={{0,8},{8,16},{16,24},{1,9},{9,17},{17,25},{2,10},{10,18},{18,26},{... | collective-permute-start | bytes 5505032 | tf_op jit(solution)/shard_map/ppermute | solution.py:24
  18.2 24.9 %collective-permute-start.8 = (bf16[7,128,1024]{2,1,0:T(8,128)(2,1)}, bf16[7,128,1024]{2,1,0:T(8,128)(2,1)}, u32[]{:S(2)}, u32[]{:S(2)}) collective-permute-start(bf16[7,128,1024]{2,1,0:T(8,128)(2,1)} %get-tuple-element.21), channel_id=1, source_target_pairs={{8,0},{16,8},{24,16},{9,1},{17,9},{25,17},{10,2},{18,10},{26,18},{... | collective-permute-start | bytes 5505032 | tf_op jit(solution)/shard_map/ppermute | solution.py:24
  22.6 3.1 %collective-permute-start.2 = (bf16[2,30,2,128]{3,2,1,0:T(2,128)(2,1)S(1)}, bf16[2,30,2,128]{3,2,1,0:T(2,128)(2,1)S(1)}, u32[]{:S(2)}, u32[]{:S(2)}) collective-permute-start(bf16[2,30,2,128]{3,2,1,0:T(2,128)(2,1)S(1)} %broadcast_select_fusion), channel_id=1, source_target_pairs={{0,1},{1,0},{2,3},{3,2},{4,5},{5,4},{6,7},{7,6},{8,9},{9,8},{10,11... | collective-permute-start | bytes 92168 | tf_op jit(solution)/shard_map/ppermute | solution.py:393
  26.6 16.4 %copy-start = (bf16[2,30,128,128]{3,2,1,0:T(8,128)(2,1)}, bf16[2,30,128,128]{3,2,1,0:T(8,128)(2,1)S(1)}, u32[]{:S(2)}) copy-start(bf16[2,30,128,128]{3,2,1,0:T(8,128)(2,1)S(1)} %fusion.5.refs_6_) | copy-start | bytes 5898244
  26.7 6.6 %copy-start.7 = (s32[2,1]{0,1:T(1,128)S(1)}, s32[2,1]{0,1:T(1,128)}, u32[]{:S(2)}) copy-start(s32[2,1]{0,1:T(1,128)} %param.9) | copy-start | bytes 28
  27.4 10.0 %collective-permute-start.6 = (bf16[2,30,2,1152]{3,2,1,0:T(2,128)(2,1)S(1)}, bf16[2,30,2,1152]{3,2,1,0:T(2,128)(2,1)S(1)}, u32[]{:S(2)}, u32[]{:S(2)}) collective-permute-start(bf16[2,30,2,1152]{3,2,1,0:T(2,128)(2,1)S(1)} %get-tuple-element.34), channel_id=1, source_target_pairs={{0,2},{2,4},{4,6},{1,3},{3,5},{5,7},{8,10},{10,12},{12,14},{9,11},... | collective-permute-start | bytes 829448 | tf_op jit(solution)/shard_map/ppermute | solution.py:24
  30.7 9.4 %collective-permute-start.5 = (bf16[2,30,2,1152]{3,2,1,0:T(2,128)(2,1)S(1)}, bf16[2,30,2,1152]{3,2,1,0:T(2,128)(2,1)S(1)}, u32[]{:S(2)}, u32[]{:S(2)}) collective-permute-start(bf16[2,30,2,1152]{3,2,1,0:T(2,128)(2,1)S(1)} %get-tuple-element.35), channel_id=1, source_target_pairs={{2,0},{4,2},{6,4},{3,1},{5,3},{7,5},{10,8},{12,10},{14,12},{11,9},... | collective-permute-start | bytes 829448 | tf_op jit(solution)/shard_map/ppermute | solution.py:24
  34.0 39.3 %collective-permute-start.3 = (bf16[7,128,1024]{2,1,0:T(8,128)(2,1)}, bf16[7,128,1024]{2,1,0:T(8,128)(2,1)}, u32[]{:S(2)}, u32[]{:S(2)}) collective-permute-start(bf16[7,128,1024]{2,1,0:T(8,128)(2,1)} %get-tuple-element.17), channel_id=1, source_target_pairs={{0,8},{8,16},{16,24},{1,9},{9,17},{17,25},{2,10},{10,18},{18,26},{... | collective-permute-start | bytes 5505032 | tf_op jit(solution)/shard_map/ppermute | solution.py:24
  37.4 5.6 %copy-start.5 = (bf16[2,30,2,1152]{3,2,1,0:T(2,128)(2,1)}, bf16[2,30,2,1152]{3,2,1,0:T(2,128)(2,1)S(1)}, u32[]{:S(2)}) copy-start(bf16[2,30,2,1152]{3,2,1,0:T(2,128)(2,1)S(1)} %collective-permute-done.6.refs_8_) | copy-start | bytes 829444
  37.4 35.8 %collective-permute-start.4 = (bf16[7,128,1024]{2,1,0:T(8,128)(2,1)}, bf16[7,128,1024]{2,1,0:T(8,128)(2,1)}, u32[]{:S(2)}, u32[]{:S(2)}) collective-permute-start(bf16[7,128,1024]{2,1,0:T(8,128)(2,1)} %get-tuple-element.18), channel_id=1, source_target_pairs={{8,0},{16,8},{24,16},{9,1},{17,9},{25,17},{10,2},{18,10},{26,18},{... | collective-permute-start | bytes 5505032 | tf_op jit(solution)/shard_map/ppermute | solution.py:24
  40.0 3.0 %copy-start.6 = (bf16[2,30,2,1152]{3,2,1,0:T(2,128)(2,1)}, bf16[2,30,2,1152]{3,2,1,0:T(2,128)(2,1)S(1)}, u32[]{:S(2)}) copy-start(bf16[2,30,2,1152]{3,2,1,0:T(2,128)(2,1)S(1)} %collective-permute-done.5.refs_7_) | copy-start | bytes 829444
  69.0 30.2 %collective-permute-start.9 = (bf16[128,256]{1,0:T(8,128)(2,1)}, bf16[128,256]{1,0:T(8,128)(2,1)S(1)}, u32[]{:S(2)}, u32[]{:S(2)}) collective-permute-start(bf16[128,256]{1,0:T(8,128)(2,1)} %get-tuple-element.25), channel_id=1, source_target_pairs={{0,7},{1,6},{2,5},{3,4},{4,3},{5,2},{6,1},{7,0},{8,15},{9,14},{10,... | collective-permute-start | bytes 196616 | tf_op jit(solution)/shard_map/ppermute | solution.py:421

commit v5 on v4

--- a/solution.py
+++ b/solution.py
@@ -71,10 +71,11 @@
     at = pl.program_id(0)
 
     def filtered(block):
-        part = block.reshape(near * 8, block.shape[2]).astype(bf16)
+        part = block.reshape(near * BLOCK, block.shape[2])
         both = jnp.dot(w1[...], part, preferred_element_type=f32)
-        both = both.reshape(frame_count, 2, 8, block.shape[2])
-        return both[:, 0] + both[:, 1]
+        both = both.reshape(frame_count, 2, BLOCK, block.shape[2])
+        both = both[:, 0] + both[:, 1]
+        return [both[:, :EDGE], both[:, EDGE:]]
 
     def keep(above, below, tile, place):
         value = jnp.concatenate([above, below], axis=1)
@@ -85,20 +86,22 @@
     @pl.when(at == 0)
     def _():
         count = 2 * frame_count
-        tall = (iota((8 * count, count), 0) // 8 == iota((8 * count, count), 1)).astype(bf16)
-        wide = (iota((near, 8 * near), 1) // 8 == iota((near, 8 * near), 0)).astype(bf16)
+        bits = BLOCK.bit_length() - 1
+        shape = (BLOCK * count, count)
+        tall = (iota(shape, 0) >> bits == iota(shape, 1)).astype(bf16)
+        shape = (near, BLOCK * near)
+        wide = (iota(shape, 1) >> bits == iota(shape, 0)).astype(bf16)
         full = jnp.dot(tall, taps_ref[...], preferred_element_type=f32).astype(bf16)
         full = jnp.dot(full, wide, preferred_element_type=f32)
-        same = iota(full.shape, 0) % 8 == iota(full.shape, 1) % 8
+        same = iota(full.shape, 0) & (BLOCK - 1) == iota(full.shape, 1) & (BLOCK - 1)
         w1[...] = jnp.where(same, full, 0.0).astype(bf16)
         for tile in range(tiles + 1):
             cols = slice(tile * TILE, tile * TILE + TILE)
             below = below_ref[0, :, :, cols].astype(f32)
             above = above_ref[0, :, :, cols].astype(f32)
-            gap = jnp.zeros((near, 8 - 2 * REACH, TILE), f32)
-            one = filtered(jnp.concatenate([below, gap, above], axis=1))
-            carry[:, tile] = one
-            outer[:, tile] = one
+            gap = jnp.zeros((near, BLOCK - 2 * REACH, TILE), f32)
+            block = jnp.concatenate([below, gap, above], axis=1).astype(bf16)
+            outer[:, tile], carry[:, tile] = filtered(block)
 
     @pl.when(at < steps_1)
     def _():
@@ -117,15 +120,17 @@
                 block = jnp.concatenate(
                     [low_ref[:, rows, cols], own_ref[0, :, rows, cols], high_ref[:, rows, cols]],
                     axis=0,
-                ).astype(f32)
-                parts += [filtered(block[:, :EDGE]), filtered(block[:, EDGE:])]
+                )
+                parts += filtered(block)
             keep_all(tile, [part[..., :TILE] for part in parts])
             keep_all(tile + 1, [part[..., TILE:] for part in parts])
+        both = jnp.concatenate(
+            [edge_ref[0, :, h : h + BLOCK, :] for h in range(0, row_step, BLOCK)], axis=2
+        )
         parts = []
-        for h in range(0, row_step, BLOCK):
-            block = edge_ref[0, :, h : h + BLOCK, :].astype(f32)
-            both = filtered(jnp.concatenate([block[:, :EDGE], block[:, EDGE:]], axis=2))
-            parts += [both[..., :TILE], both[..., TILE:]]
+        upper, lower = filtered(both)
+        for q in range(row_step // BLOCK):
+            parts += [part[..., q * TILE : (q + 1) * TILE] for part in (upper, lower)]
         keep_all(tiles, parts)
 
     @pl.when(at == steps_1 - 1)
@@ -354,7 +359,7 @@
             jax.ShapeDtypeStruct((slot_count, PATCH * PATCH), bf16),
         ],
         scratch_shapes=[
-            pltpu.VMEM((16 * frame_count, 8 * near), bf16),
+            pltpu.VMEM((2 * BLOCK * frame_count, BLOCK * near), bf16),
             pltpu.VMEM((frame_count, wide // TILE, tall, TILE), bf16),
             pltpu.VMEM((frame_count, wide // TILE, tall, TILE), bf16),
             pltpu.VMEM((frame_count, wide // TILE, EDGE, TILE), f32),
@@ -417,8 +422,9 @@
     local = jnp.stack([frame, row, tile, beside, TILE - col % TILE, live], axis=1)
 
     smoothed, second = run_slab(1, None, local[1], taps, w2, low1, frames, high1, edge, below, above)
-    count = lax.axis_size("row") * lax.axis_size("col")
-    second = lax.ppermute(second, ("row", "col"), [(i, count - 1 - i) for i in range(count)])
+    second = lax.all_gather(second, ("row", "col"))
+    mirror = second.shape[0] - 1 - lax.axis_index(("row", "col"))
+    second = lax.dynamic_index_in_dim(second, mirror, keepdims=False)
     smoothed, first = run_slab(0, smoothed, local[0], taps, w2, low0, frames, high0, edge, below, above)
     scores = (
         lax.dot_general(first, second, (((1,), (1,)), ((), ())), preferred_element_type=f32)

time: 101 us -> 138 us (1.37)
  the two profiles are of different devices: /device:TPU:1 before, /device:TPU:2 now
where the time goes in v5:
time: 138 us; the launch traced here: 136 us
  Pallas kernels  69.7 us (51%)
  blocking collectives  32 us (23%)
  starting transfers between devices  21.8 us (16%)
  local copies, waits for them, and re-layouts  4.05 us (3%)
  waiting for transfers between devices  3.99 us (3%)
  matrix products  2.52 us (2%)
    pallas_call x2, Pallas kernels, run_slab(): pl.pallas_call(body, grid=(steps_1 + steps_2 + 1,), in_specs=in_specs, ou...  62.2 us
    all_gather x1, blocking collectives, shards(): second = lax.all_gather(second, ('row', 'col'))  32 us
    ppermute x8, starting transfers between devices, shifted(): return lax.ppermute(block, axis, route)  20.2 us
    pallas_call x1, Pallas kernels, cut(): pl.pallas_call(cut_kernel, in_specs=[anywhere], out_specs=[pl.BlockSpec(m...  7.5 us
  transfers between devices with their start and end apart: 9, of which 3 were waited for; matrix products, arithmetic and copies ran while one was open for 4% of the time, Pallas kernels for 23%

profile of v5, /device:TPU:2, one launch (start us, length us, event | category | flops | bytes accessed | tf_op | source)
XLA Modules:
  0.0 136.1 jit_solution(1435030797745083967)
XLA Ops:
  0.6 0.0 copy-start.2
  0.6 0.0 copy-start.3
  0.7 0.0 copy-start.4
  0.7 7.5 %cut.1 = (bf16[2,16,4,1152]{3,2,1,0:T(4,128)(2,1)}, bf16[7,128,1024]{2,1,0:T(8,128)(2,1)}, bf16[7,128,1024]{2,1,0:T(8,128)(2,1)}, bf16[7,128,1024]{2,1,0:T(8,128)(2,1)}, bf16[7,128,1024]{2,1,0:T(8,128)(2,1)}) custom-call(bf16[2,16,128,1024]{3,2,1,0:T(8,128)(2,1)} %refs_4_.3), custom_call_target="tpu_custom_call" | custom-call | tf_op jit(solution)/shard_map/cut/pallas_call | solution.py:287
  8.2 0.0 copy-start.1
  8.2 1.1 fusion.13
  9.3 1.9 %collective-permute-start.1 = (bf16[2,7,4,1152]{3,2,1,0:T(4,128)(2,1)S(1)}, bf16[2,7,4,1152]{3,2,1,0:T(4,128)(2,1)S(1)}, u32[]{:S(2)}, u32[]{:S(2)}) collective-permute-start(bf16[2,7,4,1152]{3,2,1,0:T(4,128)(2,1)S(1)} %get-tuple-element.36), channel_id=1, source_target_pairs={{8,0},{16,8},{24,16},{9,1},{17,9},{25,17},{10,2},{18,10},{26,18},{... | collective-permute-start | bytes 387080 | tf_op jit(solution)/shard_map/ppermute | solution.py:24
  11.2 2.4 %collective-permute-start = (bf16[2,7,4,1152]{3,2,1,0:T(4,128)(2,1)S(1)}, bf16[2,7,4,1152]{3,2,1,0:T(4,128)(2,1)S(1)}, u32[]{:S(2)}, u32[]{:S(2)}) collective-permute-start(bf16[2,7,4,1152]{3,2,1,0:T(4,128)(2,1)S(1)} %get-tuple-element.37), channel_id=1, source_target_pairs={{0,8},{8,16},{16,24},{1,9},{9,17},{17,25},{2,10},{10,18},{18,26},{... | collective-permute-start | bytes 387080 | tf_op jit(solution)/shard_map/ppermute | solution.py:24
  13.6 1.9 %collective-permute-start.7 = (bf16[7,128,1024]{2,1,0:T(8,128)(2,1)}, bf16[7,128,1024]{2,1,0:T(8,128)(2,1)}, u32[]{:S(2)}, u32[]{:S(2)}) collective-permute-start(bf16[7,128,1024]{2,1,0:T(8,128)(2,1)} %get-tuple-element.20), channel_id=1, source_target_pairs={{0,8},{8,16},{16,24},{1,9},{9,17},{17,25},{2,10},{10,18},{18,26},{... | collective-permute-start | bytes 5505032 | tf_op jit(solution)/shard_map/ppermute | solution.py:24
  15.6 3.6 %collective-permute-start.8 = (bf16[7,128,1024]{2,1,0:T(8,128)(2,1)}, bf16[7,128,1024]{2,1,0:T(8,128)(2,1)}, u32[]{:S(2)}, u32[]{:S(2)}) collective-permute-start(bf16[7,128,1024]{2,1,0:T(8,128)(2,1)} %get-tuple-element.21), channel_id=1, source_target_pairs={{8,0},{16,8},{24,16},{9,1},{17,9},{25,17},{10,2},{18,10},{26,18},{... | collective-permute-start | bytes 5505032 | tf_op jit(solution)/shard_map/ppermute | solution.py:24
  19.3 0.1 copy.33
  19.4 0.2 select_reduce_fusion
  19.7 0.2 select_reduce_fusion.2
  19.8 0.1 reduce-precision_convert_fusion.1
  20.0 0.1 pad_maximum_fusion
  20.1 0.0 collective-permute-done
  20.2 0.1 constant_dynamic-update-slice_fusion.1
  20.3 0.0 collective-permute-done.1
  20.3 0.1 constant_dynamic-update-slice_fusion
  20.4 0.1 broadcast_select_fusion
  20.5 1.6 %collective-permute-start.2 = (bf16[2,30,2,128]{3,2,1,0:T(2,128)(2,1)S(1)}, bf16[2,30,2,128]{3,2,1,0:T(2,128)(2,1)S(1)}, u32[]{:S(2)}, u32[]{:S(2)}) collective-permute-start(bf16[2,30,2,128]{3,2,1,0:T(2,128)(2,1)S(1)} %broadcast_select_fusion), channel_id=1, source_target_pairs={{0,1},{1,0},{2,3},{3,2},{4,5},{5,4},{6,7},{7,6},{8,9},{9,8},{10,11... | collective-permute-start | bytes 92168 | tf_op jit(solution)/shard_map/ppermute | solution.py:398
  22.0 0.2 slice.59
  22.2 2.2 %collective-permute-done.2 = bf16[2,30,2,128]{3,2,1,0:T(2,128)(2,1)S(1)} collective-permute-done((bf16[2,30,2,128]{3,2,1,0:T(2,128)(2,1)S(1)}, bf16[2,30,2,128]{3,2,1,0:T(2,128)(2,1)S(1)}, u32[]{:S(2)}, u32[]{:S(2)}) %collective-permute-start.2) | collective-permute-done | bytes 30752 | tf_op jit(solution)/shard_map/ppermute | solution.py:398
  24.4 0.9 fusion.7.refs_6_
  25.3 0.0 copy-start.7
  25.3 0.1 fusion.11
  25.4 0.3 maximum_maximum_fusion
  25.7 0.4 fusion.12
  26.1 3.5 %collective-permute-start.6 = (bf16[2,30,2,1152]{3,2,1,0:T(2,128)(2,1)S(1)}, bf16[2,30,2,1152]{3,2,1,0:T(2,128)(2,1)S(1)}, u32[]{:S(2)}, u32[]{:S(2)}) collective-permute-start(bf16[2,30,2,1152]{3,2,1,0:T(2,128)(2,1)S(1)} %get-tuple-element.34), channel_id=1, source_target_pairs={{0,2},{2,4},{4,6},{1,3},{3,5},{5,7},{8,10},{10,12},{12,14},{9,11},... | collective-permute-start | bytes 829448 | tf_op jit(solution)/shard_map/ppermute | solution.py:24
  29.6 1.3 collective-permute-start.5
  30.9 0.6 copy.32
  31.5 0.7 copy.34
  32.2 0.0 copy-done.7
  32.2 0.1 stack_broadcast_in_dim.2
  32.3 0.6 slice_bitcast_fusion
  32.9 1.9 %collective-permute-start.3 = (bf16[7,128,1024]{2,1,0:T(8,128)(2,1)}, bf16[7,128,1024]{2,1,0:T(8,128)(2,1)}, u32[]{:S(2)}, u32[]{:S(2)}) collective-permute-start(bf16[7,128,1024]{2,1,0:T(8,128)(2,1)} %get-tuple-element.17), channel_id=1, source_target_pairs={{0,8},{8,16},{16,24},{1,9},{9,17},{17,25},{2,10},{10,18},{18,26},{... | collective-permute-start | bytes 5505032 | tf_op jit(solution)/shard_map/ppermute | solution.py:24
  34.8 0.0 collective-permute-done.6.refs_8_
  34.8 3.6 %collective-permute-start.4 = (bf16[7,128,1024]{2,1,0:T(8,128)(2,1)}, bf16[7,128,1024]{2,1,0:T(8,128)(2,1)}, u32[]{:S(2)}, u32[]{:S(2)}) collective-permute-start(bf16[7,128,1024]{2,1,0:T(8,128)(2,1)} %get-tuple-element.18), channel_id=1, source_target_pairs={{8,0},{16,8},{24,16},{9,1},{17,9},{25,17},{10,2},{18,10},{26,18},{... | collective-permute-start | bytes 5505032 | tf_op jit(solution)/shard_map/ppermute | solution.py:24
  38.5 0.5 collective-permute-done.5.refs_7_
  38.9 0.0 collective-permute-done.7.refs_3_
  39.0 1.3 collective-permute-done.8.refs_5_
  40.2 0.0 copy-done.5
  40.3 31.1 %slab_1.1 = (bf16[2,16,128,1024]{3,2,1,0:T(8,128)(2,1)}, bf16[128,256]{1,0:T(8,128)(2,1)}) custom-call(s32[6,128]{1,0:T(8,128)} %get-tuple-element.42.refs_0_, bf16[32,30]{1,0:T(8,128)(2,1)} %bitcast.39, bf16[320,240]{1,0:T(8,128)(2,1)} %bitcast.35, bf16[7,128,1024]{2,1,0:T(8,128)(2,1)} %collective-permute-done.7.refs_3_, ...), custom_call_target="tpu_custom_call" | custom-call | flops 20000000000 | bytes 16000000 | tf_op jit(solution)/shard_map/slab_1/pallas_call | solution.py:346
  71.4 32.0 %all-gather = bf16[1024,256]{1,0:T(8,128)(2,1)S(1)} all-gather(bf16[128,256]{1,0:T(8,128)(2,1)} %get-tuple-element.25), channel_id=2, replica_groups=mesh['omega'=4,'row'=4,'col'=2] {'row','col'}, dimensions={0}, use_global_device_ids=true | all-gather | bytes 589824 | tf_op jit(solution)/shard_map/all_gather | solution.py:425
  103.3 0.0 collective-permute-done.3.refs_3_
  103.3 0.0 collective-permute-done.4.refs_5_
  103.3 31.1 %slab_0.1 = (bf16[2,16,128,1024]{3,2,1,0:T(8,128)(2,1)}, bf16[128,256]{1,0:T(8,128)(2,1)}) custom-call(s32[6,128]{1,0:T(8,128)} %get-tuple-element.43.refs_0_, bf16[32,30]{1,0:T(8,128)(2,1)} %bitcast.40, bf16[320,240]{1,0:T(8,128)(2,1)} %bitcast.36, bf16[7,128,1024]{2,1,0:T(8,128)(2,1)} %collective-permute-done.3.refs_3_, ...), custom_call_target="tpu_custom_call", output_to_operand_aliasing={{0}: (9, {})} | custom-call | flops 20000000000 | bytes 16000000 | tf_op jit(solution)/shard_map/slab_0/pallas_call | solution.py:346
  134.4 1.6 %convolution_multiply_fusion = f32[128,128]{1,0:T(8,128)} fusion(bf16[128,256]{1,0:T(8,128)(2,1)} %get-tuple-element.24, bf16[8,128,256]{2,1,0:T(8,128)(2,1)S(1)} %bitcast.33, s32[]{:T(128)S(6)} %select_n.60), kind=kOutput, calls=%fused_computation | convolution fusion | flops 8404992 | bytes 196612 | tf_op jit(solution)/shard_map/dot_general | solution.py:430
  (21 shorter events, 0.2 us)
Async XLA Ops:
  0.6 18.6 %copy-start.2 = (f32[5,5]{1,0:T(8,128)S(1)}, f32[5,5]{1,0:T(8,128)}, u32[]{:S(2)}) copy-start(f32[5,5]{1,0:T(8,128)} %param.7) | copy-start | bytes 304
  0.6 19.0 %copy-start.3 = (s32[2,3,128]{2,0,1:T(2,128)S(1)}, s32[2,3,128]{2,0,1:T(2,128)}, u32[]{:S(2)}) copy-start(s32[2,3,128]{2,0,1:T(2,128)} %param.8) | copy-start | bytes 9220
  0.7 19.0 %copy-start.4 = (f32[15]{0:T(128)S(1)}, f32[15]{0:T(128)}, u32[]{:S(2)}) copy-start(f32[15]{0:T(128)} %param.6) | copy-start | bytes 184
  8.2 12.0 %copy-start.1 = (bf16[2,16,4,1152]{3,2,1,0:T(4,128)(2,1)S(1)}, bf16[2,16,4,1152]{3,2,1,0:T(4,128)(2,1)}, u32[]{:S(2)}) copy-start(bf16[2,16,4,1152]{3,2,1,0:T(4,128)(2,1)} %get-tuple-element.16) | copy-start | bytes 884740
  9.3 11.0 %collective-permute-start.1 = (bf16[2,7,4,1152]{3,2,1,0:T(4,128)(2,1)S(1)}, bf16[2,7,4,1152]{3,2,1,0:T(4,128)(2,1)S(1)}, u32[]{:S(2)}, u32[]{:S(2)}) collective-permute-start(bf16[2,7,4,1152]{3,2,1,0:T(4,128)(2,1)S(1)} %get-tuple-element.36), channel_id=1, source_target_pairs={{8,0},{16,8},{24,16},{9,1},{17,9},{25,17},{10,2},{18,10},{26,18},{... | collective-permute-start | bytes 387080 | tf_op jit(solution)/shard_map/ppermute | solution.py:24
  11.2 8.9 %collective-permute-start = (bf16[2,7,4,1152]{3,2,1,0:T(4,128)(2,1)S(1)}, bf16[2,7,4,1152]{3,2,1,0:T(4,128)(2,1)S(1)}, u32[]{:S(2)}, u32[]{:S(2)}) collective-permute-start(bf16[2,7,4,1152]{3,2,1,0:T(4,128)(2,1)S(1)} %get-tuple-element.37), channel_id=1, source_target_pairs={{0,8},{8,16},{16,24},{1,9},{9,17},{17,25},{2,10},{10,18},{18,26},{... | collective-permute-start | bytes 387080 | tf_op jit(solution)/shard_map/ppermute | solution.py:24
  13.6 25.3 %collective-permute-start.7 = (bf16[7,128,1024]{2,1,0:T(8,128)(2,1)}, bf16[7,128,1024]{2,1,0:T(8,128)(2,1)}, u32[]{:S(2)}, u32[]{:S(2)}) collective-permute-start(bf16[7,128,1024]{2,1,0:T(8,128)(2,1)} %get-tuple-element.20), channel_id=1, source_target_pairs={{0,8},{8,16},{16,24},{1,9},{9,17},{17,25},{2,10},{10,18},{18,26},{... | collective-permute-start | bytes 5505032 | tf_op jit(solution)/shard_map/ppermute | solution.py:24
  15.6 24.7 %collective-permute-start.8 = (bf16[7,128,1024]{2,1,0:T(8,128)(2,1)}, bf16[7,128,1024]{2,1,0:T(8,128)(2,1)}, u32[]{:S(2)}, u32[]{:S(2)}) collective-permute-start(bf16[7,128,1024]{2,1,0:T(8,128)(2,1)} %get-tuple-element.21), channel_id=1, source_target_pairs={{8,0},{16,8},{24,16},{9,1},{17,9},{25,17},{10,2},{18,10},{26,18},{... | collective-permute-start | bytes 5505032 | tf_op jit(solution)/shard_map/ppermute | solution.py:24
  20.5 4.0 %collective-permute-start.2 = (bf16[2,30,2,128]{3,2,1,0:T(2,128)(2,1)S(1)}, bf16[2,30,2,128]{3,2,1,0:T(2,128)(2,1)S(1)}, u32[]{:S(2)}, u32[]{:S(2)}) collective-permute-start(bf16[2,30,2,128]{3,2,1,0:T(2,128)(2,1)S(1)} %broadcast_select_fusion), channel_id=1, source_target_pairs={{0,1},{1,0},{2,3},{3,2},{4,5},{5,4},{6,7},{7,6},{8,9},{9,8},{10,11... | collective-permute-start | bytes 92168 | tf_op jit(solution)/shard_map/ppermute | solution.py:398
  25.3 14.9 %copy-start = (bf16[2,30,128,128]{3,2,1,0:T(8,128)(2,1)}, bf16[2,30,128,128]{3,2,1,0:T(8,128)(2,1)S(1)}, u32[]{:S(2)}) copy-start(bf16[2,30,128,128]{3,2,1,0:T(8,128)(2,1)S(1)} %fusion.7.refs_6_) | copy-start | bytes 5898244
  25.3 6.9 %copy-start.7 = (s32[2,1]{0,1:T(1,128)S(1)}, s32[2,1]{0,1:T(1,128)}, u32[]{:S(2)}) copy-start(s32[2,1]{0,1:T(1,128)} %param.9) | copy-start | bytes 28
  26.1 8.7 %collective-permute-start.6 = (bf16[2,30,2,1152]{3,2,1,0:T(2,128)(2,1)S(1)}, bf16[2,30,2,1152]{3,2,1,0:T(2,128)(2,1)S(1)}, u32[]{:S(2)}, u32[]{:S(2)}) collective-permute-start(bf16[2,30,2,1152]{3,2,1,0:T(2,128)(2,1)S(1)} %get-tuple-element.34), channel_id=1, source_target_pairs={{0,2},{2,4},{4,6},{1,3},{3,5},{5,7},{8,10},{10,12},{12,14},{9,11},... | collective-permute-start | bytes 829448 | tf_op jit(solution)/shard_map/ppermute | solution.py:24
  29.6 9.3 %collective-permute-start.5 = (bf16[2,30,2,1152]{3,2,1,0:T(2,128)(2,1)S(1)}, bf16[2,30,2,1152]{3,2,1,0:T(2,128)(2,1)S(1)}, u32[]{:S(2)}, u32[]{:S(2)}) collective-permute-start(bf16[2,30,2,1152]{3,2,1,0:T(2,128)(2,1)S(1)} %get-tuple-element.35), channel_id=1, source_target_pairs={{2,0},{4,2},{6,4},{3,1},{5,3},{7,5},{10,8},{12,10},{14,12},{11,9},... | collective-permute-start | bytes 829448 | tf_op jit(solution)/shard_map/ppermute | solution.py:24
  32.9 70.4 %collective-permute-start.3 = (bf16[7,128,1024]{2,1,0:T(8,128)(2,1)}, bf16[7,128,1024]{2,1,0:T(8,128)(2,1)}, u32[]{:S(2)}, u32[]{:S(2)}) collective-permute-start(bf16[7,128,1024]{2,1,0:T(8,128)(2,1)} %get-tuple-element.17), channel_id=1, source_target_pairs={{0,8},{8,16},{16,24},{1,9},{9,17},{17,25},{2,10},{10,18},{18,26},{... | collective-permute-start | bytes 5505032 | tf_op jit(solution)/shard_map/ppermute | solution.py:24
  34.8 5.4 %copy-start.5 = (bf16[2,30,2,1152]{3,2,1,0:T(2,128)(2,1)}, bf16[2,30,2,1152]{3,2,1,0:T(2,128)(2,1)S(1)}, u32[]{:S(2)}) copy-start(bf16[2,30,2,1152]{3,2,1,0:T(2,128)(2,1)S(1)} %collective-permute-done.6.refs_8_) | copy-start | bytes 829444
  34.8 68.5 %collective-permute-start.4 = (bf16[7,128,1024]{2,1,0:T(8,128)(2,1)}, bf16[7,128,1024]{2,1,0:T(8,128)(2,1)}, u32[]{:S(2)}, u32[]{:S(2)}) collective-permute-start(bf16[7,128,1024]{2,1,0:T(8,128)(2,1)} %get-tuple-element.18), channel_id=1, source_target_pairs={{8,0},{16,8},{24,16},{9,1},{17,9},{25,17},{10,2},{18,10},{26,18},{... | collective-permute-start | bytes 5505032 | tf_op jit(solution)/shard_map/ppermute | solution.py:24
  38.9 1.3 copy-start.6

commit v6 on v4

--- a/solution.py
+++ b/solution.py
@@ -1,3 +1,4 @@
+import functools
 import jax
 import jax.numpy as jnp
 from jax import lax
@@ -12,7 +13,7 @@
 REACH = SIDE // 2
 TILE = 128
 BLOCK = 16
-WINDOW = 64
+WINDOW = 32
 EDGE = 8
 bf16 = jnp.bfloat16
 f32 = jnp.float32
@@ -91,14 +92,16 @@
         full = jnp.dot(full, wide, preferred_element_type=f32)
         same = iota(full.shape, 0) % 8 == iota(full.shape, 1) % 8
         w1[...] = jnp.where(same, full, 0.0).astype(bf16)
-        for tile in range(tiles + 1):
-            cols = slice(tile * TILE, tile * TILE + TILE)
+        for tile in range(0, tiles + 1, 2):
+            pair = range(tile, min(tile + 2, tiles + 1))
+            cols = slice(tile * TILE, (tile + len(pair)) * TILE)
             below = below_ref[0, :, :, cols].astype(f32)
             above = above_ref[0, :, :, cols].astype(f32)
-            gap = jnp.zeros((near, 8 - 2 * REACH, TILE), f32)
-            one = filtered(jnp.concatenate([below, gap, above], axis=1))
-            carry[:, tile] = one
-            outer[:, tile] = one
+            gap = jnp.zeros((near, 8 - 2 * REACH, below.shape[2]), f32)
+            both = filtered(jnp.concatenate([below, gap, above], axis=1))
+            for q, one in enumerate(pair):
+                carry[:, one] = both[..., q * TILE : (q + 1) * TILE]
+                outer[:, one] = both[..., q * TILE : (q + 1) * TILE]
 
     @pl.when(at < steps_1)
     def _():
@@ -138,53 +141,60 @@
         lane = iota((BLOCK, TILE), 1)
         edge_of = [lane < 2, lane < 1, None, lane >= TILE - 1, lane >= TILE - 2]
 
-        def one_frame(k, unused):
-            frame = (at - steps_1) * frame_step + k
-            depth = WINDOW + 2 * EDGE
-            parts_of = range(WINDOW // BLOCK)
+        depth = WINDOW + 2 * EDGE
+        parts_of = range(WINDOW // BLOCK)
+
+        def two_frames(k2, unused):
             for row in range(0, row_count, WINDOW):
                 turned = {}
-
-                def finish(tile):
+                done = [0, 0]
+
+                def finish(f, tile):
+                    k = k2 * 2 + f
+                    frame = (at - steps_1) * frame_step + k
                     for m in parts_of:
-                        total = turned[m, REACH, tile]
+                        total = turned[f, m, REACH, tile]
                         for b in range(SIDE):
                             if b != REACH:
                                 beside = (tile + (1 if b > REACH else -1)) % (tiles + 1)
                                 total = total + jnp.where(
-                                    edge_of[b], turned[m, b, beside], turned[m, b, tile]
+                                    edge_of[b], turned[f, m, b, beside], turned[f, m, b, tile]
                                 )
                         value = total.astype(bf16)
                         rows = slice(row + m * BLOCK, row + (m + 1) * BLOCK)
                         out_ref[0, k, rows, tile * TILE : (tile + 1) * TILE] = value
                         kept[frame, tile, rows, :] = value.astype(f32)
 
-                order = [tiles] + list(range(tiles))
-                done = 0
+                order = [(f, tile) for f in range(2) for tile in [tiles] + list(range(tiles))]
                 for p in range(0, len(order), 2):
                     pair = order[p : p + 2]
                     stacks = []
-                    for tile in pair:
+                    for f, tile in pair:
+                        frame = (at - steps_1) * frame_step + k2 * 2 + f
                         high = chi[frame, tile, row : row + depth, :]
                         low = clo[frame, tile, row : row + depth, :]
                         stacks.append(jnp.concatenate([high, low, high], axis=0))
                     both = jnp.dot(
                         w2_ref[...], jnp.concatenate(stacks, axis=1), preferred_element_type=f32
                     )
-                    for q, tile in enumerate(pair):
+                    for q, (f, tile) in enumerate(pair):
                         for m in parts_of:
                             for b in range(SIDE):
                                 at_row = (m * SIDE + b) * BLOCK
                                 part = both[at_row : at_row + BLOCK, q * TILE : (q + 1) * TILE]
                                 if b != REACH:
                                     part = pltpu.roll(part, (REACH - b) % TILE, 1)
-                                turned[m, b, tile] = part
-                    while done < pair[-1] or (done < tiles and pair[-1] == tiles - 1):
-                        finish(done)
-                        done += 1
+                                turned[f, m, b, tile] = part
+                    for f in range(2):
+                        while done[f] < tiles and (f, 0, 0, done[f]) in turned:
+                            after = min(done[f] + 1, tiles)
+                            if (f, 0, 0, after) not in turned:
+                                break
+                            finish(f, done[f])
+                            done[f] += 1
             return unused
 
-        lax.fori_loop(0, frame_step, one_frame, 0)
+        lax.fori_loop(0, frame_step // 2, two_frames, 0)
 
     @pl.when(at == steps_1 + steps_2)
     def _():
@@ -224,80 +234,89 @@
         last_ref[...] = jnp.where(live, normed, 0.0).astype(bf16)
 
 
-def cut_kernel(frames, rim, low1, high1, low0, high0, top, bottom, left, right, pieces, sems):
-    slabs, frame_count, row_count, col_count = frames.shape
-    narrow = row_count
-    reads = [
-        (frames.at[:, :, pl.ds(0, BLOCK), :], top),
-        (frames.at[:, :, pl.ds(row_count - BLOCK, BLOCK), :], bottom),
-        (frames.at[:, :, :, pl.ds(0, TILE)], left),
-        (frames.at[:, :, :, pl.ds(col_count - TILE, TILE)], right),
-    ]
+def cut_kernel(slab, frames, *refs):
+    if slab == 0:
+        other, refs = refs[0], refs[1:]
+        rim, send_low, send_high, low, high, whole, sems = refs
+    else:
+        rim, low, high, whole, sems = refs
+    frame_count, row_count, col_count = whole.shape
+    first, last = pl.ds(0, HALF), pl.ds(frame_count - HALF, HALF)
+    middle = frame_count - HALF
     fetches = [
-        (frames.at[1, pl.ds(frame_count - HALF, HALF)], pieces.at[0]),
-        (frames.at[1, pl.ds(0, HALF)], pieces.at[1]),
-        (frames.at[0, pl.ds(frame_count - HALF, HALF)], pieces.at[2]),
-        (frames.at[0, pl.ds(0, HALF)], pieces.at[3]),
+        pltpu.make_async_copy(frames.at[slab, part], whole.at[part], sems.at[i])
+        for i, part in enumerate([pl.ds(0, middle), pl.ds(middle, HALF)])
     ]
     writes = [
-        (pieces.at[i], target) for i, target in enumerate([low1, high1, low0, high0])
+        pltpu.make_async_copy(whole.at[first], high, sems.at[2]),
+        pltpu.make_async_copy(whole.at[last], low, sems.at[3]),
     ]
-    copies = [
-        pltpu.make_async_copy(source, target, sems.at[i])
-        for i, (source, target) in enumerate(reads + fetches + writes)
-    ]
-    for copy in copies[:8]:
-        copy.start()
-    for copy in copies[:4]:
-        copy.wait()
-    for s in range(slabs):
-        rows = jnp.concatenate(
-            [
-                top[s, :, :8, :].astype(f32)[:, :REACH],
-                bottom[s, :, BLOCK - 8 :, :].astype(f32)[:, 8 - REACH :],
-            ],
-            axis=1,
-        )
-        rim[s, :, :, :col_count] = rows.astype(bf16)
-        line = iota((8, TILE), 0)
-        lane = iota((8, TILE), 1)
-        first = ((line == lane) & (line < REACH)).astype(bf16)
-        last = ((line + TILE - 2 * REACH == lane) & (line >= REACH)).astype(bf16)
-        over_lanes = (((1,), (1,)), ((), ()))
-        for f in range(frame_count):
-            cols = lax.dot_general(first, left[s, f], over_lanes, preferred_element_type=f32)
-            cols += lax.dot_general(last, right[s, f], over_lanes, preferred_element_type=f32)
-            rim[s, f, :, col_count : col_count + narrow] = cols[: 2 * REACH].astype(bf16)
-    for fetch, write in zip(copies[4:8], copies[8:]):
+    for fetch in fetches:
+        fetch.start()
+    for fetch, write in zip(fetches, writes):
         fetch.wait()
         write.start()
-    for copy in copies[8:]:
-        copy.wait()
-
-
-def cut(frames):
-    slabs, frame_count, row_count, col_count = frames.shape
+    rows = jnp.concatenate(
+        [
+            whole[:, :BLOCK, :].astype(f32)[:, :REACH],
+            whole[:, row_count - BLOCK :, :].astype(f32)[:, BLOCK - REACH :],
+        ],
+        axis=1,
+    ).astype(bf16)
+    line = iota((8, TILE), 0)
+    lane = iota((8, TILE), 1)
+    left = ((line == lane) & (line < REACH)).astype(bf16)
+    right = ((line + TILE - 2 * REACH == lane) & (line >= REACH)).astype(bf16)
+    over_lanes = (((1,), (1,)), ((), ()))
+    cols = []
+    for f in range(frame_count):
+        one = lax.dot_general(left, whole[f, :, :TILE], over_lanes, preferred_element_type=f32)
+        one += lax.dot_general(
+            right, whole[f, :, col_count - TILE :], over_lanes, preferred_element_type=f32
+        )
+        cols.append(one[: 2 * REACH].astype(bf16))
+    if slab == 0:
+        targets = [rim.at[0], send_low.at[0], send_high.at[0]]
+        starts = [0, middle, 0]
+        rim[1] = other[...]
+        send_low[1] = other[middle:]
+        send_high[1] = other[:HALF]
+    else:
+        targets, starts = [rim], [0]
+    for target, start in zip(targets, starts):
+        target[:, :, :col_count] = rows[start : start + target.shape[0]]
+        for f in range(target.shape[0]):
+            target[f, :, col_count:] = cols[start + f]
+    for write in writes:
+        write.wait()
+
+
+def cut(slab, frames, other):
+    _, frame_count, row_count, col_count = frames.shape
+    anywhere = pl.BlockSpec(memory_space=pl.ANY)
+    near = pl.BlockSpec(memory_space=pltpu.VMEM)
     piece = jax.ShapeDtypeStruct((HALF, row_count, col_count), bf16)
-    anywhere = pl.BlockSpec(memory_space=pl.ANY)
+    shape = (frame_count, 2 * REACH, col_count + row_count)
+    if slab == 0:
+        operands = [frames, other]
+        shapes = [(2,) + shape, (2, HALF) + shape[1:], (2, HALF) + shape[1:]]
+    else:
+        operands = [frames]
+        shapes = [shape]
+    rims = [jax.ShapeDtypeStruct(shape, bf16) for shape in shapes]
     return pl.pallas_call(
-        cut_kernel,
-        in_specs=[anywhere],
-        out_specs=[pl.BlockSpec(memory_space=pltpu.VMEM)] + [anywhere] * 4,
-        out_shape=[
-            jax.ShapeDtypeStruct((slabs, frame_count, 2 * REACH, col_count + row_count), bf16),
-            piece, piece, piece, piece,
-        ],
+        functools.partial(cut_kernel, slab),
+        in_specs=[anywhere] + [near] * (len(operands) - 1),
+        out_specs=[near] * len(rims) + [anywhere] * 2,
+        out_shape=rims + [piece, piece],
         scratch_shapes=[
-            pltpu.VMEM((slabs, frame_count, BLOCK, col_count), bf16),
-            pltpu.VMEM((slabs, frame_count, BLOCK, col_count), bf16),
-            pltpu.VMEM((slabs, frame_count, row_count, TILE), bf16),
-            pltpu.VMEM((slabs, frame_count, row_count, TILE), bf16),
-            pltpu.VMEM((4, HALF, row_count, col_count), bf16),
-            pltpu.SemaphoreType.DMA((12,)),
+            pltpu.VMEM((frame_count, row_count, col_count), bf16),
+            pltpu.SemaphoreType.DMA((4,)),
         ],
         compiler_params=pltpu.CompilerParams(vmem_limit_bytes=60 * 1024 * 1024),
-        name="cut",
-    )(frames)
+        cost_estimate=pl.CostEstimate(flops=0, bytes_accessed=9_000_000, transcendentals=0),
+        name=f"cut_{slab}",
+    )(*operands)
 
 
 def run_slab(slab, smoothed, spots, taps, w2, low, frames, high, edge, below, above):
@@ -377,12 +396,13 @@
     first_row = lax.axis_index("row") * row_count
     first_col = lax.axis_index("col") * col_count
 
-    rim, send_low1, send_high1, send_low0, send_high0 = cut(frames)
-    rim = jnp.concatenate(
-        [shifted(rim[:, -HALF:], "omega", 1), rim, shifted(rim[:, :HALF], "omega", -1)], axis=1
-    )
+    rim, send_low1, send_high1 = cut(1, frames, None)
     low1 = shifted(send_low1, "omega", 1)
     high1 = shifted(send_high1, "omega", -1)
+    rim, rim_low, rim_high, send_low0, send_high0 = cut(0, frames, rim)
+    rim = jnp.concatenate(
+        [shifted(rim_low, "omega", 1), rim, shifted(rim_high, "omega", -1)], axis=1
+    )
     lane = jnp.arange(TILE, dtype=jnp.int32)[None, :]
     step = jnp.arange(REACH, dtype=jnp.int32)[:, None]
     after = (lane == step).astype(bf16)

time: 101 us -> 108 us (1.069)
  the two profiles are of different devices: /device:TPU:1 before, /device:TPU:2 now
where the time goes in v6:
time: 108 us; the launch traced here: 107 us
  Pallas kernels  57.2 us (53%)
  starting transfers between devices  28.7 us (27%)
  waiting for transfers between devices  11.7 us (11%)
  local copies, waits for them, and re-layouts  4.54 us (4%)
  matrix products  2.52 us (2%)
    pallas_call x2, Pallas kernels, run_slab(): pl.pallas_call(body, grid=(steps_1 + steps_2 + 1,), in_specs=in_specs, ou...  47.7 us
    ppermute x8, starting transfers between devices, shifted(): return lax.ppermute(block, axis, route)  21.5 us
    ppermute x8, waiting for transfers between devices, shifted(): return lax.ppermute(block, axis, route)  9.55 us
    pallas_call x2, Pallas kernels, cut(): pl.pallas_call(functools.partial(cut_kernel, slab), in_specs=[anywhere] +...  9.52 us
    ppermute x1, starting transfers between devices, shards(): lax.ppermute(second, ('row', 'col'), [(i, count - 1 - i) for i in range(c...  5.63 us
    ppermute x1, waiting for transfers between devices, shards(): sides = lax.ppermute(sides, 'col', [(0, 1), (1, 0)])  2.2 us
  transfers between devices with their start and end apart: 10, of which 3 were waited for; matrix products, arithmetic and copies ran while one was open for 5% of the time, Pallas kernels for 50%

profile of v6, /device:TPU:2, one launch (start us, length us, event | category | flops | bytes accessed | tf_op | source)
XLA Modules:
  0.0 106.6 jit_solution(17232771679724555701)
XLA Ops:
  0.6 4.2 %cut_1.1 = (bf16[16,4,1152]{2,1,0:T(4,128)(2,1)}, bf16[7,128,1024]{2,1,0:T(8,128)(2,1)}, bf16[7,128,1024]{2,1,0:T(8,128)(2,1)}) custom-call(bf16[2,16,128,1024]{3,2,1,0:T(8,128)(2,1)} %refs_4_.3), custom_call_target="tpu_custom_call" | custom-call | bytes 9000000 | tf_op jit(solution)/shard_map/cut_1/pallas_call | solution.py:307
  4.8 1.9 %collective-permute-start.7 = (bf16[7,128,1024]{2,1,0:T(8,128)(2,1)}, bf16[7,128,1024]{2,1,0:T(8,128)(2,1)}, u32[]{:S(2)}, u32[]{:S(2)}) collective-permute-start(bf16[7,128,1024]{2,1,0:T(8,128)(2,1)} %get-tuple-element.26), channel_id=1, source_target_pairs={{0,8},{8,16},{16,24},{1,9},{9,17},{17,25},{2,10},{10,18},{18,26},{... | collective-permute-start | bytes 5505032 | tf_op jit(solution)/shard_map/ppermute | solution.py:25
  6.8 3.6 %collective-permute-start.8 = (bf16[7,128,1024]{2,1,0:T(8,128)(2,1)}, bf16[7,128,1024]{2,1,0:T(8,128)(2,1)}, u32[]{:S(2)}, u32[]{:S(2)}) collective-permute-start(bf16[7,128,1024]{2,1,0:T(8,128)(2,1)} %get-tuple-element.27), channel_id=1, source_target_pairs={{8,0},{16,8},{24,16},{9,1},{17,9},{25,17},{10,2},{18,10},{26,18},{... | collective-permute-start | bytes 5505032 | tf_op jit(solution)/shard_map/ppermute | solution.py:25
  10.4 0.0 copy-start.1
  10.4 0.0 copy-start.2
  10.4 0.0 copy-start.3
  10.4 5.3 %cut_0.1 = (bf16[2,16,4,1152]{3,2,1,0:T(4,128)(2,1)}, bf16[2,7,4,1152]{3,2,1,0:T(4,128)(2,1)}, bf16[2,7,4,1152]{3,2,1,0:T(4,128)(2,1)}, bf16[7,128,1024]{2,1,0:T(8,128)(2,1)}, bf16[7,128,1024]{2,1,0:T(8,128)(2,1)}) custom-call(bf16[2,16,128,1024]{3,2,1,0:T(8,128)(2,1)} %refs_4_.3, bf16[16,4,1152]{2,1,0:T(4,128)(2,1)} %get-tuple-element.17.refs_0_), custom_call_target="tpu_custom_call" | custom-call | bytes 9000000 | tf_op jit(solution)/shard_map/cut_0/pallas_call | solution.py:307
  15.8 1.9 %collective-permute-start = (bf16[2,7,4,1152]{3,2,1,0:T(4,128)(2,1)}, bf16[2,7,4,1152]{3,2,1,0:T(4,128)(2,1)S(1)}, u32[]{:S(2)}, u32[]{:S(2)}) collective-permute-start(bf16[2,7,4,1152]{3,2,1,0:T(4,128)(2,1)} %get-tuple-element.20), channel_id=1, source_target_pairs={{0,8},{8,16},{16,24},{1,9},{9,17},{17,25},{2,10},{10,18},{18,26},{... | collective-permute-start | bytes 387080 | tf_op jit(solution)/shard_map/ppermute | solution.py:25
  17.7 3.6 %collective-permute-start.1 = (bf16[2,7,4,1152]{3,2,1,0:T(4,128)(2,1)}, bf16[2,7,4,1152]{3,2,1,0:T(4,128)(2,1)S(1)}, u32[]{:S(2)}, u32[]{:S(2)}) collective-permute-start(bf16[2,7,4,1152]{3,2,1,0:T(4,128)(2,1)} %get-tuple-element.22), channel_id=1, source_target_pairs={{8,0},{16,8},{24,16},{9,1},{17,9},{25,17},{10,2},{18,10},{26,18},{... | collective-permute-start | bytes 387080 | tf_op jit(solution)/shard_map/ppermute | solution.py:25
  21.4 0.1 copy.33
  21.5 0.1 select_reduce_fusion
  21.7 0.2 select_reduce_fusion.2
  21.9 0.1 reduce-precision_convert_fusion.1
  22.0 0.1 pad_maximum_fusion
  22.1 8.8 %collective-permute-done = bf16[2,7,4,1152]{3,2,1,0:T(4,128)(2,1)S(1)} collective-permute-done((bf16[2,7,4,1152]{3,2,1,0:T(4,128)(2,1)}, bf16[2,7,4,1152]{3,2,1,0:T(4,128)(2,1)S(1)}, u32[]{:S(2)}, u32[]{:S(2)}) %collective-permute-start) | collective-permute-done | bytes 129056 | tf_op jit(solution)/shard_map/ppermute | solution.py:25
  31.0 1.1 %constant_dynamic-update-slice_fusion.1 = bf16[2,30,4,1152]{3,2,1,0:T(4,128)(2,1)S(1)} fusion(bf16[2,30,4,1152]{3,2,1,0:T(4,128)(2,1)S(1)} %constant_dynamic-update-slice_fusion.2, bf16[2,16,4,1152]{3,2,1,0:T(4,128)(2,1)} %get-tuple-element.21), kind=kLoop, calls=%fused_computation.18 | loop fusion | bytes 589824
  32.1 0.7 collective-permute-done.1
  32.8 0.1 constant_dynamic-update-slice_fusion
  32.9 0.1 broadcast_select_fusion
  33.0 1.6 %collective-permute-start.2 = (bf16[2,30,2,128]{3,2,1,0:T(2,128)(2,1)S(1)}, bf16[2,30,2,128]{3,2,1,0:T(2,128)(2,1)S(1)}, u32[]{:S(2)}, u32[]{:S(2)}) collective-permute-start(bf16[2,30,2,128]{3,2,1,0:T(2,128)(2,1)S(1)} %broadcast_select_fusion), channel_id=1, source_target_pairs={{0,1},{1,0},{2,3},{3,2},{4,5},{5,4},{6,7},{7,6},{8,9},{9,8},{10,11... | collective-permute-start | bytes 92168 | tf_op jit(solution)/shard_map/ppermute | solution.py:413
  34.5 0.2 slice.51
  34.7 2.2 %collective-permute-done.2 = bf16[2,30,2,128]{3,2,1,0:T(2,128)(2,1)S(1)} collective-permute-done((bf16[2,30,2,128]{3,2,1,0:T(2,128)(2,1)S(1)}, bf16[2,30,2,128]{3,2,1,0:T(2,128)(2,1)S(1)}, u32[]{:S(2)}, u32[]{:S(2)}) %collective-permute-start.2) | collective-permute-done | bytes 30752 | tf_op jit(solution)/shard_map/ppermute | solution.py:413
  36.9 0.9 fusion.5.refs_6_
  37.8 0.1 fusion.8
  37.9 0.3 maximum_maximum_fusion
  38.2 0.4 fusion.9
  38.6 3.5 %collective-permute-start.6 = (bf16[2,30,2,1152]{3,2,1,0:T(2,128)(2,1)S(1)}, bf16[2,30,2,1152]{3,2,1,0:T(2,128)(2,1)S(1)}, u32[]{:S(2)}, u32[]{:S(2)}) collective-permute-start(bf16[2,30,2,1152]{3,2,1,0:T(2,128)(2,1)S(1)} %get-tuple-element.40), channel_id=1, source_target_pairs={{0,2},{2,4},{4,6},{1,3},{3,5},{5,7},{8,10},{10,12},{12,14},{9,11},... | collective-permute-start | bytes 829448 | tf_op jit(solution)/shard_map/ppermute | solution.py:25
  42.1 1.3 %collective-permute-start.5 = (bf16[2,30,2,1152]{3,2,1,0:T(2,128)(2,1)S(1)}, bf16[2,30,2,1152]{3,2,1,0:T(2,128)(2,1)S(1)}, u32[]{:S(2)}, u32[]{:S(2)}) collective-permute-start(bf16[2,30,2,1152]{3,2,1,0:T(2,128)(2,1)S(1)} %get-tuple-element.41), channel_id=1, source_target_pairs={{2,0},{4,2},{6,4},{3,1},{5,3},{7,5},{10,8},{12,10},{14,12},{11,9},... | collective-permute-start | bytes 829448 | tf_op jit(solution)/shard_map/ppermute | solution.py:25
  43.4 0.6 copy.32
  44.0 0.6 copy.34
  44.6 0.1 stack_broadcast_in_dim.2
  44.7 0.6 slice_bitcast_fusion
  45.3 1.9 %collective-permute-start.3 = (bf16[7,128,1024]{2,1,0:T(8,128)(2,1)}, bf16[7,128,1024]{2,1,0:T(8,128)(2,1)}, u32[]{:S(2)}, u32[]{:S(2)}) collective-permute-start(bf16[7,128,1024]{2,1,0:T(8,128)(2,1)} %get-tuple-element.23), channel_id=1, source_target_pairs={{0,8},{8,16},{16,24},{1,9},{9,17},{17,25},{2,10},{10,18},{18,26},{... | collective-permute-start | bytes 5505032 | tf_op jit(solution)/shard_map/ppermute | solution.py:25
  47.2 0.0 collective-permute-done.6.refs_8_
  47.3 3.6 %collective-permute-start.4 = (bf16[7,128,1024]{2,1,0:T(8,128)(2,1)}, bf16[7,128,1024]{2,1,0:T(8,128)(2,1)}, u32[]{:S(2)}, u32[]{:S(2)}) collective-permute-start(bf16[7,128,1024]{2,1,0:T(8,128)(2,1)} %get-tuple-element.24), channel_id=1, source_target_pairs={{8,0},{16,8},{24,16},{9,1},{17,9},{25,17},{10,2},{18,10},{26,18},{... | collective-permute-start | bytes 5505032 | tf_op jit(solution)/shard_map/ppermute | solution.py:25
  50.9 0.0 collective-permute-done.5.refs_7_
  50.9 0.0 collective-permute-done.7.refs_3_
  51.0 0.0 collective-permute-done.8.refs_5_
  51.0 0.0 copy-done
  51.0 0.0 copy-done.4
  51.0 0.7 copy-done.5
  51.7 23.8 %slab_1.1 = (bf16[2,16,128,1024]{3,2,1,0:T(8,128)(2,1)}, bf16[128,256]{1,0:T(8,128)(2,1)}) custom-call(s32[6,128]{1,0:T(8,128)} %get-tuple-element.46.refs_0_, bf16[32,30]{1,0:T(8,128)(2,1)} %bitcast.35, bf16[160,144]{1,0:T(8,128)(2,1)} %bitcast.31, bf16[7,128,1024]{2,1,0:T(8,128)(2,1)} %collective-permute-done.7.refs_3_, ...), custom_call_target="tpu_custom_call" | custom-call | flops 20000000000 | bytes 16000000 | tf_op jit(solution)/shard_map/slab_1/pallas_call | solution.py:360
  75.5 5.6 %collective-permute-start.9 = (bf16[128,256]{1,0:T(8,128)(2,1)}, bf16[128,256]{1,0:T(8,128)(2,1)S(1)}, u32[]{:S(2)}, u32[]{:S(2)}) collective-permute-start(bf16[128,256]{1,0:T(8,128)(2,1)} %get-tuple-element.31), channel_id=1, source_target_pairs={{0,7},{1,6},{2,5},{3,4},{4,3},{5,2},{6,1},{7,0},{8,15},{9,14},{10,... | collective-permute-start | bytes 196616 | tf_op jit(solution)/shard_map/ppermute | solution.py:441
  81.1 0.0 collective-permute-done.3.refs_3_
  81.1 0.0 collective-permute-done.4.refs_5_
  81.1 23.8 %slab_0.1 = (bf16[2,16,128,1024]{3,2,1,0:T(8,128)(2,1)}, bf16[128,256]{1,0:T(8,128)(2,1)}) custom-call(s32[6,128]{1,0:T(8,128)} %get-tuple-element.47.refs_0_, bf16[32,30]{1,0:T(8,128)(2,1)} %bitcast.36, bf16[160,144]{1,0:T(8,128)(2,1)} %bitcast.32, bf16[7,128,1024]{2,1,0:T(8,128)(2,1)} %collective-permute-done.3.refs_3_, ...), custom_call_target="tpu_custom_call", output_to_operand_aliasing={{0}: (9, {})} | custom-call | flops 20000000000 | bytes 16000000 | tf_op jit(solution)/shard_map/slab_0/pallas_call | solution.py:360
  104.9 0.0 collective-permute-done.9
  105.0 1.6 %convolution_multiply_fusion = f32[128,128]{1,0:T(8,128)} fusion(bf16[128,256]{1,0:T(8,128)(2,1)} %get-tuple-element.30, bf16[128,256]{1,0:T(8,128)(2,1)S(1)} %collective-permute-done.9), kind=kOutput, calls=%fused_computation | convolution fusion | flops 8404992 | bytes 196608 | tf_op jit(solution)/shard_map/dot_general | solution.py:444
  (20 shorter events, 0.2 us)
Async XLA Ops:
  4.8 46.1 %collective-permute-start.7 = (bf16[7,128,1024]{2,1,0:T(8,128)(2,1)}, bf16[7,128,1024]{2,1,0:T(8,128)(2,1)}, u32[]{:S(2)}, u32[]{:S(2)}) collective-permute-start(bf16[7,128,1024]{2,1,0:T(8,128)(2,1)} %get-tuple-element.26), channel_id=1, source_target_pairs={{0,8},{8,16},{16,24},{1,9},{9,17},{17,25},{2,10},{10,18},{18,26},{... | collective-permute-start | bytes 5505032 | tf_op jit(solution)/shard_map/ppermute | solution.py:25
  6.8 44.2 %collective-permute-start.8 = (bf16[7,128,1024]{2,1,0:T(8,128)(2,1)}, bf16[7,128,1024]{2,1,0:T(8,128)(2,1)}, u32[]{:S(2)}, u32[]{:S(2)}) collective-permute-start(bf16[7,128,1024]{2,1,0:T(8,128)(2,1)} %get-tuple-element.27), channel_id=1, source_target_pairs={{8,0},{16,8},{24,16},{9,1},{17,9},{25,17},{10,2},{18,10},{26,18},{... | collective-permute-start | bytes 5505032 | tf_op jit(solution)/shard_map/ppermute | solution.py:25
  10.4 11.0 %copy-start.1 = (f32[5,5]{1,0:T(8,128)S(1)}, f32[5,5]{1,0:T(8,128)}, u32[]{:S(2)}) copy-start(f32[5,5]{1,0:T(8,128)} %param.7) | copy-start | bytes 304
  10.4 11.3 %copy-start.2 = (s32[2,3,128]{2,0,1:T(2,128)S(1)}, s32[2,3,128]{2,0,1:T(2,128)}, u32[]{:S(2)}) copy-start(s32[2,3,128]{2,0,1:T(2,128)} %param.8) | copy-start | bytes 9220
  10.4 11.3 %copy-start.3 = (f32[15]{0:T(128)S(1)}, f32[15]{0:T(128)}, u32[]{:S(2)}) copy-start(f32[15]{0:T(128)} %param.6) | copy-start | bytes 184
  15.8 15.2 %collective-permute-start = (bf16[2,7,4,1152]{3,2,1,0:T(4,128)(2,1)}, bf16[2,7,4,1152]{3,2,1,0:T(4,128)(2,1)S(1)}, u32[]{:S(2)}, u32[]{:S(2)}) collective-permute-start(bf16[2,7,4,1152]{3,2,1,0:T(4,128)(2,1)} %get-tuple-element.20), channel_id=1, source_target_pairs={{0,8},{8,16},{16,24},{1,9},{9,17},{17,25},{2,10},{10,18},{18,26},{... | collective-permute-start | bytes 387080 | tf_op jit(solution)/shard_map/ppermute | solution.py:25
  17.7 15.1 %collective-permute-start.1 = (bf16[2,7,4,1152]{3,2,1,0:T(4,128)(2,1)}, bf16[2,7,4,1152]{3,2,1,0:T(4,128)(2,1)S(1)}, u32[]{:S(2)}, u32[]{:S(2)}) collective-permute-start(bf16[2,7,4,1152]{3,2,1,0:T(4,128)(2,1)} %get-tuple-element.22), channel_id=1, source_target_pairs={{8,0},{16,8},{24,16},{9,1},{17,9},{25,17},{10,2},{18,10},{26,18},{... | collective-permute-start | bytes 387080 | tf_op jit(solution)/shard_map/ppermute | solution.py:25
  33.0 4.0 %collective-permute-start.2 = (bf16[2,30,2,128]{3,2,1,0:T(2,128)(2,1)S(1)}, bf16[2,30,2,128]{3,2,1,0:T(2,128)(2,1)S(1)}, u32[]{:S(2)}, u32[]{:S(2)}) collective-permute-start(bf16[2,30,2,128]{3,2,1,0:T(2,128)(2,1)S(1)} %broadcast_select_fusion), channel_id=1, source_target_pairs={{0,1},{1,0},{2,3},{3,2},{4,5},{5,4},{6,7},{7,6},{8,9},{9,8},{10,11... | collective-permute-start | bytes 92168 | tf_op jit(solution)/shard_map/ppermute | solution.py:413
  36.9 7.7 %copy-start.6 = (s32[2,1]{0,1:T(1,128)S(1)}, s32[2,1]{0,1:T(1,128)}, u32[]{:S(2)}) copy-start(s32[2,1]{0,1:T(1,128)} %param.9) | copy-start | bytes 28
  37.8 13.2 %copy-start = (bf16[2,30,128,128]{3,2,1,0:T(8,128)(2,1)}, bf16[2,30,128,128]{3,2,1,0:T(8,128)(2,1)S(1)}, u32[]{:S(2)}) copy-start(bf16[2,30,128,128]{3,2,1,0:T(8,128)(2,1)S(1)} %fusion.5.refs_6_) | copy-start | bytes 5898244
  38.6 8.7 %collective-permute-start.6 = (bf16[2,30,2,1152]{3,2,1,0:T(2,128)(2,1)S(1)}, bf16[2,30,2,1152]{3,2,1,0:T(2,128)(2,1)S(1)}, u32[]{:S(2)}, u32[]{:S(2)}) collective-permute-start(bf16[2,30,2,1152]{3,2,1,0:T(2,128)(2,1)S(1)} %get-tuple-element.40), channel_id=1, source_target_pairs={{0,2},{2,4},{4,6},{1,3},{3,5},{5,7},{8,10},{10,12},{12,14},{9,11},... | collective-permute-start | bytes 829448 | tf_op jit(solution)/shard_map/ppermute | solution.py:25
  42.1 8.8 %collective-permute-start.5 = (bf16[2,30,2,1152]{3,2,1,0:T(2,128)(2,1)S(1)}, bf16[2,30,2,1152]{3,2,1,0:T(2,128)(2,1)S(1)}, u32[]{:S(2)}, u32[]{:S(2)}) collective-permute-start(bf16[2,30,2,1152]{3,2,1,0:T(2,128)(2,1)S(1)} %get-tuple-element.41), channel_id=1, source_target_pairs={{2,0},{4,2},{6,4},{3,1},{5,3},{7,5},{10,8},{12,10},{14,12},{11,9},... | collective-permute-start | bytes 829448 | tf_op jit(solution)/shard_map/ppermute | solution.py:25
  45.3 35.8 %collective-permute-start.3 = (bf16[7,128,1024]{2,1,0:T(8,128)(2,1)}, bf16[7,128,1024]{2,1,0:T(8,128)(2,1)}, u32[]{:S(2)}, u32[]{:S(2)}) collective-permute-start(bf16[7,128,1024]{2,1,0:T(8,128)(2,1)} %get-tuple-element.23), channel_id=1, source_target_pairs={{0,8},{8,16},{16,24},{1,9},{9,17},{17,25},{2,10},{10,18},{18,26},{... | collective-permute-start | bytes 5505032 | tf_op jit(solution)/shard_map/ppermute | solution.py:25
  47.3 3.7 %copy-start.4 = (bf16[2,30,2,1152]{3,2,1,0:T(2,128)(2,1)}, bf16[2,30,2,1152]{3,2,1,0:T(2,128)(2,1)S(1)}, u32[]{:S(2)}) copy-start(bf16[2,30,2,1152]{3,2,1,0:T(2,128)(2,1)S(1)} %collective-permute-done.6.refs_8_) | copy-start | bytes 829444
  47.3 33.8 %collective-permute-start.4 = (bf16[7,128,1024]{2,1,0:T(8,128)(2,1)}, bf16[7,128,1024]{2,1,0:T(8,128)(2,1)}, u32[]{:S(2)}, u32[]{:S(2)}) collective-permute-start(bf16[7,128,1024]{2,1,0:T(8,128)(2,1)} %get-tuple-element.24), channel_id=1, source_target_pairs={{8,0},{16,8},{24,16},{9,1},{17,9},{25,17},{10,2},{18,10},{26,18},{... | collective-permute-start | bytes 5505032 | tf_op jit(solution)/shard_map/ppermute | solution.py:25
  50.9 0.7 copy-start.5
  75.5 29.5 %collective-permute-start.9 = (bf16[128,256]{1,0:T(8,128)(2,1)}, bf16[128,256]{1,0:T(8,128)(2,1)S(1)}, u32[]{:S(2)}, u32[]{:S(2)}) collective-permute-start(bf16[128,256]{1,0:T(8,128)(2,1)} %get-tuple-element.31), channel_id=1, source_target_pairs={{0,7},{1,6},{2,5},{3,4},{4,3},{5,2},{6,1},{7,0},{8,15},{9,14},{10,... | collective-permute-start | bytes 196616 | tf_op jit(solution)/shard_map/ppermute | solution.py:441

commit v7 on v6

--- a/solution.py
+++ b/solution.py
@@ -1,4 +1,3 @@
-import functools
 import jax
 import jax.numpy as jnp
 from jax import lax
@@ -15,6 +14,7 @@
 BLOCK = 16
 WINDOW = 32
 EDGE = 8
+GROUP = 4
 bf16 = jnp.bfloat16
 f32 = jnp.float32
 
@@ -92,8 +92,8 @@
         full = jnp.dot(full, wide, preferred_element_type=f32)
         same = iota(full.shape, 0) % 8 == iota(full.shape, 1) % 8
         w1[...] = jnp.where(same, full, 0.0).astype(bf16)
-        for tile in range(0, tiles + 1, 2):
-            pair = range(tile, min(tile + 2, tiles + 1))
+        for tile in range(0, tiles + 1, GROUP):
+            pair = range(tile, min(tile + GROUP, tiles + 1))
             cols = slice(tile * TILE, (tile + len(pair)) * TILE)
             below = below_ref[0, :, :, cols].astype(f32)
             above = above_ref[0, :, :, cols].astype(f32)
@@ -112,8 +112,9 @@
                 keep(parts[q], parts[q + 1], tile, place)
             carry[:, tile] = parts[-1]
 
-        for tile in range(0, tiles, 2):
-            cols = slice(tile * TILE, (tile + 2) * TILE)
+        for tile in range(0, tiles, GROUP):
+            group = range(tile, min(tile + GROUP, tiles))
+            cols = slice(tile * TILE, (tile + len(group)) * TILE)
             parts = []
             for h in range(0, row_step, BLOCK):
                 rows = slice(h, h + BLOCK)
@@ -122,13 +123,13 @@
                     axis=0,
                 ).astype(f32)
                 parts += [filtered(block[:, :EDGE]), filtered(block[:, EDGE:])]
-            keep_all(tile, [part[..., :TILE] for part in parts])
-            keep_all(tile + 1, [part[..., TILE:] for part in parts])
-        parts = []
-        for h in range(0, row_step, BLOCK):
-            block = edge_ref[0, :, h : h + BLOCK, :].astype(f32)
-            both = filtered(jnp.concatenate([block[:, :EDGE], block[:, EDGE:]], axis=2))
-            parts += [both[..., :TILE], both[..., TILE:]]
+            for q, one in enumerate(group):
+                keep_all(one, [part[..., q * TILE : (q + 1) * TILE] for part in parts])
+        wide = edge_ref[0].astype(f32)
+        both = filtered(
+            jnp.concatenate([wide[:, h : h + EDGE] for h in range(0, row_step, EDGE)], axis=2)
+        )
+        parts = [both[..., h * TILE : (h + 1) * TILE] for h in range(row_step // EDGE)]
         keep_all(tiles, parts)
 
     @pl.when(at == steps_1 - 1)
@@ -166,8 +167,8 @@
                         kept[frame, tile, rows, :] = value.astype(f32)
 
                 order = [(f, tile) for f in range(2) for tile in [tiles] + list(range(tiles))]
-                for p in range(0, len(order), 2):
-                    pair = order[p : p + 2]
+                for p in range(0, len(order), GROUP):
+                    pair = order[p : p + GROUP]
                     stacks = []
                     for f, tile in pair:
                         frame = (at - steps_1) * frame_step + k2 * 2 + f
@@ -234,89 +235,138 @@
         last_ref[...] = jnp.where(live, normed, 0.0).astype(bf16)
 
 
-def cut_kernel(slab, frames, *refs):
-    if slab == 0:
-        other, refs = refs[0], refs[1:]
-        rim, send_low, send_high, low, high, whole, sems = refs
-    else:
-        rim, low, high, whole, sems = refs
-    frame_count, row_count, col_count = whole.shape
-    first, last = pl.ds(0, HALF), pl.ds(frame_count - HALF, HALF)
+def edges_of(top, bottom, left, right):
+    rows = jnp.concatenate(
+        [top[...].astype(f32)[:, :REACH], bottom[...].astype(f32)[:, BLOCK - REACH :]], axis=1
+    )
+    line = iota((8, TILE), 0)
+    lane = iota((8, TILE), 1)
+    first = ((line == lane) & (line < REACH)).astype(bf16)
+    last = ((line + TILE - 2 * REACH == lane) & (line >= REACH)).astype(bf16)
+    over_lanes = (((1,), (1,)), ((), ()))
+    cols = []
+    for f in range(rows.shape[0]):
+        one = lax.dot_general(first, left[f], over_lanes, preferred_element_type=f32)
+        one += lax.dot_general(last, right[f], over_lanes, preferred_element_type=f32)
+        cols.append(one[: 2 * REACH].astype(bf16))
+    return rows.astype(bf16), cols
+
+
+def send_all(frames, slab, low, high, whole, sems):
+    frame_count = whole.shape[0]
     middle = frame_count - HALF
+    spans = [pl.ds(0, middle), pl.ds(middle, HALF)]
     fetches = [
-        pltpu.make_async_copy(frames.at[slab, part], whole.at[part], sems.at[i])
-        for i, part in enumerate([pl.ds(0, middle), pl.ds(middle, HALF)])
+        pltpu.make_async_copy(frames.at[slab, span], whole.at[span], sems.at[i])
+        for i, span in enumerate(spans)
     ]
     writes = [
-        pltpu.make_async_copy(whole.at[first], high, sems.at[2]),
-        pltpu.make_async_copy(whole.at[last], low, sems.at[3]),
+        pltpu.make_async_copy(whole.at[pl.ds(0, HALF)], high, sems.at[2]),
+        pltpu.make_async_copy(whole.at[pl.ds(middle, HALF)], low, sems.at[3]),
     ]
+    return fetches, writes
+
+
+def cut_kernel(frames, rim, rim_low, rim_high, low, high, whole, top, bottom, left, right, sems):
+    frame_count, row_count, col_count = whole.shape
+    reads = [
+        pltpu.make_async_copy(source, target, sems.at[4 + i])
+        for i, (source, target) in enumerate(
+            [
+                (frames.at[0, :, pl.ds(0, BLOCK), :], top),
+                (frames.at[0, :, pl.ds(row_count - BLOCK, BLOCK), :], bottom),
+                (frames.at[0, :, :, pl.ds(0, TILE)], left),
+                (frames.at[0, :, :, pl.ds(col_count - TILE, TILE)], right),
+            ]
+        )
+    ]
+    fetches, writes = send_all(frames, 1, low, high, whole, sems)
+    for copy in reads + fetches:
+        copy.start()
+
+    def put(slab, rows, cols):
+        middle = frame_count - HALF
+        for target, start in [(rim, 0), (rim_low, middle), (rim_high, 0)]:
+            count = target.shape[1]
+            target[slab, :, :, :col_count] = rows[start : start + count]
+            for f in range(count):
+                target[slab, f, :, col_count:] = cols[start + f]
+
+    for copy in reads:
+        copy.wait()
+    put(0, *edges_of(top, bottom, left, right))
+    for fetch, write in zip(fetches, writes):
+        fetch.wait()
+        write.start()
+    put(
+        1,
+        *edges_of(
+            whole.at[:, pl.ds(0, BLOCK), :],
+            whole.at[:, pl.ds(row_count - BLOCK, BLOCK), :],
+            whole.at[:, :, pl.ds(0, TILE)],
+            whole.at[:, :, pl.ds(col_count - TILE, TILE)],
+        ),
+    )
+    for write in writes:
+        write.wait()
+
+
+def late_kernel(frames, low, high, whole, sems):
+    fetches, writes = send_all(frames, 0, low, high, whole, sems)
     for fetch in fetches:
         fetch.start()
     for fetch, write in zip(fetches, writes):
         fetch.wait()
         write.start()
-    rows = jnp.concatenate(
-        [
-            whole[:, :BLOCK, :].astype(f32)[:, :REACH],
-            whole[:, row_count - BLOCK :, :].astype(f32)[:, BLOCK - REACH :],
-        ],
-        axis=1,
-    ).astype(bf16)
-    line = iota((8, TILE), 0)
-    lane = iota((8, TILE), 1)
-    left = ((line == lane) & (line < REACH)).astype(bf16)
-    right = ((line + TILE - 2 * REACH == lane) & (line >= REACH)).astype(bf16)
-    over_lanes = (((1,), (1,)), ((), ()))
-    cols = []
-    for f in range(frame_count):
-        one = lax.dot_general(left, whole[f, :, :TILE], over_lanes, preferred_element_type=f32)
-        one += lax.dot_general(
-            right, whole[f, :, col_count - TILE :], over_lanes, preferred_element_type=f32
-        )
-        cols.append(one[: 2 * REACH].astype(bf16))
-    if slab == 0:
-        targets = [rim.at[0], send_low.at[0], send_high.at[0]]
-        starts = [0, middle, 0]
-        rim[1] = other[...]
-        send_low[1] = other[middle:]
-        send_high[1] = other[:HALF]
-    else:
-        targets, starts = [rim], [0]
-    for target, start in zip(targets, starts):
-        target[:, :, :col_count] = rows[start : start + target.shape[0]]
-        for f in range(target.shape[0]):
-            target[f, :, col_count:] = cols[start + f]
     for write in writes:
         write.wait()
 
 
-def cut(slab, frames, other):
-    _, frame_count, row_count, col_count = frames.shape
+def cut(frames):
+    slabs, frame_count, row_count, col_count = frames.shape
     anywhere = pl.BlockSpec(memory_space=pl.ANY)
     near = pl.BlockSpec(memory_space=pltpu.VMEM)
     piece = jax.ShapeDtypeStruct((HALF, row_count, col_count), bf16)
-    shape = (frame_count, 2 * REACH, col_count + row_count)
-    if slab == 0:
-        operands = [frames, other]
-        shapes = [(2,) + shape, (2, HALF) + shape[1:], (2, HALF) + shape[1:]]
-    else:
-        operands = [frames]
-        shapes = [shape]
-    rims = [jax.ShapeDtypeStruct(shape, bf16) for shape in shapes]
+    wide = col_count + row_count
+    rims = [
+        jax.ShapeDtypeStruct((slabs, count, 2 * REACH, wide), bf16)
+        for count in (frame_count, HALF, HALF)
+    ]
     return pl.pallas_call(
-        functools.partial(cut_kernel, slab),
-        in_specs=[anywhere] + [near] * (len(operands) - 1),
-        out_specs=[near] * len(rims) + [anywhere] * 2,
+        cut_kernel,
+        in_specs=[anywhere],
+        out_specs=[near] * 3 + [anywhere] * 2,
         out_shape=rims + [piece, piece],
+        scratch_shapes=[
+            pltpu.VMEM((frame_count, row_count, col_count), bf16),
+            pltpu.VMEM((frame_count, BLOCK, col_count), bf16),
+            pltpu.VMEM((frame_count, BLOCK, col_count), bf16),
+            pltpu.VMEM((frame_count, row_count, TILE), bf16),
+            pltpu.VMEM((frame_count, row_count, TILE), bf16),
+            pltpu.SemaphoreType.DMA((8,)),
+        ],
+        compiler_params=pltpu.CompilerParams(vmem_limit_bytes=60 * 1024 * 1024),
+        name="cut",
+    )(frames)
+
+
+def late_cut(frames):
+    _, frame_count, row_count, col_count = frames.shape
+    anywhere = pl.BlockSpec(memory_space=pl.ANY)
+    piece = jax.ShapeDtypeStruct((HALF, row_count, col_count), bf16)
+    return pl.pallas_call(
+        late_kernel,
+        in_specs=[anywhere],
+        out_specs=[anywhere] * 2,
+        out_shape=[piece, piece],
         scratch_shapes=[
             pltpu.VMEM((frame_count, row_count, col_count), bf16),
             pltpu.SemaphoreType.DMA((4,)),
         ],
         compiler_params=pltpu.CompilerParams(vmem_limit_bytes=60 * 1024 * 1024),
         cost_estimate=pl.CostEstimate(flops=0, bytes_accessed=9_000_000, transcendentals=0),
-        name=f"cut_{slab}",
-    )(*operands)
+        name="late_cut",
+    )(frames)
 
 
 def run_slab(slab, smoothed, spots, taps, w2, low, frames, high, edge, below, above):
@@ -396,13 +446,12 @@
     first_row = lax.axis_index("row") * row_count
     first_col = lax.axis_index("col") * col_count
 
-    rim, send_low1, send_high1 = cut(1, frames, None)
-    low1 = shifted(send_low1, "omega", 1)
-    high1 = shifted(send_high1, "omega", -1)
-    rim, rim_low, rim_high, send_low0, send_high0 = cut(0, frames, rim)
+    rim, rim_low, rim_high, send_low1, send_high1 = cut(frames)
     rim = jnp.concatenate(
         [shifted(rim_low, "omega", 1), rim, shifted(rim_high, "omega", -1)], axis=1
     )
+    low1 = shifted(send_low1, "omega", 1)
+    high1 = shifted(send_high1, "omega", -1)
     lane = jnp.arange(TILE, dtype=jnp.int32)[None, :]
     step = jnp.arange(REACH, dtype=jnp.int32)[:, None]
     after = (lane == step).astype(bf16)
@@ -417,7 +466,8 @@
         right = shifted(rim[:, :, :REACH, col_count:], "col", -1)
         sides = jnp.concatenate([right, left], axis=2)
         place = jnp.concatenate([after, before], axis=0)
-    send_low0, send_high0, sides = lax.optimization_barrier((send_low0, send_high0, sides))
+    later, sides = lax.optimization_barrier((frames, sides))
+    send_low0, send_high0 = late_cut(later)
     low0 = shifted(send_low0, "omega", 1)
     high0 = shifted(send_high0, "omega", -1)
     edge = jnp.einsum("sfkr,kc->sfrc", sides, place, preferred_element_type=bf16)

time: 108 us -> 98.7 us (0.914)
  waiting for transfers between devices: 11.7 us -> 2.21 us
  local copies, waits for them, and re-layouts: 4.54 us -> 5.77 us
    ppermute x8, waiting for transfers between devices: 9.55 us -> 0.02 us  [shifted(): return lax.ppermute(block, axis, route)]
    unnamed x16 -> x18, local copies, waits for them, and re-layouts: 1.84 us -> 3.05 us
  transfers between devices with their start and end apart: 10 -> 10, of which waited for: 3 -> 1; matrix products, arithmetic and copies ran while one was open for 5% -> 6% of each run, Pallas kernels for 50% -> 52%
where the time goes in v7:
time: 98.7 us; the launch traced here: 97.6 us
  Pallas kernels  56.3 us (57%)
  starting transfers between devices  28.9 us (29%)
  local copies, waits for them, and re-layouts  5.77 us (6%)
  matrix products  2.51 us (3%)
  waiting for transfers between devices  2.21 us (2%)
  between operations  1.01 us (1%)
    pallas_call x2, Pallas kernels, run_slab(): pl.pallas_call(body, grid=(steps_1 + steps_2 + 1,), in_specs=in_specs, ou...  47.6 us
    ppermute x8, starting transfers between devices, shifted(): return lax.ppermute(block, axis, route)  21.7 us
    ppermute x1, starting transfers between devices, shards(): lax.ppermute(second, ('row', 'col'), [(i, count - 1 - i) for i in range(c...  5.63 us
    pallas_call x1, Pallas kernels, cut(): pl.pallas_call(cut_kernel, in_specs=[anywhere], out_specs=[near] * 3 + [a...  5.07 us
    pallas_call x1, Pallas kernels, late_cut(): pl.pallas_call(late_kernel, in_specs=[anywhere], out_specs=[anywhere] * 2...  3.59 us
    unnamed x18, local copies, waits for them, and re-layouts  3.05 us
    ppermute x1, waiting for transfers between devices, shards(): sides = lax.ppermute(sides, 'col', [(0, 1), (1, 0)])  2.18 us
  transfers between devices with their start and end apart: 10, of which 1 were waited for; matrix products, arithmetic and copies ran while one was open for 6% of the time, Pallas kernels for 52%

profile of v7, /device:TPU:2, one launch (start us, length us, event | category | flops | bytes accessed | tf_op | source)
XLA Modules:
  0.0 97.6 jit_solution(9551623930074755899)
XLA Ops:
  0.6 0.0 copy-start.1
  0.6 0.0 copy-start.2
  0.7 0.0 copy-start.3
  0.7 5.1 %cut.1 = (bf16[2,16,4,1152]{3,2,1,0:T(4,128)(2,1)}, bf16[2,7,4,1152]{3,2,1,0:T(4,128)(2,1)}, bf16[2,7,4,1152]{3,2,1,0:T(4,128)(2,1)}, bf16[7,128,1024]{2,1,0:T(8,128)(2,1)}, bf16[7,128,1024]{2,1,0:T(8,128)(2,1)}) custom-call(bf16[2,16,128,1024]{3,2,1,0:T(8,128)(2,1)} %refs_4_.3), custom_call_target="tpu_custom_call" | custom-call | tf_op jit(solution)/shard_map/cut/pallas_call | solution.py:335
  5.7 1.9 %collective-permute-start = (bf16[2,7,4,1152]{3,2,1,0:T(4,128)(2,1)}, bf16[2,7,4,1152]{3,2,1,0:T(4,128)(2,1)S(1)}, u32[]{:S(2)}, u32[]{:S(2)}) collective-permute-start(bf16[2,7,4,1152]{3,2,1,0:T(4,128)(2,1)} %get-tuple-element.15), channel_id=1, source_target_pairs={{0,8},{8,16},{16,24},{1,9},{9,17},{17,25},{2,10},{10,18},{18,26},{... | collective-permute-start | bytes 387080 | tf_op jit(solution)/shard_map/ppermute | solution.py:25
  7.7 3.6 %collective-permute-start.1 = (bf16[2,7,4,1152]{3,2,1,0:T(4,128)(2,1)}, bf16[2,7,4,1152]{3,2,1,0:T(4,128)(2,1)S(1)}, u32[]{:S(2)}, u32[]{:S(2)}) collective-permute-start(bf16[2,7,4,1152]{3,2,1,0:T(4,128)(2,1)} %get-tuple-element.17), channel_id=1, source_target_pairs={{8,0},{16,8},{24,16},{9,1},{17,9},{25,17},{10,2},{18,10},{26,18},{... | collective-permute-start | bytes 387080 | tf_op jit(solution)/shard_map/ppermute | solution.py:25
  11.3 1.9 %collective-permute-start.7 = (bf16[7,128,1024]{2,1,0:T(8,128)(2,1)}, bf16[7,128,1024]{2,1,0:T(8,128)(2,1)}, u32[]{:S(2)}, u32[]{:S(2)}) collective-permute-start(bf16[7,128,1024]{2,1,0:T(8,128)(2,1)} %get-tuple-element.22), channel_id=1, source_target_pairs={{0,8},{8,16},{16,24},{1,9},{9,17},{17,25},{2,10},{10,18},{18,26},{... | collective-permute-start | bytes 5505032 | tf_op jit(solution)/shard_map/ppermute | solution.py:25
  13.2 3.6 %collective-permute-start.8 = (bf16[7,128,1024]{2,1,0:T(8,128)(2,1)}, bf16[7,128,1024]{2,1,0:T(8,128)(2,1)}, u32[]{:S(2)}, u32[]{:S(2)}) collective-permute-start(bf16[7,128,1024]{2,1,0:T(8,128)(2,1)} %get-tuple-element.23), channel_id=1, source_target_pairs={{8,0},{16,8},{24,16},{9,1},{17,9},{25,17},{10,2},{18,10},{26,18},{... | collective-permute-start | bytes 5505032 | tf_op jit(solution)/shard_map/ppermute | solution.py:25
  16.9 0.1 copy.33
  17.1 0.1 select_reduce_fusion
  17.3 0.2 select_reduce_fusion.2
  17.5 0.1 reduce-precision_convert_fusion.1
  17.6 0.1 pad_maximum_fusion
  17.7 0.0 collective-permute-done
  17.8 1.1 %constant_dynamic-update-slice_fusion.1 = bf16[2,30,4,1152]{3,2,1,0:T(4,128)(2,1)S(1)} fusion(bf16[2,30,4,1152]{3,2,1,0:T(4,128)(2,1)S(1)} %constant_dynamic-update-slice_fusion.2, bf16[2,16,4,1152]{3,2,1,0:T(4,128)(2,1)} %get-tuple-element.16), kind=kLoop, calls=%fused_computation.18 | loop fusion | bytes 589824
  18.8 0.0 collective-permute-done.1
  18.9 0.1 constant_dynamic-update-slice_fusion
  18.9 0.1 broadcast_select_fusion
  19.0 1.6 %collective-permute-start.2 = (bf16[2,30,2,128]{3,2,1,0:T(2,128)(2,1)S(1)}, bf16[2,30,2,128]{3,2,1,0:T(2,128)(2,1)S(1)}, u32[]{:S(2)}, u32[]{:S(2)}) collective-permute-start(bf16[2,30,2,128]{3,2,1,0:T(2,128)(2,1)S(1)} %broadcast_select_fusion), channel_id=1, source_target_pairs={{0,1},{1,0},{2,3},{3,2},{4,5},{5,4},{6,7},{7,6},{8,9},{9,8},{10,11... | collective-permute-start | bytes 92168 | tf_op jit(solution)/shard_map/ppermute | solution.py:462
  20.6 0.2 slice.51
  20.8 0.0 copy-start.7
  20.8 2.2 %collective-permute-done.2 = bf16[2,30,2,128]{3,2,1,0:T(2,128)(2,1)S(1)} collective-permute-done((bf16[2,30,2,128]{3,2,1,0:T(2,128)(2,1)S(1)}, bf16[2,30,2,128]{3,2,1,0:T(2,128)(2,1)S(1)}, u32[]{:S(2)}, u32[]{:S(2)}) %collective-permute-start.2) | collective-permute-done | bytes 30752 | tf_op jit(solution)/shard_map/ppermute | solution.py:462
  22.9 0.9 fusion.5.refs_6_
  23.8 0.1 fusion.8
  23.9 0.3 maximum_maximum_fusion
  24.2 0.4 fusion.9
  24.6 3.5 %collective-permute-start.6 = (bf16[2,30,2,1152]{3,2,1,0:T(2,128)(2,1)S(1)}, bf16[2,30,2,1152]{3,2,1,0:T(2,128)(2,1)S(1)}, u32[]{:S(2)}, u32[]{:S(2)}) collective-permute-start(bf16[2,30,2,1152]{3,2,1,0:T(2,128)(2,1)S(1)} %get-tuple-element.36), channel_id=1, source_target_pairs={{0,2},{2,4},{4,6},{1,3},{3,5},{5,7},{8,10},{10,12},{12,14},{9,11},... | collective-permute-start | bytes 829448 | tf_op jit(solution)/shard_map/ppermute | solution.py:25
  28.1 1.3 %collective-permute-start.5 = (bf16[2,30,2,1152]{3,2,1,0:T(2,128)(2,1)S(1)}, bf16[2,30,2,1152]{3,2,1,0:T(2,128)(2,1)S(1)}, u32[]{:S(2)}, u32[]{:S(2)}) collective-permute-start(bf16[2,30,2,1152]{3,2,1,0:T(2,128)(2,1)S(1)} %get-tuple-element.37), channel_id=1, source_target_pairs={{2,0},{4,2},{6,4},{3,1},{5,3},{7,5},{10,8},{12,10},{14,12},{11,9},... | collective-permute-start | bytes 829448 | tf_op jit(solution)/shard_map/ppermute | solution.py:25
  29.4 0.6 copy.32
  30.0 0.6 copy.34
  30.7 0.1 stack_broadcast_in_dim.2
  30.8 0.6 slice_bitcast_fusion
  31.4 3.6 %late_cut.1 = (bf16[7,128,1024]{2,1,0:T(8,128)(2,1)}, bf16[7,128,1024]{2,1,0:T(8,128)(2,1)}) custom-call(bf16[2,16,128,1024]{3,2,1,0:T(8,128)(2,1)} %refs_4_.3), custom_call_target="tpu_custom_call" | custom-call | bytes 9000000 | tf_op jit(solution)/shard_map/late_cut/pallas_call | solution.py:357
  35.0 1.9 %collective-permute-start.3 = (bf16[7,128,1024]{2,1,0:T(8,128)(2,1)}, bf16[7,128,1024]{2,1,0:T(8,128)(2,1)S(1)}, u32[]{:S(2)}, u32[]{:S(2)}) collective-permute-start(bf16[7,128,1024]{2,1,0:T(8,128)(2,1)} %get-tuple-element.19), channel_id=1, source_target_pairs={{0,8},{8,16},{16,24},{1,9},{9,17},{17,25},{2,10},{10,18},{18,26},{... | collective-permute-start | bytes 5505032 | tf_op jit(solution)/shard_map/ppermute | solution.py:25
  36.9 0.0 collective-permute-done.6.refs_8_
  36.9 3.8 %collective-permute-start.4 = (bf16[7,128,1024]{2,1,0:T(8,128)(2,1)}, bf16[7,128,1024]{2,1,0:T(8,128)(2,1)}, u32[]{:S(2)}, u32[]{:S(2)}) collective-permute-start(bf16[7,128,1024]{2,1,0:T(8,128)(2,1)} %get-tuple-element.20), channel_id=1, source_target_pairs={{8,0},{16,8},{24,16},{9,1},{17,9},{25,17},{10,2},{18,10},{26,18},{... | collective-permute-start | bytes 5505032 | tf_op jit(solution)/shard_map/ppermute | solution.py:25
  40.8 0.0 collective-permute-done.5.refs_7_
  40.8 0.0 collective-permute-done.7.refs_3_
  40.8 0.0 collective-permute-done.8.refs_5_
  40.8 0.7 copy-done.6
  41.5 23.8 %slab_1.1 = (bf16[2,16,128,1024]{3,2,1,0:T(8,128)(2,1)}, bf16[128,256]{1,0:T(8,128)(2,1)}) custom-call(s32[6,128]{1,0:T(8,128)} %get-tuple-element.42.refs_0_, bf16[32,30]{1,0:T(8,128)(2,1)} %bitcast.35, bf16[160,144]{1,0:T(8,128)(2,1)} %bitcast.31, bf16[7,128,1024]{2,1,0:T(8,128)(2,1)} %collective-permute-done.7.refs_3_, ...), custom_call_target="tpu_custom_call" | custom-call | flops 20000000000 | bytes 16000000 | tf_op jit(solution)/shard_map/slab_1/pallas_call | solution.py:410
  65.3 5.6 %collective-permute-start.9 = (bf16[128,256]{1,0:T(8,128)(2,1)}, bf16[128,256]{1,0:T(8,128)(2,1)S(1)}, u32[]{:S(2)}, u32[]{:S(2)}) collective-permute-start(bf16[128,256]{1,0:T(8,128)(2,1)} %get-tuple-element.27), channel_id=1, source_target_pairs={{0,7},{1,6},{2,5},{3,4},{4,3},{5,2},{6,1},{7,0},{8,15},{9,14},{10,... | collective-permute-start | bytes 196616 | tf_op jit(solution)/shard_map/ppermute | solution.py:491
  70.9 0.0 collective-permute-done.3.refs_3_
  70.9 0.0 collective-permute-done.4.refs_5_
  70.9 1.2 %copy-done.4 = bf16[7,128,1024]{2,1,0:T(8,128)(2,1)} copy-done((bf16[7,128,1024]{2,1,0:T(8,128)(2,1)}, bf16[7,128,1024]{2,1,0:T(8,128)(2,1)S(1)}, u32[]{:S(2)}) %copy-start.4) | copy-done | bytes 1835032
  72.1 23.8 %slab_0.1 = (bf16[2,16,128,1024]{3,2,1,0:T(8,128)(2,1)}, bf16[128,256]{1,0:T(8,128)(2,1)}) custom-call(s32[6,128]{1,0:T(8,128)} %get-tuple-element.43.refs_0_, bf16[32,30]{1,0:T(8,128)(2,1)} %bitcast.36, bf16[160,144]{1,0:T(8,128)(2,1)} %bitcast.32, bf16[7,128,1024]{2,1,0:T(8,128)(2,1)} %copy-done.4, ...), custom_call_target="tpu_custom_call", output_to_operand_aliasing={{0}: (9, {})} | custom-call | flops 20000000000 | bytes 16000000 | tf_op jit(solution)/shard_map/slab_0/pallas_call | solution.py:410
  95.9 0.0 collective-permute-done.9
  96.0 1.6 %convolution_multiply_fusion = f32[128,128]{1,0:T(8,128)} fusion(bf16[128,256]{1,0:T(8,128)(2,1)} %get-tuple-element.26, bf16[128,256]{1,0:T(8,128)(2,1)S(1)} %collective-permute-done.9), kind=kOutput, calls=%fused_computation | convolution fusion | flops 8404992 | bytes 196608 | tf_op jit(solution)/shard_map/dot_general | solution.py:494
  (22 shorter events, 0.2 us)
Async XLA Ops:
  0.6 16.3 %copy-start.1 = (f32[5,5]{1,0:T(8,128)S(1)}, f32[5,5]{1,0:T(8,128)}, u32[]{:S(2)}) copy-start(f32[5,5]{1,0:T(8,128)} %param.7) | copy-start | bytes 304
  0.6 16.6 %copy-start.2 = (s32[2,3,128]{2,0,1:T(2,128)S(1)}, s32[2,3,128]{2,0,1:T(2,128)}, u32[]{:S(2)}) copy-start(s32[2,3,128]{2,0,1:T(2,128)} %param.8) | copy-start | bytes 9220
  0.7 16.6 %copy-start.3 = (f32[15]{0:T(128)S(1)}, f32[15]{0:T(128)}, u32[]{:S(2)}) copy-start(f32[15]{0:T(128)} %param.6) | copy-start | bytes 184
  5.7 12.0 %collective-permute-start = (bf16[2,7,4,1152]{3,2,1,0:T(4,128)(2,1)}, bf16[2,7,4,1152]{3,2,1,0:T(4,128)(2,1)S(1)}, u32[]{:S(2)}, u32[]{:S(2)}) collective-permute-start(bf16[2,7,4,1152]{3,2,1,0:T(4,128)(2,1)} %get-tuple-element.15), channel_id=1, source_target_pairs={{0,8},{8,16},{16,24},{1,9},{9,17},{17,25},{2,10},{10,18},{18,26},{... | collective-permute-start | bytes 387080 | tf_op jit(solution)/shard_map/ppermute | solution.py:25
  7.7 11.2 %collective-permute-start.1 = (bf16[2,7,4,1152]{3,2,1,0:T(4,128)(2,1)}, bf16[2,7,4,1152]{3,2,1,0:T(4,128)(2,1)S(1)}, u32[]{:S(2)}, u32[]{:S(2)}) collective-permute-start(bf16[2,7,4,1152]{3,2,1,0:T(4,128)(2,1)} %get-tuple-element.17), channel_id=1, source_target_pairs={{8,0},{16,8},{24,16},{9,1},{17,9},{25,17},{10,2},{18,10},{26,18},{... | collective-permute-start | bytes 387080 | tf_op jit(solution)/shard_map/ppermute | solution.py:25
  11.3 29.5 %collective-permute-start.7 = (bf16[7,128,1024]{2,1,0:T(8,128)(2,1)}, bf16[7,128,1024]{2,1,0:T(8,128)(2,1)}, u32[]{:S(2)}, u32[]{:S(2)}) collective-permute-start(bf16[7,128,1024]{2,1,0:T(8,128)(2,1)} %get-tuple-element.22), channel_id=1, source_target_pairs={{0,8},{8,16},{16,24},{1,9},{9,17},{17,25},{2,10},{10,18},{18,26},{... | collective-permute-start | bytes 5505032 | tf_op jit(solution)/shard_map/ppermute | solution.py:25
  13.2 27.6 %collective-permute-start.8 = (bf16[7,128,1024]{2,1,0:T(8,128)(2,1)}, bf16[7,128,1024]{2,1,0:T(8,128)(2,1)}, u32[]{:S(2)}, u32[]{:S(2)}) collective-permute-start(bf16[7,128,1024]{2,1,0:T(8,128)(2,1)} %get-tuple-element.23), channel_id=1, source_target_pairs={{8,0},{16,8},{24,16},{9,1},{17,9},{25,17},{10,2},{18,10},{26,18},{... | collective-permute-start | bytes 5505032 | tf_op jit(solution)/shard_map/ppermute | solution.py:25
  19.0 4.0 %collective-permute-start.2 = (bf16[2,30,2,128]{3,2,1,0:T(2,128)(2,1)S(1)}, bf16[2,30,2,128]{3,2,1,0:T(2,128)(2,1)S(1)}, u32[]{:S(2)}, u32[]{:S(2)}) collective-permute-start(bf16[2,30,2,128]{3,2,1,0:T(2,128)(2,1)S(1)} %broadcast_select_fusion), channel_id=1, source_target_pairs={{0,1},{1,0},{2,3},{3,2},{4,5},{5,4},{6,7},{7,6},{8,9},{9,8},{10,11... | collective-permute-start | bytes 92168 | tf_op jit(solution)/shard_map/ppermute | solution.py:462
  20.8 9.9 %copy-start.7 = (s32[2,1]{0,1:T(1,128)S(1)}, s32[2,1]{0,1:T(1,128)}, u32[]{:S(2)}) copy-start(s32[2,1]{0,1:T(1,128)} %param.9) | copy-start | bytes 28
  23.8 11.1 %copy-start = (bf16[2,30,128,128]{3,2,1,0:T(8,128)(2,1)}, bf16[2,30,128,128]{3,2,1,0:T(8,128)(2,1)S(1)}, u32[]{:S(2)}) copy-start(bf16[2,30,128,128]{3,2,1,0:T(8,128)(2,1)S(1)} %fusion.5.refs_6_) | copy-start | bytes 5898244
  24.6 12.3 %collective-permute-start.6 = (bf16[2,30,2,1152]{3,2,1,0:T(2,128)(2,1)S(1)}, bf16[2,30,2,1152]{3,2,1,0:T(2,128)(2,1)S(1)}, u32[]{:S(2)}, u32[]{:S(2)}) collective-permute-start(bf16[2,30,2,1152]{3,2,1,0:T(2,128)(2,1)S(1)} %get-tuple-element.36), channel_id=1, source_target_pairs={{0,2},{2,4},{4,6},{1,3},{3,5},{5,7},{8,10},{10,12},{12,14},{9,11},... | collective-permute-start | bytes 829448 | tf_op jit(solution)/shard_map/ppermute | solution.py:25
  28.1 12.7 %collective-permute-start.5 = (bf16[2,30,2,1152]{3,2,1,0:T(2,128)(2,1)S(1)}, bf16[2,30,2,1152]{3,2,1,0:T(2,128)(2,1)S(1)}, u32[]{:S(2)}, u32[]{:S(2)}) collective-permute-start(bf16[2,30,2,1152]{3,2,1,0:T(2,128)(2,1)S(1)} %get-tuple-element.37), channel_id=1, source_target_pairs={{2,0},{4,2},{6,4},{3,1},{5,3},{7,5},{10,8},{12,10},{14,12},{11,9},... | collective-permute-start | bytes 829448 | tf_op jit(solution)/shard_map/ppermute | solution.py:25
  35.0 35.9 %collective-permute-start.3 = (bf16[7,128,1024]{2,1,0:T(8,128)(2,1)}, bf16[7,128,1024]{2,1,0:T(8,128)(2,1)S(1)}, u32[]{:S(2)}, u32[]{:S(2)}) collective-permute-start(bf16[7,128,1024]{2,1,0:T(8,128)(2,1)} %get-tuple-element.19), channel_id=1, source_target_pairs={{0,8},{8,16},{16,24},{1,9},{9,17},{17,25},{2,10},{10,18},{18,26},{... | collective-permute-start | bytes 5505032 | tf_op jit(solution)/shard_map/ppermute | solution.py:25
  36.9 3.9 %copy-start.5 = (bf16[2,30,2,1152]{3,2,1,0:T(2,128)(2,1)}, bf16[2,30,2,1152]{3,2,1,0:T(2,128)(2,1)S(1)}, u32[]{:S(2)}) copy-start(bf16[2,30,2,1152]{3,2,1,0:T(2,128)(2,1)S(1)} %collective-permute-done.6.refs_8_) | copy-start | bytes 829444
  36.9 34.0 %collective-permute-start.4 = (bf16[7,128,1024]{2,1,0:T(8,128)(2,1)}, bf16[7,128,1024]{2,1,0:T(8,128)(2,1)}, u32[]{:S(2)}, u32[]{:S(2)}) collective-permute-start(bf16[7,128,1024]{2,1,0:T(8,128)(2,1)} %get-tuple-element.20), channel_id=1, source_target_pairs={{8,0},{16,8},{24,16},{9,1},{17,9},{25,17},{10,2},{18,10},{26,18},{... | collective-permute-start | bytes 5505032 | tf_op jit(solution)/shard_map/ppermute | solution.py:25
  40.8 0.7 copy-start.6
  65.3 30.6 %collective-permute-start.9 = (bf16[128,256]{1,0:T(8,128)(2,1)}, bf16[128,256]{1,0:T(8,128)(2,1)S(1)}, u32[]{:S(2)}, u32[]{:S(2)}) collective-permute-start(bf16[128,256]{1,0:T(8,128)(2,1)} %get-tuple-element.27), channel_id=1, source_target_pairs={{0,7},{1,6},{2,5},{3,4},{4,3},{5,2},{6,1},{7,0},{8,15},{9,14},{10,... | collective-permute-start | bytes 196616 | tf_op jit(solution)/shard_map/ppermute | solution.py:491
  70.9 1.2 %copy-start.4 = (bf16[7,128,1024]{2,1,0:T(8,128)(2,1)}, bf16[7,128,1024]{2,1,0:T(8,128)(2,1)S(1)}, u32[]{:S(2)}) copy-start(bf16[7,128,1024]{2,1,0:T(8,128)(2,1)S(1)} %collective-permute-done.3.refs_3_) | copy-start | bytes 5505028

commit v8 on v7

--- a/solution.py
+++ b/solution.py
@@ -15,6 +15,8 @@
 WINDOW = 32
 EDGE = 8
 GROUP = 4
+BY_VECTOR = (1, 2)
+BY_MATRIX = (0, 3, 4)
 bf16 = jnp.bfloat16
 f32 = jnp.float32
 
@@ -50,10 +52,12 @@
     in_ids = jnp.arange(depth, dtype=jnp.int32)[None, :]
     step = in_ids - out_ids - (EDGE - REACH)
     hit = step[None, :, :, None] == jnp.arange(SIDE, dtype=jnp.int32)
-    table = jnp.sum(jnp.where(hit, smooth_kernel.T[:, None, None, :], 0.0), axis=3)
-    table = jnp.swapaxes(table.reshape(SIDE, WINDOW // BLOCK, BLOCK, depth), 0, 1)
+    chosen = jnp.stack([smooth_kernel[:, b] for b in BY_MATRIX])
+    count = len(BY_MATRIX)
+    table = jnp.sum(jnp.where(hit, chosen[:, None, None, :], 0.0), axis=3)
+    table = jnp.swapaxes(table.reshape(count, WINDOW // BLOCK, BLOCK, depth), 0, 1)
     high, low = split(table)
-    return jnp.concatenate([high, high, low], axis=3).reshape(SIDE * WINDOW, 3 * depth)
+    return jnp.concatenate([high, high, low], axis=3).reshape(count * WINDOW, 3 * depth)
 
 
 def iota(shape, dim):
@@ -62,8 +66,8 @@
 
 def slab_kernel(
     row_step, frame_step,
-    spots_ref, taps_ref, w2_ref, low_ref, own_ref, high_ref, edge_ref, below_ref, above_ref,
-    out_ref, last_ref, w1, chi, clo, carry, outer, kept, flat,
+    spots_ref, kernel_ref, taps_ref, w2_ref, low_ref, own_ref, high_ref, edge_ref, below_ref, above_ref,
+    out_ref, last_ref, w1, chi, clo, full, carry, outer, kept, flat,
 ):
     frame_count, tiles, row_count, _ = kept.shape
     near = taps_ref.shape[1]
@@ -80,6 +84,7 @@
     def keep(above, below, tile, place):
         value = jnp.concatenate([above, below], axis=1)
         high = value.astype(bf16)
+        full[:, tile, place, :] = value
         chi[:, tile, place, :] = high
         clo[:, tile, place, :] = (value - high.astype(f32)).astype(bf16)
 
@@ -88,10 +93,10 @@
         count = 2 * frame_count
         tall = (iota((8 * count, count), 0) // 8 == iota((8 * count, count), 1)).astype(bf16)
         wide = (iota((near, 8 * near), 1) // 8 == iota((near, 8 * near), 0)).astype(bf16)
-        full = jnp.dot(tall, taps_ref[...], preferred_element_type=f32).astype(bf16)
-        full = jnp.dot(full, wide, preferred_element_type=f32)
-        same = iota(full.shape, 0) % 8 == iota(full.shape, 1) % 8
-        w1[...] = jnp.where(same, full, 0.0).astype(bf16)
+        matrix = jnp.dot(tall, taps_ref[...], preferred_element_type=f32).astype(bf16)
+        matrix = jnp.dot(matrix, wide, preferred_element_type=f32)
+        same = iota(matrix.shape, 0) & 7 == iota(matrix.shape, 1) & 7
+        w1[...] = jnp.where(same, matrix, 0.0).astype(bf16)
         for tile in range(0, tiles + 1, GROUP):
             pair = range(tile, min(tile + GROUP, tiles + 1))
             cols = slice(tile * TILE, (tile + len(pair)) * TILE)
@@ -179,10 +184,23 @@
                         w2_ref[...], jnp.concatenate(stacks, axis=1), preferred_element_type=f32
                     )
                     for q, (f, tile) in enumerate(pair):
+                        frame = (at - steps_1) * frame_step + k2 * 2 + f
                         for m in parts_of:
-                            for b in range(SIDE):
-                                at_row = (m * SIDE + b) * BLOCK
-                                part = both[at_row : at_row + BLOCK, q * TILE : (q + 1) * TILE]
+                            parts = {}
+                            for i, b in enumerate(BY_MATRIX):
+                                at_row = (m * len(BY_MATRIX) + i) * BLOCK
+                                parts[b] = both[at_row : at_row + BLOCK, q * TILE : (q + 1) * TILE]
+                            start = row + m * BLOCK + EDGE - REACH
+                            rows = [
+                                full[frame, tile, start + a : start + a + BLOCK, :]
+                                for a in range(SIDE)
+                            ]
+                            for b in BY_VECTOR:
+                                total = kernel_ref[0, b] * rows[0]
+                                for a in range(1, SIDE):
+                                    total = total + kernel_ref[a, b] * rows[a]
+                                parts[b] = total
+                            for b, part in parts.items():
                                 if b != REACH:
                                     part = pltpu.roll(part, (REACH - b) % TILE, 1)
                                 turned[f, m, b, tile] = part
@@ -369,7 +387,7 @@
     )(frames)
 
 
-def run_slab(slab, smoothed, spots, taps, w2, low, frames, high, edge, below, above):
+def run_slab(slab, smoothed, spots, kernel, taps, w2, low, frames, high, edge, below, above):
     _, frame_count, row_count, col_count = frames.shape
     slot_count = spots.shape[1]
     row_step, frame_step = 32, 4
@@ -384,8 +402,9 @@
     def whole(array):
         return pl.BlockSpec(array.shape, lambda at: (0,) * array.ndim)
 
-    operands = [spots, taps, w2, low, frames, high, edge, below, above]
+    operands = [spots, kernel, taps, w2, low, frames, high, edge, below, above]
     in_specs = [
+        pl.BlockSpec(memory_space=pltpu.SMEM),
         pl.BlockSpec(memory_space=pltpu.SMEM),
         whole(taps),
         whole(w2),
@@ -404,7 +423,7 @@
     count = len(operands)
 
     def body(*refs):
-        slab_kernel(row_step, frame_step, *refs[:9], *refs[count:])
+        slab_kernel(row_step, frame_step, *refs[:10], *refs[count:])
 
     tall = row_count + 2 * EDGE
     return pl.pallas_call(
@@ -426,6 +445,7 @@
             pltpu.VMEM((16 * frame_count, 8 * near), bf16),
             pltpu.VMEM((frame_count, wide // TILE, tall, TILE), bf16),
             pltpu.VMEM((frame_count, wide // TILE, tall, TILE), bf16),
+            pltpu.VMEM((frame_count, wide // TILE, tall, TILE), f32),
             pltpu.VMEM((frame_count, wide // TILE, EDGE, TILE), f32),
             pltpu.VMEM((frame_count, wide // TILE, EDGE, TILE), f32),
             pltpu.VMEM((frame_count, col_count // TILE, row_count, TILE), f32),
@@ -486,10 +506,10 @@
     live = jnp.broadcast_to(counts, frame.shape)
     local = jnp.stack([frame, row, tile, beside, TILE - col % TILE, live], axis=1)
 
-    smoothed, second = run_slab(1, None, local[1], taps, w2, low1, frames, high1, edge, below, above)
+    smoothed, second = run_slab(1, None, local[1], smooth_kernel, taps, w2, low1, frames, high1, edge, below, above)
     count = lax.axis_size("row") * lax.axis_size("col")
     second = lax.ppermute(second, ("row", "col"), [(i, count - 1 - i) for i in range(count)])
-    smoothed, first = run_slab(0, smoothed, local[0], taps, w2, low0, frames, high0, edge, below, above)
+    smoothed, first = run_slab(0, smoothed, local[0], smooth_kernel, taps, w2, low0, frames, high0, edge, below, above)
     scores = (
         lax.dot_general(first, second, (((1,), (1,)), ((), ())), preferred_element_type=f32)
         / float(PATCH * PATCH)

time: 98.7 us -> 99.5 us (level)
  transfers between devices with their start and end apart: 10 -> 10, of which waited for: 1 -> 1; matrix products, arithmetic and copies ran while one was open for 6% -> 6% of each run, Pallas kernels for 52% -> 53%
where the time goes in v8:
time: 99.5 us; the launch traced here: 98.4 us
  Pallas kernels  56.9 us (57%)
  starting transfers between devices  28.9 us (29%)
  local copies, waits for them, and re-layouts  5.85 us (6%)
  matrix products  2.51 us (3%)
  waiting for transfers between devices  2.21 us (2%)
  between operations  1.03 us (1%)
    pallas_call x2, Pallas kernels, run_slab(): pl.pallas_call(body, grid=(steps_1 + steps_2 + 1,), in_specs=in_specs, ou...  48.3 us
    ppermute x8, starting transfers between devices, shifted(): return lax.ppermute(block, axis, route)  21.7 us
    ppermute x1, starting transfers between devices, shards(): lax.ppermute(second, ('row', 'col'), [(i, count - 1 - i) for i in range(c...  5.69 us
    pallas_call x1, Pallas kernels, cut(): pl.pallas_call(cut_kernel, in_specs=[anywhere], out_specs=[near] * 3 + [a...  5.05 us
    pallas_call x1, Pallas kernels, late_cut(): pl.pallas_call(late_kernel, in_specs=[anywhere], out_specs=[anywhere] * 2...  3.53 us
    unnamed x18, local copies, waits for them, and re-layouts  3.08 us
    ppermute x1, waiting for transfers between devices, shards(): sides = lax.ppermute(sides, 'col', [(0, 1), (1, 0)])  2.18 us
  transfers between devices with their start and end apart: 10, of which 1 were waited for; matrix products, arithmetic and copies ran while one was open for 6% of the time, Pallas kernels for 53%

profile of v8, /device:TPU:2, one launch (start us, length us, event | category | flops | bytes accessed | tf_op | source)
XLA Modules:
  0.0 98.4 jit_solution(11181445883002181417)
XLA Ops:
  0.6 0.0 copy-start.1
  0.6 0.0 copy-start.2
  0.7 5.0 %cut.1 = (bf16[2,16,4,1152]{3,2,1,0:T(4,128)(2,1)}, bf16[2,7,4,1152]{3,2,1,0:T(4,128)(2,1)}, bf16[2,7,4,1152]{3,2,1,0:T(4,128)(2,1)}, bf16[7,128,1024]{2,1,0:T(8,128)(2,1)}, bf16[7,128,1024]{2,1,0:T(8,128)(2,1)}) custom-call(bf16[2,16,128,1024]{3,2,1,0:T(8,128)(2,1)} %refs_5_.3), custom_call_target="tpu_custom_call" | custom-call | tf_op jit(solution)/shard_map/cut/pallas_call | solution.py:353
  5.7 1.9 %collective-permute-start = (bf16[2,7,4,1152]{3,2,1,0:T(4,128)(2,1)}, bf16[2,7,4,1152]{3,2,1,0:T(4,128)(2,1)S(1)}, u32[]{:S(2)}, u32[]{:S(2)}) collective-permute-start(bf16[2,7,4,1152]{3,2,1,0:T(4,128)(2,1)} %get-tuple-element.15), channel_id=1, source_target_pairs={{0,8},{8,16},{16,24},{1,9},{9,17},{17,25},{2,10},{10,18},{18,26},{... | collective-permute-start | bytes 387080 | tf_op jit(solution)/shard_map/ppermute | solution.py:27
  7.6 3.6 %collective-permute-start.1 = (bf16[2,7,4,1152]{3,2,1,0:T(4,128)(2,1)}, bf16[2,7,4,1152]{3,2,1,0:T(4,128)(2,1)S(1)}, u32[]{:S(2)}, u32[]{:S(2)}) collective-permute-start(bf16[2,7,4,1152]{3,2,1,0:T(4,128)(2,1)} %get-tuple-element.17), channel_id=1, source_target_pairs={{8,0},{16,8},{24,16},{9,1},{17,9},{25,17},{10,2},{18,10},{26,18},{... | collective-permute-start | bytes 387080 | tf_op jit(solution)/shard_map/ppermute | solution.py:27
  11.3 1.9 %collective-permute-start.7 = (bf16[7,128,1024]{2,1,0:T(8,128)(2,1)}, bf16[7,128,1024]{2,1,0:T(8,128)(2,1)}, u32[]{:S(2)}, u32[]{:S(2)}) collective-permute-start(bf16[7,128,1024]{2,1,0:T(8,128)(2,1)} %get-tuple-element.22), channel_id=1, source_target_pairs={{0,8},{8,16},{16,24},{1,9},{9,17},{17,25},{2,10},{10,18},{18,26},{... | collective-permute-start | bytes 5505032 | tf_op jit(solution)/shard_map/ppermute | solution.py:27
  13.2 3.6 %collective-permute-start.8 = (bf16[7,128,1024]{2,1,0:T(8,128)(2,1)}, bf16[7,128,1024]{2,1,0:T(8,128)(2,1)}, u32[]{:S(2)}, u32[]{:S(2)}) collective-permute-start(bf16[7,128,1024]{2,1,0:T(8,128)(2,1)} %get-tuple-element.23), channel_id=1, source_target_pairs={{8,0},{16,8},{24,16},{9,1},{17,9},{25,17},{10,2},{18,10},{26,18},{... | collective-permute-start | bytes 5505032 | tf_op jit(solution)/shard_map/ppermute | solution.py:27
  16.9 0.2 slice_reduce_fusion.2
  17.2 0.1 select_reduce_fusion
  17.3 0.0 copy-done.2
  17.3 0.2 select_reduce_fusion.2
  17.5 0.1 reduce-precision_convert_fusion.1
  17.6 0.1 pad_maximum_fusion
  17.8 0.0 collective-permute-done
  17.8 1.1 %constant_dynamic-update-slice_fusion.1 = bf16[2,30,4,1152]{3,2,1,0:T(4,128)(2,1)S(1)} fusion(bf16[2,30,4,1152]{3,2,1,0:T(4,128)(2,1)S(1)} %constant_dynamic-update-slice_fusion.2, bf16[2,16,4,1152]{3,2,1,0:T(4,128)(2,1)} %get-tuple-element.16), kind=kLoop, calls=%fused_computation.18 | loop fusion | bytes 589824
  18.9 0.0 collective-permute-done.1
  18.9 0.1 constant_dynamic-update-slice_fusion
  19.0 0.1 broadcast_select_fusion
  19.1 1.6 %collective-permute-start.2 = (bf16[2,30,2,128]{3,2,1,0:T(2,128)(2,1)S(1)}, bf16[2,30,2,128]{3,2,1,0:T(2,128)(2,1)S(1)}, u32[]{:S(2)}, u32[]{:S(2)}) collective-permute-start(bf16[2,30,2,128]{3,2,1,0:T(2,128)(2,1)S(1)} %broadcast_select_fusion), channel_id=1, source_target_pairs={{0,1},{1,0},{2,3},{3,2},{4,5},{5,4},{6,7},{7,6},{8,9},{9,8},{10,11... | collective-permute-start | bytes 92168 | tf_op jit(solution)/shard_map/ppermute | solution.py:482
  20.6 0.2 slice.63
  20.8 0.0 copy-start.7
  20.8 2.2 %collective-permute-done.2 = bf16[2,30,2,128]{3,2,1,0:T(2,128)(2,1)S(1)} collective-permute-done((bf16[2,30,2,128]{3,2,1,0:T(2,128)(2,1)S(1)}, bf16[2,30,2,128]{3,2,1,0:T(2,128)(2,1)S(1)}, u32[]{:S(2)}, u32[]{:S(2)}) %collective-permute-start.2) | collective-permute-done | bytes 30752 | tf_op jit(solution)/shard_map/ppermute | solution.py:482
  23.0 0.9 fusion.5.refs_7_
  23.9 0.1 fusion.8
  24.0 0.3 maximum_maximum_fusion
  24.3 0.4 fusion.9
  24.7 3.5 %collective-permute-start.6 = (bf16[2,30,2,1152]{3,2,1,0:T(2,128)(2,1)S(1)}, bf16[2,30,2,1152]{3,2,1,0:T(2,128)(2,1)S(1)}, u32[]{:S(2)}, u32[]{:S(2)}) collective-permute-start(bf16[2,30,2,1152]{3,2,1,0:T(2,128)(2,1)S(1)} %get-tuple-element.39), channel_id=1, source_target_pairs={{0,2},{2,4},{4,6},{1,3},{3,5},{5,7},{8,10},{10,12},{12,14},{9,11},... | collective-permute-start | bytes 829448 | tf_op jit(solution)/shard_map/ppermute | solution.py:27
  28.2 1.3 %collective-permute-start.5 = (bf16[2,30,2,1152]{3,2,1,0:T(2,128)(2,1)S(1)}, bf16[2,30,2,1152]{3,2,1,0:T(2,128)(2,1)S(1)}, u32[]{:S(2)}, u32[]{:S(2)}) collective-permute-start(bf16[2,30,2,1152]{3,2,1,0:T(2,128)(2,1)S(1)} %get-tuple-element.40), channel_id=1, source_target_pairs={{2,0},{4,2},{6,4},{3,1},{5,3},{7,5},{10,8},{12,10},{14,12},{11,9},... | collective-permute-start | bytes 829448 | tf_op jit(solution)/shard_map/ppermute | solution.py:27
  29.5 0.6 copy.29
  30.1 0.6 copy.30
  30.7 0.1 stack_broadcast_in_dim.2
  30.8 0.6 slice_bitcast_fusion
  31.4 3.5 %late_cut.1 = (bf16[7,128,1024]{2,1,0:T(8,128)(2,1)}, bf16[7,128,1024]{2,1,0:T(8,128)(2,1)}) custom-call(bf16[2,16,128,1024]{3,2,1,0:T(8,128)(2,1)} %refs_5_.3), custom_call_target="tpu_custom_call" | custom-call | bytes 9000000 | tf_op jit(solution)/shard_map/late_cut/pallas_call | solution.py:375
  35.0 1.9 %collective-permute-start.3 = (bf16[7,128,1024]{2,1,0:T(8,128)(2,1)}, bf16[7,128,1024]{2,1,0:T(8,128)(2,1)S(1)}, u32[]{:S(2)}, u32[]{:S(2)}) collective-permute-start(bf16[7,128,1024]{2,1,0:T(8,128)(2,1)} %get-tuple-element.19), channel_id=1, source_target_pairs={{0,8},{8,16},{16,24},{1,9},{9,17},{17,25},{2,10},{10,18},{18,26},{... | collective-permute-start | bytes 5505032 | tf_op jit(solution)/shard_map/ppermute | solution.py:27
  36.9 0.0 collective-permute-done.6.refs_9_
  36.9 3.8 %collective-permute-start.4 = (bf16[7,128,1024]{2,1,0:T(8,128)(2,1)}, bf16[7,128,1024]{2,1,0:T(8,128)(2,1)}, u32[]{:S(2)}, u32[]{:S(2)}) collective-permute-start(bf16[7,128,1024]{2,1,0:T(8,128)(2,1)} %get-tuple-element.20), channel_id=1, source_target_pairs={{8,0},{16,8},{24,16},{9,1},{17,9},{25,17},{10,2},{18,10},{26,18},{... | collective-permute-start | bytes 5505032 | tf_op jit(solution)/shard_map/ppermute | solution.py:27
  40.7 0.0 collective-permute-done.5.refs_8_
  40.8 0.0 collective-permute-done.7.refs_4_
  40.8 0.0 collective-permute-done.8.refs_6_
  40.8 0.7 copy-done.6
  41.5 24.2 %slab_1.1 = (bf16[2,16,128,1024]{3,2,1,0:T(8,128)(2,1)}, bf16[128,256]{1,0:T(8,128)(2,1)}) custom-call(s32[6,128]{1,0:T(8,128)} %get-tuple-element.45.refs_0_, f32[5,5]{1,0:T(8,128)} %refs_1_.3, bf16[32,30]{1,0:T(8,128)(2,1)} %bitcast.37, bf16[96,144]{1,0:T(8,128)(2,1)} %bitcast.33, bf16[7,128,1024]{2,1,0:T(8,128)(2,1)} %collective-permute-done.7.refs_4_, ...), custom_call_target="tpu_custom_call" | custom-call | flops 20000000000 | bytes 16000000 | tf_op jit(solution)/shard_map/slab_1/pallas_call | solution.py:429
  65.7 5.7 %collective-permute-start.9 = (bf16[128,256]{1,0:T(8,128)(2,1)}, bf16[128,256]{1,0:T(8,128)(2,1)S(1)}, u32[]{:S(2)}, u32[]{:S(2)}) collective-permute-start(bf16[128,256]{1,0:T(8,128)(2,1)} %get-tuple-element.27), channel_id=1, source_target_pairs={{0,7},{1,6},{2,5},{3,4},{4,3},{5,2},{6,1},{7,0},{8,15},{9,14},{10,... | collective-permute-start | bytes 196616 | tf_op jit(solution)/shard_map/ppermute | solution.py:511
  71.3 0.0 collective-permute-done.3.refs_4_
  71.3 0.0 collective-permute-done.4.refs_6_
  71.4 1.2 %copy-done.4 = bf16[7,128,1024]{2,1,0:T(8,128)(2,1)} copy-done((bf16[7,128,1024]{2,1,0:T(8,128)(2,1)}, bf16[7,128,1024]{2,1,0:T(8,128)(2,1)S(1)}, u32[]{:S(2)}) %copy-start.4) | copy-done | bytes 1835032
  72.6 24.2 %slab_0.1 = (bf16[2,16,128,1024]{3,2,1,0:T(8,128)(2,1)}, bf16[128,256]{1,0:T(8,128)(2,1)}) custom-call(s32[6,128]{1,0:T(8,128)} %get-tuple-element.46.refs_0_, f32[5,5]{1,0:T(8,128)} %refs_1_.3, bf16[32,30]{1,0:T(8,128)(2,1)} %bitcast.38, bf16[96,144]{1,0:T(8,128)(2,1)} %bitcast.34, ...), custom_call_target="tpu_custom_call", output_to_operand_aliasing={{0}: (10, {})} | custom-call | flops 20000000000 | bytes 16000000 | tf_op jit(solution)/shard_map/slab_0/pallas_call | solution.py:429
  96.8 0.0 collective-permute-done.9
  96.8 1.6 %convolution_multiply_fusion = f32[128,128]{1,0:T(8,128)} fusion(bf16[128,256]{1,0:T(8,128)(2,1)} %get-tuple-element.26, bf16[128,256]{1,0:T(8,128)(2,1)S(1)} %collective-permute-done.9), kind=kOutput, calls=%fused_computation | convolution fusion | flops 8404992 | bytes 196608 | tf_op jit(solution)/shard_map/dot_general | solution.py:514
  (23 shorter events, 0.2 us)
Async XLA Ops:
  0.6 16.3 %copy-start.1 = (f32[5,5]{1,0:T(8,128)S(1)}, f32[5,5]{1,0:T(8,128)}, u32[]{:S(2)}) copy-start(f32[5,5]{1,0:T(8,128)} %refs_1_.3) | copy-start | bytes 304
  0.6 16.6 %copy-start.2 = (s32[2,3,128]{2,0,1:T(2,128)S(1)}, s32[2,3,128]{2,0,1:T(2,128)}, u32[]{:S(2)}) copy-start(s32[2,3,128]{2,0,1:T(2,128)} %param.8) | copy-start | bytes 9220
  0.7 16.7 %copy-start.3 = (f32[15]{0:T(128)S(1)}, f32[15]{0:T(128)}, u32[]{:S(2)}) copy-start(f32[15]{0:T(128)} %param.6) | copy-start | bytes 184
  5.7 12.0 %collective-permute-start = (bf16[2,7,4,1152]{3,2,1,0:T(4,128)(2,1)}, bf16[2,7,4,1152]{3,2,1,0:T(4,128)(2,1)S(1)}, u32[]{:S(2)}, u32[]{:S(2)}) collective-permute-start(bf16[2,7,4,1152]{3,2,1,0:T(4,128)(2,1)} %get-tuple-element.15), channel_id=1, source_target_pairs={{0,8},{8,16},{16,24},{1,9},{9,17},{17,25},{2,10},{10,18},{18,26},{... | collective-permute-start | bytes 387080 | tf_op jit(solution)/shard_map/ppermute | solution.py:27
  7.6 11.3 %collective-permute-start.1 = (bf16[2,7,4,1152]{3,2,1,0:T(4,128)(2,1)}, bf16[2,7,4,1152]{3,2,1,0:T(4,128)(2,1)S(1)}, u32[]{:S(2)}, u32[]{:S(2)}) collective-permute-start(bf16[2,7,4,1152]{3,2,1,0:T(4,128)(2,1)} %get-tuple-element.17), channel_id=1, source_target_pairs={{8,0},{16,8},{24,16},{9,1},{17,9},{25,17},{10,2},{18,10},{26,18},{... | collective-permute-start | bytes 387080 | tf_op jit(solution)/shard_map/ppermute | solution.py:27
  11.3 29.5 %collective-permute-start.7 = (bf16[7,128,1024]{2,1,0:T(8,128)(2,1)}, bf16[7,128,1024]{2,1,0:T(8,128)(2,1)}, u32[]{:S(2)}, u32[]{:S(2)}) collective-permute-start(bf16[7,128,1024]{2,1,0:T(8,128)(2,1)} %get-tuple-element.22), channel_id=1, source_target_pairs={{0,8},{8,16},{16,24},{1,9},{9,17},{17,25},{2,10},{10,18},{18,26},{... | collective-permute-start | bytes 5505032 | tf_op jit(solution)/shard_map/ppermute | solution.py:27
  13.2 27.6 %collective-permute-start.8 = (bf16[7,128,1024]{2,1,0:T(8,128)(2,1)}, bf16[7,128,1024]{2,1,0:T(8,128)(2,1)}, u32[]{:S(2)}, u32[]{:S(2)}) collective-permute-start(bf16[7,128,1024]{2,1,0:T(8,128)(2,1)} %get-tuple-element.23), channel_id=1, source_target_pairs={{8,0},{16,8},{24,16},{9,1},{17,9},{25,17},{10,2},{18,10},{26,18},{... | collective-permute-start | bytes 5505032 | tf_op jit(solution)/shard_map/ppermute | solution.py:27
  19.1 4.0 %collective-permute-start.2 = (bf16[2,30,2,128]{3,2,1,0:T(2,128)(2,1)S(1)}, bf16[2,30,2,128]{3,2,1,0:T(2,128)(2,1)S(1)}, u32[]{:S(2)}, u32[]{:S(2)}) collective-permute-start(bf16[2,30,2,128]{3,2,1,0:T(2,128)(2,1)S(1)} %broadcast_select_fusion), channel_id=1, source_target_pairs={{0,1},{1,0},{2,3},{3,2},{4,5},{5,4},{6,7},{7,6},{8,9},{9,8},{10,11... | collective-permute-start | bytes 92168 | tf_op jit(solution)/shard_map/ppermute | solution.py:482
  20.8 9.9 %copy-start.7 = (s32[2,1]{0,1:T(1,128)S(1)}, s32[2,1]{0,1:T(1,128)}, u32[]{:S(2)}) copy-start(s32[2,1]{0,1:T(1,128)} %param.9) | copy-start | bytes 28
  23.9 11.1 %copy-start = (bf16[2,30,128,128]{3,2,1,0:T(8,128)(2,1)}, bf16[2,30,128,128]{3,2,1,0:T(8,128)(2,1)S(1)}, u32[]{:S(2)}) copy-start(bf16[2,30,128,128]{3,2,1,0:T(8,128)(2,1)S(1)} %fusion.5.refs_7_) | copy-start | bytes 5898244
  24.7 12.2 %collective-permute-start.6 = (bf16[2,30,2,1152]{3,2,1,0:T(2,128)(2,1)S(1)}, bf16[2,30,2,1152]{3,2,1,0:T(2,128)(2,1)S(1)}, u32[]{:S(2)}, u32[]{:S(2)}) collective-permute-start(bf16[2,30,2,1152]{3,2,1,0:T(2,128)(2,1)S(1)} %get-tuple-element.39), channel_id=1, source_target_pairs={{0,2},{2,4},{4,6},{1,3},{3,5},{5,7},{8,10},{10,12},{12,14},{9,11},... | collective-permute-start | bytes 829448 | tf_op jit(solution)/shard_map/ppermute | solution.py:27
  28.2 12.6 %collective-permute-start.5 = (bf16[2,30,2,1152]{3,2,1,0:T(2,128)(2,1)S(1)}, bf16[2,30,2,1152]{3,2,1,0:T(2,128)(2,1)S(1)}, u32[]{:S(2)}, u32[]{:S(2)}) collective-permute-start(bf16[2,30,2,1152]{3,2,1,0:T(2,128)(2,1)S(1)} %get-tuple-element.40), channel_id=1, source_target_pairs={{2,0},{4,2},{6,4},{3,1},{5,3},{7,5},{10,8},{12,10},{14,12},{11,9},... | collective-permute-start | bytes 829448 | tf_op jit(solution)/shard_map/ppermute | solution.py:27
  35.0 36.4 %collective-permute-start.3 = (bf16[7,128,1024]{2,1,0:T(8,128)(2,1)}, bf16[7,128,1024]{2,1,0:T(8,128)(2,1)S(1)}, u32[]{:S(2)}, u32[]{:S(2)}) collective-permute-start(bf16[7,128,1024]{2,1,0:T(8,128)(2,1)} %get-tuple-element.19), channel_id=1, source_target_pairs={{0,8},{8,16},{16,24},{1,9},{9,17},{17,25},{2,10},{10,18},{18,26},{... | collective-permute-start | bytes 5505032 | tf_op jit(solution)/shard_map/ppermute | solution.py:27
  36.9 3.9 %copy-start.5 = (bf16[2,30,2,1152]{3,2,1,0:T(2,128)(2,1)}, bf16[2,30,2,1152]{3,2,1,0:T(2,128)(2,1)S(1)}, u32[]{:S(2)}) copy-start(bf16[2,30,2,1152]{3,2,1,0:T(2,128)(2,1)S(1)} %collective-permute-done.6.refs_9_) | copy-start | bytes 829444
  36.9 34.4 %collective-permute-start.4 = (bf16[7,128,1024]{2,1,0:T(8,128)(2,1)}, bf16[7,128,1024]{2,1,0:T(8,128)(2,1)}, u32[]{:S(2)}, u32[]{:S(2)}) collective-permute-start(bf16[7,128,1024]{2,1,0:T(8,128)(2,1)} %get-tuple-element.20), channel_id=1, source_target_pairs={{8,0},{16,8},{24,16},{9,1},{17,9},{25,17},{10,2},{18,10},{26,18},{... | collective-permute-start | bytes 5505032 | tf_op jit(solution)/shard_map/ppermute | solution.py:27
  40.8 0.7 copy-start.6
  65.7 31.1 %collective-permute-start.9 = (bf16[128,256]{1,0:T(8,128)(2,1)}, bf16[128,256]{1,0:T(8,128)(2,1)S(1)}, u32[]{:S(2)}, u32[]{:S(2)}) collective-permute-start(bf16[128,256]{1,0:T(8,128)(2,1)} %get-tuple-element.27), channel_id=1, source_target_pairs={{0,7},{1,6},{2,5},{3,4},{4,3},{5,2},{6,1},{7,0},{8,15},{9,14},{10,... | collective-permute-start | bytes 196616 | tf_op jit(solution)/shard_map/ppermute | solution.py:511
  71.3 1.2 %copy-start.4 = (bf16[7,128,1024]{2,1,0:T(8,128)(2,1)}, bf16[7,128,1024]{2,1,0:T(8,128)(2,1)S(1)}, u32[]{:S(2)}) copy-start(bf16[7,128,1024]{2,1,0:T(8,128)(2,1)S(1)} %collective-permute-done.3.refs_4_) | copy-start | bytes 5505028

commit v9 on v7

--- a/solution.py
+++ b/solution.py
@@ -72,7 +72,7 @@
     at = pl.program_id(0)
 
     def filtered(block):
-        part = block.reshape(near * 8, block.shape[2]).astype(bf16)
+        part = block.reshape(near * 8, block.shape[2])
         both = jnp.dot(w1[...], part, preferred_element_type=f32)
         both = both.reshape(frame_count, 2, 8, block.shape[2])
         return both[:, 0] + both[:, 1]
@@ -98,7 +98,7 @@
             below = below_ref[0, :, :, cols].astype(f32)
             above = above_ref[0, :, :, cols].astype(f32)
             gap = jnp.zeros((near, 8 - 2 * REACH, below.shape[2]), f32)
-            both = filtered(jnp.concatenate([below, gap, above], axis=1))
+            both = filtered(jnp.concatenate([below, gap, above], axis=1).astype(bf16))
             for q, one in enumerate(pair):
                 carry[:, one] = both[..., q * TILE : (q + 1) * TILE]
                 outer[:, one] = both[..., q * TILE : (q + 1) * TILE]
@@ -112,22 +112,23 @@
                 keep(parts[q], parts[q + 1], tile, place)
             carry[:, tile] = parts[-1]
 
-        for tile in range(0, tiles, GROUP):
-            group = range(tile, min(tile + GROUP, tiles))
+        for tile in range(0, tiles, 2):
+            group = range(tile, min(tile + 2, tiles))
             cols = slice(tile * TILE, (tile + len(group)) * TILE)
             parts = []
-            for h in range(0, row_step, BLOCK):
-                rows = slice(h, h + BLOCK)
+            for h in range(0, row_step, EDGE):
+                rows = slice(h, h + EDGE)
                 block = jnp.concatenate(
                     [low_ref[:, rows, cols], own_ref[0, :, rows, cols], high_ref[:, rows, cols]],
                     axis=0,
-                ).astype(f32)
-                parts += [filtered(block[:, :EDGE]), filtered(block[:, EDGE:])]
+                )
+                parts.append(filtered(block))
             for q, one in enumerate(group):
                 keep_all(one, [part[..., q * TILE : (q + 1) * TILE] for part in parts])
-        wide = edge_ref[0].astype(f32)
         both = filtered(
-            jnp.concatenate([wide[:, h : h + EDGE] for h in range(0, row_step, EDGE)], axis=2)
+            jnp.concatenate(
+                [edge_ref[0, :, h : h + EDGE] for h in range(0, row_step, EDGE)], axis=2
+            )
         )
         parts = [both[..., h * TILE : (h + 1) * TILE] for h in range(row_step // EDGE)]
         keep_all(tiles, parts)
@@ -204,8 +205,8 @@
         lane = iota((PATCH, TILE), 1)
 
         def some(i8, unused):
-            for j in range(8):
-                i = i8 * 8 + j
+            for j in range(16):
+                i = i8 * 16 + j
                 frame, row, tile = spots_ref[0, i], spots_ref[1, i], spots_ref[2, i]
                 beside, turn = spots_ref[3, i], spots_ref[4, i]
                 here = kept[frame, tile, pl.ds(row, PATCH), :]
@@ -216,7 +217,7 @@
                 flat[pl.ds(pl.multiple_of(i * PATCH, PATCH), PATCH), :] = part.astype(bf16)
             return unused
 
-        lax.fori_loop(0, slot_count // 8, some, 0)
+        lax.fori_loop(0, slot_count // 16, some, 0)
         low_bits = PATCH - 1
         bits = low_bits.bit_length()
         shape = (TILE, PATCH * PATCH)

time: 98.7 us -> 97.2 us (0.985)
  Pallas kernels: 56.3 us -> 54.8 us
    pallas_call x2, Pallas kernels: 47.6 us -> 46.2 us  [run_slab(): pl.pallas_call(body, grid=(steps_1 + steps_2 + 1,), in_specs=in_specs, ou...]
where the time goes in v9:
time: 97.2 us; the launch traced here: 96.1 us
  Pallas kernels  54.8 us (56%)
  starting transfers between devices  28.8 us (30%)
  local copies, waits for them, and re-layouts  5.77 us (6%)
  matrix products  2.52 us (3%)
  waiting for transfers between devices  2.21 us (2%)
  between operations  1.01 us (1%)
    pallas_call x2, Pallas kernels, run_slab(): pl.pallas_call(body, grid=(steps_1 + steps_2 + 1,), in_specs=in_specs, ou...  46.2 us
    ppermute x8, starting transfers between devices, shifted(): return lax.ppermute(block, axis, route)  21.7 us
    ppermute x1, starting transfers between devices, shards(): lax.ppermute(second, ('row', 'col'), [(i, count - 1 - i) for i in range(c...  5.6 us
    pallas_call x1, Pallas kernels, cut(): pl.pallas_call(cut_kernel, in_specs=[anywhere], out_specs=[near] * 3 + [a...  5.07 us
    pallas_call x1, Pallas kernels, late_cut(): pl.pallas_call(late_kernel, in_specs=[anywhere], out_specs=[anywhere] * 2...  3.59 us
    unnamed x18, local copies, waits for them, and re-layouts  3.05 us
    ppermute x1, waiting for transfers between devices, shards(): sides = lax.ppermute(sides, 'col', [(0, 1), (1, 0)])  2.18 us
  transfers between devices with their start and end apart: 10, of which 1 were waited for; matrix products, arithmetic and copies ran while one was open for 6% of the time, Pallas kernels for 52%

profile of v9, /device:TPU:2, one launch (start us, length us, event | category | flops | bytes accessed | tf_op | source)
XLA Modules:
  0.0 96.1 jit_solution(12534561859202803149)
XLA Ops:
  0.6 0.0 copy-start.1
  0.6 0.0 copy-start.2
  0.7 0.0 copy-start.3
  0.7 5.1 %cut.1 = (bf16[2,16,4,1152]{3,2,1,0:T(4,128)(2,1)}, bf16[2,7,4,1152]{3,2,1,0:T(4,128)(2,1)}, bf16[2,7,4,1152]{3,2,1,0:T(4,128)(2,1)}, bf16[7,128,1024]{2,1,0:T(8,128)(2,1)}, bf16[7,128,1024]{2,1,0:T(8,128)(2,1)}) custom-call(bf16[2,16,128,1024]{3,2,1,0:T(8,128)(2,1)} %refs_4_.3), custom_call_target="tpu_custom_call" | custom-call | tf_op jit(solution)/shard_map/cut/pallas_call | solution.py:336
  5.7 1.9 %collective-permute-start = (bf16[2,7,4,1152]{3,2,1,0:T(4,128)(2,1)}, bf16[2,7,4,1152]{3,2,1,0:T(4,128)(2,1)S(1)}, u32[]{:S(2)}, u32[]{:S(2)}) collective-permute-start(bf16[2,7,4,1152]{3,2,1,0:T(4,128)(2,1)} %get-tuple-element.15), channel_id=1, source_target_pairs={{0,8},{8,16},{16,24},{1,9},{9,17},{17,25},{2,10},{10,18},{18,26},{... | collective-permute-start | bytes 387080 | tf_op jit(solution)/shard_map/ppermute | solution.py:25
  7.7 3.6 %collective-permute-start.1 = (bf16[2,7,4,1152]{3,2,1,0:T(4,128)(2,1)}, bf16[2,7,4,1152]{3,2,1,0:T(4,128)(2,1)S(1)}, u32[]{:S(2)}, u32[]{:S(2)}) collective-permute-start(bf16[2,7,4,1152]{3,2,1,0:T(4,128)(2,1)} %get-tuple-element.17), channel_id=1, source_target_pairs={{8,0},{16,8},{24,16},{9,1},{17,9},{25,17},{10,2},{18,10},{26,18},{... | collective-permute-start | bytes 387080 | tf_op jit(solution)/shard_map/ppermute | solution.py:25
  11.3 1.9 %collective-permute-start.7 = (bf16[7,128,1024]{2,1,0:T(8,128)(2,1)}, bf16[7,128,1024]{2,1,0:T(8,128)(2,1)}, u32[]{:S(2)}, u32[]{:S(2)}) collective-permute-start(bf16[7,128,1024]{2,1,0:T(8,128)(2,1)} %get-tuple-element.22), channel_id=1, source_target_pairs={{0,8},{8,16},{16,24},{1,9},{9,17},{17,25},{2,10},{10,18},{18,26},{... | collective-permute-start | bytes 5505032 | tf_op jit(solution)/shard_map/ppermute | solution.py:25
  13.2 3.6 %collective-permute-start.8 = (bf16[7,128,1024]{2,1,0:T(8,128)(2,1)}, bf16[7,128,1024]{2,1,0:T(8,128)(2,1)}, u32[]{:S(2)}, u32[]{:S(2)}) collective-permute-start(bf16[7,128,1024]{2,1,0:T(8,128)(2,1)} %get-tuple-element.23), channel_id=1, source_target_pairs={{8,0},{16,8},{24,16},{9,1},{17,9},{25,17},{10,2},{18,10},{26,18},{... | collective-permute-start | bytes 5505032 | tf_op jit(solution)/shard_map/ppermute | solution.py:25
  16.9 0.1 copy.33
  17.1 0.1 select_reduce_fusion
  17.3 0.2 select_reduce_fusion.2
  17.5 0.1 reduce-precision_convert_fusion.1
  17.6 0.1 pad_maximum_fusion
  17.7 0.0 collective-permute-done
  17.8 1.1 %constant_dynamic-update-slice_fusion.1 = bf16[2,30,4,1152]{3,2,1,0:T(4,128)(2,1)S(1)} fusion(bf16[2,30,4,1152]{3,2,1,0:T(4,128)(2,1)S(1)} %constant_dynamic-update-slice_fusion.2, bf16[2,16,4,1152]{3,2,1,0:T(4,128)(2,1)} %get-tuple-element.16), kind=kLoop, calls=%fused_computation.18 | loop fusion | bytes 589824
  18.8 0.0 collective-permute-done.1
  18.9 0.1 constant_dynamic-update-slice_fusion
  18.9 0.1 broadcast_select_fusion
  19.0 1.6 %collective-permute-start.2 = (bf16[2,30,2,128]{3,2,1,0:T(2,128)(2,1)S(1)}, bf16[2,30,2,128]{3,2,1,0:T(2,128)(2,1)S(1)}, u32[]{:S(2)}, u32[]{:S(2)}) collective-permute-start(bf16[2,30,2,128]{3,2,1,0:T(2,128)(2,1)S(1)} %broadcast_select_fusion), channel_id=1, source_target_pairs={{0,1},{1,0},{2,3},{3,2},{4,5},{5,4},{6,7},{7,6},{8,9},{9,8},{10,11... | collective-permute-start | bytes 92168 | tf_op jit(solution)/shard_map/ppermute | solution.py:463
  20.6 0.2 slice.51
  20.8 0.0 copy-start.7
  20.8 2.2 %collective-permute-done.2 = bf16[2,30,2,128]{3,2,1,0:T(2,128)(2,1)S(1)} collective-permute-done((bf16[2,30,2,128]{3,2,1,0:T(2,128)(2,1)S(1)}, bf16[2,30,2,128]{3,2,1,0:T(2,128)(2,1)S(1)}, u32[]{:S(2)}, u32[]{:S(2)}) %collective-permute-start.2) | collective-permute-done | bytes 30752 | tf_op jit(solution)/shard_map/ppermute | solution.py:463
  22.9 0.9 fusion.5.refs_6_
  23.8 0.1 fusion.8
  23.9 0.3 maximum_maximum_fusion
  24.2 0.4 fusion.9
  24.6 3.5 %collective-permute-start.6 = (bf16[2,30,2,1152]{3,2,1,0:T(2,128)(2,1)S(1)}, bf16[2,30,2,1152]{3,2,1,0:T(2,128)(2,1)S(1)}, u32[]{:S(2)}, u32[]{:S(2)}) collective-permute-start(bf16[2,30,2,1152]{3,2,1,0:T(2,128)(2,1)S(1)} %get-tuple-element.36), channel_id=1, source_target_pairs={{0,2},{2,4},{4,6},{1,3},{3,5},{5,7},{8,10},{10,12},{12,14},{9,11},... | collective-permute-start | bytes 829448 | tf_op jit(solution)/shard_map/ppermute | solution.py:25
  28.1 1.3 %collective-permute-start.5 = (bf16[2,30,2,1152]{3,2,1,0:T(2,128)(2,1)S(1)}, bf16[2,30,2,1152]{3,2,1,0:T(2,128)(2,1)S(1)}, u32[]{:S(2)}, u32[]{:S(2)}) collective-permute-start(bf16[2,30,2,1152]{3,2,1,0:T(2,128)(2,1)S(1)} %get-tuple-element.37), channel_id=1, source_target_pairs={{2,0},{4,2},{6,4},{3,1},{5,3},{7,5},{10,8},{12,10},{14,12},{11,9},... | collective-permute-start | bytes 829448 | tf_op jit(solution)/shard_map/ppermute | solution.py:25
  29.4 0.6 copy.32
  30.0 0.6 copy.34
  30.7 0.1 stack_broadcast_in_dim.2
  30.8 0.6 slice_bitcast_fusion
  31.4 3.6 %late_cut.1 = (bf16[7,128,1024]{2,1,0:T(8,128)(2,1)}, bf16[7,128,1024]{2,1,0:T(8,128)(2,1)}) custom-call(bf16[2,16,128,1024]{3,2,1,0:T(8,128)(2,1)} %refs_4_.3), custom_call_target="tpu_custom_call" | custom-call | bytes 9000000 | tf_op jit(solution)/shard_map/late_cut/pallas_call | solution.py:358
  35.0 1.9 %collective-permute-start.3 = (bf16[7,128,1024]{2,1,0:T(8,128)(2,1)}, bf16[7,128,1024]{2,1,0:T(8,128)(2,1)S(1)}, u32[]{:S(2)}, u32[]{:S(2)}) collective-permute-start(bf16[7,128,1024]{2,1,0:T(8,128)(2,1)} %get-tuple-element.19), channel_id=1, source_target_pairs={{0,8},{8,16},{16,24},{1,9},{9,17},{17,25},{2,10},{10,18},{18,26},{... | collective-permute-start | bytes 5505032 | tf_op jit(solution)/shard_map/ppermute | solution.py:25
  36.9 0.0 collective-permute-done.6.refs_8_
  36.9 3.8 %collective-permute-start.4 = (bf16[7,128,1024]{2,1,0:T(8,128)(2,1)}, bf16[7,128,1024]{2,1,0:T(8,128)(2,1)}, u32[]{:S(2)}, u32[]{:S(2)}) collective-permute-start(bf16[7,128,1024]{2,1,0:T(8,128)(2,1)} %get-tuple-element.20), channel_id=1, source_target_pairs={{8,0},{16,8},{24,16},{9,1},{17,9},{25,17},{10,2},{18,10},{26,18},{... | collective-permute-start | bytes 5505032 | tf_op jit(solution)/shard_map/ppermute | solution.py:25
  40.8 0.0 collective-permute-done.5.refs_7_
  40.8 0.0 collective-permute-done.7.refs_3_
  40.8 0.0 collective-permute-done.8.refs_5_
  40.8 0.7 copy-done.6
  41.5 23.1 %slab_1.1 = (bf16[2,16,128,1024]{3,2,1,0:T(8,128)(2,1)}, bf16[128,256]{1,0:T(8,128)(2,1)}) custom-call(s32[6,128]{1,0:T(8,128)} %get-tuple-element.42.refs_0_, bf16[32,30]{1,0:T(8,128)(2,1)} %bitcast.35, bf16[160,144]{1,0:T(8,128)(2,1)} %bitcast.31, bf16[7,128,1024]{2,1,0:T(8,128)(2,1)} %collective-permute-done.7.refs_3_, ...), custom_call_target="tpu_custom_call" | custom-call | flops 20000000000 | bytes 16000000 | tf_op jit(solution)/shard_map/slab_1/pallas_call | solution.py:411
  64.6 5.6 %collective-permute-start.9 = (bf16[128,256]{1,0:T(8,128)(2,1)}, bf16[128,256]{1,0:T(8,128)(2,1)S(1)}, u32[]{:S(2)}, u32[]{:S(2)}) collective-permute-start(bf16[128,256]{1,0:T(8,128)(2,1)} %get-tuple-element.27), channel_id=1, source_target_pairs={{0,7},{1,6},{2,5},{3,4},{4,3},{5,2},{6,1},{7,0},{8,15},{9,14},{10,... | collective-permute-start | bytes 196616 | tf_op jit(solution)/shard_map/ppermute | solution.py:492
  70.2 0.0 collective-permute-done.3.refs_3_
  70.2 0.0 collective-permute-done.4.refs_5_
  70.2 1.2 %copy-done.4 = bf16[7,128,1024]{2,1,0:T(8,128)(2,1)} copy-done((bf16[7,128,1024]{2,1,0:T(8,128)(2,1)}, bf16[7,128,1024]{2,1,0:T(8,128)(2,1)S(1)}, u32[]{:S(2)}) %copy-start.4) | copy-done | bytes 1835032
  71.4 23.1 %slab_0.1 = (bf16[2,16,128,1024]{3,2,1,0:T(8,128)(2,1)}, bf16[128,256]{1,0:T(8,128)(2,1)}) custom-call(s32[6,128]{1,0:T(8,128)} %get-tuple-element.43.refs_0_, bf16[32,30]{1,0:T(8,128)(2,1)} %bitcast.36, bf16[160,144]{1,0:T(8,128)(2,1)} %bitcast.32, bf16[7,128,1024]{2,1,0:T(8,128)(2,1)} %copy-done.4, ...), custom_call_target="tpu_custom_call", output_to_operand_aliasing={{0}: (9, {})} | custom-call | flops 20000000000 | bytes 16000000 | tf_op jit(solution)/shard_map/slab_0/pallas_call | solution.py:411
  94.5 0.0 collective-permute-done.9
  94.5 1.6 %convolution_multiply_fusion = f32[128,128]{1,0:T(8,128)} fusion(bf16[128,256]{1,0:T(8,128)(2,1)} %get-tuple-element.26, bf16[128,256]{1,0:T(8,128)(2,1)S(1)} %collective-permute-done.9), kind=kOutput, calls=%fused_computation | convolution fusion | flops 8404992 | bytes 196608 | tf_op jit(solution)/shard_map/dot_general | solution.py:495
  (22 shorter events, 0.2 us)
Async XLA Ops:
  0.6 16.3 %copy-start.1 = (f32[5,5]{1,0:T(8,128)S(1)}, f32[5,5]{1,0:T(8,128)}, u32[]{:S(2)}) copy-start(f32[5,5]{1,0:T(8,128)} %param.7) | copy-start | bytes 304
  0.6 16.6 %copy-start.2 = (s32[2,3,128]{2,0,1:T(2,128)S(1)}, s32[2,3,128]{2,0,1:T(2,128)}, u32[]{:S(2)}) copy-start(s32[2,3,128]{2,0,1:T(2,128)} %param.8) | copy-start | bytes 9220
  0.7 16.6 %copy-start.3 = (f32[15]{0:T(128)S(1)}, f32[15]{0:T(128)}, u32[]{:S(2)}) copy-start(f32[15]{0:T(128)} %param.6) | copy-start | bytes 184
  5.7 12.0 %collective-permute-start = (bf16[2,7,4,1152]{3,2,1,0:T(4,128)(2,1)}, bf16[2,7,4,1152]{3,2,1,0:T(4,128)(2,1)S(1)}, u32[]{:S(2)}, u32[]{:S(2)}) collective-permute-start(bf16[2,7,4,1152]{3,2,1,0:T(4,128)(2,1)} %get-tuple-element.15), channel_id=1, source_target_pairs={{0,8},{8,16},{16,24},{1,9},{9,17},{17,25},{2,10},{10,18},{18,26},{... | collective-permute-start | bytes 387080 | tf_op jit(solution)/shard_map/ppermute | solution.py:25
  7.7 11.2 %collective-permute-start.1 = (bf16[2,7,4,1152]{3,2,1,0:T(4,128)(2,1)}, bf16[2,7,4,1152]{3,2,1,0:T(4,128)(2,1)S(1)}, u32[]{:S(2)}, u32[]{:S(2)}) collective-permute-start(bf16[2,7,4,1152]{3,2,1,0:T(4,128)(2,1)} %get-tuple-element.17), channel_id=1, source_target_pairs={{8,0},{16,8},{24,16},{9,1},{17,9},{25,17},{10,2},{18,10},{26,18},{... | collective-permute-start | bytes 387080 | tf_op jit(solution)/shard_map/ppermute | solution.py:25
  11.3 29.5 %collective-permute-start.7 = (bf16[7,128,1024]{2,1,0:T(8,128)(2,1)}, bf16[7,128,1024]{2,1,0:T(8,128)(2,1)}, u32[]{:S(2)}, u32[]{:S(2)}) collective-permute-start(bf16[7,128,1024]{2,1,0:T(8,128)(2,1)} %get-tuple-element.22), channel_id=1, source_target_pairs={{0,8},{8,16},{16,24},{1,9},{9,17},{17,25},{2,10},{10,18},{18,26},{... | collective-permute-start | bytes 5505032 | tf_op jit(solution)/shard_map/ppermute | solution.py:25
  13.2 27.6 %collective-permute-start.8 = (bf16[7,128,1024]{2,1,0:T(8,128)(2,1)}, bf16[7,128,1024]{2,1,0:T(8,128)(2,1)}, u32[]{:S(2)}, u32[]{:S(2)}) collective-permute-start(bf16[7,128,1024]{2,1,0:T(8,128)(2,1)} %get-tuple-element.23), channel_id=1, source_target_pairs={{8,0},{16,8},{24,16},{9,1},{17,9},{25,17},{10,2},{18,10},{26,18},{... | collective-permute-start | bytes 5505032 | tf_op jit(solution)/shard_map/ppermute | solution.py:25
  19.0 4.0 %collective-permute-start.2 = (bf16[2,30,2,128]{3,2,1,0:T(2,128)(2,1)S(1)}, bf16[2,30,2,128]{3,2,1,0:T(2,128)(2,1)S(1)}, u32[]{:S(2)}, u32[]{:S(2)}) collective-permute-start(bf16[2,30,2,128]{3,2,1,0:T(2,128)(2,1)S(1)} %broadcast_select_fusion), channel_id=1, source_target_pairs={{0,1},{1,0},{2,3},{3,2},{4,5},{5,4},{6,7},{7,6},{8,9},{9,8},{10,11... | collective-permute-start | bytes 92168 | tf_op jit(solution)/shard_map/ppermute | solution.py:463
  20.8 9.9 %copy-start.7 = (s32[2,1]{0,1:T(1,128)S(1)}, s32[2,1]{0,1:T(1,128)}, u32[]{:S(2)}) copy-start(s32[2,1]{0,1:T(1,128)} %param.9) | copy-start | bytes 28
  23.8 11.1 %copy-start = (bf16[2,30,128,128]{3,2,1,0:T(8,128)(2,1)}, bf16[2,30,128,128]{3,2,1,0:T(8,128)(2,1)S(1)}, u32[]{:S(2)}) copy-start(bf16[2,30,128,128]{3,2,1,0:T(8,128)(2,1)S(1)} %fusion.5.refs_6_) | copy-start | bytes 5898244
  24.6 12.3 %collective-permute-start.6 = (bf16[2,30,2,1152]{3,2,1,0:T(2,128)(2,1)S(1)}, bf16[2,30,2,1152]{3,2,1,0:T(2,128)(2,1)S(1)}, u32[]{:S(2)}, u32[]{:S(2)}) collective-permute-start(bf16[2,30,2,1152]{3,2,1,0:T(2,128)(2,1)S(1)} %get-tuple-element.36), channel_id=1, source_target_pairs={{0,2},{2,4},{4,6},{1,3},{3,5},{5,7},{8,10},{10,12},{12,14},{9,11},... | collective-permute-start | bytes 829448 | tf_op jit(solution)/shard_map/ppermute | solution.py:25
  28.1 12.7 %collective-permute-start.5 = (bf16[2,30,2,1152]{3,2,1,0:T(2,128)(2,1)S(1)}, bf16[2,30,2,1152]{3,2,1,0:T(2,128)(2,1)S(1)}, u32[]{:S(2)}, u32[]{:S(2)}) collective-permute-start(bf16[2,30,2,1152]{3,2,1,0:T(2,128)(2,1)S(1)} %get-tuple-element.37), channel_id=1, source_target_pairs={{2,0},{4,2},{6,4},{3,1},{5,3},{7,5},{10,8},{12,10},{14,12},{11,9},... | collective-permute-start | bytes 829448 | tf_op jit(solution)/shard_map/ppermute | solution.py:25
  35.0 35.2 %collective-permute-start.3 = (bf16[7,128,1024]{2,1,0:T(8,128)(2,1)}, bf16[7,128,1024]{2,1,0:T(8,128)(2,1)S(1)}, u32[]{:S(2)}, u32[]{:S(2)}) collective-permute-start(bf16[7,128,1024]{2,1,0:T(8,128)(2,1)} %get-tuple-element.19), channel_id=1, source_target_pairs={{0,8},{8,16},{16,24},{1,9},{9,17},{17,25},{2,10},{10,18},{18,26},{... | collective-permute-start | bytes 5505032 | tf_op jit(solution)/shard_map/ppermute | solution.py:25
  36.9 3.9 %copy-start.5 = (bf16[2,30,2,1152]{3,2,1,0:T(2,128)(2,1)}, bf16[2,30,2,1152]{3,2,1,0:T(2,128)(2,1)S(1)}, u32[]{:S(2)}) copy-start(bf16[2,30,2,1152]{3,2,1,0:T(2,128)(2,1)S(1)} %collective-permute-done.6.refs_8_) | copy-start | bytes 829444
  36.9 33.3 %collective-permute-start.4 = (bf16[7,128,1024]{2,1,0:T(8,128)(2,1)}, bf16[7,128,1024]{2,1,0:T(8,128)(2,1)}, u32[]{:S(2)}, u32[]{:S(2)}) collective-permute-start(bf16[7,128,1024]{2,1,0:T(8,128)(2,1)} %get-tuple-element.20), channel_id=1, source_target_pairs={{8,0},{16,8},{24,16},{9,1},{17,9},{25,17},{10,2},{18,10},{26,18},{... | collective-permute-start | bytes 5505032 | tf_op jit(solution)/shard_map/ppermute | solution.py:25
  40.8 0.7 copy-start.6
  64.6 29.9 %collective-permute-start.9 = (bf16[128,256]{1,0:T(8,128)(2,1)}, bf16[128,256]{1,0:T(8,128)(2,1)S(1)}, u32[]{:S(2)}, u32[]{:S(2)}) collective-permute-start(bf16[128,256]{1,0:T(8,128)(2,1)} %get-tuple-element.27), channel_id=1, source_target_pairs={{0,7},{1,6},{2,5},{3,4},{4,3},{5,2},{6,1},{7,0},{8,15},{9,14},{10,... | collective-permute-start | bytes 196616 | tf_op jit(solution)/shard_map/ppermute | solution.py:492
  70.2 1.2 %copy-start.4 = (bf16[7,128,1024]{2,1,0:T(8,128)(2,1)}, bf16[7,128,1024]{2,1,0:T(8,128)(2,1)S(1)}, u32[]{:S(2)}) copy-start(bf16[7,128,1024]{2,1,0:T(8,128)(2,1)S(1)} %collective-permute-done.3.refs_3_) | copy-start | bytes 5505028

commit v10 on v9

--- a/solution.py
+++ b/solution.py
@@ -12,7 +12,7 @@
 REACH = SIDE // 2
 TILE = 128
 BLOCK = 16
-WINDOW = 32
+WINDOW = 16
 EDGE = 8
 GROUP = 4
 bf16 = jnp.bfloat16
@@ -50,10 +50,12 @@
     in_ids = jnp.arange(depth, dtype=jnp.int32)[None, :]
     step = in_ids - out_ids - (EDGE - REACH)
     hit = step[None, :, :, None] == jnp.arange(SIDE, dtype=jnp.int32)
-    table = jnp.sum(jnp.where(hit, smooth_kernel.T[:, None, None, :], 0.0), axis=3)
-    table = jnp.swapaxes(table.reshape(SIDE, WINDOW // BLOCK, BLOCK, depth), 0, 1)
+    steps = jnp.concatenate([smooth_kernel.T, jnp.zeros((1, SIDE), f32)], axis=0)
+    table = jnp.sum(jnp.where(hit, steps[:, None, None, :], 0.0), axis=3)
     high, low = split(table)
-    return jnp.concatenate([high, high, low], axis=3).reshape(SIDE * WINDOW, 3 * depth)
+    table = jnp.concatenate([high, high, low], axis=2)
+    table = table.reshape((SIDE + 1) // 2, 2, WINDOW, 3 * depth)
+    return jnp.concatenate([table[:, 0], table[:, 1]], axis=2).reshape(-1, 6 * depth)
 
 
 def iota(shape, dim):
@@ -63,7 +65,7 @@
 def slab_kernel(
     row_step, frame_step,
     spots_ref, taps_ref, w2_ref, low_ref, own_ref, high_ref, edge_ref, below_ref, above_ref,
-    out_ref, last_ref, w1, chi, clo, carry, outer, kept, flat,
+    out_ref, last_ref, w1, chi, clo, chi1, clo1, carry, outer, kept, flat,
 ):
     frame_count, tiles, row_count, _ = kept.shape
     near = taps_ref.shape[1]
@@ -77,11 +79,20 @@
         both = both.reshape(frame_count, 2, 8, block.shape[2])
         return both[:, 0] + both[:, 1]
 
-    def keep(above, below, tile, place):
-        value = jnp.concatenate([above, below], axis=1)
+    def keep_one(value, highs, lows, tile, place):
         high = value.astype(bf16)
-        chi[:, tile, place, :] = high
-        clo[:, tile, place, :] = (value - high.astype(f32)).astype(bf16)
+        highs[:, tile, place, :] = high
+        lows[:, tile, place, :] = (value - high.astype(f32)).astype(bf16)
+
+    def keep(value, tile, place):
+        keep_one(value, chi, clo, tile, place)
+
+    def keep_shifted(turned, after, tile, place):
+        last = iota(turned.shape, 2) == TILE - 1
+        keep_one(jnp.where(last, after, turned), chi1, clo1, tile, place)
+
+    def turn(value):
+        return pltpu.roll(value, TILE - 1, 2)
 
     @pl.when(at == 0)
     def _():
@@ -105,13 +116,31 @@
 
     @pl.when(at < steps_1)
     def _():
+        places = [
+            pl.ds(pl.multiple_of(at * row_step + q * BLOCK, BLOCK), BLOCK)
+            for q in range(row_step // BLOCK)
+        ]
+        turns = {}
+
         def keep_all(tile, parts):
             parts = [carry[:, tile]] + parts
-            for q in range(0, len(parts) - 1, 2):
-                place = pl.ds(pl.multiple_of(at * row_step + EDGE * q, BLOCK), BLOCK)
-                keep(parts[q], parts[q + 1], tile, place)
+            turns[tile] = []
+            for q, place in enumerate(places):
+                value = jnp.concatenate(parts[2 * q : 2 * q + 2], axis=1)
+                keep(value, tile, place)
+                turns[tile].append(turn(value))
             carry[:, tile] = parts[-1]
-
+            before = (tile - 1) % (tiles + 1)
+            if before in turns:
+                for one, after, place in zip(turns[before], turns[tile], places):
+                    keep_shifted(one, after, before, place)
+
+        both = filtered(
+            jnp.concatenate(
+                [edge_ref[0, :, h : h + EDGE] for h in range(0, row_step, EDGE)], axis=2
+            )
+        )
+        keep_all(tiles, [both[..., h * TILE : (h + 1) * TILE] for h in range(row_step // EDGE)])
         for tile in range(0, tiles, 2):
             group = range(tile, min(tile + 2, tiles))
             cols = slice(tile * TILE, (tile + len(group)) * TILE)
@@ -125,26 +154,28 @@
                 parts.append(filtered(block))
             for q, one in enumerate(group):
                 keep_all(one, [part[..., q * TILE : (q + 1) * TILE] for part in parts])
-        both = filtered(
-            jnp.concatenate(
-                [edge_ref[0, :, h : h + EDGE] for h in range(0, row_step, EDGE)], axis=2
-            )
-        )
-        parts = [both[..., h * TILE : (h + 1) * TILE] for h in range(row_step // EDGE)]
-        keep_all(tiles, parts)
+        for one, after, place in zip(turns[tiles - 1], turns[tiles], places):
+            keep_shifted(one, after, tiles - 1, place)
 
     @pl.when(at == steps_1 - 1)
     def _():
-        for tile in range(tiles + 1):
-            keep(carry[:, tile], outer[:, tile], tile, slice(row_count, row_count + BLOCK))
+        place = slice(row_count, row_count + BLOCK)
+        first = None
+        for tile in range(tiles, -1, -1):
+            value = jnp.concatenate([carry[:, tile], outer[:, tile]], axis=1)
+            keep(value, tile, place)
+            turned = turn(value)
+            if tile == tiles:
+                first = turned
+            else:
+                keep_shifted(turned, after, tile, place)
+            after = turned
+        keep_shifted(first, after, tiles, place)
 
     @pl.when((at >= steps_1) & (at < steps_1 + steps_2))
     def _():
         lane = iota((BLOCK, TILE), 1)
-        edge_of = [lane < 2, lane < 1, None, lane >= TILE - 1, lane >= TILE - 2]
-
         depth = WINDOW + 2 * EDGE
-        parts_of = range(WINDOW // BLOCK)
 
         def two_frames(k2, unused):
             for row in range(0, row_count, WINDOW):
@@ -154,18 +185,15 @@
                 def finish(f, tile):
                     k = k2 * 2 + f
                     frame = (at - steps_1) * frame_step + k
-                    for m in parts_of:
-                        total = turned[f, m, REACH, tile]
-                        for b in range(SIDE):
-                            if b != REACH:
-                                beside = (tile + (1 if b > REACH else -1)) % (tiles + 1)
-                                total = total + jnp.where(
-                                    edge_of[b], turned[f, m, b, beside], turned[f, m, b, tile]
-                                )
-                        value = total.astype(bf16)
-                        rows = slice(row + m * BLOCK, row + (m + 1) * BLOCK)
-                        out_ref[0, k, rows, tile * TILE : (tile + 1) * TILE] = value
-                        kept[frame, tile, rows, :] = value.astype(f32)
+                    before, beyond = (tile - 1) % (tiles + 1), (tile + 1) % (tiles + 1)
+                    left = jnp.where(lane < REACH, turned[f, 0, before], turned[f, 0, tile])
+                    right = jnp.where(
+                        lane >= TILE - REACH, turned[f, 2, beyond], turned[f, 2, tile]
+                    )
+                    value = (turned[f, 1, tile] + left + right).astype(bf16)
+                    rows = slice(row, row + BLOCK)
+                    out_ref[0, k, rows, tile * TILE : (tile + 1) * TILE] = value
+                    kept[frame, tile, rows, :] = value.astype(f32)
 
                 order = [(f, tile) for f in range(2) for tile in [tiles] + list(range(tiles))]
                 for p in range(0, len(order), GROUP):
@@ -173,24 +201,25 @@
                     stacks = []
                     for f, tile in pair:
                         frame = (at - steps_1) * frame_step + k2 * 2 + f
-                        high = chi[frame, tile, row : row + depth, :]
-                        low = clo[frame, tile, row : row + depth, :]
-                        stacks.append(jnp.concatenate([high, low, high], axis=0))
+                        stack = []
+                        for highs, lows in ((chi, clo), (chi1, clo1)):
+                            high = highs[frame, tile, row : row + depth, :]
+                            low = lows[frame, tile, row : row + depth, :]
+                            stack += [high, low, high]
+                        stacks.append(jnp.concatenate(stack, axis=0))
                     both = jnp.dot(
                         w2_ref[...], jnp.concatenate(stacks, axis=1), preferred_element_type=f32
                     )
                     for q, (f, tile) in enumerate(pair):
-                        for m in parts_of:
-                            for b in range(SIDE):
-                                at_row = (m * SIDE + b) * BLOCK
-                                part = both[at_row : at_row + BLOCK, q * TILE : (q + 1) * TILE]
-                                if b != REACH:
-                                    part = pltpu.roll(part, (REACH - b) % TILE, 1)
-                                turned[f, m, b, tile] = part
+                        for g in range((SIDE + 1) // 2):
+                            part = both[g * BLOCK : (g + 1) * BLOCK, q * TILE : (q + 1) * TILE]
+                            if g != 1:
+                                part = pltpu.roll(part, (REACH - 2 * g) % TILE, 1)
+                            turned[f, g, tile] = part
                     for f in range(2):
-                        while done[f] < tiles and (f, 0, 0, done[f]) in turned:
+                        while done[f] < tiles and (f, 0, done[f]) in turned:
                             after = min(done[f] + 1, tiles)
-                            if (f, 0, 0, after) not in turned:
+                            if (f, 0, after) not in turned:
                                 break
                             finish(f, done[f])
                             done[f] += 1
@@ -425,6 +454,8 @@
         ],
         scratch_shapes=[
             pltpu.VMEM((16 * frame_count, 8 * near), bf16),
+            pltpu.VMEM((frame_count, wide // TILE, tall, TILE), bf16),
+            pltpu.VMEM((frame_count, wide // TILE, tall, TILE), bf16),
             pltpu.VMEM((frame_count, wide // TILE, tall, TILE), bf16),
             pltpu.VMEM((frame_count, wide // TILE, tall, TILE), bf16),
             pltpu.VMEM((frame_count, wide // TILE, EDGE, TILE), f32),

time: 97.2 us -> 98.2 us (1.010)
  Pallas kernels: 54.8 us -> 55.8 us
    unnamed x18 -> x19, local copies, waits for them, and re-layouts: 3.05 us -> 3.14 us
where the time goes in v10:
time: 98.2 us; the launch traced here: 97.1 us
  Pallas kernels  55.8 us (57%)
  starting transfers between devices  28.9 us (29%)
  local copies, waits for them, and re-layouts  5.13 us (5%)
  matrix products  2.52 us (3%)
  waiting for transfers between devices  2.21 us (2%)
  other arithmetic  1.6 us (2%)
  between operations  1.01 us (1%)
    pallas_call x2, Pallas kernels, run_slab(): pl.pallas_call(body, grid=(steps_1 + steps_2 + 1,), in_specs=in_specs, ou...  47.1 us
    ppermute x8, starting transfers between devices, shifted(): return lax.ppermute(block, axis, route)  21.7 us
    ppermute x1, starting transfers between devices, shards(): lax.ppermute(second, ('row', 'col'), [(i, count - 1 - i) for i in range(c...  5.63 us
    pallas_call x1, Pallas kernels, cut(): pl.pallas_call(cut_kernel, in_specs=[anywhere], out_specs=[near] * 3 + [a...  5.08 us
    pallas_call x1, Pallas kernels, late_cut(): pl.pallas_call(late_kernel, in_specs=[anywhere], out_specs=[anywhere] * 2...  3.58 us
    unnamed x19, local copies, waits for them, and re-layouts  3.14 us
    ppermute x1, waiting for transfers between devices, shards(): sides = lax.ppermute(sides, 'col', [(0, 1), (1, 0)])  2.18 us
  transfers between devices with their start and end apart: 10, of which 1 were waited for; matrix products, arithmetic and copies ran while one was open for 6% of the time, Pallas kernels for 52%

profile of v10, /device:TPU:2, one launch (start us, length us, event | category | flops | bytes accessed | tf_op | source)
XLA Modules:
  0.0 97.1 jit_solution(8334128466699884724)
XLA Ops:
  0.6 0.0 copy-start.1
  0.6 0.0 copy-start.2
  0.7 0.0 copy-start.3
  0.7 5.1 %cut.1 = (bf16[2,16,4,1152]{3,2,1,0:T(4,128)(2,1)}, bf16[2,7,4,1152]{3,2,1,0:T(4,128)(2,1)}, bf16[2,7,4,1152]{3,2,1,0:T(4,128)(2,1)}, bf16[7,128,1024]{2,1,0:T(8,128)(2,1)}, bf16[7,128,1024]{2,1,0:T(8,128)(2,1)}) custom-call(bf16[2,16,128,1024]{3,2,1,0:T(8,128)(2,1)} %refs_4_.3), custom_call_target="tpu_custom_call" | custom-call | tf_op jit(solution)/shard_map/cut/pallas_call | solution.py:365
  5.8 1.9 %collective-permute-start = (bf16[2,7,4,1152]{3,2,1,0:T(4,128)(2,1)}, bf16[2,7,4,1152]{3,2,1,0:T(4,128)(2,1)S(1)}, u32[]{:S(2)}, u32[]{:S(2)}) collective-permute-start(bf16[2,7,4,1152]{3,2,1,0:T(4,128)(2,1)} %get-tuple-element.15), channel_id=1, source_target_pairs={{0,8},{8,16},{16,24},{1,9},{9,17},{17,25},{2,10},{10,18},{18,26},{... | collective-permute-start | bytes 387080 | tf_op jit(solution)/shard_map/ppermute | solution.py:25
  7.7 3.6 %collective-permute-start.1 = (bf16[2,7,4,1152]{3,2,1,0:T(4,128)(2,1)}, bf16[2,7,4,1152]{3,2,1,0:T(4,128)(2,1)S(1)}, u32[]{:S(2)}, u32[]{:S(2)}) collective-permute-start(bf16[2,7,4,1152]{3,2,1,0:T(4,128)(2,1)} %get-tuple-element.17), channel_id=1, source_target_pairs={{8,0},{16,8},{24,16},{9,1},{17,9},{25,17},{10,2},{18,10},{26,18},{... | collective-permute-start | bytes 387080 | tf_op jit(solution)/shard_map/ppermute | solution.py:25
  11.3 1.9 %collective-permute-start.7 = (bf16[7,128,1024]{2,1,0:T(8,128)(2,1)}, bf16[7,128,1024]{2,1,0:T(8,128)(2,1)}, u32[]{:S(2)}, u32[]{:S(2)}) collective-permute-start(bf16[7,128,1024]{2,1,0:T(8,128)(2,1)} %get-tuple-element.22), channel_id=1, source_target_pairs={{0,8},{8,16},{16,24},{1,9},{9,17},{17,25},{2,10},{10,18},{18,26},{... | collective-permute-start | bytes 5505032 | tf_op jit(solution)/shard_map/ppermute | solution.py:25
  13.3 3.6 %collective-permute-start.8 = (bf16[7,128,1024]{2,1,0:T(8,128)(2,1)}, bf16[7,128,1024]{2,1,0:T(8,128)(2,1)}, u32[]{:S(2)}, u32[]{:S(2)}) collective-permute-start(bf16[7,128,1024]{2,1,0:T(8,128)(2,1)} %get-tuple-element.23), channel_id=1, source_target_pairs={{8,0},{16,8},{24,16},{9,1},{17,9},{25,17},{10,2},{18,10},{26,18},{... | collective-permute-start | bytes 5505032 | tf_op jit(solution)/shard_map/ppermute | solution.py:25
  17.0 0.1 copy.33
  17.1 0.1 select_reduce_fusion
  17.2 0.1 pad_maximum_fusion
  17.4 0.2 select_reduce_fusion.2
  17.6 0.1 reduce-precision_convert_fusion.1
  17.7 0.7 pad_maximum_fusion.1.refs_2_
  18.4 0.0 collective-permute-done
  18.4 1.1 %constant_dynamic-update-slice_fusion.1 = bf16[2,30,4,1152]{3,2,1,0:T(4,128)(2,1)S(1)} fusion(bf16[2,30,4,1152]{3,2,1,0:T(4,128)(2,1)S(1)} %constant_dynamic-update-slice_fusion.2, bf16[2,16,4,1152]{3,2,1,0:T(4,128)(2,1)} %get-tuple-element.16), kind=kLoop, calls=%fused_computation.18 | loop fusion | bytes 589824
  19.5 0.0 collective-permute-done.1
  19.5 0.1 constant_dynamic-update-slice_fusion
  19.6 0.1 broadcast_select_fusion
  19.7 1.6 %collective-permute-start.2 = (bf16[2,30,2,128]{3,2,1,0:T(2,128)(2,1)S(1)}, bf16[2,30,2,128]{3,2,1,0:T(2,128)(2,1)S(1)}, u32[]{:S(2)}, u32[]{:S(2)}) collective-permute-start(bf16[2,30,2,128]{3,2,1,0:T(2,128)(2,1)S(1)} %broadcast_select_fusion), channel_id=1, source_target_pairs={{0,1},{1,0},{2,3},{3,2},{4,5},{5,4},{6,7},{7,6},{8,9},{9,8},{10,11... | collective-permute-start | bytes 92168 | tf_op jit(solution)/shard_map/ppermute | solution.py:494
  21.2 0.2 slice.61
  21.4 0.0 copy-start.7
  21.4 2.2 %collective-permute-done.2 = bf16[2,30,2,128]{3,2,1,0:T(2,128)(2,1)S(1)} collective-permute-done((bf16[2,30,2,128]{3,2,1,0:T(2,128)(2,1)S(1)}, bf16[2,30,2,128]{3,2,1,0:T(2,128)(2,1)S(1)}, u32[]{:S(2)}, u32[]{:S(2)}) %collective-permute-start.2) | collective-permute-done | bytes 30752 | tf_op jit(solution)/shard_map/ppermute | solution.py:494
  23.6 0.9 fusion.5.refs_6_
  24.5 0.1 fusion.8
  24.6 0.3 maximum_maximum_fusion
  24.9 0.4 fusion.9
  25.3 3.5 %collective-permute-start.6 = (bf16[2,30,2,1152]{3,2,1,0:T(2,128)(2,1)S(1)}, bf16[2,30,2,1152]{3,2,1,0:T(2,128)(2,1)S(1)}, u32[]{:S(2)}, u32[]{:S(2)}) collective-permute-start(bf16[2,30,2,1152]{3,2,1,0:T(2,128)(2,1)S(1)} %get-tuple-element.36), channel_id=1, source_target_pairs={{0,2},{2,4},{4,6},{1,3},{3,5},{5,7},{8,10},{10,12},{12,14},{9,11},... | collective-permute-start | bytes 829448 | tf_op jit(solution)/shard_map/ppermute | solution.py:25
  28.8 1.3 %collective-permute-start.5 = (bf16[2,30,2,1152]{3,2,1,0:T(2,128)(2,1)S(1)}, bf16[2,30,2,1152]{3,2,1,0:T(2,128)(2,1)S(1)}, u32[]{:S(2)}, u32[]{:S(2)}) collective-permute-start(bf16[2,30,2,1152]{3,2,1,0:T(2,128)(2,1)S(1)} %get-tuple-element.37), channel_id=1, source_target_pairs={{2,0},{4,2},{6,4},{3,1},{5,3},{7,5},{10,8},{12,10},{14,12},{11,9},... | collective-permute-start | bytes 829448 | tf_op jit(solution)/shard_map/ppermute | solution.py:25
  30.1 0.6 copy.30
  30.7 0.1 stack_broadcast_in_dim.2
  30.8 0.6 slice_bitcast_fusion
  31.4 3.6 %late_cut.1 = (bf16[7,128,1024]{2,1,0:T(8,128)(2,1)}, bf16[7,128,1024]{2,1,0:T(8,128)(2,1)}) custom-call(bf16[2,16,128,1024]{3,2,1,0:T(8,128)(2,1)} %refs_4_.3), custom_call_target="tpu_custom_call" | custom-call | bytes 9000000 | tf_op jit(solution)/shard_map/late_cut/pallas_call | solution.py:387
  35.0 1.9 %collective-permute-start.3 = (bf16[7,128,1024]{2,1,0:T(8,128)(2,1)}, bf16[7,128,1024]{2,1,0:T(8,128)(2,1)S(1)}, u32[]{:S(2)}, u32[]{:S(2)}) collective-permute-start(bf16[7,128,1024]{2,1,0:T(8,128)(2,1)} %get-tuple-element.19), channel_id=1, source_target_pairs={{0,8},{8,16},{16,24},{1,9},{9,17},{17,25},{2,10},{10,18},{18,26},{... | collective-permute-start | bytes 5505032 | tf_op jit(solution)/shard_map/ppermute | solution.py:25
  36.9 0.0 collective-permute-done.6.refs_8_
  36.9 3.8 %collective-permute-start.4 = (bf16[7,128,1024]{2,1,0:T(8,128)(2,1)}, bf16[7,128,1024]{2,1,0:T(8,128)(2,1)}, u32[]{:S(2)}, u32[]{:S(2)}) collective-permute-start(bf16[7,128,1024]{2,1,0:T(8,128)(2,1)} %get-tuple-element.20), channel_id=1, source_target_pairs={{8,0},{16,8},{24,16},{9,1},{17,9},{25,17},{10,2},{18,10},{26,18},{... | collective-permute-start | bytes 5505032 | tf_op jit(solution)/shard_map/ppermute | solution.py:25
  40.8 0.0 collective-permute-done.5.refs_7_
  40.8 0.0 collective-permute-done.7.refs_3_
  40.8 0.0 collective-permute-done.8.refs_5_
  40.8 0.7 copy-done.6
  41.5 23.6 %slab_1.1 = (bf16[2,16,128,1024]{3,2,1,0:T(8,128)(2,1)}, bf16[128,256]{1,0:T(8,128)(2,1)}) custom-call(s32[6,128]{1,0:T(8,128)} %get-tuple-element.44.refs_0_, bf16[32,30]{1,0:T(8,128)(2,1)} %bitcast.34, bf16[48,192]{1,0:T(8,128)(2,1)} %pad_maximum_fusion.1.refs_2_, bf16[7,128,1024]{2,1,0:T(8,128)(2,1)} %collective-permute-done.7.refs_3_, ...), custom_call_target="tpu_custom_call" | custom-call | flops 20000000000 | bytes 16000000 | tf_op jit(solution)/shard_map/slab_1/pallas_call | solution.py:440
  65.1 5.6 %collective-permute-start.9 = (bf16[128,256]{1,0:T(8,128)(2,1)}, bf16[128,256]{1,0:T(8,128)(2,1)S(1)}, u32[]{:S(2)}, u32[]{:S(2)}) collective-permute-start(bf16[128,256]{1,0:T(8,128)(2,1)} %get-tuple-element.27), channel_id=1, source_target_pairs={{0,7},{1,6},{2,5},{3,4},{4,3},{5,2},{6,1},{7,0},{8,15},{9,14},{10,... | collective-permute-start | bytes 196616 | tf_op jit(solution)/shard_map/ppermute | solution.py:523
  70.7 0.0 collective-permute-done.3.refs_3_
  70.7 0.0 collective-permute-done.4.refs_5_
  70.7 1.2 %copy-done.4 = bf16[7,128,1024]{2,1,0:T(8,128)(2,1)} copy-done((bf16[7,128,1024]{2,1,0:T(8,128)(2,1)}, bf16[7,128,1024]{2,1,0:T(8,128)(2,1)S(1)}, u32[]{:S(2)}) %copy-start.4) | copy-done | bytes 1835032
  71.9 23.6 %slab_0.1 = (bf16[2,16,128,1024]{3,2,1,0:T(8,128)(2,1)}, bf16[128,256]{1,0:T(8,128)(2,1)}) custom-call(s32[6,128]{1,0:T(8,128)} %get-tuple-element.45.refs_0_, bf16[32,30]{1,0:T(8,128)(2,1)} %bitcast.35, bf16[48,192]{1,0:T(8,128)(2,1)} %pad_maximum_fusion.1.refs_2_, bf16[7,128,1024]{2,1,0:T(8,128)(2,1)} %copy-done.4, ...), custom_call_target="tpu_custom_call", output_to_operand_aliasing={{0}: (9, {})} | custom-call | flops 20000000000 | bytes 16000000 | tf_op jit(solution)/shard_map/slab_0/pallas_call | solution.py:440
  95.5 0.0 collective-permute-done.9
  95.5 1.6 %convolution_multiply_fusion = f32[128,128]{1,0:T(8,128)} fusion(bf16[128,256]{1,0:T(8,128)(2,1)} %get-tuple-element.26, bf16[128,256]{1,0:T(8,128)(2,1)S(1)} %collective-permute-done.9), kind=kOutput, calls=%fused_computation | convolution fusion | flops 8404992 | bytes 196608 | tf_op jit(solution)/shard_map/dot_general | solution.py:526
  (24 shorter events, 0.2 us)
Async XLA Ops:
  0.6 16.3 %copy-start.1 = (f32[5,5]{1,0:T(8,128)S(1)}, f32[5,5]{1,0:T(8,128)}, u32[]{:S(2)}) copy-start(f32[5,5]{1,0:T(8,128)} %param.7) | copy-start | bytes 304
  0.6 16.7 %copy-start.2 = (s32[2,3,128]{2,0,1:T(2,128)S(1)}, s32[2,3,128]{2,0,1:T(2,128)}, u32[]{:S(2)}) copy-start(s32[2,3,128]{2,0,1:T(2,128)} %param.8) | copy-start | bytes 9220
  0.7 16.7 %copy-start.3 = (f32[15]{0:T(128)S(1)}, f32[15]{0:T(128)}, u32[]{:S(2)}) copy-start(f32[15]{0:T(128)} %param.6) | copy-start | bytes 184
  5.8 12.6 %collective-permute-start = (bf16[2,7,4,1152]{3,2,1,0:T(4,128)(2,1)}, bf16[2,7,4,1152]{3,2,1,0:T(4,128)(2,1)S(1)}, u32[]{:S(2)}, u32[]{:S(2)}) collective-permute-start(bf16[2,7,4,1152]{3,2,1,0:T(4,128)(2,1)} %get-tuple-element.15), channel_id=1, source_target_pairs={{0,8},{8,16},{16,24},{1,9},{9,17},{17,25},{2,10},{10,18},{18,26},{... | collective-permute-start | bytes 387080 | tf_op jit(solution)/shard_map/ppermute | solution.py:25
  7.7 11.8 %collective-permute-start.1 = (bf16[2,7,4,1152]{3,2,1,0:T(4,128)(2,1)}, bf16[2,7,4,1152]{3,2,1,0:T(4,128)(2,1)S(1)}, u32[]{:S(2)}, u32[]{:S(2)}) collective-permute-start(bf16[2,7,4,1152]{3,2,1,0:T(4,128)(2,1)} %get-tuple-element.17), channel_id=1, source_target_pairs={{8,0},{16,8},{24,16},{9,1},{17,9},{25,17},{10,2},{18,10},{26,18},{... | collective-permute-start | bytes 387080 | tf_op jit(solution)/shard_map/ppermute | solution.py:25
  11.3 29.5 %collective-permute-start.7 = (bf16[7,128,1024]{2,1,0:T(8,128)(2,1)}, bf16[7,128,1024]{2,1,0:T(8,128)(2,1)}, u32[]{:S(2)}, u32[]{:S(2)}) collective-permute-start(bf16[7,128,1024]{2,1,0:T(8,128)(2,1)} %get-tuple-element.22), channel_id=1, source_target_pairs={{0,8},{8,16},{16,24},{1,9},{9,17},{17,25},{2,10},{10,18},{18,26},{... | collective-permute-start | bytes 5505032 | tf_op jit(solution)/shard_map/ppermute | solution.py:25
  13.3 27.6 %collective-permute-start.8 = (bf16[7,128,1024]{2,1,0:T(8,128)(2,1)}, bf16[7,128,1024]{2,1,0:T(8,128)(2,1)}, u32[]{:S(2)}, u32[]{:S(2)}) collective-permute-start(bf16[7,128,1024]{2,1,0:T(8,128)(2,1)} %get-tuple-element.23), channel_id=1, source_target_pairs={{8,0},{16,8},{24,16},{9,1},{17,9},{25,17},{10,2},{18,10},{26,18},{... | collective-permute-start | bytes 5505032 | tf_op jit(solution)/shard_map/ppermute | solution.py:25
  19.7 4.0 %collective-permute-start.2 = (bf16[2,30,2,128]{3,2,1,0:T(2,128)(2,1)S(1)}, bf16[2,30,2,128]{3,2,1,0:T(2,128)(2,1)S(1)}, u32[]{:S(2)}, u32[]{:S(2)}) collective-permute-start(bf16[2,30,2,128]{3,2,1,0:T(2,128)(2,1)S(1)} %broadcast_select_fusion), channel_id=1, source_target_pairs={{0,1},{1,0},{2,3},{3,2},{4,5},{5,4},{6,7},{7,6},{8,9},{9,8},{10,11... | collective-permute-start | bytes 92168 | tf_op jit(solution)/shard_map/ppermute | solution.py:494
  21.4 9.3 %copy-start.7 = (s32[2,1]{0,1:T(1,128)S(1)}, s32[2,1]{0,1:T(1,128)}, u32[]{:S(2)}) copy-start(s32[2,1]{0,1:T(1,128)} %param.9) | copy-start | bytes 28
  24.5 10.5 %copy-start = (bf16[2,30,128,128]{3,2,1,0:T(8,128)(2,1)}, bf16[2,30,128,128]{3,2,1,0:T(8,128)(2,1)S(1)}, u32[]{:S(2)}) copy-start(bf16[2,30,128,128]{3,2,1,0:T(8,128)(2,1)S(1)} %fusion.5.refs_6_) | copy-start | bytes 5898244
  25.3 11.7 %collective-permute-start.6 = (bf16[2,30,2,1152]{3,2,1,0:T(2,128)(2,1)S(1)}, bf16[2,30,2,1152]{3,2,1,0:T(2,128)(2,1)S(1)}, u32[]{:S(2)}, u32[]{:S(2)}) collective-permute-start(bf16[2,30,2,1152]{3,2,1,0:T(2,128)(2,1)S(1)} %get-tuple-element.36), channel_id=1, source_target_pairs={{0,2},{2,4},{4,6},{1,3},{3,5},{5,7},{8,10},{10,12},{12,14},{9,11},... | collective-permute-start | bytes 829448 | tf_op jit(solution)/shard_map/ppermute | solution.py:25
  28.8 12.0 %collective-permute-start.5 = (bf16[2,30,2,1152]{3,2,1,0:T(2,128)(2,1)S(1)}, bf16[2,30,2,1152]{3,2,1,0:T(2,128)(2,1)S(1)}, u32[]{:S(2)}, u32[]{:S(2)}) collective-permute-start(bf16[2,30,2,1152]{3,2,1,0:T(2,128)(2,1)S(1)} %get-tuple-element.37), channel_id=1, source_target_pairs={{2,0},{4,2},{6,4},{3,1},{5,3},{7,5},{10,8},{12,10},{14,12},{11,9},... | collective-permute-start | bytes 829448 | tf_op jit(solution)/shard_map/ppermute | solution.py:25
  35.0 35.7 %collective-permute-start.3 = (bf16[7,128,1024]{2,1,0:T(8,128)(2,1)}, bf16[7,128,1024]{2,1,0:T(8,128)(2,1)S(1)}, u32[]{:S(2)}, u32[]{:S(2)}) collective-permute-start(bf16[7,128,1024]{2,1,0:T(8,128)(2,1)} %get-tuple-element.19), channel_id=1, source_target_pairs={{0,8},{8,16},{16,24},{1,9},{9,17},{17,25},{2,10},{10,18},{18,26},{... | collective-permute-start | bytes 5505032 | tf_op jit(solution)/shard_map/ppermute | solution.py:25
  36.9 3.9 %copy-start.5 = (bf16[2,30,2,1152]{3,2,1,0:T(2,128)(2,1)}, bf16[2,30,2,1152]{3,2,1,0:T(2,128)(2,1)S(1)}, u32[]{:S(2)}) copy-start(bf16[2,30,2,1152]{3,2,1,0:T(2,128)(2,1)S(1)} %collective-permute-done.6.refs_8_) | copy-start | bytes 829444
  36.9 33.8 %collective-permute-start.4 = (bf16[7,128,1024]{2,1,0:T(8,128)(2,1)}, bf16[7,128,1024]{2,1,0:T(8,128)(2,1)}, u32[]{:S(2)}, u32[]{:S(2)}) collective-permute-start(bf16[7,128,1024]{2,1,0:T(8,128)(2,1)} %get-tuple-element.20), channel_id=1, source_target_pairs={{8,0},{16,8},{24,16},{9,1},{17,9},{25,17},{10,2},{18,10},{26,18},{... | collective-permute-start | bytes 5505032 | tf_op jit(solution)/shard_map/ppermute | solution.py:25
  40.8 0.7 copy-start.6
  65.1 30.4 %collective-permute-start.9 = (bf16[128,256]{1,0:T(8,128)(2,1)}, bf16[128,256]{1,0:T(8,128)(2,1)S(1)}, u32[]{:S(2)}, u32[]{:S(2)}) collective-permute-start(bf16[128,256]{1,0:T(8,128)(2,1)} %get-tuple-element.27), channel_id=1, source_target_pairs={{0,7},{1,6},{2,5},{3,4},{4,3},{5,2},{6,1},{7,0},{8,15},{9,14},{10,... | collective-permute-start | bytes 196616 | tf_op jit(solution)/shard_map/ppermute | solution.py:523
  70.7 1.2 %copy-start.4 = (bf16[7,128,1024]{2,1,0:T(8,128)(2,1)}, bf16[7,128,1024]{2,1,0:T(8,128)(2,1)S(1)}, u32[]{:S(2)}) copy-start(bf16[7,128,1024]{2,1,0:T(8,128)(2,1)S(1)} %collective-permute-done.3.refs_3_) | copy-start | bytes 5505028

commit v11 on v9

--- a/solution.py
+++ b/solution.py
@@ -63,7 +63,7 @@
 def slab_kernel(
     row_step, frame_step,
     spots_ref, taps_ref, w2_ref, low_ref, own_ref, high_ref, edge_ref, below_ref, above_ref,
-    out_ref, last_ref, w1, chi, clo, carry, outer, kept, flat,
+    out_ref, last_ref, w1, chi, clo, carry, outer, kept, flat, offsets, placed,
 ):
     frame_count, tiles, row_count, _ = kept.shape
     near = taps_ref.shape[1]
@@ -201,33 +201,46 @@
     @pl.when(at == steps_1 + steps_2)
     def _():
         slot_count = flat.shape[0] // PATCH
-
         lane = iota((PATCH, TILE), 1)
 
-        def some(i8, unused):
+        def some(i16, unused):
             for j in range(16):
-                i = i8 * 16 + j
+                i = i16 * 16 + j
                 frame, row, tile = spots_ref[0, i], spots_ref[1, i], spots_ref[2, i]
-                beside, turn = spots_ref[3, i], spots_ref[4, i]
+                beside, offset = spots_ref[3, i], spots_ref[4, i]
                 here = kept[frame, tile, pl.ds(row, PATCH), :]
                 there = kept[frame, beside, pl.ds(row, PATCH), :]
-                shift = turn & (TILE - 1)
-                here, there = pltpu.roll(here, shift, 1), pltpu.roll(there, shift, 1)
-                part = jnp.where(lane < turn, here, there)
-                flat[pl.ds(pl.multiple_of(i * PATCH, PATCH), PATCH), :] = part.astype(bf16)
+                place = pl.ds(pl.multiple_of(i * PATCH, PATCH), PATCH)
+                flat[place, :] = jnp.where(lane >= offset, here, there)
+                offsets[place, :] = jnp.full((PATCH, TILE), offset, jnp.int32)
             return unused
 
         lax.fori_loop(0, slot_count // 16, some, 0)
-        low_bits = PATCH - 1
-        bits = low_bits.bit_length()
-        shape = (TILE, PATCH * PATCH)
-        repeat = (iota(shape, 1) & low_bits == iota(shape, 0)).astype(bf16)
-        rows = jnp.dot(flat[...], repeat, preferred_element_type=f32)
-        mine = iota(rows.shape, 1) >> bits == iota(rows.shape, 0) & low_bits
-        rows = jnp.where(mine, rows, 0.0).astype(bf16)
-        shape = (slot_count, rows.shape[0])
-        owner = (iota(shape, 1) >> bits == iota(shape, 0)).astype(bf16)
-        values = jnp.dot(owner, rows, preferred_element_type=f32)
+        bits = PATCH.bit_length() - 1
+        per = TILE // PATCH
+        chunk = 16 * PATCH
+        group = iota((chunk, TILE), 0) & (per - 1)
+        mine = iota((chunk, TILE), 1) >> bits == group
+
+        def place_rows(n, unused):
+            place = pl.ds(pl.multiple_of(n * chunk, chunk), chunk)
+            rows = flat[place, :]
+            turn = ((group << bits) - offsets[place, :]) & (TILE - 1)
+            for bit in range(TILE.bit_length() - 1):
+                rows = jnp.where(
+                    (turn & (1 << bit)) != 0, pltpu.roll(rows, 1 << bit, 1), rows
+                )
+            placed[place, :] = jnp.where(mine, rows, 0.0).astype(bf16)
+            return unused
+
+        lax.fori_loop(0, slot_count * PATCH // chunk, place_rows, 0)
+        shape = (slot_count, slot_count * PATCH)
+        source = iota(shape, 1) >> (per.bit_length() - 1)
+        halves = []
+        for half in range(PATCH // per):
+            owner = (source == iota(shape, 0) * (PATCH // per) + half).astype(bf16)
+            halves.append(jnp.dot(owner, placed[...], preferred_element_type=f32))
+        values = jnp.concatenate(halves, axis=1)
         mean = jnp.sum(values, axis=1, keepdims=True) / (PATCH * PATCH)
         centered = values - mean
         spread = jnp.sum(centered * centered, axis=1, keepdims=True) / (PATCH * PATCH)
@@ -430,6 +443,8 @@
             pltpu.VMEM((frame_count, wide // TILE, EDGE, TILE), f32),
             pltpu.VMEM((frame_count, wide // TILE, EDGE, TILE), f32),
             pltpu.VMEM((frame_count, col_count // TILE, row_count, TILE), f32),
+            pltpu.VMEM((slot_count * PATCH, TILE), f32),
+            pltpu.VMEM((slot_count * PATCH, TILE), jnp.int32),
             pltpu.VMEM((slot_count * PATCH, TILE), bf16),
         ],
         input_output_aliases=aliases,
@@ -485,7 +500,7 @@
     tile = col // TILE
     beside = jnp.minimum(tile + 1, col_count // TILE - 1)
     live = jnp.broadcast_to(counts, frame.shape)
-    local = jnp.stack([frame, row, tile, beside, TILE - col % TILE, live], axis=1)
+    local = jnp.stack([frame, row, tile, beside, col % TILE, live], axis=1)
 
     smoothed, second = run_slab(1, None, local[1], taps, w2, low1, frames, high1, edge, below, above)
     count = lax.axis_size("row") * lax.axis_size("col")

time: 97.2 us -> 104 us (1.070)
  Pallas kernels: 54.8 us -> 61.3 us
    pallas_call x2, Pallas kernels: 46.2 us -> 52.7 us  [run_slab(): pl.pallas_call(body, grid=(steps_1 + steps_2 + 1,), in_specs=in_specs, ou...]
  transfers between devices with their start and end apart: 10 -> 10, of which waited for: 1 -> 1; matrix products, arithmetic and copies ran while one was open for 6% -> 6% of each run, Pallas kernels for 52% -> 55%
where the time goes in v11:
time: 104 us; the launch traced here: 103 us
  Pallas kernels  61.3 us (59%)
  starting transfers between devices  28.9 us (28%)
  local copies, waits for them, and re-layouts  5.77 us (6%)
  matrix products  2.52 us (2%)
  waiting for transfers between devices  2.21 us (2%)
    pallas_call x2, Pallas kernels, run_slab(): pl.pallas_call(body, grid=(steps_1 + steps_2 + 1,), in_specs=in_specs, ou...  52.7 us
    ppermute x8, starting transfers between devices, shifted(): return lax.ppermute(block, axis, route)  21.7 us
    ppermute x1, starting transfers between devices, shards(): lax.ppermute(second, ('row', 'col'), [(i, count - 1 - i) for i in range(c...  5.63 us
    pallas_call x1, Pallas kernels, cut(): pl.pallas_call(cut_kernel, in_specs=[anywhere], out_specs=[near] * 3 + [a...  5.07 us
    pallas_call x1, Pallas kernels, late_cut(): pl.pallas_call(late_kernel, in_specs=[anywhere], out_specs=[anywhere] * 2...  3.59 us
    unnamed x18, local copies, waits for them, and re-layouts  3.05 us
    ppermute x1, waiting for transfers between devices, shards(): sides = lax.ppermute(sides, 'col', [(0, 1), (1, 0)])  2.18 us
  transfers between devices with their start and end apart: 10, of which 1 were waited for; matrix products, arithmetic and copies ran while one was open for 6% of the time, Pallas kernels for 55%

profile of v11, /device:TPU:2, one launch (start us, length us, event | category | flops | bytes accessed | tf_op | source)
XLA Modules:
  0.0 102.7 jit_solution(14949809981924191740)
XLA Ops:
  0.6 0.0 copy-start.1
  0.6 0.0 copy-start.2
  0.7 0.0 copy-start.3
  0.7 5.1 %cut.1 = (bf16[2,16,4,1152]{3,2,1,0:T(4,128)(2,1)}, bf16[2,7,4,1152]{3,2,1,0:T(4,128)(2,1)}, bf16[2,7,4,1152]{3,2,1,0:T(4,128)(2,1)}, bf16[7,128,1024]{2,1,0:T(8,128)(2,1)}, bf16[7,128,1024]{2,1,0:T(8,128)(2,1)}) custom-call(bf16[2,16,128,1024]{3,2,1,0:T(8,128)(2,1)} %refs_4_.3), custom_call_target="tpu_custom_call" | custom-call | tf_op jit(solution)/shard_map/cut/pallas_call | solution.py:349
  5.7 1.9 %collective-permute-start = (bf16[2,7,4,1152]{3,2,1,0:T(4,128)(2,1)}, bf16[2,7,4,1152]{3,2,1,0:T(4,128)(2,1)S(1)}, u32[]{:S(2)}, u32[]{:S(2)}) collective-permute-start(bf16[2,7,4,1152]{3,2,1,0:T(4,128)(2,1)} %get-tuple-element.15), channel_id=1, source_target_pairs={{0,8},{8,16},{16,24},{1,9},{9,17},{17,25},{2,10},{10,18},{18,26},{... | collective-permute-start | bytes 387080 | tf_op jit(solution)/shard_map/ppermute | solution.py:25
  7.7 3.6 %collective-permute-start.1 = (bf16[2,7,4,1152]{3,2,1,0:T(4,128)(2,1)}, bf16[2,7,4,1152]{3,2,1,0:T(4,128)(2,1)S(1)}, u32[]{:S(2)}, u32[]{:S(2)}) collective-permute-start(bf16[2,7,4,1152]{3,2,1,0:T(4,128)(2,1)} %get-tuple-element.17), channel_id=1, source_target_pairs={{8,0},{16,8},{24,16},{9,1},{17,9},{25,17},{10,2},{18,10},{26,18},{... | collective-permute-start | bytes 387080 | tf_op jit(solution)/shard_map/ppermute | solution.py:25
  11.3 1.9 %collective-permute-start.7 = (bf16[7,128,1024]{2,1,0:T(8,128)(2,1)}, bf16[7,128,1024]{2,1,0:T(8,128)(2,1)}, u32[]{:S(2)}, u32[]{:S(2)}) collective-permute-start(bf16[7,128,1024]{2,1,0:T(8,128)(2,1)} %get-tuple-element.22), channel_id=1, source_target_pairs={{0,8},{8,16},{16,24},{1,9},{9,17},{17,25},{2,10},{10,18},{18,26},{... | collective-permute-start | bytes 5505032 | tf_op jit(solution)/shard_map/ppermute | solution.py:25
  13.2 3.6 %collective-permute-start.8 = (bf16[7,128,1024]{2,1,0:T(8,128)(2,1)}, bf16[7,128,1024]{2,1,0:T(8,128)(2,1)}, u32[]{:S(2)}, u32[]{:S(2)}) collective-permute-start(bf16[7,128,1024]{2,1,0:T(8,128)(2,1)} %get-tuple-element.23), channel_id=1, source_target_pairs={{8,0},{16,8},{24,16},{9,1},{17,9},{25,17},{10,2},{18,10},{26,18},{... | collective-permute-start | bytes 5505032 | tf_op jit(solution)/shard_map/ppermute | solution.py:25
  16.9 0.1 copy.33
  17.1 0.1 select_reduce_fusion
  17.3 0.2 select_reduce_fusion.2
  17.5 0.1 reduce-precision_convert_fusion.1
  17.6 0.1 pad_maximum_fusion
  17.7 0.0 collective-permute-done
  17.8 1.1 %constant_dynamic-update-slice_fusion.1 = bf16[2,30,4,1152]{3,2,1,0:T(4,128)(2,1)S(1)} fusion(bf16[2,30,4,1152]{3,2,1,0:T(4,128)(2,1)S(1)} %constant_dynamic-update-slice_fusion.2, bf16[2,16,4,1152]{3,2,1,0:T(4,128)(2,1)} %get-tuple-element.16), kind=kLoop, calls=%fused_computation.18 | loop fusion | bytes 589824
  18.8 0.0 collective-permute-done.1
  18.9 0.1 constant_dynamic-update-slice_fusion
  18.9 0.1 broadcast_select_fusion
  19.0 1.6 %collective-permute-start.2 = (bf16[2,30,2,128]{3,2,1,0:T(2,128)(2,1)S(1)}, bf16[2,30,2,128]{3,2,1,0:T(2,128)(2,1)S(1)}, u32[]{:S(2)}, u32[]{:S(2)}) collective-permute-start(bf16[2,30,2,128]{3,2,1,0:T(2,128)(2,1)S(1)} %broadcast_select_fusion), channel_id=1, source_target_pairs={{0,1},{1,0},{2,3},{3,2},{4,5},{5,4},{6,7},{7,6},{8,9},{9,8},{10,11... | collective-permute-start | bytes 92168 | tf_op jit(solution)/shard_map/ppermute | solution.py:478
  20.6 0.2 slice.51
  20.7 0.0 copy-start.7
  20.8 2.2 %collective-permute-done.2 = bf16[2,30,2,128]{3,2,1,0:T(2,128)(2,1)S(1)} collective-permute-done((bf16[2,30,2,128]{3,2,1,0:T(2,128)(2,1)S(1)}, bf16[2,30,2,128]{3,2,1,0:T(2,128)(2,1)S(1)}, u32[]{:S(2)}, u32[]{:S(2)}) %collective-permute-start.2) | collective-permute-done | bytes 30752 | tf_op jit(solution)/shard_map/ppermute | solution.py:478
  22.9 0.9 fusion.4.refs_6_
  23.8 0.1 fusion.7
  23.9 0.3 maximum_maximum_fusion
  24.2 0.4 fusion.8
  24.6 3.5 %collective-permute-start.6 = (bf16[2,30,2,1152]{3,2,1,0:T(2,128)(2,1)S(1)}, bf16[2,30,2,1152]{3,2,1,0:T(2,128)(2,1)S(1)}, u32[]{:S(2)}, u32[]{:S(2)}) collective-permute-start(bf16[2,30,2,1152]{3,2,1,0:T(2,128)(2,1)S(1)} %get-tuple-element.36), channel_id=1, source_target_pairs={{0,2},{2,4},{4,6},{1,3},{3,5},{5,7},{8,10},{10,12},{12,14},{9,11},... | collective-permute-start | bytes 829448 | tf_op jit(solution)/shard_map/ppermute | solution.py:25
  28.1 1.3 %collective-permute-start.5 = (bf16[2,30,2,1152]{3,2,1,0:T(2,128)(2,1)S(1)}, bf16[2,30,2,1152]{3,2,1,0:T(2,128)(2,1)S(1)}, u32[]{:S(2)}, u32[]{:S(2)}) collective-permute-start(bf16[2,30,2,1152]{3,2,1,0:T(2,128)(2,1)S(1)} %get-tuple-element.37), channel_id=1, source_target_pairs={{2,0},{4,2},{6,4},{3,1},{5,3},{7,5},{10,8},{12,10},{14,12},{11,9},... | collective-permute-start | bytes 829448 | tf_op jit(solution)/shard_map/ppermute | solution.py:25
  29.4 0.6 copy.32
  30.0 0.6 copy.34
  30.7 0.1 stack_broadcast_in_dim.2
  30.8 0.6 slice_bitcast_fusion
  31.4 3.6 %late_cut.1 = (bf16[7,128,1024]{2,1,0:T(8,128)(2,1)}, bf16[7,128,1024]{2,1,0:T(8,128)(2,1)}) custom-call(bf16[2,16,128,1024]{3,2,1,0:T(8,128)(2,1)} %refs_4_.3), custom_call_target="tpu_custom_call" | custom-call | bytes 9000000 | tf_op jit(solution)/shard_map/late_cut/pallas_call | solution.py:371
  35.0 1.9 %collective-permute-start.3 = (bf16[7,128,1024]{2,1,0:T(8,128)(2,1)}, bf16[7,128,1024]{2,1,0:T(8,128)(2,1)S(1)}, u32[]{:S(2)}, u32[]{:S(2)}) collective-permute-start(bf16[7,128,1024]{2,1,0:T(8,128)(2,1)} %get-tuple-element.19), channel_id=1, source_target_pairs={{0,8},{8,16},{16,24},{1,9},{9,17},{17,25},{2,10},{10,18},{18,26},{... | collective-permute-start | bytes 5505032 | tf_op jit(solution)/shard_map/ppermute | solution.py:25
  36.9 0.0 collective-permute-done.6.refs_8_
  36.9 3.8 %collective-permute-start.4 = (bf16[7,128,1024]{2,1,0:T(8,128)(2,1)}, bf16[7,128,1024]{2,1,0:T(8,128)(2,1)}, u32[]{:S(2)}, u32[]{:S(2)}) collective-permute-start(bf16[7,128,1024]{2,1,0:T(8,128)(2,1)} %get-tuple-element.20), channel_id=1, source_target_pairs={{8,0},{16,8},{24,16},{9,1},{17,9},{25,17},{10,2},{18,10},{26,18},{... | collective-permute-start | bytes 5505032 | tf_op jit(solution)/shard_map/ppermute | solution.py:25
  40.8 0.0 collective-permute-done.5.refs_7_
  40.8 0.0 collective-permute-done.7.refs_3_
  40.8 0.0 collective-permute-done.8.refs_5_
  40.8 0.7 copy-done.6
  41.5 26.3 %slab_1.1 = (bf16[2,16,128,1024]{3,2,1,0:T(8,128)(2,1)}, bf16[128,256]{1,0:T(8,128)(2,1)}) custom-call(s32[6,128]{1,0:T(8,128)} %get-tuple-element.42.refs_0_, bf16[32,30]{1,0:T(8,128)(2,1)} %bitcast.35, bf16[160,144]{1,0:T(8,128)(2,1)} %bitcast.31, bf16[7,128,1024]{2,1,0:T(8,128)(2,1)} %collective-permute-done.7.refs_3_, ...), custom_call_target="tpu_custom_call" | custom-call | flops 20000000000 | bytes 16000000 | tf_op jit(solution)/shard_map/slab_1/pallas_call | solution.py:424
  67.8 5.6 %collective-permute-start.9 = (bf16[128,256]{1,0:T(8,128)(2,1)}, bf16[128,256]{1,0:T(8,128)(2,1)S(1)}, u32[]{:S(2)}, u32[]{:S(2)}) collective-permute-start(bf16[128,256]{1,0:T(8,128)(2,1)} %get-tuple-element.27), channel_id=1, source_target_pairs={{0,7},{1,6},{2,5},{3,4},{4,3},{5,2},{6,1},{7,0},{8,15},{9,14},{10,... | collective-permute-start | bytes 196616 | tf_op jit(solution)/shard_map/ppermute | solution.py:507
  73.5 0.0 collective-permute-done.3.refs_3_
  73.5 0.0 collective-permute-done.4.refs_5_
  73.5 1.2 %copy-done.4 = bf16[7,128,1024]{2,1,0:T(8,128)(2,1)} copy-done((bf16[7,128,1024]{2,1,0:T(8,128)(2,1)}, bf16[7,128,1024]{2,1,0:T(8,128)(2,1)S(1)}, u32[]{:S(2)}) %copy-start.4) | copy-done | bytes 1835032
  74.7 26.3 %slab_0.1 = (bf16[2,16,128,1024]{3,2,1,0:T(8,128)(2,1)}, bf16[128,256]{1,0:T(8,128)(2,1)}) custom-call(s32[6,128]{1,0:T(8,128)} %get-tuple-element.43.refs_0_, bf16[32,30]{1,0:T(8,128)(2,1)} %bitcast.36, bf16[160,144]{1,0:T(8,128)(2,1)} %bitcast.32, bf16[7,128,1024]{2,1,0:T(8,128)(2,1)} %copy-done.4, ...), custom_call_target="tpu_custom_call", output_to_operand_aliasing={{0}: (9, {})} | custom-call | flops 20000000000 | bytes 16000000 | tf_op jit(solution)/shard_map/slab_0/pallas_call | solution.py:424
  101.0 0.0 collective-permute-done.9
  101.0 1.6 %convolution_multiply_fusion = f32[128,128]{1,0:T(8,128)} fusion(bf16[128,256]{1,0:T(8,128)(2,1)} %get-tuple-element.26, bf16[128,256]{1,0:T(8,128)(2,1)S(1)} %collective-permute-done.9), kind=kOutput, calls=%fused_computation | convolution fusion | flops 8404992 | bytes 196608 | tf_op jit(solution)/shard_map/dot_general | solution.py:510
  (22 shorter events, 0.2 us)
Async XLA Ops:
  0.6 16.3 %copy-start.1 = (f32[5,5]{1,0:T(8,128)S(1)}, f32[5,5]{1,0:T(8,128)}, u32[]{:S(2)}) copy-start(f32[5,5]{1,0:T(8,128)} %param.7) | copy-start | bytes 304
  0.6 16.6 %copy-start.2 = (s32[2,3,128]{2,0,1:T(2,128)S(1)}, s32[2,3,128]{2,0,1:T(2,128)}, u32[]{:S(2)}) copy-start(s32[2,3,128]{2,0,1:T(2,128)} %param.8) | copy-start | bytes 9220
  0.7 16.6 %copy-start.3 = (f32[15]{0:T(128)S(1)}, f32[15]{0:T(128)}, u32[]{:S(2)}) copy-start(f32[15]{0:T(128)} %param.6) | copy-start | bytes 184
  5.7 12.0 %collective-permute-start = (bf16[2,7,4,1152]{3,2,1,0:T(4,128)(2,1)}, bf16[2,7,4,1152]{3,2,1,0:T(4,128)(2,1)S(1)}, u32[]{:S(2)}, u32[]{:S(2)}) collective-permute-start(bf16[2,7,4,1152]{3,2,1,0:T(4,128)(2,1)} %get-tuple-element.15), channel_id=1, source_target_pairs={{0,8},{8,16},{16,24},{1,9},{9,17},{17,25},{2,10},{10,18},{18,26},{... | collective-permute-start | bytes 387080 | tf_op jit(solution)/shard_map/ppermute | solution.py:25
  7.7 11.2 %collective-permute-start.1 = (bf16[2,7,4,1152]{3,2,1,0:T(4,128)(2,1)}, bf16[2,7,4,1152]{3,2,1,0:T(4,128)(2,1)S(1)}, u32[]{:S(2)}, u32[]{:S(2)}) collective-permute-start(bf16[2,7,4,1152]{3,2,1,0:T(4,128)(2,1)} %get-tuple-element.17), channel_id=1, source_target_pairs={{8,0},{16,8},{24,16},{9,1},{17,9},{25,17},{10,2},{18,10},{26,18},{... | collective-permute-start | bytes 387080 | tf_op jit(solution)/shard_map/ppermute | solution.py:25
  11.3 29.5 %collective-permute-start.7 = (bf16[7,128,1024]{2,1,0:T(8,128)(2,1)}, bf16[7,128,1024]{2,1,0:T(8,128)(2,1)}, u32[]{:S(2)}, u32[]{:S(2)}) collective-permute-start(bf16[7,128,1024]{2,1,0:T(8,128)(2,1)} %get-tuple-element.22), channel_id=1, source_target_pairs={{0,8},{8,16},{16,24},{1,9},{9,17},{17,25},{2,10},{10,18},{18,26},{... | collective-permute-start | bytes 5505032 | tf_op jit(solution)/shard_map/ppermute | solution.py:25
  13.2 27.6 %collective-permute-start.8 = (bf16[7,128,1024]{2,1,0:T(8,128)(2,1)}, bf16[7,128,1024]{2,1,0:T(8,128)(2,1)}, u32[]{:S(2)}, u32[]{:S(2)}) collective-permute-start(bf16[7,128,1024]{2,1,0:T(8,128)(2,1)} %get-tuple-element.23), channel_id=1, source_target_pairs={{8,0},{16,8},{24,16},{9,1},{17,9},{25,17},{10,2},{18,10},{26,18},{... | collective-permute-start | bytes 5505032 | tf_op jit(solution)/shard_map/ppermute | solution.py:25
  19.0 4.0 %collective-permute-start.2 = (bf16[2,30,2,128]{3,2,1,0:T(2,128)(2,1)S(1)}, bf16[2,30,2,128]{3,2,1,0:T(2,128)(2,1)S(1)}, u32[]{:S(2)}, u32[]{:S(2)}) collective-permute-start(bf16[2,30,2,128]{3,2,1,0:T(2,128)(2,1)S(1)} %broadcast_select_fusion), channel_id=1, source_target_pairs={{0,1},{1,0},{2,3},{3,2},{4,5},{5,4},{6,7},{7,6},{8,9},{9,8},{10,11... | collective-permute-start | bytes 92168 | tf_op jit(solution)/shard_map/ppermute | solution.py:478
  20.7 9.9 %copy-start.7 = (s32[2,1]{0,1:T(1,128)S(1)}, s32[2,1]{0,1:T(1,128)}, u32[]{:S(2)}) copy-start(s32[2,1]{0,1:T(1,128)} %param.9) | copy-start | bytes 28
  23.8 11.1 %copy-start = (bf16[2,30,128,128]{3,2,1,0:T(8,128)(2,1)}, bf16[2,30,128,128]{3,2,1,0:T(8,128)(2,1)S(1)}, u32[]{:S(2)}) copy-start(bf16[2,30,128,128]{3,2,1,0:T(8,128)(2,1)S(1)} %fusion.4.refs_6_) | copy-start | bytes 5898244
  24.6 12.3 %collective-permute-start.6 = (bf16[2,30,2,1152]{3,2,1,0:T(2,128)(2,1)S(1)}, bf16[2,30,2,1152]{3,2,1,0:T(2,128)(2,1)S(1)}, u32[]{:S(2)}, u32[]{:S(2)}) collective-permute-start(bf16[2,30,2,1152]{3,2,1,0:T(2,128)(2,1)S(1)} %get-tuple-element.36), channel_id=1, source_target_pairs={{0,2},{2,4},{4,6},{1,3},{3,5},{5,7},{8,10},{10,12},{12,14},{9,11},... | collective-permute-start | bytes 829448 | tf_op jit(solution)/shard_map/ppermute | solution.py:25
  28.1 12.7 %collective-permute-start.5 = (bf16[2,30,2,1152]{3,2,1,0:T(2,128)(2,1)S(1)}, bf16[2,30,2,1152]{3,2,1,0:T(2,128)(2,1)S(1)}, u32[]{:S(2)}, u32[]{:S(2)}) collective-permute-start(bf16[2,30,2,1152]{3,2,1,0:T(2,128)(2,1)S(1)} %get-tuple-element.37), channel_id=1, source_target_pairs={{2,0},{4,2},{6,4},{3,1},{5,3},{7,5},{10,8},{12,10},{14,12},{11,9},... | collective-permute-start | bytes 829448 | tf_op jit(solution)/shard_map/ppermute | solution.py:25
  35.0 38.5 %collective-permute-start.3 = (bf16[7,128,1024]{2,1,0:T(8,128)(2,1)}, bf16[7,128,1024]{2,1,0:T(8,128)(2,1)S(1)}, u32[]{:S(2)}, u32[]{:S(2)}) collective-permute-start(bf16[7,128,1024]{2,1,0:T(8,128)(2,1)} %get-tuple-element.19), channel_id=1, source_target_pairs={{0,8},{8,16},{16,24},{1,9},{9,17},{17,25},{2,10},{10,18},{18,26},{... | collective-permute-start | bytes 5505032 | tf_op jit(solution)/shard_map/ppermute | solution.py:25
  36.9 3.9 %copy-start.5 = (bf16[2,30,2,1152]{3,2,1,0:T(2,128)(2,1)}, bf16[2,30,2,1152]{3,2,1,0:T(2,128)(2,1)S(1)}, u32[]{:S(2)}) copy-start(bf16[2,30,2,1152]{3,2,1,0:T(2,128)(2,1)S(1)} %collective-permute-done.6.refs_8_) | copy-start | bytes 829444
  36.9 36.5 %collective-permute-start.4 = (bf16[7,128,1024]{2,1,0:T(8,128)(2,1)}, bf16[7,128,1024]{2,1,0:T(8,128)(2,1)}, u32[]{:S(2)}, u32[]{:S(2)}) collective-permute-start(bf16[7,128,1024]{2,1,0:T(8,128)(2,1)} %get-tuple-element.20), channel_id=1, source_target_pairs={{8,0},{16,8},{24,16},{9,1},{17,9},{25,17},{10,2},{18,10},{26,18},{... | collective-permute-start | bytes 5505032 | tf_op jit(solution)/shard_map/ppermute | solution.py:25
  40.8 0.7 copy-start.6
  67.8 33.2 %collective-permute-start.9 = (bf16[128,256]{1,0:T(8,128)(2,1)}, bf16[128,256]{1,0:T(8,128)(2,1)S(1)}, u32[]{:S(2)}, u32[]{:S(2)}) collective-permute-start(bf16[128,256]{1,0:T(8,128)(2,1)} %get-tuple-element.27), channel_id=1, source_target_pairs={{0,7},{1,6},{2,5},{3,4},{4,3},{5,2},{6,1},{7,0},{8,15},{9,14},{10,... | collective-permute-start | bytes 196616 | tf_op jit(solution)/shard_map/ppermute | solution.py:507
  73.5 1.2 %copy-start.4 = (bf16[7,128,1024]{2,1,0:T(8,128)(2,1)}, bf16[7,128,1024]{2,1,0:T(8,128)(2,1)S(1)}, u32[]{:S(2)}) copy-start(bf16[7,128,1024]{2,1,0:T(8,128)(2,1)S(1)} %collective-permute-done.3.refs_3_) | copy-start | bytes 5505028

commit v12 on v9

--- a/solution.py
+++ b/solution.py
@@ -15,6 +15,7 @@
 WINDOW = 32
 EDGE = 8
 GROUP = 4
+BY_MATRIX = (0, 1, 3, 4)
 bf16 = jnp.bfloat16
 f32 = jnp.float32
 
@@ -25,13 +26,9 @@
     return lax.ppermute(block, axis, route)
 
 
-def split(values):
-    high = lax.reduce_precision(values, 8, 7)
-    return high.astype(bf16), (values - high).astype(bf16)
-
-
 def omega_matrix(omega_taps, first_frame, frame_count, frame_total):
-    out_ids = jnp.arange(frame_count, dtype=jnp.int32)[:, None]
+    row = jnp.arange(2 * frame_count, dtype=jnp.int32)[:, None]
+    out_ids = row // 2
     in_ids = jnp.arange(frame_count + 2 * HALF, dtype=jnp.int32)[None, :]
     source = first_frame + in_ids - HALF
     valid = (source >= 0) & (source < frame_total)
@@ -41,19 +38,24 @@
     norm = jnp.sum(weights, axis=1, keepdims=True)
     center = (in_ids - out_ids == HALF).astype(f32)
     matrix = center - weights / norm
-    return jnp.stack(split(matrix), axis=1).reshape(2 * frame_count, matrix.shape[1])
+    high = lax.reduce_precision(matrix, 8, 7)
+    return jnp.where(row % 2 == 0, high, matrix - high).astype(bf16)
 
 
 def smooth_matrix(smooth_kernel):
     depth = WINDOW + 2 * EDGE
-    out_ids = jnp.arange(WINDOW, dtype=jnp.int32)[:, None]
-    in_ids = jnp.arange(depth, dtype=jnp.int32)[None, :]
-    step = in_ids - out_ids - (EDGE - REACH)
-    hit = step[None, :, :, None] == jnp.arange(SIDE, dtype=jnp.int32)
-    table = jnp.sum(jnp.where(hit, smooth_kernel.T[:, None, None, :], 0.0), axis=3)
-    table = jnp.swapaxes(table.reshape(SIDE, WINDOW // BLOCK, BLOCK, depth), 0, 1)
-    high, low = split(table)
-    return jnp.concatenate([high, high, low], axis=3).reshape(SIDE * WINDOW, 3 * depth)
+    count = len(BY_MATRIX)
+    row = jnp.arange(count * WINDOW, dtype=jnp.int32)[:, None]
+    out_ids = row // (count * BLOCK) * BLOCK + row % BLOCK
+    step_id = row // BLOCK % count
+    col = jnp.arange(3 * depth, dtype=jnp.int32)[None, :]
+    step = col % depth - out_ids - (EDGE - REACH)
+    table = jnp.zeros((count * WINDOW, 3 * depth), f32)
+    for i, b in enumerate(BY_MATRIX):
+        for a in range(SIDE):
+            table = jnp.where((step_id == i) & (step == a), smooth_kernel[a, b], table)
+    high = lax.reduce_precision(table, 8, 7)
+    return jnp.where(col < 2 * depth, high, table - high).astype(bf16)
 
 
 def iota(shape, dim):
@@ -61,9 +63,9 @@
 
 
 def slab_kernel(
-    row_step, frame_step,
-    spots_ref, taps_ref, w2_ref, low_ref, own_ref, high_ref, edge_ref, below_ref, above_ref,
-    out_ref, last_ref, w1, chi, clo, carry, outer, kept, flat,
+    slab, row_step, frame_step,
+    spots_ref, kernel_ref, taps_ref, w2_ref, low_ref, own_ref, high_ref, edge_ref, below_ref, above_ref,
+    out_ref, last_ref, w1, chi, clo, full, carry, outer, kept, flat,
 ):
     frame_count, tiles, row_count, _ = kept.shape
     near = taps_ref.shape[1]
@@ -80,6 +82,7 @@
     def keep(above, below, tile, place):
         value = jnp.concatenate([above, below], axis=1)
         high = value.astype(bf16)
+        full[:, tile, place, :] = value
         chi[:, tile, place, :] = high
         clo[:, tile, place, :] = (value - high.astype(f32)).astype(bf16)
 
@@ -88,10 +91,10 @@
         count = 2 * frame_count
         tall = (iota((8 * count, count), 0) // 8 == iota((8 * count, count), 1)).astype(bf16)
         wide = (iota((near, 8 * near), 1) // 8 == iota((near, 8 * near), 0)).astype(bf16)
-        full = jnp.dot(tall, taps_ref[...], preferred_element_type=f32).astype(bf16)
-        full = jnp.dot(full, wide, preferred_element_type=f32)
-        same = iota(full.shape, 0) % 8 == iota(full.shape, 1) % 8
-        w1[...] = jnp.where(same, full, 0.0).astype(bf16)
+        matrix = jnp.dot(tall, taps_ref[...], preferred_element_type=f32).astype(bf16)
+        matrix = jnp.dot(matrix, wide, preferred_element_type=f32)
+        same = iota(matrix.shape, 0) & 7 == iota(matrix.shape, 1) & 7
+        w1[...] = jnp.where(same, matrix, 0.0).astype(bf16)
         for tile in range(0, tiles + 1, GROUP):
             pair = range(tile, min(tile + GROUP, tiles + 1))
             cols = slice(tile * TILE, (tile + len(pair)) * TILE)
@@ -155,13 +158,16 @@
                     k = k2 * 2 + f
                     frame = (at - steps_1) * frame_step + k
                     for m in parts_of:
-                        total = turned[f, m, REACH, tile]
-                        for b in range(SIDE):
-                            if b != REACH:
-                                beside = (tile + (1 if b > REACH else -1)) % (tiles + 1)
-                                total = total + jnp.where(
-                                    edge_of[b], turned[f, m, b, beside], turned[f, m, b, tile]
-                                )
+                        start = row + m * BLOCK + EDGE - REACH
+                        total = kernel_ref[0, REACH] * full[frame, tile, start : start + BLOCK, :]
+                        for a in range(1, SIDE):
+                            rows = slice(start + a, start + a + BLOCK)
+                            total = total + kernel_ref[a, REACH] * full[frame, tile, rows, :]
+                        for b in BY_MATRIX:
+                            beside = (tile + (1 if b > REACH else -1)) % (tiles + 1)
+                            total = total + jnp.where(
+                                edge_of[b], turned[f, m, b, beside], turned[f, m, b, tile]
+                            )
                         value = total.astype(bf16)
                         rows = slice(row + m * BLOCK, row + (m + 1) * BLOCK)
                         out_ref[0, k, rows, tile * TILE : (tile + 1) * TILE] = value
@@ -181,12 +187,10 @@
                     )
                     for q, (f, tile) in enumerate(pair):
                         for m in parts_of:
-                            for b in range(SIDE):
-                                at_row = (m * SIDE + b) * BLOCK
+                            for i, b in enumerate(BY_MATRIX):
+                                at_row = (m * len(BY_MATRIX) + i) * BLOCK
                                 part = both[at_row : at_row + BLOCK, q * TILE : (q + 1) * TILE]
-                                if b != REACH:
-                                    part = pltpu.roll(part, (REACH - b) % TILE, 1)
-                                turned[f, m, b, tile] = part
+                                turned[f, m, b, tile] = pltpu.roll(part, (REACH - b) % TILE, 1)
                     for f in range(2):
                         while done[f] < tiles and (f, 0, 0, done[f]) in turned:
                             after = min(done[f] + 1, tiles)
@@ -207,8 +211,8 @@
         def some(i8, unused):
             for j in range(16):
                 i = i8 * 16 + j
-                frame, row, tile = spots_ref[0, i], spots_ref[1, i], spots_ref[2, i]
-                beside, turn = spots_ref[3, i], spots_ref[4, i]
+                frame, row, tile = spots_ref[slab, 0, i], spots_ref[slab, 1, i], spots_ref[slab, 2, i]
+                beside, turn = spots_ref[slab, 3, i], spots_ref[slab, 4, i]
                 here = kept[frame, tile, pl.ds(row, PATCH), :]
                 there = kept[frame, beside, pl.ds(row, PATCH), :]
                 shift = turn & (TILE - 1)
@@ -232,7 +236,7 @@
         centered = values - mean
         spread = jnp.sum(centered * centered, axis=1, keepdims=True) / (PATCH * PATCH)
         normed = centered / jnp.sqrt(spread + 1e-05)
-        live = iota((slot_count, 1), 0) < spots_ref[5, 0]
+        live = iota((slot_count, 1), 0) < spots_ref[slab, 5, 0]
         last_ref[...] = jnp.where(live, normed, 0.0).astype(bf16)
 
 
@@ -370,9 +374,9 @@
     )(frames)
 
 
-def run_slab(slab, smoothed, spots, taps, w2, low, frames, high, edge, below, above):
+def run_slab(slab, smoothed, spots, kernel, taps, w2, low, frames, high, edge, below, above):
     _, frame_count, row_count, col_count = frames.shape
-    slot_count = spots.shape[1]
+    slot_count = spots.shape[2]
     row_step, frame_step = 32, 4
     steps_1 = row_count // row_step
     steps_2 = frame_count // frame_step
@@ -385,8 +389,9 @@
     def whole(array):
         return pl.BlockSpec(array.shape, lambda at: (0,) * array.ndim)
 
-    operands = [spots, taps, w2, low, frames, high, edge, below, above]
+    operands = [spots, kernel, taps, w2, low, frames, high, edge, below, above]
     in_specs = [
+        pl.BlockSpec(memory_space=pltpu.SMEM),
         pl.BlockSpec(memory_space=pltpu.SMEM),
         whole(taps),
         whole(w2),
@@ -405,7 +410,7 @@
     count = len(operands)
 
     def body(*refs):
-        slab_kernel(row_step, frame_step, *refs[:9], *refs[count:])
+        slab_kernel(slab, row_step, frame_step, *refs[:10], *refs[count:])
 
     tall = row_count + 2 * EDGE
     return pl.pallas_call(
@@ -427,6 +432,7 @@
             pltpu.VMEM((16 * frame_count, 8 * near), bf16),
             pltpu.VMEM((frame_count, wide // TILE, tall, TILE), bf16),
             pltpu.VMEM((frame_count, wide // TILE, tall, TILE), bf16),
+            pltpu.VMEM((frame_count, wide // TILE, tall, TILE), f32),
             pltpu.VMEM((frame_count, wide // TILE, EDGE, TILE), f32),
             pltpu.VMEM((frame_count, wide // TILE, EDGE, TILE), f32),
             pltpu.VMEM((frame_count, col_count // TILE, row_count, TILE), f32),
@@ -448,9 +454,8 @@
     first_col = lax.axis_index("col") * col_count
 
     rim, rim_low, rim_high, send_low1, send_high1 = cut(frames)
-    rim = jnp.concatenate(
-        [shifted(rim_low, "omega", 1), rim, shifted(rim_high, "omega", -1)], axis=1
-    )
+    rims = [shifted(rim_low, "omega", 1), rim, shifted(rim_high, "omega", -1)]
+    rim_cols = jnp.concatenate([part[..., col_count:] for part in rims], axis=1)
     low1 = shifted(send_low1, "omega", 1)
     high1 = shifted(send_high1, "omega", -1)
     lane = jnp.arange(TILE, dtype=jnp.int32)[None, :]
@@ -459,12 +464,12 @@
     before = (lane == TILE - REACH + step).astype(bf16)
     if lax.axis_size("col") == 2:
         first = lax.axis_index("col") == 0
-        sides = jnp.where(first, rim[:, :, REACH:, col_count:], rim[:, :, :REACH, col_count:])
+        sides = jnp.where(first, rim_cols[:, :, REACH:], rim_cols[:, :, :REACH])
         sides = lax.ppermute(sides, "col", [(0, 1), (1, 0)])
         place = jnp.where(first, after, before)
     else:
-        left = shifted(rim[:, :, REACH:, col_count:], "col", 1)
-        right = shifted(rim[:, :, :REACH, col_count:], "col", -1)
+        left = shifted(rim_cols[:, :, REACH:], "col", 1)
+        right = shifted(rim_cols[:, :, :REACH], "col", -1)
         sides = jnp.concatenate([right, left], axis=2)
         place = jnp.concatenate([after, before], axis=0)
     later, sides = lax.optimization_barrier((frames, sides))
@@ -473,7 +478,8 @@
     high0 = shifted(send_high0, "omega", -1)
     edge = jnp.einsum("sfkr,kc->sfrc", sides, place, preferred_element_type=bf16)
     ends = jnp.concatenate([edge[:, :, :REACH], edge[:, :, -REACH:]], axis=2)
-    line = jnp.concatenate([rim[..., :col_count], ends], axis=3)
+    rim_rows = jnp.concatenate([part[..., :col_count] for part in rims], axis=1)
+    line = jnp.concatenate([rim_rows, ends], axis=3)
     above = shifted(line[:, :, REACH:], "row", 1)
     below = shifted(line[:, :, :REACH], "row", -1)
 
@@ -487,10 +493,10 @@
     live = jnp.broadcast_to(counts, frame.shape)
     local = jnp.stack([frame, row, tile, beside, TILE - col % TILE, live], axis=1)
 
-    smoothed, second = run_slab(1, None, local[1], taps, w2, low1, frames, high1, edge, below, above)
+    smoothed, second = run_slab(1, None, local, smooth_kernel, taps, w2, low1, frames, high1, edge, below, above)
     count = lax.axis_size("row") * lax.axis_size("col")
     second = lax.ppermute(second, ("row", "col"), [(i, count - 1 - i) for i in range(count)])
-    smoothed, first = run_slab(0, smoothed, local[0], taps, w2, low0, frames, high0, edge, below, above)
+    smoothed, first = run_slab(0, smoothed, local, smooth_kernel, taps, w2, low0, frames, high0, edge, below, above)
     scores = (
         lax.dot_general(first, second, (((1,), (1,)), ((), ())), preferred_element_type=f32)
         / float(PATCH * PATCH)

time: 97.2 us -> 113 us (1.16)
  other arithmetic: 0.96 us -> 15.1 us
  Pallas kernels: 54.8 us -> 57.1 us
    convert_element_type x2, other arithmetic: 0.1 us -> 14.3 us  [the longest x1 13.6 us: smooth_matrix(): return jnp.where(col < 2 * depth, high, table - high).astype(bf16)]
    slice x1 -> x8, local copies, waits for them, and re-layouts: 0.17 us -> 3.17 us  [the longest x2 1.26 us: smooth_matrix(): table = jnp.where((step_id == i) & (step == a), smooth_kernel[a, b], table)]
    pallas_call x2, Pallas kernels: 46.2 us -> 48.5 us  [run_slab(): pl.pallas_call(body, grid=(steps_1 + steps_2 + 1,), in_specs=in_specs, ou...]
    unnamed x18 -> x16, local copies, waits for them, and re-layouts: 3.05 us -> 1.91 us
  transfers between devices with their start and end apart: 10 -> 10, of which waited for: 1 -> 1; matrix products, arithmetic and copies ran while one was open for 6% -> 18% of each run, Pallas kernels for 52% -> 46%
where the time goes in v12:
time: 113 us; the launch traced here: 112 us
  Pallas kernels  57.1 us (51%)
  starting transfers between devices  28.9 us (26%)
  other arithmetic  15.1 us (13%)
  local copies, waits for them, and re-layouts  6.2 us (5%)
  matrix products  2.51 us (2%)
  waiting for transfers between devices  1.23 us (1%)
    pallas_call x2, Pallas kernels, run_slab(): pl.pallas_call(body, grid=(steps_1 + steps_2 + 1,), in_specs=in_specs, ou...  48.5 us
    ppermute x8, starting transfers between devices, shifted(): return lax.ppermute(block, axis, route)  21.7 us
    convert_element_type x1, other arithmetic, smooth_matrix(): return jnp.where(col < 2 * depth, high, table - high).astype(bf16)  13.6 us
    ppermute x1, starting transfers between devices, shards(): lax.ppermute(second, ('row', 'col'), [(i, count - 1 - i) for i in range(c...  5.67 us
    pallas_call x1, Pallas kernels, cut(): pl.pallas_call(cut_kernel, in_specs=[anywhere], out_specs=[near] * 3 + [a...  5.07 us
    pallas_call x1, Pallas kernels, late_cut(): pl.pallas_call(late_kernel, in_specs=[anywhere], out_specs=[anywhere] * 2...  3.59 us
  transfers between devices with their start and end apart: 10, of which 1 were waited for; matrix products, arithmetic and copies ran while one was open for 18% of the time, Pallas kernels for 46%

profile of v12, /device:TPU:2, one launch (start us, length us, event | category | flops | bytes accessed | tf_op | source)
XLA Modules:
  0.0 112.1 jit_solution(16543804033497803254)
XLA Ops:
  0.6 0.0 copy-start.1
  0.7 5.1 %cut.1 = (bf16[2,16,4,1152]{3,2,1,0:T(4,128)(2,1)}, bf16[2,7,4,1152]{3,2,1,0:T(4,128)(2,1)}, bf16[2,7,4,1152]{3,2,1,0:T(4,128)(2,1)}, bf16[7,128,1024]{2,1,0:T(8,128)(2,1)}, bf16[7,128,1024]{2,1,0:T(8,128)(2,1)}) custom-call(bf16[2,16,128,1024]{3,2,1,0:T(8,128)(2,1)} %refs_5_.3), custom_call_target="tpu_custom_call" | custom-call | tf_op jit(solution)/shard_map/cut/pallas_call | solution.py:340
  5.7 1.9 %collective-permute-start = (bf16[2,7,4,1152]{3,2,1,0:T(4,128)(2,1)}, bf16[2,7,4,1152]{3,2,1,0:T(4,128)(2,1)S(1)}, u32[]{:S(2)}, u32[]{:S(2)}) collective-permute-start(bf16[2,7,4,1152]{3,2,1,0:T(4,128)(2,1)} %get-tuple-element.15), channel_id=1, source_target_pairs={{0,8},{8,16},{16,24},{1,9},{9,17},{17,25},{2,10},{10,18},{18,26},{... | collective-permute-start | bytes 387080 | tf_op jit(solution)/shard_map/ppermute | solution.py:26
  7.7 3.6 %collective-permute-start.1 = (bf16[2,7,4,1152]{3,2,1,0:T(4,128)(2,1)}, bf16[2,7,4,1152]{3,2,1,0:T(4,128)(2,1)S(1)}, u32[]{:S(2)}, u32[]{:S(2)}) collective-permute-start(bf16[2,7,4,1152]{3,2,1,0:T(4,128)(2,1)} %get-tuple-element.17), channel_id=1, source_target_pairs={{8,0},{16,8},{24,16},{9,1},{17,9},{25,17},{10,2},{18,10},{26,18},{... | collective-permute-start | bytes 387080 | tf_op jit(solution)/shard_map/ppermute | solution.py:26
  11.3 1.9 %collective-permute-start.7 = (bf16[7,128,1024]{2,1,0:T(8,128)(2,1)}, bf16[7,128,1024]{2,1,0:T(8,128)(2,1)}, u32[]{:S(2)}, u32[]{:S(2)}) collective-permute-start(bf16[7,128,1024]{2,1,0:T(8,128)(2,1)} %get-tuple-element.22), channel_id=1, source_target_pairs={{0,8},{8,16},{16,24},{1,9},{9,17},{17,25},{2,10},{10,18},{18,26},{... | collective-permute-start | bytes 5505032 | tf_op jit(solution)/shard_map/ppermute | solution.py:26
  13.2 3.6 %collective-permute-start.8 = (bf16[7,128,1024]{2,1,0:T(8,128)(2,1)}, bf16[7,128,1024]{2,1,0:T(8,128)(2,1)}, u32[]{:S(2)}, u32[]{:S(2)}) collective-permute-start(bf16[7,128,1024]{2,1,0:T(8,128)(2,1)} %get-tuple-element.23), channel_id=1, source_target_pairs={{8,0},{16,8},{24,16},{9,1},{17,9},{25,17},{10,2},{18,10},{26,18},{... | collective-permute-start | bytes 5505032 | tf_op jit(solution)/shard_map/ppermute | solution.py:26
  17.0 0.0 copy-done.2
  17.1 0.1 fusion.7
  17.1 0.0 copy-done.3
  17.1 0.2 select_reduce_fusion
  17.3 0.7 fusion.6.refs_2_
  18.0 0.8 slice.129
  18.8 0.7 fusion.20
  19.5 0.0 collective-permute-done
  19.6 0.0 collective-permute-done.1
  19.6 0.1 broadcast_select_fusion
  19.7 1.6 %collective-permute-start.2 = (bf16[2,30,2,128]{3,2,1,0:T(2,128)(2,1)S(1)}, bf16[2,30,2,128]{3,2,1,0:T(2,128)(2,1)S(1)}, u32[]{:S(2)}, u32[]{:S(2)}) collective-permute-start(bf16[2,30,2,128]{3,2,1,0:T(2,128)(2,1)S(1)} %broadcast_select_fusion), channel_id=1, source_target_pairs={{0,1},{1,0},{2,3},{3,2},{4,5},{5,4},{6,7},{7,6},{8,9},{9,8},{10,11... | collective-permute-start | bytes 92168 | tf_op jit(solution)/shard_map/ppermute | solution.py:468
  21.3 1.0 slice.134
  22.4 0.0 copy-start.7
  22.4 1.2 %collective-permute-done.2 = bf16[2,30,2,128]{3,2,1,0:T(2,128)(2,1)S(1)} collective-permute-done((bf16[2,30,2,128]{3,2,1,0:T(2,128)(2,1)S(1)}, bf16[2,30,2,128]{3,2,1,0:T(2,128)(2,1)S(1)}, u32[]{:S(2)}, u32[]{:S(2)}) %collective-permute-start.2) | collective-permute-done | bytes 30752 | tf_op jit(solution)/shard_map/ppermute | solution.py:468
  23.7 0.9 fusion.13.refs_7_
  24.5 0.0 copy-start
  24.6 0.1 fusion.18
  24.6 0.3 maximum_maximum_fusion
  24.9 0.4 fusion.19
  25.3 3.5 %collective-permute-start.6 = (bf16[2,30,2,1152]{3,2,1,0:T(2,128)(2,1)S(1)}, bf16[2,30,2,1152]{3,2,1,0:T(2,128)(2,1)S(1)}, u32[]{:S(2)}, u32[]{:S(2)}) collective-permute-start(bf16[2,30,2,1152]{3,2,1,0:T(2,128)(2,1)S(1)} %get-tuple-element.36), channel_id=1, source_target_pairs={{0,2},{2,4},{4,6},{1,3},{3,5},{5,7},{8,10},{10,12},{12,14},{9,11},... | collective-permute-start | bytes 829448 | tf_op jit(solution)/shard_map/ppermute | solution.py:26
  28.8 1.3 %collective-permute-start.5 = (bf16[2,30,2,1152]{3,2,1,0:T(2,128)(2,1)S(1)}, bf16[2,30,2,1152]{3,2,1,0:T(2,128)(2,1)S(1)}, u32[]{:S(2)}, u32[]{:S(2)}) collective-permute-start(bf16[2,30,2,1152]{3,2,1,0:T(2,128)(2,1)S(1)} %get-tuple-element.37), channel_id=1, source_target_pairs={{2,0},{4,2},{6,4},{3,1},{5,3},{7,5},{10,8},{12,10},{14,12},{11,9},... | collective-permute-start | bytes 829448 | tf_op jit(solution)/shard_map/ppermute | solution.py:26
  30.1 0.6 slice.109
  30.7 0.1 stack_broadcast_in_dim.2
  30.8 0.6 stack.2.refs_0_
  31.4 13.6 %fusion.refs_3_ = bf16[128,144]{1,0:T(8,128)(2,1)} fusion(f32[]{:T(128)} %bitcast.23, f32[]{:T(128)} %bitcast.22, f32[]{:T(128)} %bitcast.21, f32[]{:T(128)} %bitcast.20, f32[]{:T(128)} %bitcast.19, f32[]{:T(128)} %bitcast.18, f32[]{:T(128)} %bitcast.17, f32[]{:T(128)} %bitcast.16, f32[]{:T(128)} %bitcast.15, f32[]{:T(128)} %bitcast.14, f32[]{:T(128)} %bitcast.13, ...), kind=kLoop, calls=%fused_computation.6 | loop fusion | flops 940032 | bytes 38688 | tf_op jit(solution)/shard_map/convert_element_type | solution.py:58
  45.0 3.6 %late_cut.1 = (bf16[7,128,1024]{2,1,0:T(8,128)(2,1)}, bf16[7,128,1024]{2,1,0:T(8,128)(2,1)}) custom-call(bf16[2,16,128,1024]{3,2,1,0:T(8,128)(2,1)} %refs_5_.3), custom_call_target="tpu_custom_call" | custom-call | bytes 9000000 | tf_op jit(solution)/shard_map/late_cut/pallas_call | solution.py:362
  48.6 0.0 copy-done
  48.6 1.9 %collective-permute-start.3 = (bf16[7,128,1024]{2,1,0:T(8,128)(2,1)}, bf16[7,128,1024]{2,1,0:T(8,128)(2,1)S(1)}, u32[]{:S(2)}, u32[]{:S(2)}) collective-permute-start(bf16[7,128,1024]{2,1,0:T(8,128)(2,1)} %get-tuple-element.19), channel_id=1, source_target_pairs={{0,8},{8,16},{16,24},{1,9},{9,17},{17,25},{2,10},{10,18},{18,26},{... | collective-permute-start | bytes 5505032 | tf_op jit(solution)/shard_map/ppermute | solution.py:26
  50.5 0.0 collective-permute-done.6.refs_9_
  50.5 3.8 %collective-permute-start.4 = (bf16[7,128,1024]{2,1,0:T(8,128)(2,1)}, bf16[7,128,1024]{2,1,0:T(8,128)(2,1)}, u32[]{:S(2)}, u32[]{:S(2)}) collective-permute-start(bf16[7,128,1024]{2,1,0:T(8,128)(2,1)} %get-tuple-element.20), channel_id=1, source_target_pairs={{8,0},{16,8},{24,16},{9,1},{17,9},{25,17},{10,2},{18,10},{26,18},{... | collective-permute-start | bytes 5505032 | tf_op jit(solution)/shard_map/ppermute | solution.py:26
  54.3 0.0 collective-permute-done.5.refs_8_
  54.4 0.0 collective-permute-done.7.refs_4_
  54.4 0.0 collective-permute-done.8.refs_6_
  54.4 0.7 copy-done.6
  55.1 24.3 %slab_1.1 = (bf16[2,16,128,1024]{3,2,1,0:T(8,128)(2,1)}, bf16[128,256]{1,0:T(8,128)(2,1)}) custom-call(s32[2,6,128]{2,1,0:T(8,128)} %stack.2.refs_0_, f32[5,5]{1,0:T(8,128)} %refs_1_.3, bf16[32,30]{1,0:T(8,128)(2,1)} %fusion.6.refs_2_, bf16[128,144]{1,0:T(8,128)(2,1)} %fusion.refs_3_, bf16[7,128,1024]{2,1,0:T(8,128)(2,1)} %collective-permute-done.7.refs_4_, ...), custom_call_target="tpu_custom_call" | custom-call | flops 20000000000 | bytes 16000000 | tf_op jit(solution)/shard_map/slab_1/pallas_call | solution.py:416
  79.4 5.7 %collective-permute-start.9 = (bf16[128,256]{1,0:T(8,128)(2,1)}, bf16[128,256]{1,0:T(8,128)(2,1)S(1)}, u32[]{:S(2)}, u32[]{:S(2)}) collective-permute-start(bf16[128,256]{1,0:T(8,128)(2,1)} %get-tuple-element.27), channel_id=1, source_target_pairs={{0,7},{1,6},{2,5},{3,4},{4,3},{5,2},{6,1},{7,0},{8,15},{9,14},{10,... | collective-permute-start | bytes 196616 | tf_op jit(solution)/shard_map/ppermute | solution.py:498
  85.1 0.0 collective-permute-done.3.refs_4_
  85.1 0.0 collective-permute-done.4.refs_6_
  85.1 1.2 %copy-done.4 = bf16[7,128,1024]{2,1,0:T(8,128)(2,1)} copy-done((bf16[7,128,1024]{2,1,0:T(8,128)(2,1)}, bf16[7,128,1024]{2,1,0:T(8,128)(2,1)S(1)}, u32[]{:S(2)}) %copy-start.4) | copy-done | bytes 1835032
  86.3 24.1 %slab_0.1 = (bf16[2,16,128,1024]{3,2,1,0:T(8,128)(2,1)}, bf16[128,256]{1,0:T(8,128)(2,1)}) custom-call(s32[2,6,128]{2,1,0:T(8,128)} %stack.2.refs_0_, f32[5,5]{1,0:T(8,128)} %refs_1_.3, bf16[32,30]{1,0:T(8,128)(2,1)} %fusion.6.refs_2_, bf16[128,144]{1,0:T(8,128)(2,1)} %fusion.refs_3_, ...), custom_call_target="tpu_custom_call", output_to_operand_aliasing={{0}: (10, {})} | custom-call | flops 20000000000 | bytes 16000000 | tf_op jit(solution)/shard_map/slab_0/pallas_call | solution.py:416
  110.4 0.0 collective-permute-done.9
  110.4 1.6 %convolution_multiply_fusion = f32[128,128]{1,0:T(8,128)} fusion(bf16[128,256]{1,0:T(8,128)(2,1)} %get-tuple-element.26, bf16[128,256]{1,0:T(8,128)(2,1)S(1)} %collective-permute-done.9), kind=kOutput, calls=%fused_computation | convolution fusion | flops 8404992 | bytes 196608 | tf_op jit(solution)/shard_map/dot_general | solution.py:501
  (25 shorter events, 0.3 us)
Async XLA Ops:
  0.6 16.4 %copy-start.2 = (s32[2,3,128]{2,0,1:T(2,128)S(1)}, s32[2,3,128]{2,0,1:T(2,128)}, u32[]{:S(2)}) copy-start(s32[2,3,128]{2,0,1:T(2,128)} %param.8) | copy-start | bytes 9220
  0.6 16.5 %copy-start.3 = (f32[15]{0:T(128)S(1)}, f32[15]{0:T(128)}, u32[]{:S(2)}) copy-start(f32[15]{0:T(128)} %param.6) | copy-start | bytes 184
  0.6 18.2 %copy-start.1 = (f32[5,5]{1,0:T(8,128)S(1)}, f32[5,5]{1,0:T(8,128)}, u32[]{:S(2)}) copy-start(f32[5,5]{1,0:T(8,128)} %refs_1_.3) | copy-start | bytes 304
  5.7 13.8 %collective-permute-start = (bf16[2,7,4,1152]{3,2,1,0:T(4,128)(2,1)}, bf16[2,7,4,1152]{3,2,1,0:T(4,128)(2,1)S(1)}, u32[]{:S(2)}, u32[]{:S(2)}) collective-permute-start(bf16[2,7,4,1152]{3,2,1,0:T(4,128)(2,1)} %get-tuple-element.15), channel_id=1, source_target_pairs={{0,8},{8,16},{16,24},{1,9},{9,17},{17,25},{2,10},{10,18},{18,26},{... | collective-permute-start | bytes 387080 | tf_op jit(solution)/shard_map/ppermute | solution.py:26
  7.7 11.9 %collective-permute-start.1 = (bf16[2,7,4,1152]{3,2,1,0:T(4,128)(2,1)}, bf16[2,7,4,1152]{3,2,1,0:T(4,128)(2,1)S(1)}, u32[]{:S(2)}, u32[]{:S(2)}) collective-permute-start(bf16[2,7,4,1152]{3,2,1,0:T(4,128)(2,1)} %get-tuple-element.17), channel_id=1, source_target_pairs={{8,0},{16,8},{24,16},{9,1},{17,9},{25,17},{10,2},{18,10},{26,18},{... | collective-permute-start | bytes 387080 | tf_op jit(solution)/shard_map/ppermute | solution.py:26
  11.3 43.0 %collective-permute-start.7 = (bf16[7,128,1024]{2,1,0:T(8,128)(2,1)}, bf16[7,128,1024]{2,1,0:T(8,128)(2,1)}, u32[]{:S(2)}, u32[]{:S(2)}) collective-permute-start(bf16[7,128,1024]{2,1,0:T(8,128)(2,1)} %get-tuple-element.22), channel_id=1, source_target_pairs={{0,8},{8,16},{16,24},{1,9},{9,17},{17,25},{2,10},{10,18},{18,26},{... | collective-permute-start | bytes 5505032 | tf_op jit(solution)/shard_map/ppermute | solution.py:26
  13.2 41.1 %collective-permute-start.8 = (bf16[7,128,1024]{2,1,0:T(8,128)(2,1)}, bf16[7,128,1024]{2,1,0:T(8,128)(2,1)}, u32[]{:S(2)}, u32[]{:S(2)}) collective-permute-start(bf16[7,128,1024]{2,1,0:T(8,128)(2,1)} %get-tuple-element.23), channel_id=1, source_target_pairs={{8,0},{16,8},{24,16},{9,1},{17,9},{25,17},{10,2},{18,10},{26,18},{... | collective-permute-start | bytes 5505032 | tf_op jit(solution)/shard_map/ppermute | solution.py:26
  19.7 4.0 %collective-permute-start.2 = (bf16[2,30,2,128]{3,2,1,0:T(2,128)(2,1)S(1)}, bf16[2,30,2,128]{3,2,1,0:T(2,128)(2,1)S(1)}, u32[]{:S(2)}, u32[]{:S(2)}) collective-permute-start(bf16[2,30,2,128]{3,2,1,0:T(2,128)(2,1)S(1)} %broadcast_select_fusion), channel_id=1, source_target_pairs={{0,1},{1,0},{2,3},{3,2},{4,5},{5,4},{6,7},{7,6},{8,9},{9,8},{10,11... | collective-permute-start | bytes 92168 | tf_op jit(solution)/shard_map/ppermute | solution.py:468
  22.4 8.3 %copy-start.7 = (s32[2,1]{0,1:T(1,128)S(1)}, s32[2,1]{0,1:T(1,128)}, u32[]{:S(2)}) copy-start(s32[2,1]{0,1:T(1,128)} %param.9) | copy-start | bytes 28
  24.5 24.0 %copy-start = (bf16[2,30,128,128]{3,2,1,0:T(8,128)(2,1)}, bf16[2,30,128,128]{3,2,1,0:T(8,128)(2,1)S(1)}, u32[]{:S(2)}) copy-start(bf16[2,30,128,128]{3,2,1,0:T(8,128)(2,1)S(1)} %fusion.13.refs_7_) | copy-start | bytes 5898244
  25.3 25.2 %collective-permute-start.6 = (bf16[2,30,2,1152]{3,2,1,0:T(2,128)(2,1)S(1)}, bf16[2,30,2,1152]{3,2,1,0:T(2,128)(2,1)S(1)}, u32[]{:S(2)}, u32[]{:S(2)}) collective-permute-start(bf16[2,30,2,1152]{3,2,1,0:T(2,128)(2,1)S(1)} %get-tuple-element.36), channel_id=1, source_target_pairs={{0,2},{2,4},{4,6},{1,3},{3,5},{5,7},{8,10},{10,12},{12,14},{9,11},... | collective-permute-start | bytes 829448 | tf_op jit(solution)/shard_map/ppermute | solution.py:26
  28.8 25.5 %collective-permute-start.5 = (bf16[2,30,2,1152]{3,2,1,0:T(2,128)(2,1)S(1)}, bf16[2,30,2,1152]{3,2,1,0:T(2,128)(2,1)S(1)}, u32[]{:S(2)}, u32[]{:S(2)}) collective-permute-start(bf16[2,30,2,1152]{3,2,1,0:T(2,128)(2,1)S(1)} %get-tuple-element.37), channel_id=1, source_target_pairs={{2,0},{4,2},{6,4},{3,1},{5,3},{7,5},{10,8},{12,10},{14,12},{11,9},... | collective-permute-start | bytes 829448 | tf_op jit(solution)/shard_map/ppermute | solution.py:26
  48.6 36.5 %collective-permute-start.3 = (bf16[7,128,1024]{2,1,0:T(8,128)(2,1)}, bf16[7,128,1024]{2,1,0:T(8,128)(2,1)S(1)}, u32[]{:S(2)}, u32[]{:S(2)}) collective-permute-start(bf16[7,128,1024]{2,1,0:T(8,128)(2,1)} %get-tuple-element.19), channel_id=1, source_target_pairs={{0,8},{8,16},{16,24},{1,9},{9,17},{17,25},{2,10},{10,18},{18,26},{... | collective-permute-start | bytes 5505032 | tf_op jit(solution)/shard_map/ppermute | solution.py:26
  50.5 3.9 %copy-start.5 = (bf16[2,30,2,1152]{3,2,1,0:T(2,128)(2,1)}, bf16[2,30,2,1152]{3,2,1,0:T(2,128)(2,1)S(1)}, u32[]{:S(2)}) copy-start(bf16[2,30,2,1152]{3,2,1,0:T(2,128)(2,1)S(1)} %collective-permute-done.6.refs_9_) | copy-start | bytes 829444
  50.5 34.6 %collective-permute-start.4 = (bf16[7,128,1024]{2,1,0:T(8,128)(2,1)}, bf16[7,128,1024]{2,1,0:T(8,128)(2,1)}, u32[]{:S(2)}, u32[]{:S(2)}) collective-permute-start(bf16[7,128,1024]{2,1,0:T(8,128)(2,1)} %get-tuple-element.20), channel_id=1, source_target_pairs={{8,0},{16,8},{24,16},{9,1},{17,9},{25,17},{10,2},{18,10},{26,18},{... | collective-permute-start | bytes 5505032 | tf_op jit(solution)/shard_map/ppermute | solution.py:26
  54.4 0.7 copy-start.6
  79.4 31.0 %collective-permute-start.9 = (bf16[128,256]{1,0:T(8,128)(2,1)}, bf16[128,256]{1,0:T(8,128)(2,1)S(1)}, u32[]{:S(2)}, u32[]{:S(2)}) collective-permute-start(bf16[128,256]{1,0:T(8,128)(2,1)} %get-tuple-element.27), channel_id=1, source_target_pairs={{0,7},{1,6},{2,5},{3,4},{4,3},{5,2},{6,1},{7,0},{8,15},{9,14},{10,... | collective-permute-start | bytes 196616 | tf_op jit(solution)/shard_map/ppermute | solution.py:498
  85.1 1.2 %copy-start.4 = (bf16[7,128,1024]{2,1,0:T(8,128)(2,1)}, bf16[7,128,1024]{2,1,0:T(8,128)(2,1)S(1)}, u32[]{:S(2)}) copy-start(bf16[7,128,1024]{2,1,0:T(8,128)(2,1)S(1)} %collective-permute-done.3.refs_4_) | copy-start | bytes 5505028

commit v13 on v9

--- a/solution.py
+++ b/solution.py
@@ -46,12 +46,12 @@
 
 def smooth_matrix(smooth_kernel):
     depth = WINDOW + 2 * EDGE
-    out_ids = jnp.arange(WINDOW, dtype=jnp.int32)[:, None]
-    in_ids = jnp.arange(depth, dtype=jnp.int32)[None, :]
+    parts = WINDOW // BLOCK
+    out_ids = jnp.arange(WINDOW, dtype=jnp.int32).reshape(parts, 1, BLOCK, 1)
+    in_ids = jnp.arange(depth, dtype=jnp.int32)
     step = in_ids - out_ids - (EDGE - REACH)
-    hit = step[None, :, :, None] == jnp.arange(SIDE, dtype=jnp.int32)
-    table = jnp.sum(jnp.where(hit, smooth_kernel.T[:, None, None, :], 0.0), axis=3)
-    table = jnp.swapaxes(table.reshape(SIDE, WINDOW // BLOCK, BLOCK, depth), 0, 1)
+    hit = step[..., None] == jnp.arange(SIDE, dtype=jnp.int32)
+    table = jnp.sum(jnp.where(hit, smooth_kernel.T[None, :, None, None, :], 0.0), axis=4)
     high, low = split(table)
     return jnp.concatenate([high, high, low], axis=3).reshape(SIDE * WINDOW, 3 * depth)
 
@@ -255,29 +255,35 @@
 
 def send_all(frames, slab, low, high, whole, sems):
     frame_count = whole.shape[0]
-    middle = frame_count - HALF
-    spans = [pl.ds(0, middle), pl.ds(middle, HALF)]
-    fetches = [
-        pltpu.make_async_copy(frames.at[slab, span], whole.at[span], sems.at[i])
-        for i, span in enumerate(spans)
-    ]
-    writes = [
-        pltpu.make_async_copy(whole.at[pl.ds(0, HALF)], high, sems.at[2]),
-        pltpu.make_async_copy(whole.at[pl.ds(middle, HALF)], low, sems.at[3]),
-    ]
+    half = (HALF + 1) // 2
+    spans = []
+    for target, base in ((high, 0), (low, frame_count - HALF)):
+        for start, count in ((0, half), (half, HALF - half)):
+            spans.append((target, base + start, start, count))
+    fetches, writes = [], []
+    for i, (target, source, start, count) in enumerate(spans):
+        here = whole.at[pl.ds(source, count)]
+        fetches.append(
+            pltpu.make_async_copy(frames.at[slab, pl.ds(source, count)], here, sems.at[2 * i])
+        )
+        writes.append(
+            pltpu.make_async_copy(here, target.at[pl.ds(start, count)], sems.at[2 * i + 1])
+        )
     return fetches, writes
 
 
 def cut_kernel(frames, rim, rim_low, rim_high, low, high, whole, top, bottom, left, right, sems):
     frame_count, row_count, col_count = whole.shape
     reads = [
-        pltpu.make_async_copy(source, target, sems.at[4 + i])
+        pltpu.make_async_copy(source, target, sems.at[8 + i])
         for i, (source, target) in enumerate(
             [
                 (frames.at[0, :, pl.ds(0, BLOCK), :], top),
                 (frames.at[0, :, pl.ds(row_count - BLOCK, BLOCK), :], bottom),
                 (frames.at[0, :, :, pl.ds(0, TILE)], left),
                 (frames.at[0, :, :, pl.ds(col_count - TILE, TILE)], right),
+                (frames.at[1, pl.ds(HALF, frame_count - 2 * HALF)],
+                 whole.at[pl.ds(HALF, frame_count - 2 * HALF)]),
             ]
         )
     ]
@@ -344,7 +350,7 @@
             pltpu.VMEM((frame_count, BLOCK, col_count), bf16),
             pltpu.VMEM((frame_count, row_count, TILE), bf16),
             pltpu.VMEM((frame_count, row_count, TILE), bf16),
-            pltpu.SemaphoreType.DMA((8,)),
+            pltpu.SemaphoreType.DMA((13,)),
         ],
         compiler_params=pltpu.CompilerParams(vmem_limit_bytes=60 * 1024 * 1024),
         name="cut",
@@ -362,7 +368,7 @@
         out_shape=[piece, piece],
         scratch_shapes=[
             pltpu.VMEM((frame_count, row_count, col_count), bf16),
-            pltpu.SemaphoreType.DMA((4,)),
+            pltpu.SemaphoreType.DMA((8,)),
         ],
         compiler_params=pltpu.CompilerParams(vmem_limit_bytes=60 * 1024 * 1024),
         cost_estimate=pl.CostEstimate(flops=0, bytes_accessed=9_000_000, transcendentals=0),
@@ -373,7 +379,7 @@
 def run_slab(slab, smoothed, spots, taps, w2, low, frames, high, edge, below, above):
     _, frame_count, row_count, col_count = frames.shape
     slot_count = spots.shape[1]
-    row_step, frame_step = 32, 4
+    row_step, frame_step = 32, 8
     steps_1 = row_count // row_step
     steps_2 = frame_count // frame_step
     wide = col_count + TILE
@@ -433,7 +439,7 @@
             pltpu.VMEM((slot_count * PATCH, TILE), bf16),
         ],
         input_output_aliases=aliases,
-        compiler_params=pltpu.CompilerParams(vmem_limit_bytes=60 * 1024 * 1024),
+        compiler_params=pltpu.CompilerParams(vmem_limit_bytes=40 * 1024 * 1024),
         cost_estimate=pl.CostEstimate(
             flops=20_000_000_000, bytes_accessed=16_000_000, transcendentals=0
         ),

time: 97.2 us -> 91.2 us (0.938)
  local copies, waits for them, and re-layouts: 5.77 us -> 2.03 us
  Pallas kernels: 54.8 us -> 53.1 us
    unnamed x18 -> x10, local copies, waits for them, and re-layouts: 3.05 us -> 1.16 us
    pallas_call x2, Pallas kernels: 46.2 us -> 44.8 us  [run_slab(): pl.pallas_call(body, grid=(steps_1 + steps_2 + 1,), in_specs=in_specs, ou...]
  transfers between devices with their start and end apart: 10 -> 10, of which waited for: 1 -> 1; matrix products, arithmetic and copies ran while one was open for 6% -> 4% of each run, Pallas kernels for 52% -> 53%
where the time goes in v13:
time: 91.2 us; the launch traced here: 90 us
  Pallas kernels  53.1 us (58%)
  starting transfers between devices  28.9 us (32%)
  waiting for transfers between devices  2.21 us (2%)
  local copies, waits for them, and re-layouts  2.03 us (2%)
  matrix products  1.67 us (2%)
  other arithmetic  1.04 us (1%)
  between operations  0.98 us (1%)
    pallas_call x2, Pallas kernels, run_slab(): pl.pallas_call(body, grid=(steps_1 + steps_2 + 1,), in_specs=in_specs, ou...  44.8 us
    ppermute x8, starting transfers between devices, shifted(): return lax.ppermute(block, axis, route)  21.7 us
    ppermute x1, starting transfers between devices, shards(): lax.ppermute(second, ('row', 'col'), [(i, count - 1 - i) for i in range(c...  5.64 us
    pallas_call x1, Pallas kernels, cut(): pl.pallas_call(cut_kernel, in_specs=[anywhere], out_specs=[near] * 3 + [a...  5.19 us
    pallas_call x1, Pallas kernels, late_cut(): pl.pallas_call(late_kernel, in_specs=[anywhere], out_specs=[anywhere] * 2...  3.12 us
    ppermute x1, waiting for transfers between devices, shards(): sides = lax.ppermute(sides, 'col', [(0, 1), (1, 0)])  2.18 us
  transfers between devices with their start and end apart: 10, of which 1 were waited for; matrix products, arithmetic and copies ran while one was open for 4% of the time, Pallas kernels for 53%

profile of v13, /device:TPU:2, one launch (start us, length us, event | category | flops | bytes accessed | tf_op | source)
XLA Modules:
  0.0 90.0 jit_solution(13051953055611271445)
XLA Ops:
  0.6 0.0 copy-start
  0.6 0.0 copy-start.1
  0.7 0.0 copy-start.2
  0.7 5.2 %cut.1 = (bf16[2,16,4,1152]{3,2,1,0:T(4,128)(2,1)}, bf16[2,7,4,1152]{3,2,1,0:T(4,128)(2,1)}, bf16[2,7,4,1152]{3,2,1,0:T(4,128)(2,1)}, bf16[7,128,1024]{2,1,0:T(8,128)(2,1)}, bf16[7,128,1024]{2,1,0:T(8,128)(2,1)}) custom-call(bf16[2,16,128,1024]{3,2,1,0:T(8,128)(2,1)} %refs_4_.3), custom_call_target="tpu_custom_call" | custom-call | tf_op jit(solution)/shard_map/cut/pallas_call | solution.py:342
  5.9 1.9 %collective-permute-start = (bf16[2,7,4,1152]{3,2,1,0:T(4,128)(2,1)}, bf16[2,7,4,1152]{3,2,1,0:T(4,128)(2,1)S(1)}, u32[]{:S(2)}, u32[]{:S(2)}) collective-permute-start(bf16[2,7,4,1152]{3,2,1,0:T(4,128)(2,1)} %get-tuple-element.15), channel_id=1, source_target_pairs={{0,8},{8,16},{16,24},{1,9},{9,17},{17,25},{2,10},{10,18},{18,26},{... | collective-permute-start | bytes 387080 | tf_op jit(solution)/shard_map/ppermute | solution.py:25
  7.8 3.6 %collective-permute-start.1 = (bf16[2,7,4,1152]{3,2,1,0:T(4,128)(2,1)}, bf16[2,7,4,1152]{3,2,1,0:T(4,128)(2,1)S(1)}, u32[]{:S(2)}, u32[]{:S(2)}) collective-permute-start(bf16[2,7,4,1152]{3,2,1,0:T(4,128)(2,1)} %get-tuple-element.17), channel_id=1, source_target_pairs={{8,0},{16,8},{24,16},{9,1},{17,9},{25,17},{10,2},{18,10},{26,18},{... | collective-permute-start | bytes 387080 | tf_op jit(solution)/shard_map/ppermute | solution.py:25
  11.4 1.9 %collective-permute-start.7 = (bf16[7,128,1024]{2,1,0:T(8,128)(2,1)}, bf16[7,128,1024]{2,1,0:T(8,128)(2,1)}, u32[]{:S(2)}, u32[]{:S(2)}) collective-permute-start(bf16[7,128,1024]{2,1,0:T(8,128)(2,1)} %get-tuple-element.22), channel_id=1, source_target_pairs={{0,8},{8,16},{16,24},{1,9},{9,17},{17,25},{2,10},{10,18},{18,26},{... | collective-permute-start | bytes 5505032 | tf_op jit(solution)/shard_map/ppermute | solution.py:25
  13.4 3.6 %collective-permute-start.8 = (bf16[7,128,1024]{2,1,0:T(8,128)(2,1)}, bf16[7,128,1024]{2,1,0:T(8,128)(2,1)}, u32[]{:S(2)}, u32[]{:S(2)}) collective-permute-start(bf16[7,128,1024]{2,1,0:T(8,128)(2,1)} %get-tuple-element.23), channel_id=1, source_target_pairs={{8,0},{16,8},{24,16},{9,1},{17,9},{25,17},{10,2},{18,10},{26,18},{... | collective-permute-start | bytes 5505032 | tf_op jit(solution)/shard_map/ppermute | solution.py:25
  17.1 0.0 copy-done
  17.1 0.1 copy.25
  17.2 0.1 subtract_add_fusion
  17.3 0.1 select_reduce_fusion
  17.4 0.0 copy-done.1
  17.5 0.0 copy-done.2
  17.5 0.2 select_reduce_fusion.2
  17.7 0.1 reduce-precision_convert_fusion.1
  17.8 0.1 pad_maximum_fusion.refs_2_
  17.9 0.0 collective-permute-done
  18.0 1.1 %constant_dynamic-update-slice_fusion.1 = bf16[2,30,4,1152]{3,2,1,0:T(4,128)(2,1)S(1)} fusion(bf16[2,30,4,1152]{3,2,1,0:T(4,128)(2,1)S(1)} %constant_dynamic-update-slice_fusion.2, bf16[2,16,4,1152]{3,2,1,0:T(4,128)(2,1)} %get-tuple-element.16), kind=kLoop, calls=%fused_computation.18 | loop fusion | bytes 589824
  19.1 0.0 collective-permute-done.1
  19.1 0.1 constant_dynamic-update-slice_fusion
  19.1 0.1 broadcast_select_fusion
  19.2 1.6 %collective-permute-start.2 = (bf16[2,30,2,128]{3,2,1,0:T(2,128)(2,1)S(1)}, bf16[2,30,2,128]{3,2,1,0:T(2,128)(2,1)S(1)}, u32[]{:S(2)}, u32[]{:S(2)}) collective-permute-start(bf16[2,30,2,128]{3,2,1,0:T(2,128)(2,1)S(1)} %broadcast_select_fusion), channel_id=1, source_target_pairs={{0,1},{1,0},{2,3},{3,2},{4,5},{5,4},{6,7},{7,6},{8,9},{9,8},{10,11... | collective-permute-start | bytes 92168 | tf_op jit(solution)/shard_map/ppermute | solution.py:469
  20.8 0.2 slice.51
  21.0 0.0 copy-start.3
  21.0 2.2 %collective-permute-done.2 = bf16[2,30,2,128]{3,2,1,0:T(2,128)(2,1)S(1)} collective-permute-done((bf16[2,30,2,128]{3,2,1,0:T(2,128)(2,1)S(1)}, bf16[2,30,2,128]{3,2,1,0:T(2,128)(2,1)S(1)}, u32[]{:S(2)}, u32[]{:S(2)}) %collective-permute-start.2) | collective-permute-done | bytes 30752 | tf_op jit(solution)/shard_map/ppermute | solution.py:469
  23.1 0.9 fusion.5.refs_6_
  24.0 0.1 fusion.8
  24.1 0.3 maximum_maximum_fusion
  24.4 0.4 fusion.9
  24.8 3.5 %collective-permute-start.6 = (bf16[2,30,2,1152]{3,2,1,0:T(2,128)(2,1)S(1)}, bf16[2,30,2,1152]{3,2,1,0:T(2,128)(2,1)S(1)}, u32[]{:S(2)}, u32[]{:S(2)}) collective-permute-start(bf16[2,30,2,1152]{3,2,1,0:T(2,128)(2,1)S(1)} %get-tuple-element.36), channel_id=1, source_target_pairs={{0,2},{2,4},{4,6},{1,3},{3,5},{5,7},{8,10},{10,12},{12,14},{9,11},... | collective-permute-start | bytes 829448 | tf_op jit(solution)/shard_map/ppermute | solution.py:25
  28.3 1.3 %collective-permute-start.5 = (bf16[2,30,2,1152]{3,2,1,0:T(2,128)(2,1)S(1)}, bf16[2,30,2,1152]{3,2,1,0:T(2,128)(2,1)S(1)}, u32[]{:S(2)}, u32[]{:S(2)}) collective-permute-start(bf16[2,30,2,1152]{3,2,1,0:T(2,128)(2,1)S(1)} %get-tuple-element.37), channel_id=1, source_target_pairs={{2,0},{4,2},{6,4},{3,1},{5,3},{7,5},{10,8},{12,10},{14,12},{11,9},... | collective-permute-start | bytes 829448 | tf_op jit(solution)/shard_map/ppermute | solution.py:25
  29.6 0.0 copy-done.3
  29.6 0.1 stack_broadcast_in_dim.2
  29.8 3.1 %late_cut.1 = (bf16[7,128,1024]{2,1,0:T(8,128)(2,1)}, bf16[7,128,1024]{2,1,0:T(8,128)(2,1)}) custom-call(bf16[2,16,128,1024]{3,2,1,0:T(8,128)(2,1)} %refs_4_.3), custom_call_target="tpu_custom_call" | custom-call | bytes 9000000 | tf_op jit(solution)/shard_map/late_cut/pallas_call | solution.py:364
  32.9 1.9 %collective-permute-start.3 = (bf16[7,128,1024]{2,1,0:T(8,128)(2,1)}, bf16[7,128,1024]{2,1,0:T(8,128)(2,1)S(1)}, u32[]{:S(2)}, u32[]{:S(2)}) collective-permute-start(bf16[7,128,1024]{2,1,0:T(8,128)(2,1)} %get-tuple-element.19), channel_id=1, source_target_pairs={{0,8},{8,16},{16,24},{1,9},{9,17},{17,25},{2,10},{10,18},{18,26},{... | collective-permute-start | bytes 5505032 | tf_op jit(solution)/shard_map/ppermute | solution.py:25
  34.8 0.0 collective-permute-done.6.refs_8_
  34.8 3.8 %collective-permute-start.4 = (bf16[7,128,1024]{2,1,0:T(8,128)(2,1)}, bf16[7,128,1024]{2,1,0:T(8,128)(2,1)S(1)}, u32[]{:S(2)}, u32[]{:S(2)}) collective-permute-start(bf16[7,128,1024]{2,1,0:T(8,128)(2,1)} %get-tuple-element.20), channel_id=1, source_target_pairs={{8,0},{16,8},{24,16},{9,1},{17,9},{25,17},{10,2},{18,10},{26,18},{... | collective-permute-start | bytes 5505032 | tf_op jit(solution)/shard_map/ppermute | solution.py:25
  38.6 0.0 collective-permute-done.5.refs_7_
  38.7 0.0 collective-permute-done.7.refs_3_
  38.7 0.0 collective-permute-done.8.refs_5_
  38.7 22.7 %slab_1.1 = (bf16[2,16,128,1024]{3,2,1,0:T(8,128)(2,1)}, bf16[128,256]{1,0:T(8,128)(2,1)S(1)}) custom-call(s32[6,128]{1,0:T(8,128)S(1)} %get-tuple-element.42.refs_0_, bf16[32,30]{1,0:T(8,128)(2,1)S(1)} %bitcast.29, bf16[160,144]{1,0:T(8,128)(2,1)S(1)} %pad_maximum_fusion.refs_2_, bf16[7,128,1024]{2,1,0:T(8,128)(2,1)} %collective-permute-done.7.refs_3_, ...), custom_call_target="tpu_custom_call" | custom-call | flops 20000000000 | bytes 16000000 | tf_op jit(solution)/shard_map/slab_1/pallas_call | solution.py:417
  61.3 5.6 %collective-permute-start.9 = (bf16[128,256]{1,0:T(8,128)(2,1)S(1)}, bf16[128,256]{1,0:T(8,128)(2,1)S(1)}, u32[]{:S(2)}, u32[]{:S(2)}) collective-permute-start(bf16[128,256]{1,0:T(8,128)(2,1)S(1)} %get-tuple-element.27), channel_id=1, source_target_pairs={{0,7},{1,6},{2,5},{3,4},{4,3},{5,2},{6,1},{7,0},{8,15},{9,14},{10,... | collective-permute-start | bytes 196616 | tf_op jit(solution)/shard_map/ppermute | solution.py:498
  67.0 0.0 collective-permute-done.3.refs_3_
  67.0 0.0 collective-permute-done.4.refs_5_
  67.0 22.2 %slab_0.1 = (bf16[2,16,128,1024]{3,2,1,0:T(8,128)(2,1)}, bf16[128,256]{1,0:T(8,128)(2,1)S(1)}) custom-call(s32[6,128]{1,0:T(8,128)S(1)} %get-tuple-element.43.refs_0_, bf16[32,30]{1,0:T(8,128)(2,1)S(1)} %bitcast.30, bf16[160,144]{1,0:T(8,128)(2,1)S(1)} %pad_maximum_fusion.refs_2_, ...), custom_call_target="tpu_custom_call", output_to_operand_aliasing={{0}: (9, {})} | custom-call | flops 20000000000 | bytes 16000000 | tf_op jit(solution)/shard_map/slab_0/pallas_call | solution.py:417
  89.2 0.0 collective-permute-done.9
  89.2 0.8 convolution_multiply_fusion
  (14 shorter events, 0.2 us)
Async XLA Ops:
  0.6 16.4 %copy-start = (f32[5,5]{1,0:T(8,128)S(1)}, f32[5,5]{1,0:T(8,128)}, u32[]{:S(2)}) copy-start(f32[5,5]{1,0:T(8,128)} %param.7) | copy-start | bytes 304
  0.6 16.8 %copy-start.1 = (s32[2,3,128]{2,0,1:T(2,128)S(1)}, s32[2,3,128]{2,0,1:T(2,128)}, u32[]{:S(2)}) copy-start(s32[2,3,128]{2,0,1:T(2,128)} %param.8) | copy-start | bytes 9220
  0.7 16.8 %copy-start.2 = (f32[15]{0:T(128)S(1)}, f32[15]{0:T(128)}, u32[]{:S(2)}) copy-start(f32[15]{0:T(128)} %param.6) | copy-start | bytes 184
  5.9 12.0 %collective-permute-start = (bf16[2,7,4,1152]{3,2,1,0:T(4,128)(2,1)}, bf16[2,7,4,1152]{3,2,1,0:T(4,128)(2,1)S(1)}, u32[]{:S(2)}, u32[]{:S(2)}) collective-permute-start(bf16[2,7,4,1152]{3,2,1,0:T(4,128)(2,1)} %get-tuple-element.15), channel_id=1, source_target_pairs={{0,8},{8,16},{16,24},{1,9},{9,17},{17,25},{2,10},{10,18},{18,26},{... | collective-permute-start | bytes 387080 | tf_op jit(solution)/shard_map/ppermute | solution.py:25
  7.8 11.3 %collective-permute-start.1 = (bf16[2,7,4,1152]{3,2,1,0:T(4,128)(2,1)}, bf16[2,7,4,1152]{3,2,1,0:T(4,128)(2,1)S(1)}, u32[]{:S(2)}, u32[]{:S(2)}) collective-permute-start(bf16[2,7,4,1152]{3,2,1,0:T(4,128)(2,1)} %get-tuple-element.17), channel_id=1, source_target_pairs={{8,0},{16,8},{24,16},{9,1},{17,9},{25,17},{10,2},{18,10},{26,18},{... | collective-permute-start | bytes 387080 | tf_op jit(solution)/shard_map/ppermute | solution.py:25
  11.4 27.2 %collective-permute-start.7 = (bf16[7,128,1024]{2,1,0:T(8,128)(2,1)}, bf16[7,128,1024]{2,1,0:T(8,128)(2,1)}, u32[]{:S(2)}, u32[]{:S(2)}) collective-permute-start(bf16[7,128,1024]{2,1,0:T(8,128)(2,1)} %get-tuple-element.22), channel_id=1, source_target_pairs={{0,8},{8,16},{16,24},{1,9},{9,17},{17,25},{2,10},{10,18},{18,26},{... | collective-permute-start | bytes 5505032 | tf_op jit(solution)/shard_map/ppermute | solution.py:25
  13.4 25.3 %collective-permute-start.8 = (bf16[7,128,1024]{2,1,0:T(8,128)(2,1)}, bf16[7,128,1024]{2,1,0:T(8,128)(2,1)}, u32[]{:S(2)}, u32[]{:S(2)}) collective-permute-start(bf16[7,128,1024]{2,1,0:T(8,128)(2,1)} %get-tuple-element.23), channel_id=1, source_target_pairs={{8,0},{16,8},{24,16},{9,1},{17,9},{25,17},{10,2},{18,10},{26,18},{... | collective-permute-start | bytes 5505032 | tf_op jit(solution)/shard_map/ppermute | solution.py:25
  19.2 4.0 %collective-permute-start.2 = (bf16[2,30,2,128]{3,2,1,0:T(2,128)(2,1)S(1)}, bf16[2,30,2,128]{3,2,1,0:T(2,128)(2,1)S(1)}, u32[]{:S(2)}, u32[]{:S(2)}) collective-permute-start(bf16[2,30,2,128]{3,2,1,0:T(2,128)(2,1)S(1)} %broadcast_select_fusion), channel_id=1, source_target_pairs={{0,1},{1,0},{2,3},{3,2},{4,5},{5,4},{6,7},{7,6},{8,9},{9,8},{10,11... | collective-permute-start | bytes 92168 | tf_op jit(solution)/shard_map/ppermute | solution.py:469
  21.0 8.7 %copy-start.3 = (s32[2,1]{0,1:T(1,128)S(1)}, s32[2,1]{0,1:T(1,128)}, u32[]{:S(2)}) copy-start(s32[2,1]{0,1:T(1,128)} %param.9) | copy-start | bytes 28
  24.8 10.0 %collective-permute-start.6 = (bf16[2,30,2,1152]{3,2,1,0:T(2,128)(2,1)S(1)}, bf16[2,30,2,1152]{3,2,1,0:T(2,128)(2,1)S(1)}, u32[]{:S(2)}, u32[]{:S(2)}) collective-permute-start(bf16[2,30,2,1152]{3,2,1,0:T(2,128)(2,1)S(1)} %get-tuple-element.36), channel_id=1, source_target_pairs={{0,2},{2,4},{4,6},{1,3},{3,5},{5,7},{8,10},{10,12},{12,14},{9,11},... | collective-permute-start | bytes 829448 | tf_op jit(solution)/shard_map/ppermute | solution.py:25
  28.3 10.3 %collective-permute-start.5 = (bf16[2,30,2,1152]{3,2,1,0:T(2,128)(2,1)S(1)}, bf16[2,30,2,1152]{3,2,1,0:T(2,128)(2,1)S(1)}, u32[]{:S(2)}, u32[]{:S(2)}) collective-permute-start(bf16[2,30,2,1152]{3,2,1,0:T(2,128)(2,1)S(1)} %get-tuple-element.37), channel_id=1, source_target_pairs={{2,0},{4,2},{6,4},{3,1},{5,3},{7,5},{10,8},{12,10},{14,12},{11,9},... | collective-permute-start | bytes 829448 | tf_op jit(solution)/shard_map/ppermute | solution.py:25
  32.9 34.1 %collective-permute-start.3 = (bf16[7,128,1024]{2,1,0:T(8,128)(2,1)}, bf16[7,128,1024]{2,1,0:T(8,128)(2,1)S(1)}, u32[]{:S(2)}, u32[]{:S(2)}) collective-permute-start(bf16[7,128,1024]{2,1,0:T(8,128)(2,1)} %get-tuple-element.19), channel_id=1, source_target_pairs={{0,8},{8,16},{16,24},{1,9},{9,17},{17,25},{2,10},{10,18},{18,26},{... | collective-permute-start | bytes 5505032 | tf_op jit(solution)/shard_map/ppermute | solution.py:25
  34.8 32.2 %collective-permute-start.4 = (bf16[7,128,1024]{2,1,0:T(8,128)(2,1)}, bf16[7,128,1024]{2,1,0:T(8,128)(2,1)S(1)}, u32[]{:S(2)}, u32[]{:S(2)}) collective-permute-start(bf16[7,128,1024]{2,1,0:T(8,128)(2,1)} %get-tuple-element.20), channel_id=1, source_target_pairs={{8,0},{16,8},{24,16},{9,1},{17,9},{25,17},{10,2},{18,10},{26,18},{... | collective-permute-start | bytes 5505032 | tf_op jit(solution)/shard_map/ppermute | solution.py:25
  61.3 27.8 %collective-permute-start.9 = (bf16[128,256]{1,0:T(8,128)(2,1)S(1)}, bf16[128,256]{1,0:T(8,128)(2,1)S(1)}, u32[]{:S(2)}, u32[]{:S(2)}) collective-permute-start(bf16[128,256]{1,0:T(8,128)(2,1)S(1)} %get-tuple-element.27), channel_id=1, source_target_pairs={{0,7},{1,6},{2,5},{3,4},{4,3},{5,2},{6,1},{7,0},{8,15},{9,14},{10,... | collective-permute-start | bytes 196616 | tf_op jit(solution)/shard_map/ppermute | solution.py:498

commit v14 on v13

--- a/solution.py
+++ b/solution.py
@@ -208,12 +208,11 @@
             for j in range(16):
                 i = i8 * 16 + j
                 frame, row, tile = spots_ref[0, i], spots_ref[1, i], spots_ref[2, i]
-                beside, turn = spots_ref[3, i], spots_ref[4, i]
+                beside, offset = spots_ref[3, i], spots_ref[4, i]
                 here = kept[frame, tile, pl.ds(row, PATCH), :]
                 there = kept[frame, beside, pl.ds(row, PATCH), :]
-                shift = turn & (TILE - 1)
-                here, there = pltpu.roll(here, shift, 1), pltpu.roll(there, shift, 1)
-                part = jnp.where(lane < turn, here, there)
+                part = jnp.where(lane >= offset, here, there)
+                part = pltpu.roll(part, (TILE - offset) & (TILE - 1), 1)
                 flat[pl.ds(pl.multiple_of(i * PATCH, PATCH), PATCH), :] = part.astype(bf16)
             return unused
 
@@ -240,16 +239,21 @@
     rows = jnp.concatenate(
         [top[...].astype(f32)[:, :REACH], bottom[...].astype(f32)[:, BLOCK - REACH :]], axis=1
     )
-    line = iota((8, TILE), 0)
-    lane = iota((8, TILE), 1)
-    first = ((line == lane) & (line < REACH)).astype(bf16)
-    last = ((line + TILE - 2 * REACH == lane) & (line >= REACH)).astype(bf16)
-    over_lanes = (((1,), (1,)), ((), ()))
+    line = iota((8, 2 * TILE), 0)
+    lane = iota((8, 2 * TILE), 1)
+    first = (line == lane) & (line < REACH)
+    last = (line + 2 * TILE - 2 * REACH == lane) & (line >= REACH)
+    chosen = (first | last).astype(bf16)
+    row_count = left.shape[1]
     cols = []
-    for f in range(rows.shape[0]):
-        one = lax.dot_general(first, left[f], over_lanes, preferred_element_type=f32)
-        one += lax.dot_general(last, right[f], over_lanes, preferred_element_type=f32)
-        cols.append(one[: 2 * REACH].astype(bf16))
+    for f in range(0, rows.shape[0], 2):
+        both = jnp.concatenate([left[f : f + 2], right[f : f + 2]], axis=2)
+        both = both.reshape(2 * row_count, 2 * TILE)
+        one = lax.dot_general(
+            chosen, both, (((1,), (1,)), ((), ())), preferred_element_type=f32
+        )
+        one = one[: 2 * REACH].astype(bf16)
+        cols += [one[:, :row_count], one[:, row_count:]]
     return rows.astype(bf16), cols
 
 
@@ -491,7 +495,7 @@
     tile = col // TILE
     beside = jnp.minimum(tile + 1, col_count // TILE - 1)
     live = jnp.broadcast_to(counts, frame.shape)
-    local = jnp.stack([frame, row, tile, beside, TILE - col % TILE, live], axis=1)
+    local = jnp.stack([frame, row, tile, beside, col % TILE, live], axis=1)
 
     smoothed, second = run_slab(1, None, local[1], taps, w2, low1, frames, high1, edge, below, above)
     count = lax.axis_size("row") * lax.axis_size("col")

time: 91.2 us -> 90.8 us (level)
  no operation moved by 1% of the time
where the time goes in v14:
time: 90.8 us; the launch traced here: 89.6 us
  Pallas kernels  52.8 us (58%)
  starting transfers between devices  28.9 us (32%)
  waiting for transfers between devices  2.21 us (2%)
  local copies, waits for them, and re-layouts  2.03 us (2%)
  matrix products  1.68 us (2%)
  other arithmetic  1.03 us (1%)
  between operations  0.98 us (1%)
    pallas_call x2, Pallas kernels, run_slab(): pl.pallas_call(body, grid=(steps_1 + steps_2 + 1,), in_specs=in_specs, ou...  44.7 us
    ppermute x8, starting transfers between devices, shifted(): return lax.ppermute(block, axis, route)  21.7 us
    ppermute x1, starting transfers between devices, shards(): lax.ppermute(second, ('row', 'col'), [(i, count - 1 - i) for i in range(c...  5.61 us
    pallas_call x1, Pallas kernels, cut(): pl.pallas_call(cut_kernel, in_specs=[anywhere], out_specs=[near] * 3 + [a...  4.92 us
    pallas_call x1, Pallas kernels, late_cut(): pl.pallas_call(late_kernel, in_specs=[anywhere], out_specs=[anywhere] * 2...  3.12 us
    ppermute x1, waiting for transfers between devices, shards(): sides = lax.ppermute(sides, 'col', [(0, 1), (1, 0)])  2.18 us
  transfers between devices with their start and end apart: 10, of which 1 were waited for; matrix products, arithmetic and copies ran while one was open for 4% of the time, Pallas kernels for 53%

profile of v14, /device:TPU:2, one launch (start us, length us, event | category | flops | bytes accessed | tf_op | source)
XLA Modules:
  0.0 89.6 jit_solution(15964288870823489030)
XLA Ops:
  0.6 0.0 copy-start
  0.6 0.0 copy-start.1
  0.7 0.0 copy-start.2
  0.7 4.9 %cut.1 = (bf16[2,16,4,1152]{3,2,1,0:T(4,128)(2,1)}, bf16[2,7,4,1152]{3,2,1,0:T(4,128)(2,1)}, bf16[2,7,4,1152]{3,2,1,0:T(4,128)(2,1)}, bf16[7,128,1024]{2,1,0:T(8,128)(2,1)}, bf16[7,128,1024]{2,1,0:T(8,128)(2,1)}) custom-call(bf16[2,16,128,1024]{3,2,1,0:T(8,128)(2,1)} %refs_4_.3), custom_call_target="tpu_custom_call" | custom-call | tf_op jit(solution)/shard_map/cut/pallas_call | solution.py:346
  5.6 1.9 %collective-permute-start = (bf16[2,7,4,1152]{3,2,1,0:T(4,128)(2,1)}, bf16[2,7,4,1152]{3,2,1,0:T(4,128)(2,1)S(1)}, u32[]{:S(2)}, u32[]{:S(2)}) collective-permute-start(bf16[2,7,4,1152]{3,2,1,0:T(4,128)(2,1)} %get-tuple-element.15), channel_id=1, source_target_pairs={{0,8},{8,16},{16,24},{1,9},{9,17},{17,25},{2,10},{10,18},{18,26},{... | collective-permute-start | bytes 387080 | tf_op jit(solution)/shard_map/ppermute | solution.py:25
  7.5 3.6 %collective-permute-start.1 = (bf16[2,7,4,1152]{3,2,1,0:T(4,128)(2,1)}, bf16[2,7,4,1152]{3,2,1,0:T(4,128)(2,1)S(1)}, u32[]{:S(2)}, u32[]{:S(2)}) collective-permute-start(bf16[2,7,4,1152]{3,2,1,0:T(4,128)(2,1)} %get-tuple-element.17), channel_id=1, source_target_pairs={{8,0},{16,8},{24,16},{9,1},{17,9},{25,17},{10,2},{18,10},{26,18},{... | collective-permute-start | bytes 387080 | tf_op jit(solution)/shard_map/ppermute | solution.py:25
  11.2 1.9 %collective-permute-start.7 = (bf16[7,128,1024]{2,1,0:T(8,128)(2,1)}, bf16[7,128,1024]{2,1,0:T(8,128)(2,1)}, u32[]{:S(2)}, u32[]{:S(2)}) collective-permute-start(bf16[7,128,1024]{2,1,0:T(8,128)(2,1)} %get-tuple-element.22), channel_id=1, source_target_pairs={{0,8},{8,16},{16,24},{1,9},{9,17},{17,25},{2,10},{10,18},{18,26},{... | collective-permute-start | bytes 5505032 | tf_op jit(solution)/shard_map/ppermute | solution.py:25
  13.1 3.6 %collective-permute-start.8 = (bf16[7,128,1024]{2,1,0:T(8,128)(2,1)}, bf16[7,128,1024]{2,1,0:T(8,128)(2,1)}, u32[]{:S(2)}, u32[]{:S(2)}) collective-permute-start(bf16[7,128,1024]{2,1,0:T(8,128)(2,1)} %get-tuple-element.23), channel_id=1, source_target_pairs={{8,0},{16,8},{24,16},{9,1},{17,9},{25,17},{10,2},{18,10},{26,18},{... | collective-permute-start | bytes 5505032 | tf_op jit(solution)/shard_map/ppermute | solution.py:25
  16.8 0.0 copy-done
  16.8 0.1 copy.25
  16.9 0.1 subtract_add_fusion
  17.0 0.1 select_reduce_fusion
  17.1 0.0 copy-done.1
  17.2 0.0 copy-done.2
  17.2 0.2 select_reduce_fusion.2
  17.4 0.1 reduce-precision_convert_fusion.1
  17.5 0.1 pad_maximum_fusion.refs_2_
  17.6 0.0 collective-permute-done
  17.7 1.1 %constant_dynamic-update-slice_fusion.1 = bf16[2,30,4,1152]{3,2,1,0:T(4,128)(2,1)S(1)} fusion(bf16[2,30,4,1152]{3,2,1,0:T(4,128)(2,1)S(1)} %constant_dynamic-update-slice_fusion.2, bf16[2,16,4,1152]{3,2,1,0:T(4,128)(2,1)} %get-tuple-element.16), kind=kLoop, calls=%fused_computation.18 | loop fusion | bytes 589824
  18.8 0.0 collective-permute-done.1
  18.8 0.1 constant_dynamic-update-slice_fusion
  18.9 0.1 broadcast_select_fusion
  18.9 1.6 %collective-permute-start.2 = (bf16[2,30,2,128]{3,2,1,0:T(2,128)(2,1)S(1)}, bf16[2,30,2,128]{3,2,1,0:T(2,128)(2,1)S(1)}, u32[]{:S(2)}, u32[]{:S(2)}) collective-permute-start(bf16[2,30,2,128]{3,2,1,0:T(2,128)(2,1)S(1)} %broadcast_select_fusion), channel_id=1, source_target_pairs={{0,1},{1,0},{2,3},{3,2},{4,5},{5,4},{6,7},{7,6},{8,9},{9,8},{10,11... | collective-permute-start | bytes 92168 | tf_op jit(solution)/shard_map/ppermute | solution.py:473
  20.5 0.2 slice.51
  20.7 0.0 copy-start.3
  20.7 2.2 %collective-permute-done.2 = bf16[2,30,2,128]{3,2,1,0:T(2,128)(2,1)S(1)} collective-permute-done((bf16[2,30,2,128]{3,2,1,0:T(2,128)(2,1)S(1)}, bf16[2,30,2,128]{3,2,1,0:T(2,128)(2,1)S(1)}, u32[]{:S(2)}, u32[]{:S(2)}) %collective-permute-start.2) | collective-permute-done | bytes 30752 | tf_op jit(solution)/shard_map/ppermute | solution.py:473
  22.9 0.9 fusion.4.refs_6_
  23.8 0.1 fusion.7
  23.8 0.3 maximum_maximum_fusion
  24.1 0.4 fusion.8
  24.5 3.5 %collective-permute-start.6 = (bf16[2,30,2,1152]{3,2,1,0:T(2,128)(2,1)S(1)}, bf16[2,30,2,1152]{3,2,1,0:T(2,128)(2,1)S(1)}, u32[]{:S(2)}, u32[]{:S(2)}) collective-permute-start(bf16[2,30,2,1152]{3,2,1,0:T(2,128)(2,1)S(1)} %get-tuple-element.36), channel_id=1, source_target_pairs={{0,2},{2,4},{4,6},{1,3},{3,5},{5,7},{8,10},{10,12},{12,14},{9,11},... | collective-permute-start | bytes 829448 | tf_op jit(solution)/shard_map/ppermute | solution.py:25
  28.0 1.3 %collective-permute-start.5 = (bf16[2,30,2,1152]{3,2,1,0:T(2,128)(2,1)S(1)}, bf16[2,30,2,1152]{3,2,1,0:T(2,128)(2,1)S(1)}, u32[]{:S(2)}, u32[]{:S(2)}) collective-permute-start(bf16[2,30,2,1152]{3,2,1,0:T(2,128)(2,1)S(1)} %get-tuple-element.37), channel_id=1, source_target_pairs={{2,0},{4,2},{6,4},{3,1},{5,3},{7,5},{10,8},{12,10},{14,12},{11,9},... | collective-permute-start | bytes 829448 | tf_op jit(solution)/shard_map/ppermute | solution.py:25
  29.4 0.0 copy-done.3
  29.4 0.1 stack_broadcast_in_dim.2
  29.5 3.1 %late_cut.1 = (bf16[7,128,1024]{2,1,0:T(8,128)(2,1)}, bf16[7,128,1024]{2,1,0:T(8,128)(2,1)}) custom-call(bf16[2,16,128,1024]{3,2,1,0:T(8,128)(2,1)} %refs_4_.3), custom_call_target="tpu_custom_call" | custom-call | bytes 9000000 | tf_op jit(solution)/shard_map/late_cut/pallas_call | solution.py:368
  32.6 1.9 %collective-permute-start.3 = (bf16[7,128,1024]{2,1,0:T(8,128)(2,1)}, bf16[7,128,1024]{2,1,0:T(8,128)(2,1)S(1)}, u32[]{:S(2)}, u32[]{:S(2)}) collective-permute-start(bf16[7,128,1024]{2,1,0:T(8,128)(2,1)} %get-tuple-element.19), channel_id=1, source_target_pairs={{0,8},{8,16},{16,24},{1,9},{9,17},{17,25},{2,10},{10,18},{18,26},{... | collective-permute-start | bytes 5505032 | tf_op jit(solution)/shard_map/ppermute | solution.py:25
  34.5 0.0 collective-permute-done.6.refs_8_
  34.5 3.8 %collective-permute-start.4 = (bf16[7,128,1024]{2,1,0:T(8,128)(2,1)}, bf16[7,128,1024]{2,1,0:T(8,128)(2,1)S(1)}, u32[]{:S(2)}, u32[]{:S(2)}) collective-permute-start(bf16[7,128,1024]{2,1,0:T(8,128)(2,1)} %get-tuple-element.20), channel_id=1, source_target_pairs={{8,0},{16,8},{24,16},{9,1},{17,9},{25,17},{10,2},{18,10},{26,18},{... | collective-permute-start | bytes 5505032 | tf_op jit(solution)/shard_map/ppermute | solution.py:25
  38.4 0.0 collective-permute-done.5.refs_7_
  38.4 0.0 collective-permute-done.7.refs_3_
  38.4 0.0 collective-permute-done.8.refs_5_
  38.4 22.6 %slab_1.1 = (bf16[2,16,128,1024]{3,2,1,0:T(8,128)(2,1)}, bf16[128,256]{1,0:T(8,128)(2,1)S(1)}) custom-call(s32[6,128]{1,0:T(8,128)S(1)} %get-tuple-element.42.refs_0_, bf16[32,30]{1,0:T(8,128)(2,1)S(1)} %bitcast.29, bf16[160,144]{1,0:T(8,128)(2,1)S(1)} %pad_maximum_fusion.refs_2_, bf16[7,128,1024]{2,1,0:T(8,128)(2,1)} %collective-permute-done.7.refs_3_, ...), custom_call_target="tpu_custom_call" | custom-call | flops 20000000000 | bytes 16000000 | tf_op jit(solution)/shard_map/slab_1/pallas_call | solution.py:421
  61.0 5.6 %collective-permute-start.9 = (bf16[128,256]{1,0:T(8,128)(2,1)S(1)}, bf16[128,256]{1,0:T(8,128)(2,1)S(1)}, u32[]{:S(2)}, u32[]{:S(2)}) collective-permute-start(bf16[128,256]{1,0:T(8,128)(2,1)S(1)} %get-tuple-element.27), channel_id=1, source_target_pairs={{0,7},{1,6},{2,5},{3,4},{4,3},{5,2},{6,1},{7,0},{8,15},{9,14},{10,... | collective-permute-start | bytes 196616 | tf_op jit(solution)/shard_map/ppermute | solution.py:502
  66.6 0.0 collective-permute-done.3.refs_3_
  66.6 0.0 collective-permute-done.4.refs_5_
  66.6 22.1 %slab_0.1 = (bf16[2,16,128,1024]{3,2,1,0:T(8,128)(2,1)}, bf16[128,256]{1,0:T(8,128)(2,1)S(1)}) custom-call(s32[6,128]{1,0:T(8,128)S(1)} %get-tuple-element.43.refs_0_, bf16[32,30]{1,0:T(8,128)(2,1)S(1)} %bitcast.30, bf16[160,144]{1,0:T(8,128)(2,1)S(1)} %pad_maximum_fusion.refs_2_, ...), custom_call_target="tpu_custom_call", output_to_operand_aliasing={{0}: (9, {})} | custom-call | flops 20000000000 | bytes 16000000 | tf_op jit(solution)/shard_map/slab_0/pallas_call | solution.py:421
  88.8 0.0 collective-permute-done.9
  88.8 0.8 convolution_multiply_fusion
  (14 shorter events, 0.2 us)
Async XLA Ops:
  0.6 16.2 %copy-start = (f32[5,5]{1,0:T(8,128)S(1)}, f32[5,5]{1,0:T(8,128)}, u32[]{:S(2)}) copy-start(f32[5,5]{1,0:T(8,128)} %param.7) | copy-start | bytes 304
  0.6 16.5 %copy-start.1 = (s32[2,3,128]{2,0,1:T(2,128)S(1)}, s32[2,3,128]{2,0,1:T(2,128)}, u32[]{:S(2)}) copy-start(s32[2,3,128]{2,0,1:T(2,128)} %param.8) | copy-start | bytes 9220
  0.7 16.5 %copy-start.2 = (f32[15]{0:T(128)S(1)}, f32[15]{0:T(128)}, u32[]{:S(2)}) copy-start(f32[15]{0:T(128)} %param.6) | copy-start | bytes 184
  5.6 12.0 %collective-permute-start = (bf16[2,7,4,1152]{3,2,1,0:T(4,128)(2,1)}, bf16[2,7,4,1152]{3,2,1,0:T(4,128)(2,1)S(1)}, u32[]{:S(2)}, u32[]{:S(2)}) collective-permute-start(bf16[2,7,4,1152]{3,2,1,0:T(4,128)(2,1)} %get-tuple-element.15), channel_id=1, source_target_pairs={{0,8},{8,16},{16,24},{1,9},{9,17},{17,25},{2,10},{10,18},{18,26},{... | collective-permute-start | bytes 387080 | tf_op jit(solution)/shard_map/ppermute | solution.py:25
  7.5 11.3 %collective-permute-start.1 = (bf16[2,7,4,1152]{3,2,1,0:T(4,128)(2,1)}, bf16[2,7,4,1152]{3,2,1,0:T(4,128)(2,1)S(1)}, u32[]{:S(2)}, u32[]{:S(2)}) collective-permute-start(bf16[2,7,4,1152]{3,2,1,0:T(4,128)(2,1)} %get-tuple-element.17), channel_id=1, source_target_pairs={{8,0},{16,8},{24,16},{9,1},{17,9},{25,17},{10,2},{18,10},{26,18},{... | collective-permute-start | bytes 387080 | tf_op jit(solution)/shard_map/ppermute | solution.py:25
  11.2 27.2 %collective-permute-start.7 = (bf16[7,128,1024]{2,1,0:T(8,128)(2,1)}, bf16[7,128,1024]{2,1,0:T(8,128)(2,1)}, u32[]{:S(2)}, u32[]{:S(2)}) collective-permute-start(bf16[7,128,1024]{2,1,0:T(8,128)(2,1)} %get-tuple-element.22), channel_id=1, source_target_pairs={{0,8},{8,16},{16,24},{1,9},{9,17},{17,25},{2,10},{10,18},{18,26},{... | collective-permute-start | bytes 5505032 | tf_op jit(solution)/shard_map/ppermute | solution.py:25
  13.1 25.3 %collective-permute-start.8 = (bf16[7,128,1024]{2,1,0:T(8,128)(2,1)}, bf16[7,128,1024]{2,1,0:T(8,128)(2,1)}, u32[]{:S(2)}, u32[]{:S(2)}) collective-permute-start(bf16[7,128,1024]{2,1,0:T(8,128)(2,1)} %get-tuple-element.23), channel_id=1, source_target_pairs={{8,0},{16,8},{24,16},{9,1},{17,9},{25,17},{10,2},{18,10},{26,18},{... | collective-permute-start | bytes 5505032 | tf_op jit(solution)/shard_map/ppermute | solution.py:25
  18.9 4.0 %collective-permute-start.2 = (bf16[2,30,2,128]{3,2,1,0:T(2,128)(2,1)S(1)}, bf16[2,30,2,128]{3,2,1,0:T(2,128)(2,1)S(1)}, u32[]{:S(2)}, u32[]{:S(2)}) collective-permute-start(bf16[2,30,2,128]{3,2,1,0:T(2,128)(2,1)S(1)} %broadcast_select_fusion), channel_id=1, source_target_pairs={{0,1},{1,0},{2,3},{3,2},{4,5},{5,4},{6,7},{7,6},{8,9},{9,8},{10,11... | collective-permute-start | bytes 92168 | tf_op jit(solution)/shard_map/ppermute | solution.py:473
  20.7 8.7 %copy-start.3 = (s32[2,1]{0,1:T(1,128)S(1)}, s32[2,1]{0,1:T(1,128)}, u32[]{:S(2)}) copy-start(s32[2,1]{0,1:T(1,128)} %param.9) | copy-start | bytes 28
  24.5 10.0 %collective-permute-start.6 = (bf16[2,30,2,1152]{3,2,1,0:T(2,128)(2,1)S(1)}, bf16[2,30,2,1152]{3,2,1,0:T(2,128)(2,1)S(1)}, u32[]{:S(2)}, u32[]{:S(2)}) collective-permute-start(bf16[2,30,2,1152]{3,2,1,0:T(2,128)(2,1)S(1)} %get-tuple-element.36), channel_id=1, source_target_pairs={{0,2},{2,4},{4,6},{1,3},{3,5},{5,7},{8,10},{10,12},{12,14},{9,11},... | collective-permute-start | bytes 829448 | tf_op jit(solution)/shard_map/ppermute | solution.py:25
  28.0 10.3 %collective-permute-start.5 = (bf16[2,30,2,1152]{3,2,1,0:T(2,128)(2,1)S(1)}, bf16[2,30,2,1152]{3,2,1,0:T(2,128)(2,1)S(1)}, u32[]{:S(2)}, u32[]{:S(2)}) collective-permute-start(bf16[2,30,2,1152]{3,2,1,0:T(2,128)(2,1)S(1)} %get-tuple-element.37), channel_id=1, source_target_pairs={{2,0},{4,2},{6,4},{3,1},{5,3},{7,5},{10,8},{12,10},{14,12},{11,9},... | collective-permute-start | bytes 829448 | tf_op jit(solution)/shard_map/ppermute | solution.py:25
  32.6 34.0 %collective-permute-start.3 = (bf16[7,128,1024]{2,1,0:T(8,128)(2,1)}, bf16[7,128,1024]{2,1,0:T(8,128)(2,1)S(1)}, u32[]{:S(2)}, u32[]{:S(2)}) collective-permute-start(bf16[7,128,1024]{2,1,0:T(8,128)(2,1)} %get-tuple-element.19), channel_id=1, source_target_pairs={{0,8},{8,16},{16,24},{1,9},{9,17},{17,25},{2,10},{10,18},{18,26},{... | collective-permute-start | bytes 5505032 | tf_op jit(solution)/shard_map/ppermute | solution.py:25
  34.5 32.1 %collective-permute-start.4 = (bf16[7,128,1024]{2,1,0:T(8,128)(2,1)}, bf16[7,128,1024]{2,1,0:T(8,128)(2,1)S(1)}, u32[]{:S(2)}, u32[]{:S(2)}) collective-permute-start(bf16[7,128,1024]{2,1,0:T(8,128)(2,1)} %get-tuple-element.20), channel_id=1, source_target_pairs={{8,0},{16,8},{24,16},{9,1},{17,9},{25,17},{10,2},{18,10},{26,18},{... | collective-permute-start | bytes 5505032 | tf_op jit(solution)/shard_map/ppermute | solution.py:25
  61.0 27.8 %collective-permute-start.9 = (bf16[128,256]{1,0:T(8,128)(2,1)S(1)}, bf16[128,256]{1,0:T(8,128)(2,1)S(1)}, u32[]{:S(2)}, u32[]{:S(2)}) collective-permute-start(bf16[128,256]{1,0:T(8,128)(2,1)S(1)} %get-tuple-element.27), channel_id=1, source_target_pairs={{0,7},{1,6},{2,5},{3,4},{4,3},{5,2},{6,1},{7,0},{8,15},{9,14},{10,... | collective-permute-start | bytes 196616 | tf_op jit(solution)/shard_map/ppermute | solution.py:502

commit v15 on v14

--- a/solution.py
+++ b/solution.py
@@ -200,33 +200,34 @@
 
     @pl.when(at == steps_1 + steps_2)
     def _():
-        slot_count = flat.shape[0] // PATCH
-
+        slot_count = flat.shape[0]
         lane = iota((PATCH, TILE), 1)
-
-        def some(i8, unused):
-            for j in range(16):
-                i = i8 * 16 + j
+        low_bits = PATCH - 1
+        bits = low_bits.bit_length()
+        size = PATCH * PATCH
+        repeat = (iota((TILE, size), 1) & low_bits == iota((TILE, size), 0)).astype(bf16)
+        mine = iota((size, size), 1) >> bits == iota((size, size), 0) & low_bits
+        owner = (iota((PATCH, size), 1) >> bits == iota((PATCH, size), 0)).astype(bf16)
+
+        def some(i16, unused):
+            parts = []
+            for j in range(PATCH):
+                i = i16 * PATCH + j
                 frame, row, tile = spots_ref[0, i], spots_ref[1, i], spots_ref[2, i]
                 beside, offset = spots_ref[3, i], spots_ref[4, i]
                 here = kept[frame, tile, pl.ds(row, PATCH), :]
                 there = kept[frame, beside, pl.ds(row, PATCH), :]
                 part = jnp.where(lane >= offset, here, there)
-                part = pltpu.roll(part, (TILE - offset) & (TILE - 1), 1)
-                flat[pl.ds(pl.multiple_of(i * PATCH, PATCH), PATCH), :] = part.astype(bf16)
+                parts.append(pltpu.roll(part, (TILE - offset) & (TILE - 1), 1))
+            rows = jnp.concatenate(parts, axis=0).astype(bf16)
+            rows = jnp.dot(rows, repeat, preferred_element_type=f32)
+            rows = jnp.where(mine, rows, 0.0).astype(bf16)
+            place = pl.ds(pl.multiple_of(i16 * PATCH, PATCH), PATCH)
+            flat[place, :] = jnp.dot(owner, rows, preferred_element_type=f32)
             return unused
 
-        lax.fori_loop(0, slot_count // 16, some, 0)
-        low_bits = PATCH - 1
-        bits = low_bits.bit_length()
-        shape = (TILE, PATCH * PATCH)
-        repeat = (iota(shape, 1) & low_bits == iota(shape, 0)).astype(bf16)
-        rows = jnp.dot(flat[...], repeat, preferred_element_type=f32)
-        mine = iota(rows.shape, 1) >> bits == iota(rows.shape, 0) & low_bits
-        rows = jnp.where(mine, rows, 0.0).astype(bf16)
-        shape = (slot_count, rows.shape[0])
-        owner = (iota(shape, 1) >> bits == iota(shape, 0)).astype(bf16)
-        values = jnp.dot(owner, rows, preferred_element_type=f32)
+        lax.fori_loop(0, slot_count // PATCH, some, 0)
+        values = flat[...]
         mean = jnp.sum(values, axis=1, keepdims=True) / (PATCH * PATCH)
         centered = values - mean
         spread = jnp.sum(centered * centered, axis=1, keepdims=True) / (PATCH * PATCH)
@@ -440,7 +441,7 @@
             pltpu.VMEM((frame_count, wide // TILE, EDGE, TILE), f32),
             pltpu.VMEM((frame_count, wide // TILE, EDGE, TILE), f32),
             pltpu.VMEM((frame_count, col_count // TILE, row_count, TILE), f32),
-            pltpu.VMEM((slot_count * PATCH, TILE), bf16),
+            pltpu.VMEM((slot_count, PATCH * PATCH), f32),
         ],
         input_output_aliases=aliases,
         compiler_params=pltpu.CompilerParams(vmem_limit_bytes=40 * 1024 * 1024),

time: 90.8 us -> 93.2 us (1.026)
  Pallas kernels: 52.8 us -> 55.2 us
    pallas_call x2, Pallas kernels: 44.7 us -> 47.1 us  [run_slab(): pl.pallas_call(body, grid=(steps_1 + steps_2 + 1,), in_specs=in_specs, ou...]
  transfers between devices with their start and end apart: 10 -> 10, of which waited for: 1 -> 1; matrix products, arithmetic and copies ran while one was open for 4% -> 4% of each run, Pallas kernels for 53% -> 55%
where the time goes in v15:
time: 93.2 us; the launch traced here: 91.8 us
  Pallas kernels  55.2 us (59%)
  starting transfers between devices  28.7 us (31%)
  waiting for transfers between devices  2.21 us (2%)
  local copies, waits for them, and re-layouts  2.03 us (2%)
  matrix products  1.68 us (2%)
  other arithmetic  1.03 us (1%)
  between operations  0.98 us (1%)
    pallas_call x2, Pallas kernels, run_slab(): pl.pallas_call(body, grid=(steps_1 + steps_2 + 1,), in_specs=in_specs, ou...  47.1 us
    ppermute x8, starting transfers between devices, shifted(): return lax.ppermute(block, axis, route)  21.5 us
    ppermute x1, starting transfers between devices, shards(): lax.ppermute(second, ('row', 'col'), [(i, count - 1 - i) for i in range(c...  5.63 us
    pallas_call x1, Pallas kernels, cut(): pl.pallas_call(cut_kernel, in_specs=[anywhere], out_specs=[near] * 3 + [a...  4.92 us
    pallas_call x1, Pallas kernels, late_cut(): pl.pallas_call(late_kernel, in_specs=[anywhere], out_specs=[anywhere] * 2...  3.12 us
    ppermute x1, waiting for transfers between devices, shards(): sides = lax.ppermute(sides, 'col', [(0, 1), (1, 0)])  2.18 us
  transfers between devices with their start and end apart: 10, of which 1 were waited for; matrix products, arithmetic and copies ran while one was open for 4% of the time, Pallas kernels for 55%

profile of v15, /device:TPU:2, one launch (start us, length us, event | category | flops | bytes accessed | tf_op | source)
XLA Modules:
  0.0 91.8 jit_solution(2144078143865626980)
XLA Ops:
  0.6 0.0 copy-start
  0.6 0.0 copy-start.1
  0.7 0.0 copy-start.2
  0.7 4.9 %cut.1 = (bf16[2,16,4,1152]{3,2,1,0:T(4,128)(2,1)}, bf16[2,7,4,1152]{3,2,1,0:T(4,128)(2,1)}, bf16[2,7,4,1152]{3,2,1,0:T(4,128)(2,1)}, bf16[7,128,1024]{2,1,0:T(8,128)(2,1)}, bf16[7,128,1024]{2,1,0:T(8,128)(2,1)}) custom-call(bf16[2,16,128,1024]{3,2,1,0:T(8,128)(2,1)} %refs_4_.3), custom_call_target="tpu_custom_call" | custom-call | tf_op jit(solution)/shard_map/cut/pallas_call | solution.py:347
  5.6 1.9 %collective-permute-start = (bf16[2,7,4,1152]{3,2,1,0:T(4,128)(2,1)}, bf16[2,7,4,1152]{3,2,1,0:T(4,128)(2,1)S(1)}, u32[]{:S(2)}, u32[]{:S(2)}) collective-permute-start(bf16[2,7,4,1152]{3,2,1,0:T(4,128)(2,1)} %get-tuple-element.15), channel_id=1, source_target_pairs={{0,8},{8,16},{16,24},{1,9},{9,17},{17,25},{2,10},{10,18},{18,26},{... | collective-permute-start | bytes 387080 | tf_op jit(solution)/shard_map/ppermute | solution.py:25
  7.5 3.6 %collective-permute-start.1 = (bf16[2,7,4,1152]{3,2,1,0:T(4,128)(2,1)}, bf16[2,7,4,1152]{3,2,1,0:T(4,128)(2,1)S(1)}, u32[]{:S(2)}, u32[]{:S(2)}) collective-permute-start(bf16[2,7,4,1152]{3,2,1,0:T(4,128)(2,1)} %get-tuple-element.17), channel_id=1, source_target_pairs={{8,0},{16,8},{24,16},{9,1},{17,9},{25,17},{10,2},{18,10},{26,18},{... | collective-permute-start | bytes 387080 | tf_op jit(solution)/shard_map/ppermute | solution.py:25
  11.2 1.9 %collective-permute-start.7 = (bf16[7,128,1024]{2,1,0:T(8,128)(2,1)}, bf16[7,128,1024]{2,1,0:T(8,128)(2,1)}, u32[]{:S(2)}, u32[]{:S(2)}) collective-permute-start(bf16[7,128,1024]{2,1,0:T(8,128)(2,1)} %get-tuple-element.22), channel_id=1, source_target_pairs={{0,8},{8,16},{16,24},{1,9},{9,17},{17,25},{2,10},{10,18},{18,26},{... | collective-permute-start | bytes 5505032 | tf_op jit(solution)/shard_map/ppermute | solution.py:25
  13.1 3.6 %collective-permute-start.8 = (bf16[7,128,1024]{2,1,0:T(8,128)(2,1)}, bf16[7,128,1024]{2,1,0:T(8,128)(2,1)}, u32[]{:S(2)}, u32[]{:S(2)}) collective-permute-start(bf16[7,128,1024]{2,1,0:T(8,128)(2,1)} %get-tuple-element.23), channel_id=1, source_target_pairs={{8,0},{16,8},{24,16},{9,1},{17,9},{25,17},{10,2},{18,10},{26,18},{... | collective-permute-start | bytes 5505032 | tf_op jit(solution)/shard_map/ppermute | solution.py:25
  16.8 0.0 copy-done
  16.8 0.1 copy.25
  16.9 0.1 subtract_add_fusion
  17.0 0.1 select_reduce_fusion
  17.1 0.0 copy-done.1
  17.2 0.0 copy-done.2
  17.2 0.2 select_reduce_fusion.2
  17.4 0.1 reduce-precision_convert_fusion.1
  17.5 0.1 pad_maximum_fusion.refs_2_
  17.6 0.0 collective-permute-done
  17.7 1.1 %constant_dynamic-update-slice_fusion.1 = bf16[2,30,4,1152]{3,2,1,0:T(4,128)(2,1)S(1)} fusion(bf16[2,30,4,1152]{3,2,1,0:T(4,128)(2,1)S(1)} %constant_dynamic-update-slice_fusion.2, bf16[2,16,4,1152]{3,2,1,0:T(4,128)(2,1)} %get-tuple-element.16), kind=kLoop, calls=%fused_computation.18 | loop fusion | bytes 589824
  18.8 0.0 collective-permute-done.1
  18.8 0.1 constant_dynamic-update-slice_fusion
  18.9 0.1 broadcast_select_fusion
  18.9 1.6 %collective-permute-start.2 = (bf16[2,30,2,128]{3,2,1,0:T(2,128)(2,1)S(1)}, bf16[2,30,2,128]{3,2,1,0:T(2,128)(2,1)S(1)}, u32[]{:S(2)}, u32[]{:S(2)}) collective-permute-start(bf16[2,30,2,128]{3,2,1,0:T(2,128)(2,1)S(1)} %broadcast_select_fusion), channel_id=1, source_target_pairs={{0,1},{1,0},{2,3},{3,2},{4,5},{5,4},{6,7},{7,6},{8,9},{9,8},{10,11... | collective-permute-start | bytes 92168 | tf_op jit(solution)/shard_map/ppermute | solution.py:474
  20.5 0.2 slice.51
  20.7 0.0 copy-start.3
  20.7 2.2 %collective-permute-done.2 = bf16[2,30,2,128]{3,2,1,0:T(2,128)(2,1)S(1)} collective-permute-done((bf16[2,30,2,128]{3,2,1,0:T(2,128)(2,1)S(1)}, bf16[2,30,2,128]{3,2,1,0:T(2,128)(2,1)S(1)}, u32[]{:S(2)}, u32[]{:S(2)}) %collective-permute-start.2) | collective-permute-done | bytes 30752 | tf_op jit(solution)/shard_map/ppermute | solution.py:474
  22.9 0.9 fusion.4.refs_6_
  23.8 0.1 fusion.7
  23.8 0.3 maximum_maximum_fusion
  24.1 0.4 fusion.8
  24.5 3.5 %collective-permute-start.6 = (bf16[2,30,2,1152]{3,2,1,0:T(2,128)(2,1)S(1)}, bf16[2,30,2,1152]{3,2,1,0:T(2,128)(2,1)S(1)}, u32[]{:S(2)}, u32[]{:S(2)}) collective-permute-start(bf16[2,30,2,1152]{3,2,1,0:T(2,128)(2,1)S(1)} %get-tuple-element.36), channel_id=1, source_target_pairs={{0,2},{2,4},{4,6},{1,3},{3,5},{5,7},{8,10},{10,12},{12,14},{9,11},... | collective-permute-start | bytes 829448 | tf_op jit(solution)/shard_map/ppermute | solution.py:25
  28.0 1.3 %collective-permute-start.5 = (bf16[2,30,2,1152]{3,2,1,0:T(2,128)(2,1)S(1)}, bf16[2,30,2,1152]{3,2,1,0:T(2,128)(2,1)S(1)}, u32[]{:S(2)}, u32[]{:S(2)}) collective-permute-start(bf16[2,30,2,1152]{3,2,1,0:T(2,128)(2,1)S(1)} %get-tuple-element.37), channel_id=1, source_target_pairs={{2,0},{4,2},{6,4},{3,1},{5,3},{7,5},{10,8},{12,10},{14,12},{11,9},... | collective-permute-start | bytes 829448 | tf_op jit(solution)/shard_map/ppermute | solution.py:25
  29.4 0.0 copy-done.3
  29.4 0.1 stack_broadcast_in_dim.2
  29.5 3.1 %late_cut.1 = (bf16[7,128,1024]{2,1,0:T(8,128)(2,1)}, bf16[7,128,1024]{2,1,0:T(8,128)(2,1)}) custom-call(bf16[2,16,128,1024]{3,2,1,0:T(8,128)(2,1)} %refs_4_.3), custom_call_target="tpu_custom_call" | custom-call | bytes 9000000 | tf_op jit(solution)/shard_map/late_cut/pallas_call | solution.py:369
  32.6 1.9 %collective-permute-start.3 = (bf16[7,128,1024]{2,1,0:T(8,128)(2,1)}, bf16[7,128,1024]{2,1,0:T(8,128)(2,1)S(1)}, u32[]{:S(2)}, u32[]{:S(2)}) collective-permute-start(bf16[7,128,1024]{2,1,0:T(8,128)(2,1)} %get-tuple-element.19), channel_id=1, source_target_pairs={{0,8},{8,16},{16,24},{1,9},{9,17},{17,25},{2,10},{10,18},{18,26},{... | collective-permute-start | bytes 5505032 | tf_op jit(solution)/shard_map/ppermute | solution.py:25
  34.5 0.0 collective-permute-done.6.refs_8_
  34.5 3.6 %collective-permute-start.4 = (bf16[7,128,1024]{2,1,0:T(8,128)(2,1)}, bf16[7,128,1024]{2,1,0:T(8,128)(2,1)S(1)}, u32[]{:S(2)}, u32[]{:S(2)}) collective-permute-start(bf16[7,128,1024]{2,1,0:T(8,128)(2,1)} %get-tuple-element.20), channel_id=1, source_target_pairs={{8,0},{16,8},{24,16},{9,1},{17,9},{25,17},{10,2},{18,10},{26,18},{... | collective-permute-start | bytes 5505032 | tf_op jit(solution)/shard_map/ppermute | solution.py:25
  38.2 0.0 collective-permute-done.5.refs_7_
  38.2 0.0 collective-permute-done.7.refs_3_
  38.2 0.0 collective-permute-done.8.refs_5_
  38.2 23.8 %slab_1.1 = (bf16[2,16,128,1024]{3,2,1,0:T(8,128)(2,1)}, bf16[128,256]{1,0:T(8,128)(2,1)S(1)}) custom-call(s32[6,128]{1,0:T(8,128)S(1)} %get-tuple-element.42.refs_0_, bf16[32,30]{1,0:T(8,128)(2,1)S(1)} %bitcast.29, bf16[160,144]{1,0:T(8,128)(2,1)S(1)} %pad_maximum_fusion.refs_2_, bf16[7,128,1024]{2,1,0:T(8,128)(2,1)} %collective-permute-done.7.refs_3_, ...), custom_call_target="tpu_custom_call" | custom-call | flops 20000000000 | bytes 16000000 | tf_op jit(solution)/shard_map/slab_1/pallas_call | solution.py:422
  62.0 5.6 %collective-permute-start.9 = (bf16[128,256]{1,0:T(8,128)(2,1)S(1)}, bf16[128,256]{1,0:T(8,128)(2,1)S(1)}, u32[]{:S(2)}, u32[]{:S(2)}) collective-permute-start(bf16[128,256]{1,0:T(8,128)(2,1)S(1)} %get-tuple-element.27), channel_id=1, source_target_pairs={{0,7},{1,6},{2,5},{3,4},{4,3},{5,2},{6,1},{7,0},{8,15},{9,14},{10,... | collective-permute-start | bytes 196616 | tf_op jit(solution)/shard_map/ppermute | solution.py:503
  67.7 0.0 collective-permute-done.3.refs_3_
  67.7 0.0 collective-permute-done.4.refs_5_
  67.7 23.3 %slab_0.1 = (bf16[2,16,128,1024]{3,2,1,0:T(8,128)(2,1)}, bf16[128,256]{1,0:T(8,128)(2,1)S(1)}) custom-call(s32[6,128]{1,0:T(8,128)S(1)} %get-tuple-element.43.refs_0_, bf16[32,30]{1,0:T(8,128)(2,1)S(1)} %bitcast.30, bf16[160,144]{1,0:T(8,128)(2,1)S(1)} %pad_maximum_fusion.refs_2_, ...), custom_call_target="tpu_custom_call", output_to_operand_aliasing={{0}: (9, {})} | custom-call | flops 20000000000 | bytes 16000000 | tf_op jit(solution)/shard_map/slab_0/pallas_call | solution.py:422
  91.0 0.0 collective-permute-done.9
  91.0 0.8 convolution_multiply_fusion
  (14 shorter events, 0.2 us)
Async XLA Ops:
  0.6 16.2 %copy-start = (f32[5,5]{1,0:T(8,128)S(1)}, f32[5,5]{1,0:T(8,128)}, u32[]{:S(2)}) copy-start(f32[5,5]{1,0:T(8,128)} %param.7) | copy-start | bytes 304
  0.6 16.5 %copy-start.1 = (s32[2,3,128]{2,0,1:T(2,128)S(1)}, s32[2,3,128]{2,0,1:T(2,128)}, u32[]{:S(2)}) copy-start(s32[2,3,128]{2,0,1:T(2,128)} %param.8) | copy-start | bytes 9220
  0.7 16.5 %copy-start.2 = (f32[15]{0:T(128)S(1)}, f32[15]{0:T(128)}, u32[]{:S(2)}) copy-start(f32[15]{0:T(128)} %param.6) | copy-start | bytes 184
  5.6 12.0 %collective-permute-start = (bf16[2,7,4,1152]{3,2,1,0:T(4,128)(2,1)}, bf16[2,7,4,1152]{3,2,1,0:T(4,128)(2,1)S(1)}, u32[]{:S(2)}, u32[]{:S(2)}) collective-permute-start(bf16[2,7,4,1152]{3,2,1,0:T(4,128)(2,1)} %get-tuple-element.15), channel_id=1, source_target_pairs={{0,8},{8,16},{16,24},{1,9},{9,17},{17,25},{2,10},{10,18},{18,26},{... | collective-permute-start | bytes 387080 | tf_op jit(solution)/shard_map/ppermute | solution.py:25
  7.5 11.3 %collective-permute-start.1 = (bf16[2,7,4,1152]{3,2,1,0:T(4,128)(2,1)}, bf16[2,7,4,1152]{3,2,1,0:T(4,128)(2,1)S(1)}, u32[]{:S(2)}, u32[]{:S(2)}) collective-permute-start(bf16[2,7,4,1152]{3,2,1,0:T(4,128)(2,1)} %get-tuple-element.17), channel_id=1, source_target_pairs={{8,0},{16,8},{24,16},{9,1},{17,9},{25,17},{10,2},{18,10},{26,18},{... | collective-permute-start | bytes 387080 | tf_op jit(solution)/shard_map/ppermute | solution.py:25
  11.2 27.0 %collective-permute-start.7 = (bf16[7,128,1024]{2,1,0:T(8,128)(2,1)}, bf16[7,128,1024]{2,1,0:T(8,128)(2,1)}, u32[]{:S(2)}, u32[]{:S(2)}) collective-permute-start(bf16[7,128,1024]{2,1,0:T(8,128)(2,1)} %get-tuple-element.22), channel_id=1, source_target_pairs={{0,8},{8,16},{16,24},{1,9},{9,17},{17,25},{2,10},{10,18},{18,26},{... | collective-permute-start | bytes 5505032 | tf_op jit(solution)/shard_map/ppermute | solution.py:25
  13.1 25.1 %collective-permute-start.8 = (bf16[7,128,1024]{2,1,0:T(8,128)(2,1)}, bf16[7,128,1024]{2,1,0:T(8,128)(2,1)}, u32[]{:S(2)}, u32[]{:S(2)}) collective-permute-start(bf16[7,128,1024]{2,1,0:T(8,128)(2,1)} %get-tuple-element.23), channel_id=1, source_target_pairs={{8,0},{16,8},{24,16},{9,1},{17,9},{25,17},{10,2},{18,10},{26,18},{... | collective-permute-start | bytes 5505032 | tf_op jit(solution)/shard_map/ppermute | solution.py:25
  18.9 4.0 %collective-permute-start.2 = (bf16[2,30,2,128]{3,2,1,0:T(2,128)(2,1)S(1)}, bf16[2,30,2,128]{3,2,1,0:T(2,128)(2,1)S(1)}, u32[]{:S(2)}, u32[]{:S(2)}) collective-permute-start(bf16[2,30,2,128]{3,2,1,0:T(2,128)(2,1)S(1)} %broadcast_select_fusion), channel_id=1, source_target_pairs={{0,1},{1,0},{2,3},{3,2},{4,5},{5,4},{6,7},{7,6},{8,9},{9,8},{10,11... | collective-permute-start | bytes 92168 | tf_op jit(solution)/shard_map/ppermute | solution.py:474
  20.7 8.7 %copy-start.3 = (s32[2,1]{0,1:T(1,128)S(1)}, s32[2,1]{0,1:T(1,128)}, u32[]{:S(2)}) copy-start(s32[2,1]{0,1:T(1,128)} %param.9) | copy-start | bytes 28
  24.5 10.0 %collective-permute-start.6 = (bf16[2,30,2,1152]{3,2,1,0:T(2,128)(2,1)S(1)}, bf16[2,30,2,1152]{3,2,1,0:T(2,128)(2,1)S(1)}, u32[]{:S(2)}, u32[]{:S(2)}) collective-permute-start(bf16[2,30,2,1152]{3,2,1,0:T(2,128)(2,1)S(1)} %get-tuple-element.36), channel_id=1, source_target_pairs={{0,2},{2,4},{4,6},{1,3},{3,5},{5,7},{8,10},{10,12},{12,14},{9,11},... | collective-permute-start | bytes 829448 | tf_op jit(solution)/shard_map/ppermute | solution.py:25
  28.0 10.2 %collective-permute-start.5 = (bf16[2,30,2,1152]{3,2,1,0:T(2,128)(2,1)S(1)}, bf16[2,30,2,1152]{3,2,1,0:T(2,128)(2,1)S(1)}, u32[]{:S(2)}, u32[]{:S(2)}) collective-permute-start(bf16[2,30,2,1152]{3,2,1,0:T(2,128)(2,1)S(1)} %get-tuple-element.37), channel_id=1, source_target_pairs={{2,0},{4,2},{6,4},{3,1},{5,3},{7,5},{10,8},{12,10},{14,12},{11,9},... | collective-permute-start | bytes 829448 | tf_op jit(solution)/shard_map/ppermute | solution.py:25
  32.6 35.1 %collective-permute-start.3 = (bf16[7,128,1024]{2,1,0:T(8,128)(2,1)}, bf16[7,128,1024]{2,1,0:T(8,128)(2,1)S(1)}, u32[]{:S(2)}, u32[]{:S(2)}) collective-permute-start(bf16[7,128,1024]{2,1,0:T(8,128)(2,1)} %get-tuple-element.19), channel_id=1, source_target_pairs={{0,8},{8,16},{16,24},{1,9},{9,17},{17,25},{2,10},{10,18},{18,26},{... | collective-permute-start | bytes 5505032 | tf_op jit(solution)/shard_map/ppermute | solution.py:25
  34.5 33.1 %collective-permute-start.4 = (bf16[7,128,1024]{2,1,0:T(8,128)(2,1)}, bf16[7,128,1024]{2,1,0:T(8,128)(2,1)S(1)}, u32[]{:S(2)}, u32[]{:S(2)}) collective-permute-start(bf16[7,128,1024]{2,1,0:T(8,128)(2,1)} %get-tuple-element.20), channel_id=1, source_target_pairs={{8,0},{16,8},{24,16},{9,1},{17,9},{25,17},{10,2},{18,10},{26,18},{... | collective-permute-start | bytes 5505032 | tf_op jit(solution)/shard_map/ppermute | solution.py:25
  62.0 29.0 %collective-permute-start.9 = (bf16[128,256]{1,0:T(8,128)(2,1)S(1)}, bf16[128,256]{1,0:T(8,128)(2,1)S(1)}, u32[]{:S(2)}, u32[]{:S(2)}) collective-permute-start(bf16[128,256]{1,0:T(8,128)(2,1)S(1)} %get-tuple-element.27), channel_id=1, source_target_pairs={{0,7},{1,6},{2,5},{3,4},{4,3},{5,2},{6,1},{7,0},{8,15},{9,14},{10,... | collective-permute-start | bytes 196616 | tf_op jit(solution)/shard_map/ppermute | solution.py:503

commit v16 on v14

--- a/solution.py
+++ b/solution.py
@@ -383,7 +383,7 @@
 def run_slab(slab, smoothed, spots, taps, w2, low, frames, high, edge, below, above):
     _, frame_count, row_count, col_count = frames.shape
     slot_count = spots.shape[1]
-    row_step, frame_step = 32, 8
+    row_step, frame_step = 64, 8
     steps_1 = row_count // row_step
     steps_2 = frame_count // frame_step
     wide = col_count + TILE

time: 90.8 us -> 90.1 us (level)
  no operation moved by 1% of the time
where the time goes in v16:
time: 90.1 us; the launch traced here: 89 us
  Pallas kernels  52.2 us (58%)
  starting transfers between devices  28.9 us (32%)
  waiting for transfers between devices  2.21 us (2%)
  local copies, waits for them, and re-layouts  2.03 us (2%)
  matrix products  1.68 us (2%)
  other arithmetic  1.03 us (1%)
  between operations  0.98 us (1%)
    pallas_call x2, Pallas kernels, run_slab(): pl.pallas_call(body, grid=(steps_1 + steps_2 + 1,), in_specs=in_specs, ou...  44.1 us
    ppermute x8, starting transfers between devices, shifted(): return lax.ppermute(block, axis, route)  21.7 us
    ppermute x1, starting transfers between devices, shards(): lax.ppermute(second, ('row', 'col'), [(i, count - 1 - i) for i in range(c...  5.61 us
    pallas_call x1, Pallas kernels, cut(): pl.pallas_call(cut_kernel, in_specs=[anywhere], out_specs=[near] * 3 + [a...  4.92 us
    pallas_call x1, Pallas kernels, late_cut(): pl.pallas_call(late_kernel, in_specs=[anywhere], out_specs=[anywhere] * 2...  3.12 us
    ppermute x1, waiting for transfers between devices, shards(): sides = lax.ppermute(sides, 'col', [(0, 1), (1, 0)])  2.18 us
  transfers between devices with their start and end apart: 10, of which 1 were waited for; matrix products, arithmetic and copies ran while one was open for 4% of the time, Pallas kernels for 53%

profile of v16, /device:TPU:2, one launch (start us, length us, event | category | flops | bytes accessed | tf_op | source)
XLA Modules:
  0.0 89.0 jit_solution(12828638714581620474)
XLA Ops:
  0.6 0.0 copy-start
  0.6 0.0 copy-start.1
  0.7 0.0 copy-start.2
  0.7 4.9 %cut.1 = (bf16[2,16,4,1152]{3,2,1,0:T(4,128)(2,1)}, bf16[2,7,4,1152]{3,2,1,0:T(4,128)(2,1)}, bf16[2,7,4,1152]{3,2,1,0:T(4,128)(2,1)}, bf16[7,128,1024]{2,1,0:T(8,128)(2,1)}, bf16[7,128,1024]{2,1,0:T(8,128)(2,1)}) custom-call(bf16[2,16,128,1024]{3,2,1,0:T(8,128)(2,1)} %refs_4_.3), custom_call_target="tpu_custom_call" | custom-call | tf_op jit(solution)/shard_map/cut/pallas_call | solution.py:346
  5.6 1.9 %collective-permute-start = (bf16[2,7,4,1152]{3,2,1,0:T(4,128)(2,1)}, bf16[2,7,4,1152]{3,2,1,0:T(4,128)(2,1)S(1)}, u32[]{:S(2)}, u32[]{:S(2)}) collective-permute-start(bf16[2,7,4,1152]{3,2,1,0:T(4,128)(2,1)} %get-tuple-element.15), channel_id=1, source_target_pairs={{0,8},{8,16},{16,24},{1,9},{9,17},{17,25},{2,10},{10,18},{18,26},{... | collective-permute-start | bytes 387080 | tf_op jit(solution)/shard_map/ppermute | solution.py:25
  7.5 3.6 %collective-permute-start.1 = (bf16[2,7,4,1152]{3,2,1,0:T(4,128)(2,1)}, bf16[2,7,4,1152]{3,2,1,0:T(4,128)(2,1)S(1)}, u32[]{:S(2)}, u32[]{:S(2)}) collective-permute-start(bf16[2,7,4,1152]{3,2,1,0:T(4,128)(2,1)} %get-tuple-element.17), channel_id=1, source_target_pairs={{8,0},{16,8},{24,16},{9,1},{17,9},{25,17},{10,2},{18,10},{26,18},{... | collective-permute-start | bytes 387080 | tf_op jit(solution)/shard_map/ppermute | solution.py:25
  11.2 1.9 %collective-permute-start.7 = (bf16[7,128,1024]{2,1,0:T(8,128)(2,1)}, bf16[7,128,1024]{2,1,0:T(8,128)(2,1)}, u32[]{:S(2)}, u32[]{:S(2)}) collective-permute-start(bf16[7,128,1024]{2,1,0:T(8,128)(2,1)} %get-tuple-element.22), channel_id=1, source_target_pairs={{0,8},{8,16},{16,24},{1,9},{9,17},{17,25},{2,10},{10,18},{18,26},{... | collective-permute-start | bytes 5505032 | tf_op jit(solution)/shard_map/ppermute | solution.py:25
  13.1 3.6 %collective-permute-start.8 = (bf16[7,128,1024]{2,1,0:T(8,128)(2,1)}, bf16[7,128,1024]{2,1,0:T(8,128)(2,1)}, u32[]{:S(2)}, u32[]{:S(2)}) collective-permute-start(bf16[7,128,1024]{2,1,0:T(8,128)(2,1)} %get-tuple-element.23), channel_id=1, source_target_pairs={{8,0},{16,8},{24,16},{9,1},{17,9},{25,17},{10,2},{18,10},{26,18},{... | collective-permute-start | bytes 5505032 | tf_op jit(solution)/shard_map/ppermute | solution.py:25
  16.8 0.0 copy-done
  16.8 0.1 copy.25
  16.9 0.1 subtract_add_fusion
  17.0 0.1 select_reduce_fusion
  17.1 0.0 copy-done.1
  17.2 0.0 copy-done.2
  17.2 0.2 select_reduce_fusion.2
  17.4 0.1 reduce-precision_convert_fusion.1
  17.5 0.1 pad_maximum_fusion.refs_2_
  17.6 0.0 collective-permute-done
  17.7 1.1 %constant_dynamic-update-slice_fusion.1 = bf16[2,30,4,1152]{3,2,1,0:T(4,128)(2,1)S(1)} fusion(bf16[2,30,4,1152]{3,2,1,0:T(4,128)(2,1)S(1)} %constant_dynamic-update-slice_fusion.2, bf16[2,16,4,1152]{3,2,1,0:T(4,128)(2,1)} %get-tuple-element.16), kind=kLoop, calls=%fused_computation.18 | loop fusion | bytes 589824
  18.8 0.0 collective-permute-done.1
  18.8 0.1 constant_dynamic-update-slice_fusion
  18.9 0.1 broadcast_select_fusion
  18.9 1.6 %collective-permute-start.2 = (bf16[2,30,2,128]{3,2,1,0:T(2,128)(2,1)S(1)}, bf16[2,30,2,128]{3,2,1,0:T(2,128)(2,1)S(1)}, u32[]{:S(2)}, u32[]{:S(2)}) collective-permute-start(bf16[2,30,2,128]{3,2,1,0:T(2,128)(2,1)S(1)} %broadcast_select_fusion), channel_id=1, source_target_pairs={{0,1},{1,0},{2,3},{3,2},{4,5},{5,4},{6,7},{7,6},{8,9},{9,8},{10,11... | collective-permute-start | bytes 92168 | tf_op jit(solution)/shard_map/ppermute | solution.py:473
  20.5 0.2 slice.51
  20.7 0.0 copy-start.3
  20.7 2.2 %collective-permute-done.2 = bf16[2,30,2,128]{3,2,1,0:T(2,128)(2,1)S(1)} collective-permute-done((bf16[2,30,2,128]{3,2,1,0:T(2,128)(2,1)S(1)}, bf16[2,30,2,128]{3,2,1,0:T(2,128)(2,1)S(1)}, u32[]{:S(2)}, u32[]{:S(2)}) %collective-permute-start.2) | collective-permute-done | bytes 30752 | tf_op jit(solution)/shard_map/ppermute | solution.py:473
  22.9 0.9 fusion.4.refs_6_
  23.8 0.1 fusion.7
  23.8 0.3 maximum_maximum_fusion
  24.1 0.4 fusion.8
  24.5 3.5 %collective-permute-start.6 = (bf16[2,30,2,1152]{3,2,1,0:T(2,128)(2,1)S(1)}, bf16[2,30,2,1152]{3,2,1,0:T(2,128)(2,1)S(1)}, u32[]{:S(2)}, u32[]{:S(2)}) collective-permute-start(bf16[2,30,2,1152]{3,2,1,0:T(2,128)(2,1)S(1)} %get-tuple-element.36), channel_id=1, source_target_pairs={{0,2},{2,4},{4,6},{1,3},{3,5},{5,7},{8,10},{10,12},{12,14},{9,11},... | collective-permute-start | bytes 829448 | tf_op jit(solution)/shard_map/ppermute | solution.py:25
  28.0 1.3 %collective-permute-start.5 = (bf16[2,30,2,1152]{3,2,1,0:T(2,128)(2,1)S(1)}, bf16[2,30,2,1152]{3,2,1,0:T(2,128)(2,1)S(1)}, u32[]{:S(2)}, u32[]{:S(2)}) collective-permute-start(bf16[2,30,2,1152]{3,2,1,0:T(2,128)(2,1)S(1)} %get-tuple-element.37), channel_id=1, source_target_pairs={{2,0},{4,2},{6,4},{3,1},{5,3},{7,5},{10,8},{12,10},{14,12},{11,9},... | collective-permute-start | bytes 829448 | tf_op jit(solution)/shard_map/ppermute | solution.py:25
  29.4 0.0 copy-done.3
  29.4 0.1 stack_broadcast_in_dim.2
  29.5 3.1 %late_cut.1 = (bf16[7,128,1024]{2,1,0:T(8,128)(2,1)}, bf16[7,128,1024]{2,1,0:T(8,128)(2,1)}) custom-call(bf16[2,16,128,1024]{3,2,1,0:T(8,128)(2,1)} %refs_4_.3), custom_call_target="tpu_custom_call" | custom-call | bytes 9000000 | tf_op jit(solution)/shard_map/late_cut/pallas_call | solution.py:368
  32.6 1.9 %collective-permute-start.3 = (bf16[7,128,1024]{2,1,0:T(8,128)(2,1)}, bf16[7,128,1024]{2,1,0:T(8,128)(2,1)S(1)}, u32[]{:S(2)}, u32[]{:S(2)}) collective-permute-start(bf16[7,128,1024]{2,1,0:T(8,128)(2,1)} %get-tuple-element.19), channel_id=1, source_target_pairs={{0,8},{8,16},{16,24},{1,9},{9,17},{17,25},{2,10},{10,18},{18,26},{... | collective-permute-start | bytes 5505032 | tf_op jit(solution)/shard_map/ppermute | solution.py:25
  34.5 0.0 collective-permute-done.6.refs_8_
  34.5 3.8 %collective-permute-start.4 = (bf16[7,128,1024]{2,1,0:T(8,128)(2,1)}, bf16[7,128,1024]{2,1,0:T(8,128)(2,1)S(1)}, u32[]{:S(2)}, u32[]{:S(2)}) collective-permute-start(bf16[7,128,1024]{2,1,0:T(8,128)(2,1)} %get-tuple-element.20), channel_id=1, source_target_pairs={{8,0},{16,8},{24,16},{9,1},{17,9},{25,17},{10,2},{18,10},{26,18},{... | collective-permute-start | bytes 5505032 | tf_op jit(solution)/shard_map/ppermute | solution.py:25
  38.4 0.0 collective-permute-done.5.refs_7_
  38.4 0.0 collective-permute-done.7.refs_3_
  38.4 0.0 collective-permute-done.8.refs_5_
  38.4 22.3 %slab_1.1 = (bf16[2,16,128,1024]{3,2,1,0:T(8,128)(2,1)}, bf16[128,256]{1,0:T(8,128)(2,1)S(1)}) custom-call(s32[6,128]{1,0:T(8,128)S(1)} %get-tuple-element.42.refs_0_, bf16[32,30]{1,0:T(8,128)(2,1)S(1)} %bitcast.29, bf16[160,144]{1,0:T(8,128)(2,1)S(1)} %pad_maximum_fusion.refs_2_, bf16[7,128,1024]{2,1,0:T(8,128)(2,1)} %collective-permute-done.7.refs_3_, ...), custom_call_target="tpu_custom_call" | custom-call | flops 20000000000 | bytes 16000000 | tf_op jit(solution)/shard_map/slab_1/pallas_call | solution.py:421
  60.7 5.6 %collective-permute-start.9 = (bf16[128,256]{1,0:T(8,128)(2,1)S(1)}, bf16[128,256]{1,0:T(8,128)(2,1)S(1)}, u32[]{:S(2)}, u32[]{:S(2)}) collective-permute-start(bf16[128,256]{1,0:T(8,128)(2,1)S(1)} %get-tuple-element.27), channel_id=1, source_target_pairs={{0,7},{1,6},{2,5},{3,4},{4,3},{5,2},{6,1},{7,0},{8,15},{9,14},{10,... | collective-permute-start | bytes 196616 | tf_op jit(solution)/shard_map/ppermute | solution.py:502
  66.3 0.0 collective-permute-done.3.refs_3_
  66.3 0.0 collective-permute-done.4.refs_5_
  66.3 21.8 %slab_0.1 = (bf16[2,16,128,1024]{3,2,1,0:T(8,128)(2,1)}, bf16[128,256]{1,0:T(8,128)(2,1)S(1)}) custom-call(s32[6,128]{1,0:T(8,128)S(1)} %get-tuple-element.43.refs_0_, bf16[32,30]{1,0:T(8,128)(2,1)S(1)} %bitcast.30, bf16[160,144]{1,0:T(8,128)(2,1)S(1)} %pad_maximum_fusion.refs_2_, ...), custom_call_target="tpu_custom_call", output_to_operand_aliasing={{0}: (9, {})} | custom-call | flops 20000000000 | bytes 16000000 | tf_op jit(solution)/shard_map/slab_0/pallas_call | solution.py:421
  88.2 0.0 collective-permute-done.9
  88.2 0.8 convolution_multiply_fusion
  (14 shorter events, 0.2 us)
Async XLA Ops:
  0.6 16.2 %copy-start = (f32[5,5]{1,0:T(8,128)S(1)}, f32[5,5]{1,0:T(8,128)}, u32[]{:S(2)}) copy-start(f32[5,5]{1,0:T(8,128)} %param.7) | copy-start | bytes 304
  0.6 16.5 %copy-start.1 = (s32[2,3,128]{2,0,1:T(2,128)S(1)}, s32[2,3,128]{2,0,1:T(2,128)}, u32[]{:S(2)}) copy-start(s32[2,3,128]{2,0,1:T(2,128)} %param.8) | copy-start | bytes 9220
  0.7 16.5 %copy-start.2 = (f32[15]{0:T(128)S(1)}, f32[15]{0:T(128)}, u32[]{:S(2)}) copy-start(f32[15]{0:T(128)} %param.6) | copy-start | bytes 184
  5.6 12.0 %collective-permute-start = (bf16[2,7,4,1152]{3,2,1,0:T(4,128)(2,1)}, bf16[2,7,4,1152]{3,2,1,0:T(4,128)(2,1)S(1)}, u32[]{:S(2)}, u32[]{:S(2)}) collective-permute-start(bf16[2,7,4,1152]{3,2,1,0:T(4,128)(2,1)} %get-tuple-element.15), channel_id=1, source_target_pairs={{0,8},{8,16},{16,24},{1,9},{9,17},{17,25},{2,10},{10,18},{18,26},{... | collective-permute-start | bytes 387080 | tf_op jit(solution)/shard_map/ppermute | solution.py:25
  7.5 11.3 %collective-permute-start.1 = (bf16[2,7,4,1152]{3,2,1,0:T(4,128)(2,1)}, bf16[2,7,4,1152]{3,2,1,0:T(4,128)(2,1)S(1)}, u32[]{:S(2)}, u32[]{:S(2)}) collective-permute-start(bf16[2,7,4,1152]{3,2,1,0:T(4,128)(2,1)} %get-tuple-element.17), channel_id=1, source_target_pairs={{8,0},{16,8},{24,16},{9,1},{17,9},{25,17},{10,2},{18,10},{26,18},{... | collective-permute-start | bytes 387080 | tf_op jit(solution)/shard_map/ppermute | solution.py:25
  11.2 27.2 %collective-permute-start.7 = (bf16[7,128,1024]{2,1,0:T(8,128)(2,1)}, bf16[7,128,1024]{2,1,0:T(8,128)(2,1)}, u32[]{:S(2)}, u32[]{:S(2)}) collective-permute-start(bf16[7,128,1024]{2,1,0:T(8,128)(2,1)} %get-tuple-element.22), channel_id=1, source_target_pairs={{0,8},{8,16},{16,24},{1,9},{9,17},{17,25},{2,10},{10,18},{18,26},{... | collective-permute-start | bytes 5505032 | tf_op jit(solution)/shard_map/ppermute | solution.py:25
  13.1 25.3 %collective-permute-start.8 = (bf16[7,128,1024]{2,1,0:T(8,128)(2,1)}, bf16[7,128,1024]{2,1,0:T(8,128)(2,1)}, u32[]{:S(2)}, u32[]{:S(2)}) collective-permute-start(bf16[7,128,1024]{2,1,0:T(8,128)(2,1)} %get-tuple-element.23), channel_id=1, source_target_pairs={{8,0},{16,8},{24,16},{9,1},{17,9},{25,17},{10,2},{18,10},{26,18},{... | collective-permute-start | bytes 5505032 | tf_op jit(solution)/shard_map/ppermute | solution.py:25
  18.9 4.0 %collective-permute-start.2 = (bf16[2,30,2,128]{3,2,1,0:T(2,128)(2,1)S(1)}, bf16[2,30,2,128]{3,2,1,0:T(2,128)(2,1)S(1)}, u32[]{:S(2)}, u32[]{:S(2)}) collective-permute-start(bf16[2,30,2,128]{3,2,1,0:T(2,128)(2,1)S(1)} %broadcast_select_fusion), channel_id=1, source_target_pairs={{0,1},{1,0},{2,3},{3,2},{4,5},{5,4},{6,7},{7,6},{8,9},{9,8},{10,11... | collective-permute-start | bytes 92168 | tf_op jit(solution)/shard_map/ppermute | solution.py:473
  20.7 8.7 %copy-start.3 = (s32[2,1]{0,1:T(1,128)S(1)}, s32[2,1]{0,1:T(1,128)}, u32[]{:S(2)}) copy-start(s32[2,1]{0,1:T(1,128)} %param.9) | copy-start | bytes 28
  24.5 10.0 %collective-permute-start.6 = (bf16[2,30,2,1152]{3,2,1,0:T(2,128)(2,1)S(1)}, bf16[2,30,2,1152]{3,2,1,0:T(2,128)(2,1)S(1)}, u32[]{:S(2)}, u32[]{:S(2)}) collective-permute-start(bf16[2,30,2,1152]{3,2,1,0:T(2,128)(2,1)S(1)} %get-tuple-element.36), channel_id=1, source_target_pairs={{0,2},{2,4},{4,6},{1,3},{3,5},{5,7},{8,10},{10,12},{12,14},{9,11},... | collective-permute-start | bytes 829448 | tf_op jit(solution)/shard_map/ppermute | solution.py:25
  28.0 10.3 %collective-permute-start.5 = (bf16[2,30,2,1152]{3,2,1,0:T(2,128)(2,1)S(1)}, bf16[2,30,2,1152]{3,2,1,0:T(2,128)(2,1)S(1)}, u32[]{:S(2)}, u32[]{:S(2)}) collective-permute-start(bf16[2,30,2,1152]{3,2,1,0:T(2,128)(2,1)S(1)} %get-tuple-element.37), channel_id=1, source_target_pairs={{2,0},{4,2},{6,4},{3,1},{5,3},{7,5},{10,8},{12,10},{14,12},{11,9},... | collective-permute-start | bytes 829448 | tf_op jit(solution)/shard_map/ppermute | solution.py:25
  32.6 33.7 %collective-permute-start.3 = (bf16[7,128,1024]{2,1,0:T(8,128)(2,1)}, bf16[7,128,1024]{2,1,0:T(8,128)(2,1)S(1)}, u32[]{:S(2)}, u32[]{:S(2)}) collective-permute-start(bf16[7,128,1024]{2,1,0:T(8,128)(2,1)} %get-tuple-element.19), channel_id=1, source_target_pairs={{0,8},{8,16},{16,24},{1,9},{9,17},{17,25},{2,10},{10,18},{18,26},{... | collective-permute-start | bytes 5505032 | tf_op jit(solution)/shard_map/ppermute | solution.py:25
  34.5 31.8 %collective-permute-start.4 = (bf16[7,128,1024]{2,1,0:T(8,128)(2,1)}, bf16[7,128,1024]{2,1,0:T(8,128)(2,1)S(1)}, u32[]{:S(2)}, u32[]{:S(2)}) collective-permute-start(bf16[7,128,1024]{2,1,0:T(8,128)(2,1)} %get-tuple-element.20), channel_id=1, source_target_pairs={{8,0},{16,8},{24,16},{9,1},{17,9},{25,17},{10,2},{18,10},{26,18},{... | collective-permute-start | bytes 5505032 | tf_op jit(solution)/shard_map/ppermute | solution.py:25
  60.7 27.4 %collective-permute-start.9 = (bf16[128,256]{1,0:T(8,128)(2,1)S(1)}, bf16[128,256]{1,0:T(8,128)(2,1)S(1)}, u32[]{:S(2)}, u32[]{:S(2)}) collective-permute-start(bf16[128,256]{1,0:T(8,128)(2,1)S(1)} %get-tuple-element.27), channel_id=1, source_target_pairs={{0,7},{1,6},{2,5},{3,4},{4,3},{5,2},{6,1},{7,0},{8,15},{9,14},{10,... | collective-permute-start | bytes 196616 | tf_op jit(solution)/shard_map/ppermute | solution.py:502
